TPU v7x, 512 devices: a whole 4x8x8 slice. The times are simulated.
512 devices in a mesh: row: 16 (over y, x_lo), col: 16 (over z, core), lag: 2 (over x_hi).
Axes of the slice: x: 4 (x_hi: 2, x_lo: 2; x = x_hi * 2 + x_lo), y: 8, z: 8, core: 2. Of those that a mesh axis runs over, the one named last changes fastest.
Arguments:
- trajectories: bfloat16 [16384, 4096], P(('row', 'col'), 'lag'), may hold values from -6 to 6
- pair_live: int32 [16, 16], replicated, may hold values from 0 to 1, as said below
Outputs:
- gram: bfloat16 [16384, 16384], P(('row', 'lag'), 'col')
Inputs may be any that keep to these rules, and one draw needn't show every extreme that they name: `pair_live`: Symmetric, with every diagonal entry 1.
All inputs are finite; a program needn't handle non-finite values.
Results may differ from a plain program's by a relative error of at most 0.0015.
Values may be sent and summed in bfloat16 or wider, within the bound.
No kernel may reach another device: no remote copies, remote signals or barrier semaphores. Data moves between devices by JAX's collectives and lax.ppermute only.
A program may use at most 64 MiB of HBM per device.

v0:
```python
import jax
import jax.numpy as jnp
from jax import lax
from jax.sharding import PartitionSpec as P


def from_root(value, axis, source):
    kept = jnp.where(lax.axis_index(axis) == source, value, 0).astype(value.dtype)
    return lax.psum(kept, axis)


def pair_distance(left, right, left_norm, right_norm):
    inner = lax.dot_general(
        left, right, (((1,), (1,)), ((), ())), preferred_element_type=jnp.float32
    )
    return left_norm[:, None] + right_norm[None, :] - 2.0 * inner


def squares(block):
    return jnp.sum(jnp.square(block.astype(jnp.float32)), axis=1)


def on_device(trajectories, pair_live):
    row_block = lax.all_gather(trajectories, "col", axis=0, tiled=True)
    col_block = from_root(row_block, "row", lax.axis_index("col"))
    live = pair_live[lax.axis_index("row"), lax.axis_index("col")]
    samples = trajectories.shape[1] * lax.axis_size("lag")
    row_norm = squares(row_block)
    col_norm = squares(col_block)
    dist = lax.psum_scatter(
        pair_distance(row_block, col_block, row_norm, col_norm),
        "lag",
        scatter_dimension=0,
        tiled=True,
    )
    gram = jnp.exp(-2.0 * dist / samples) * live.astype(jnp.float32)
    return gram.astype(jnp.bfloat16)


def solution(mesh):
    return jax.shard_map(
        on_device,
        mesh=mesh,
        in_specs=(P(("row", "col"), "lag"), P()),
        out_specs=P(("row", "lag"), "col"),
        check_vma=False,
    )
```

profile of v0, /device:TPU:6, one launch (start us, length us, event | category | flops | bytes accessed | tf_op | source)
XLA Modules:
  0.0 351.4 jit_solution(6171792190010791576)
XLA Ops:
  6.5 0.0 all-gather.2.cloned.1.call-start
  6.5 0.7 all-gather.2.cloned.1.call-update
  7.3 0.0 all-reduce.2.cloned.1.call-start
  7.3 52.5 %all-gather.2.cloned.1.call-done = bf16[1024,2048]{1,0:T(8,128)(2,1)} async-done(((bf16[64,2048]{1,0:T(8,128)(2,1)}), bf16[1024,2048]{1,0:T(8,128)(2,1)}) %all-gather.2.cloned.1.call-update) | async-done | bytes 4194320 | tf_op jit(solution)/shard_map/all_gather | solution.py:24
  59.8 2.3 broadcast_select_fusion
  62.0 0.0 all-reduce.2.cloned.1.call-update
  62.1 0.0 reduce-scatter.2.cloned.1.call-start
  62.1 3.1 multiply_reduce_fusion.1
  65.2 201.2 %all-reduce.2.cloned.1.call-done = bf16[1024,2048]{1,0:T(8,128)(2,1)} async-done(((bf16[1024,2048]{1,0:T(8,128)(2,1)}), bf16[1024,2048]{1,0:T(8,128)(2,1)}) %all-reduce.2.cloned.1.call-update) | async-done | bytes 4194320 | tf_op jit(solution)/shard_map/psum | solution.py:9
  266.4 0.0 copy-start
  266.4 3.2 multiply_reduce_fusion
  269.6 0.2 copy-done
  269.8 8.3 %bitcast_subtract_fusion = f32[1024,1024]{0,1:T(8,128)} fusion(bf16[1024,2048]{1,0:T(8,128)(2,1)} %all-reduce.2.cloned.1.call-done, bf16[1024,2048]{1,0:T(8,128)(2,1)S(1)} %copy-done, f32[1024]{0:T(1024)S(1)} %multiply_reduce_fusion, f32[1024]{0:T(1024)S(1)} %multiply_reduce_fusion.1), kind=kOutput, calls=%fused_computation.2 | convolution fusion | flops 4298113024 | bytes 12591104 | tf_op jit(solution)/shard_map/dot_general | solution.py:13
  278.1 0.0 reduce-scatter.2.cloned.1.call-update
  278.1 1.3 dynamic_slice.3
  280.1 61.6 %reduce-scatter.2.cloned.1.call-done = f32[512,1024]{0,1:T(8,128)} async-done(((f32[1024,1024]{0,1:T(8,128)}), f32[512,1024]{0,1:T(8,128)}) %reduce-scatter.2.cloned.1.call-update) | async-done | bytes 2097168 | tf_op jit(solution)/shard_map/reduce_scatter | solution.py:30
  341.7 1.9 multiply_convert_fusion
  343.6 1.3 copy.3
Async XLA Ops:
  6.5 53.2 %all-gather.2.cloned.1.call-start = ((), (), s32[]{:S(2)}) async-start(), calls=%async_computation.1 | async-start | bytes 4456448 | tf_op jit(solution)/shard_map/all_gather | solution.py:24
  7.3 259.1 %all-reduce.2.cloned.1.call-start = ((), (), s32[]{:S(2)}) async-start(), calls=%async_computation.2 | async-start | bytes 8388608 | tf_op jit(solution)/shard_map/psum | solution.py:9
  62.1 279.6 %reduce-scatter.2.cloned.1.call-start = ((), (), s32[]{:S(2)}) async-start(), calls=%async_computation.3 | async-start | bytes 6291456 | tf_op jit(solution)/shard_map/reduce_scatter | solution.py:30
  266.4 3.4 copy-start
Sparse Core Ops, SparseCore 0:
  9.5 50.2 all-gather.1
  62.7 203.6 all-reduce.1
  278.3 63.3 reduce-scatter.1
where the time goes:
time: 354 us; the launch traced here: 351 us
  waiting for transfers between devices  316 us (89%)
  between operations  13.8 us (4%)
  other arithmetic  10.5 us (3%)
  matrix products  8.28 us (2%)
    psum x1, waiting for transfers between devices, from_root(): return lax.psum(kept, axis)  201 us
    reduce_scatter x1, waiting for transfers between devices, on_device(): lax.psum_scatter(pair_distance(row_block, col_block, row_norm, col_norm),...  61.6 us
    all_gather x1, waiting for transfers between devices, on_device(): row_block = lax.all_gather(trajectories, 'col', axis=0, tiled=True)  52.5 us
    dot_general x1, matrix products, pair_distance(): lax.dot_general(left, right, (((1,), (1,)), ((), ())), preferred_element_...  8.28 us
  transfers between devices with their start and end apart: 3, of which 3 were waited for; matrix products, arithmetic and copies ran while one was open for 1% of the time, Pallas kernels for 0%

commit v1 on v0

v1 whole, which is shorter than its diff:
```python
import jax
import jax.numpy as jnp
from jax import lax
from jax.experimental import pallas as pl
from jax.experimental.pallas import tpu as pltpu
from jax.sharding import Mesh
from jax.sharding import PartitionSpec as P

AX = ("y", "xl", "z", "a", "xh")
N = 8
SUB = 64


def every():
    for y in range(N):
        for xl in range(2):
            for z in range(N):
                for a in range(2):
                    for xh in range(2):
                        yield y, xl, z, a, xh


def index(y, xl, z, a, xh):
    return (((y % N * 2 + xl) * N + z % N) * 2 + a) * 2 + xh


def pairs(target):
    return [(index(*d), index(*target(*d))) for d in every()]


def row_pairs(stage):
    def target(y, xl, z, a, half):
        k = 2 * z + a
        return y, xl, k % N, k // N, half ^ xl ^ stage

    return pairs(target)


def col_pairs(stage):
    def target(y, xl, z, a, half):
        return y + (z if a == 0 else -z), half ^ xl ^ stage, y, a, xl

    return pairs(target)


def shift_y(step):
    return pairs(lambda y, xl, z, a, xh: (y + step, xl, z, a, xh))


def swap_core():
    return pairs(lambda y, xl, z, a, xh: (y, xl, z, 1 - a, xh))


def exchange():
    return pairs(
        lambda y, xl, z, a, xh: (y, xl, z, a, xh) if a == xh else (y, xl, z, xh, a)
    )


def gram_kernel(where_ref, rows_hbm, *refs):
    own, mate = refs[0:5], refs[5:10]
    out_ref, rows, cols, row_norm, sem_rows, sem_cols = refs[10:]
    y, z, a, live = where_ref[0], where_ref[1], where_ref[2], where_ref[3]
    rows_copy = pltpu.make_async_copy(rows_hbm, rows, sem_rows)
    rows_copy.start()
    copies = []
    for side, group in enumerate((own, mate)):
        core = a if side == 0 else 1 - a
        for d in range(-3, 5):
            ref = group[abs(d)]
            start = SUB if d < 0 else 0
            there = y - d
            m = jnp.where(core == 0, there - z, z - there) & (N - 1)
            copy = pltpu.make_async_copy(
                ref.at[pl.ds(start, SUB), :],
                cols.at[m, pl.ds(pl.multiple_of(core * SUB, SUB), SUB), :],
                sem_cols.at[side * N + d + 3],
            )
            copy.start()
            copies.append(copy)
    rows_copy.wait()

    @pl.loop(0, rows.shape[0] // 32)
    def _(i):
        at = pl.ds(pl.multiple_of(i * 32, 32), 32)
        total = jnp.zeros((32, 128), jnp.float32)
        for c in range(rows.shape[1] // 128):
            x = rows[at, c * 128 : (c + 1) * 128].astype(jnp.float32)
            total += x * x
        row_norm[at, :] = jnp.broadcast_to(
            jnp.sum(total, axis=1, keepdims=True), (32, 128)
        )

    for copy in copies:
        copy.wait()
    scale = live.astype(jnp.float32)
    samples = rows.shape[1]

    @pl.loop(0, 4)
    def _(i):
        b = cols[pl.ds(i * 2, 2)].reshape(256, samples)
        inner = lax.dot_general(
            rows[...], b, (((1,), (1,)), ((), ())), preferred_element_type=jnp.float32
        )
        total = jnp.zeros((256, 128), jnp.float32)
        for c in range(samples // 128):
            x = b[:, c * 128 : (c + 1) * 128].astype(jnp.float32)
            total += x * x
        col_norm = jnp.sum(total.T, axis=0, keepdims=True)
        dist = row_norm[:, :1] + col_norm - 2.0 * inner
        gram = jnp.exp(dist * (-2.0 / samples)) * scale
        out_ref[:, pl.ds(pl.multiple_of(i * 256, 256), 256)] = gram.astype(jnp.bfloat16)


def gram_tile(where, rows, own, mate):
    samples = rows.shape[1]
    anywhere = pl.BlockSpec(memory_space=pl.ANY)
    return pl.pallas_call(
        gram_kernel,
        out_shape=jax.ShapeDtypeStruct((512, 1024), jnp.bfloat16),
        in_specs=[pl.BlockSpec(memory_space=pltpu.SMEM)] + [anywhere] * 11,
        out_specs=pl.BlockSpec(memory_space=pltpu.VMEM),
        scratch_shapes=[
            pltpu.VMEM((512, samples), jnp.bfloat16),
            pltpu.VMEM((N, 2 * SUB, samples), jnp.bfloat16),
            pltpu.VMEM((512, 128), jnp.float32),
            pltpu.SemaphoreType.DMA,
            pltpu.SemaphoreType.DMA((2 * N,)),
        ],
        compiler_params=pltpu.CompilerParams(vmem_limit_bytes=32 * 1024 * 1024),
        cost_estimate=pl.CostEstimate(
            flops=2 * 512 * 1024 * samples,
            bytes_accessed=13 * 1024 * 1024,
            transcendentals=512 * 1024,
        ),
    )(where, rows, *own, *mate)


def on_device(trajectories, pair_live):
    y, xl, z, a, xh = (lax.axis_index(name) for name in AX)
    live = pair_live[y * 2 + xl, z * 2 + xh]
    send = lambda value, to: lax.ppermute(value, AX, to)

    rows = jnp.concatenate([send(trajectories, row_pairs(s)) for s in range(2)], axis=1)
    rows = lax.all_gather(rows, "z", axis=0, tiled=True)
    cols = jnp.concatenate([send(trajectories, col_pairs(s)) for s in range(2)], axis=1)

    own = [cols]
    up = down = cols
    for step in range(4):
        if step == 3:
            up, down = up[: SUB // 2], down[SUB // 2 :]
        up, down = send(up, shift_y(1)), send(down, shift_y(-1))
        own.append(jnp.concatenate([up, down], axis=0))
    mate = [send(chunk, swap_core()) for chunk in own]

    where = jnp.stack([y, z, a, live]).astype(jnp.int32)
    return send(gram_tile(where, rows, own, mate), exchange())


def solution(mesh):
    fine = Mesh(mesh.devices.reshape(N, 2, N, 2, 2), AX)
    return jax.shard_map(
        on_device,
        mesh=fine,
        in_specs=(P(("y", "xl", "z", "a"), "xh"), P()),
        out_specs=P(("y", "xl", "xh"), ("z", "a")),
        check_vma=False,
    )
```

time: 354 us -> 178 us (0.50)
  the two profiles are of different devices: /device:TPU:6 before, /device:TPU:35 now
where the time goes in v1:
time: 178 us; the launch traced here: 177 us
  starting transfers between devices  86.4 us (49%)
  waiting for transfers between devices  58.9 us (33%)
  between operations  13.7 us (8%)
  Pallas kernels  9.08 us (5%)
  local copies, waits for them, and re-layouts  7.62 us (4%)
    ppermute x18, starting transfers between devices, on_device(): send = lambda value, to: lax.ppermute(value, AX, to)  86.4 us
    ppermute x18, waiting for transfers between devices, on_device(): send = lambda value, to: lax.ppermute(value, AX, to)  58.9 us
    pallas_call x1, Pallas kernels, gram_tile(): pl.pallas_call(gram_kernel, out_shape=jax.ShapeDtypeStruct((512, 1024), j...  9.08 us
    unnamed x8, local copies, waits for them, and re-layouts  4.74 us
  transfers between devices with their start and end apart: 19, of which 9 were waited for; matrix products, arithmetic and copies ran while one was open for 3% of the time, Pallas kernels for 0%

profile of v1, /device:TPU:35, one launch (start us, length us, event | category | flops | bytes accessed | tf_op | source)
XLA Modules:
  0.0 177.2 jit_solution(9707455978122510793)
XLA Ops:
  6.5 0.0 all-gather.2.cloned.1.call-start
  6.5 4.6 %collective-permute-start.1 = (bf16[64,2048]{1,0:T(8,128)(2,1)}, bf16[64,2048]{1,0:T(8,128)(2,1)S(1)}, u32[]{:S(2)}, u32[]{:S(2)}) collective-permute-start(bf16[64,2048]{1,0:T(8,128)(2,1)} %param.2), channel_id=1, source_target_pairs={{0,1},{1,0},{2,5},{3,4},{4,9},{5,8},{6,13},{7,12},{8,17},{9,16},{1... | collective-permute-start | bytes 786440 | tf_op jit(solution)/shard_map/ppermute | solution.py:142
  11.1 5.8 %collective-permute-start = (bf16[64,2048]{1,0:T(8,128)(2,1)}, bf16[64,2048]{1,0:T(8,128)(2,1)S(1)}, u32[]{:S(2)}, u32[]{:S(2)}) collective-permute-start(bf16[64,2048]{1,0:T(8,128)(2,1)} %param.2), channel_id=1, source_target_pairs={{0,0},{1,1},{2,4},{3,5},{4,8},{5,9},{6,12},{7,13},{8,16},{9,17},{1... | collective-permute-start | bytes 786440 | tf_op jit(solution)/shard_map/ppermute | solution.py:142
  16.9 5.0 %collective-permute-done.1 = bf16[64,2048]{1,0:T(8,128)(2,1)S(1)} collective-permute-done((bf16[64,2048]{1,0:T(8,128)(2,1)}, bf16[64,2048]{1,0:T(8,128)(2,1)S(1)}, u32[]{:S(2)}, u32[]{:S(2)}) %collective-permute-start.1) | collective-permute-done | bytes 262176 | tf_op jit(solution)/shard_map/ppermute | solution.py:142
  22.0 6.6 %collective-permute-done = bf16[64,2048]{1,0:T(8,128)(2,1)S(1)} collective-permute-done((bf16[64,2048]{1,0:T(8,128)(2,1)}, bf16[64,2048]{1,0:T(8,128)(2,1)S(1)}, u32[]{:S(2)}, u32[]{:S(2)}) %collective-permute-start) | collective-permute-done | bytes 262176 | tf_op jit(solution)/shard_map/ppermute | solution.py:142
  28.6 0.8 pad_maximum_fusion
  29.4 0.0 all-gather.2.cloned.1.call-update
  29.5 7.9 %collective-permute-start.2 = (bf16[64,2048]{1,0:T(8,128)(2,1)}, bf16[64,2048]{1,0:T(8,128)(2,1)S(1)}, u32[]{:S(2)}, u32[]{:S(2)}) collective-permute-start(bf16[64,2048]{1,0:T(8,128)(2,1)} %param.2), channel_id=1, source_target_pairs={{0,0},{1,32},{2,2},{3,34},{4,64},{5,96},{6,450},{7,482},{8,128},{9... | collective-permute-start | bytes 786440 | tf_op jit(solution)/shard_map/ppermute | solution.py:142
  37.4 1.9 %collective-permute-start.3 = (bf16[64,2048]{1,0:T(8,128)(2,1)}, bf16[64,2048]{1,0:T(8,128)(2,1)S(1)}, u32[]{:S(2)}, u32[]{:S(2)}) collective-permute-start(bf16[64,2048]{1,0:T(8,128)(2,1)} %param.2), channel_id=1, source_target_pairs={{0,32},{1,0},{2,34},{3,2},{4,96},{5,64},{6,482},{7,450},{8,160},{9... | collective-permute-start | bytes 786440 | tf_op jit(solution)/shard_map/ppermute | solution.py:142
  39.3 12.0 %collective-permute-done.2 = bf16[64,2048]{1,0:T(8,128)(2,1)S(1)} collective-permute-done((bf16[64,2048]{1,0:T(8,128)(2,1)}, bf16[64,2048]{1,0:T(8,128)(2,1)S(1)}, u32[]{:S(2)}, u32[]{:S(2)}) %collective-permute-start.2) | collective-permute-done | bytes 262176 | tf_op jit(solution)/shard_map/ppermute | solution.py:142
  51.3 0.7 constant_dynamic-update-slice_fusion.1
  52.0 10.8 %collective-permute-done.3 = bf16[64,2048]{1,0:T(8,128)(2,1)S(1)} collective-permute-done((bf16[64,2048]{1,0:T(8,128)(2,1)}, bf16[64,2048]{1,0:T(8,128)(2,1)S(1)}, u32[]{:S(2)}, u32[]{:S(2)}) %collective-permute-start.3) | collective-permute-done | bytes 262176 | tf_op jit(solution)/shard_map/ppermute | solution.py:142
  62.8 0.7 constant_dynamic-update-slice_fusion.refs_0_
  63.6 14.7 %collective-permute-start.5 = (bf16[64,4096]{1,0:T(8,128)(2,1)}, bf16[64,4096]{1,0:T(8,128)(2,1)S(1)}, u32[]{:S(2)}, u32[]{:S(2)}) collective-permute-start(bf16[64,4096]{1,0:T(8,128)(2,1)} %constant_dynamic-update-slice_fusion.refs_0_), channel_id=1, source_target_pairs={{0,448},{1,449},{2,450},{3,451},{4,452},{5,453},{6,454},{7,455},{8... | collective-permute-start | bytes 1572872 | tf_op jit(solution)/shard_map/ppermute | solution.py:142
  78.3 1.9 %collective-permute-start.4 = (bf16[64,4096]{1,0:T(8,128)(2,1)}, bf16[64,4096]{1,0:T(8,128)(2,1)S(1)}, u32[]{:S(2)}, u32[]{:S(2)}) collective-permute-start(bf16[64,4096]{1,0:T(8,128)(2,1)} %constant_dynamic-update-slice_fusion.refs_0_), channel_id=1, source_target_pairs={{0,64},{1,65},{2,66},{3,67},{4,68},{5,69},{6,70},{7,71},{8,72},{9,... | collective-permute-start | bytes 1572872 | tf_op jit(solution)/shard_map/ppermute | solution.py:142
  80.2 4.8 %collective-permute-start.12 = (bf16[64,4096]{1,0:T(8,128)(2,1)}, bf16[64,4096]{1,0:T(8,128)(2,1)}, u32[]{:S(2)}, u32[]{:S(2)}) collective-permute-start(bf16[64,4096]{1,0:T(8,128)(2,1)} %constant_dynamic-update-slice_fusion.refs_0_), channel_id=1, source_target_pairs={{0,2},{1,3},{2,0},{3,1},{4,6},{5,7},{6,4},{7,5},{8,10},{9,11},{10,... | collective-permute-start | bytes 1572872 | tf_op jit(solution)/shard_map/ppermute | solution.py:142
  85.1 2.1 %collective-permute-done.5 = bf16[64,4096]{1,0:T(8,128)(2,1)S(1)} collective-permute-done((bf16[64,4096]{1,0:T(8,128)(2,1)}, bf16[64,4096]{1,0:T(8,128)(2,1)S(1)}, u32[]{:S(2)}, u32[]{:S(2)}) %collective-permute-start.5) | collective-permute-done | bytes 524320 | tf_op jit(solution)/shard_map/ppermute | solution.py:142
  87.2 5.3 %collective-permute-start.7 = (bf16[64,4096]{1,0:T(8,128)(2,1)S(1)}, bf16[64,4096]{1,0:T(8,128)(2,1)S(1)}, u32[]{:S(2)}, u32[]{:S(2)}) collective-permute-start(bf16[64,4096]{1,0:T(8,128)(2,1)S(1)} %collective-permute-done.5), channel_id=1, source_target_pairs={{0,448},{1,449},{2,450},{3,451},{4,452},{5,453},{6,454},{7,455},{8... | collective-permute-start | bytes 1572872 | tf_op jit(solution)/shard_map/ppermute | solution.py:142
  92.5 0.0 collective-permute-done.4
  92.5 1.9 %collective-permute-start.6 = (bf16[64,4096]{1,0:T(8,128)(2,1)S(1)}, bf16[64,4096]{1,0:T(8,128)(2,1)S(1)}, u32[]{:S(2)}, u32[]{:S(2)}) collective-permute-start(bf16[64,4096]{1,0:T(8,128)(2,1)S(1)} %collective-permute-done.4), channel_id=1, source_target_pairs={{0,64},{1,65},{2,66},{3,67},{4,68},{5,69},{6,70},{7,71},{8,72},{9,... | collective-permute-start | bytes 1572872 | tf_op jit(solution)/shard_map/ppermute | solution.py:142
  94.5 5.6 %collective-permute-start.13 = (bf16[128,4096]{1,0:T(8,128)(2,1)S(1)}, bf16[128,4096]{1,0:T(8,128)(2,1)}, u32[]{:S(2)}, u32[]{:S(2)}) collective-permute-start(bf16[128,4096]{1,0:T(8,128)(2,1)S(1)} %constant_dynamic-update-slice_fusion.2.refs_1_), channel_id=1, source_target_pairs={{0,2},{1,3},{2,0},{3,1},{4,6},{5,7},{6,4},{7,5},{8,10},{9,11},{10,... | collective-permute-start | bytes 3145736 | tf_op jit(solution)/shard_map/ppermute | solution.py:142
  100.2 0.1 collective-permute-done.7
  100.3 5.4 %collective-permute-start.9 = (bf16[64,4096]{1,0:T(8,128)(2,1)S(1)}, bf16[64,4096]{1,0:T(8,128)(2,1)S(1)}, u32[]{:S(2)}, u32[]{:S(2)}) collective-permute-start(bf16[64,4096]{1,0:T(8,128)(2,1)S(1)} %collective-permute-done.7), channel_id=1, source_target_pairs={{0,448},{1,449},{2,450},{3,451},{4,452},{5,453},{6,454},{7,455},{8... | collective-permute-start | bytes 1572872 | tf_op jit(solution)/shard_map/ppermute | solution.py:142
  105.7 0.0 collective-permute-done.6
  105.7 1.9 %collective-permute-start.8 = (bf16[64,4096]{1,0:T(8,128)(2,1)S(1)}, bf16[64,4096]{1,0:T(8,128)(2,1)S(1)}, u32[]{:S(2)}, u32[]{:S(2)}) collective-permute-start(bf16[64,4096]{1,0:T(8,128)(2,1)S(1)} %collective-permute-done.6), channel_id=1, source_target_pairs={{0,64},{1,65},{2,66},{3,67},{4,68},{5,69},{6,70},{7,71},{8,72},{9,... | collective-permute-start | bytes 1572872 | tf_op jit(solution)/shard_map/ppermute | solution.py:142
  107.7 6.5 %collective-permute-start.14 = (bf16[128,4096]{1,0:T(8,128)(2,1)S(1)}, bf16[128,4096]{1,0:T(8,128)(2,1)}, u32[]{:S(2)}, u32[]{:S(2)}) collective-permute-start(bf16[128,4096]{1,0:T(8,128)(2,1)S(1)} %constant_dynamic-update-slice_fusion.4.refs_2_), channel_id=1, source_target_pairs={{0,2},{1,3},{2,0},{3,1},{4,6},{5,7},{6,4},{7,5},{8,10},{9,11},{10,... | collective-permute-start | bytes 3145736 | tf_op jit(solution)/shard_map/ppermute | solution.py:142
  114.2 0.0 collective-permute-done.9
  114.2 4.9 %collective-permute-start.11 = (bf16[32,4096]{1,0:T(8,128)(2,1)S(1)}, bf16[32,4096]{1,0:T(8,128)(2,1)S(1)}, u32[]{:S(2)}, u32[]{:S(2)}) collective-permute-start(bf16[32,4096]{1,0:T(8,128)(2,1)S(1)} %slice.9), channel_id=1, source_target_pairs={{0,448},{1,449},{2,450},{3,451},{4,452},{5,453},{6,454},{7,455},{8... | collective-permute-start | bytes 786440 | tf_op jit(solution)/shard_map/ppermute | solution.py:142
  119.1 0.0 collective-permute-done.8
  119.1 1.9 %collective-permute-start.10 = (bf16[32,4096]{1,0:T(8,128)(2,1)S(1)}, bf16[32,4096]{1,0:T(8,128)(2,1)S(1)}, u32[]{:S(2)}, u32[]{:S(2)}) collective-permute-start(bf16[32,4096]{1,0:T(8,128)(2,1)S(1)} %slice.8), channel_id=1, source_target_pairs={{0,64},{1,65},{2,66},{3,67},{4,68},{5,69},{6,70},{7,71},{8,72},{9,... | collective-permute-start | bytes 786440 | tf_op jit(solution)/shard_map/ppermute | solution.py:142
  121.1 6.3 %collective-permute-done.10 = bf16[32,4096]{1,0:T(8,128)(2,1)S(1)} collective-permute-done((bf16[32,4096]{1,0:T(8,128)(2,1)S(1)}, bf16[32,4096]{1,0:T(8,128)(2,1)S(1)}, u32[]{:S(2)}, u32[]{:S(2)}) %collective-permute-start.10) | collective-permute-done | bytes 262176 | tf_op jit(solution)/shard_map/ppermute | solution.py:142
  127.4 7.4 %collective-permute-start.15 = (bf16[128,4096]{1,0:T(8,128)(2,1)S(1)}, bf16[128,4096]{1,0:T(8,128)(2,1)}, u32[]{:S(2)}, u32[]{:S(2)}) collective-permute-start(bf16[128,4096]{1,0:T(8,128)(2,1)S(1)} %constant_dynamic-update-slice_fusion.6.refs_3_), channel_id=1, source_target_pairs={{0,2},{1,3},{2,0},{3,1},{4,6},{5,7},{6,4},{7,5},{8,10},{9,11},{10,... | collective-permute-start | bytes 3145736 | tf_op jit(solution)/shard_map/ppermute | solution.py:142
  134.8 0.7 constant_dynamic-update-slice_fusion.9
  135.6 0.0 collective-permute-done.11
  135.6 0.7 constant_dynamic-update-slice_fusion.8.refs_4_
  136.3 1.9 %collective-permute-start.16 = (bf16[64,4096]{1,0:T(8,128)(2,1)}, bf16[64,4096]{1,0:T(8,128)(2,1)}, u32[]{:S(2)}, u32[]{:S(2)}) collective-permute-start(bf16[64,4096]{1,0:T(8,128)(2,1)} %constant_dynamic-update-slice_fusion.8.refs_4_), channel_id=1, source_target_pairs={{0,2},{1,3},{2,0},{3,1},{4,6},{5,7},{6,4},{7,5},{8,10},{9,11},{10,... | collective-permute-start | bytes 1572872 | tf_op jit(solution)/shard_map/ppermute | solution.py:142
  138.2 1.3 dynamic_slice.3
  139.5 0.7 pad_add_fusion.where_ref
  140.2 0.0 collective-permute-done.12.refs_5_
  140.2 0.0 collective-permute-done.13.refs_6_
  140.2 0.0 collective-permute-done.14.refs_7_
  140.2 0.3 collective-permute-done.16.refs_9_
  140.4 0.0 collective-permute-done.15.refs_8_
  140.4 0.0 all-gather.2.cloned.1.call-done.rows_hbm
  140.4 0.0 copy-start
  140.4 2.2 %copy-done = bf16[512,4096]{1,0:T(8,128)(2,1)S(1)} copy-done((bf16[512,4096]{1,0:T(8,128)(2,1)S(1)}, bf16[512,4096]{1,0:T(8,128)(2,1)}, u32[]{:S(2)}) %copy-start) | copy-done | bytes 4194328
  142.6 9.1 %shard_map.28 = bf16[512,1024]{1,0:T(8,128)(2,1)S(1)} custom-call(s32[4]{0:T(128)S(1)} %pad_add_fusion.where_ref, bf16[512,4096]{1,0:T(8,128)(2,1)S(1)} %copy-done, bf16[64,4096]{1,0:T(8,128)(2,1)} %constant_dynamic-update-slice_fusion.refs_0_, bf16[128,4096]{1,0:T(8,128)(2,1)S(1)} %constant_dynamic-update-slice_fusion.2.refs_1_, ...), custom_call_target="tpu_custom_call" | custom-call | flops 4294967296 | bytes 13631488 | tf_op jit(solution)/shard_map/pallas_call | solution.py:118
  151.7 1.9 %collective-permute-start.17 = (bf16[512,1024]{1,0:T(8,128)(2,1)S(1)}, bf16[512,1024]{1,0:T(8,128)(2,1)S(1)}, u32[]{:S(2)}, u32[]{:S(2)}) collective-permute-start(bf16[512,1024]{1,0:T(8,128)(2,1)S(1)} %shard_map.28), channel_id=1, source_target_pairs={{0,0},{1,2},{2,1},{3,3},{4,4},{5,6},{6,5},{7,7},{8,8},{9,10},{10,9... | collective-permute-start | bytes 3145736 | tf_op jit(solution)/shard_map/ppermute | solution.py:142
  153.7 15.7 %collective-permute-done.17 = bf16[512,1024]{1,0:T(8,128)(2,1)S(1)} collective-permute-done((bf16[512,1024]{1,0:T(8,128)(2,1)S(1)}, bf16[512,1024]{1,0:T(8,128)(2,1)S(1)}, u32[]{:S(2)}, u32[]{:S(2)}) %collective-permute-start.17) | collective-permute-done | bytes 1048608 | tf_op jit(solution)/shard_map/ppermute | solution.py:142
  169.3 1.0 copy.9
  (8 shorter events, 0.3 us)
Async XLA Ops:
  6.5 133.9 %all-gather.2.cloned.1.call-start = ((), (), s32[]{:S(2)}) async-start(), calls=%async_computation | async-start | bytes 4718592 | tf_op jit(solution)/shard_map/all_gather | solution.py:145
  6.5 15.4 %collective-permute-start.1 = (bf16[64,2048]{1,0:T(8,128)(2,1)}, bf16[64,2048]{1,0:T(8,128)(2,1)S(1)}, u32[]{:S(2)}, u32[]{:S(2)}) collective-permute-start(bf16[64,2048]{1,0:T(8,128)(2,1)} %param.2), channel_id=1, source_target_pairs={{0,1},{1,0},{2,5},{3,4},{4,9},{5,8},{6,13},{7,12},{8,17},{9,16},{1... | collective-permute-start | bytes 786440 | tf_op jit(solution)/shard_map/ppermute | solution.py:142
  11.1 17.5 %collective-permute-start = (bf16[64,2048]{1,0:T(8,128)(2,1)}, bf16[64,2048]{1,0:T(8,128)(2,1)S(1)}, u32[]{:S(2)}, u32[]{:S(2)}) collective-permute-start(bf16[64,2048]{1,0:T(8,128)(2,1)} %param.2), channel_id=1, source_target_pairs={{0,0},{1,1},{2,4},{3,5},{4,8},{5,9},{6,12},{7,13},{8,16},{9,17},{1... | collective-permute-start | bytes 786440 | tf_op jit(solution)/shard_map/ppermute | solution.py:142
  29.5 21.8 %collective-permute-start.2 = (bf16[64,2048]{1,0:T(8,128)(2,1)}, bf16[64,2048]{1,0:T(8,128)(2,1)S(1)}, u32[]{:S(2)}, u32[]{:S(2)}) collective-permute-start(bf16[64,2048]{1,0:T(8,128)(2,1)} %param.2), channel_id=1, source_target_pairs={{0,0},{1,32},{2,2},{3,34},{4,64},{5,96},{6,450},{7,482},{8,128},{9... | collective-permute-start | bytes 786440 | tf_op jit(solution)/shard_map/ppermute | solution.py:142
  37.4 25.4 %collective-permute-start.3 = (bf16[64,2048]{1,0:T(8,128)(2,1)}, bf16[64,2048]{1,0:T(8,128)(2,1)S(1)}, u32[]{:S(2)}, u32[]{:S(2)}) collective-permute-start(bf16[64,2048]{1,0:T(8,128)(2,1)} %param.2), channel_id=1, source_target_pairs={{0,32},{1,0},{2,34},{3,2},{4,96},{5,64},{6,482},{7,450},{8,160},{9... | collective-permute-start | bytes 786440 | tf_op jit(solution)/shard_map/ppermute | solution.py:142
  63.6 23.6 %collective-permute-start.5 = (bf16[64,4096]{1,0:T(8,128)(2,1)}, bf16[64,4096]{1,0:T(8,128)(2,1)S(1)}, u32[]{:S(2)}, u32[]{:S(2)}) collective-permute-start(bf16[64,4096]{1,0:T(8,128)(2,1)} %constant_dynamic-update-slice_fusion.refs_0_), channel_id=1, source_target_pairs={{0,448},{1,449},{2,450},{3,451},{4,452},{5,453},{6,454},{7,455},{8... | collective-permute-start | bytes 1572872 | tf_op jit(solution)/shard_map/ppermute | solution.py:142
  78.3 14.2 %collective-permute-start.4 = (bf16[64,4096]{1,0:T(8,128)(2,1)}, bf16[64,4096]{1,0:T(8,128)(2,1)S(1)}, u32[]{:S(2)}, u32[]{:S(2)}) collective-permute-start(bf16[64,4096]{1,0:T(8,128)(2,1)} %constant_dynamic-update-slice_fusion.refs_0_), channel_id=1, source_target_pairs={{0,64},{1,65},{2,66},{3,67},{4,68},{5,69},{6,70},{7,71},{8,72},{9,... | collective-permute-start | bytes 1572872 | tf_op jit(solution)/shard_map/ppermute | solution.py:142
  80.2 59.9 %collective-permute-start.12 = (bf16[64,4096]{1,0:T(8,128)(2,1)}, bf16[64,4096]{1,0:T(8,128)(2,1)}, u32[]{:S(2)}, u32[]{:S(2)}) collective-permute-start(bf16[64,4096]{1,0:T(8,128)(2,1)} %constant_dynamic-update-slice_fusion.refs_0_), channel_id=1, source_target_pairs={{0,2},{1,3},{2,0},{3,1},{4,6},{5,7},{6,4},{7,5},{8,10},{9,11},{10,... | collective-permute-start | bytes 1572872 | tf_op jit(solution)/shard_map/ppermute | solution.py:142
  87.2 13.1 %collective-permute-start.7 = (bf16[64,4096]{1,0:T(8,128)(2,1)S(1)}, bf16[64,4096]{1,0:T(8,128)(2,1)S(1)}, u32[]{:S(2)}, u32[]{:S(2)}) collective-permute-start(bf16[64,4096]{1,0:T(8,128)(2,1)S(1)} %collective-permute-done.5), channel_id=1, source_target_pairs={{0,448},{1,449},{2,450},{3,451},{4,452},{5,453},{6,454},{7,455},{8... | collective-permute-start | bytes 1572872 | tf_op jit(solution)/shard_map/ppermute | solution.py:142
  92.5 13.2 %collective-permute-start.6 = (bf16[64,4096]{1,0:T(8,128)(2,1)S(1)}, bf16[64,4096]{1,0:T(8,128)(2,1)S(1)}, u32[]{:S(2)}, u32[]{:S(2)}) collective-permute-start(bf16[64,4096]{1,0:T(8,128)(2,1)S(1)} %collective-permute-done.4), channel_id=1, source_target_pairs={{0,64},{1,65},{2,66},{3,67},{4,68},{5,69},{6,70},{7,71},{8,72},{9,... | collective-permute-start | bytes 1572872 | tf_op jit(solution)/shard_map/ppermute | solution.py:142
  94.5 45.6 %collective-permute-start.13 = (bf16[128,4096]{1,0:T(8,128)(2,1)S(1)}, bf16[128,4096]{1,0:T(8,128)(2,1)}, u32[]{:S(2)}, u32[]{:S(2)}) collective-permute-start(bf16[128,4096]{1,0:T(8,128)(2,1)S(1)} %constant_dynamic-update-slice_fusion.2.refs_1_), channel_id=1, source_target_pairs={{0,2},{1,3},{2,0},{3,1},{4,6},{5,7},{6,4},{7,5},{8,10},{9,11},{10,... | collective-permute-start | bytes 3145736 | tf_op jit(solution)/shard_map/ppermute | solution.py:142
  100.3 13.9 %collective-permute-start.9 = (bf16[64,4096]{1,0:T(8,128)(2,1)S(1)}, bf16[64,4096]{1,0:T(8,128)(2,1)S(1)}, u32[]{:S(2)}, u32[]{:S(2)}) collective-permute-start(bf16[64,4096]{1,0:T(8,128)(2,1)S(1)} %collective-permute-done.7), channel_id=1, source_target_pairs={{0,448},{1,449},{2,450},{3,451},{4,452},{5,453},{6,454},{7,455},{8... | collective-permute-start | bytes 1572872 | tf_op jit(solution)/shard_map/ppermute | solution.py:142
  105.7 13.4 %collective-permute-start.8 = (bf16[64,4096]{1,0:T(8,128)(2,1)S(1)}, bf16[64,4096]{1,0:T(8,128)(2,1)S(1)}, u32[]{:S(2)}, u32[]{:S(2)}) collective-permute-start(bf16[64,4096]{1,0:T(8,128)(2,1)S(1)} %collective-permute-done.6), channel_id=1, source_target_pairs={{0,64},{1,65},{2,66},{3,67},{4,68},{5,69},{6,70},{7,71},{8,72},{9,... | collective-permute-start | bytes 1572872 | tf_op jit(solution)/shard_map/ppermute | solution.py:142
  107.7 32.5 %collective-permute-start.14 = (bf16[128,4096]{1,0:T(8,128)(2,1)S(1)}, bf16[128,4096]{1,0:T(8,128)(2,1)}, u32[]{:S(2)}, u32[]{:S(2)}) collective-permute-start(bf16[128,4096]{1,0:T(8,128)(2,1)S(1)} %constant_dynamic-update-slice_fusion.4.refs_2_), channel_id=1, source_target_pairs={{0,2},{1,3},{2,0},{3,1},{4,6},{5,7},{6,4},{7,5},{8,10},{9,11},{10,... | collective-permute-start | bytes 3145736 | tf_op jit(solution)/shard_map/ppermute | solution.py:142
  114.2 21.4 %collective-permute-start.11 = (bf16[32,4096]{1,0:T(8,128)(2,1)S(1)}, bf16[32,4096]{1,0:T(8,128)(2,1)S(1)}, u32[]{:S(2)}, u32[]{:S(2)}) collective-permute-start(bf16[32,4096]{1,0:T(8,128)(2,1)S(1)} %slice.9), channel_id=1, source_target_pairs={{0,448},{1,449},{2,450},{3,451},{4,452},{5,453},{6,454},{7,455},{8... | collective-permute-start | bytes 786440 | tf_op jit(solution)/shard_map/ppermute | solution.py:142
  119.1 8.3 %collective-permute-start.10 = (bf16[32,4096]{1,0:T(8,128)(2,1)S(1)}, bf16[32,4096]{1,0:T(8,128)(2,1)S(1)}, u32[]{:S(2)}, u32[]{:S(2)}) collective-permute-start(bf16[32,4096]{1,0:T(8,128)(2,1)S(1)} %slice.8), channel_id=1, source_target_pairs={{0,64},{1,65},{2,66},{3,67},{4,68},{5,69},{6,70},{7,71},{8,72},{9,... | collective-permute-start | bytes 786440 | tf_op jit(solution)/shard_map/ppermute | solution.py:142
  127.4 13.0 %collective-permute-start.15 = (bf16[128,4096]{1,0:T(8,128)(2,1)S(1)}, bf16[128,4096]{1,0:T(8,128)(2,1)}, u32[]{:S(2)}, u32[]{:S(2)}) collective-permute-start(bf16[128,4096]{1,0:T(8,128)(2,1)S(1)} %constant_dynamic-update-slice_fusion.6.refs_3_), channel_id=1, source_target_pairs={{0,2},{1,3},{2,0},{3,1},{4,6},{5,7},{6,4},{7,5},{8,10},{9,11},{10,... | collective-permute-start | bytes 3145736 | tf_op jit(solution)/shard_map/ppermute | solution.py:142
  136.3 4.1 %collective-permute-start.16 = (bf16[64,4096]{1,0:T(8,128)(2,1)}, bf16[64,4096]{1,0:T(8,128)(2,1)}, u32[]{:S(2)}, u32[]{:S(2)}) collective-permute-start(bf16[64,4096]{1,0:T(8,128)(2,1)} %constant_dynamic-update-slice_fusion.8.refs_4_), channel_id=1, source_target_pairs={{0,2},{1,3},{2,0},{3,1},{4,6},{5,7},{6,4},{7,5},{8,10},{9,11},{10,... | collective-permute-start | bytes 1572872 | tf_op jit(solution)/shard_map/ppermute | solution.py:142
  140.4 2.2 %copy-start = (bf16[512,4096]{1,0:T(8,128)(2,1)S(1)}, bf16[512,4096]{1,0:T(8,128)(2,1)}, u32[]{:S(2)}) copy-start(bf16[512,4096]{1,0:T(8,128)(2,1)} %all-gather.2.cloned.1.call-done.rows_hbm) | copy-start | bytes 12582916
  151.7 17.6 %collective-permute-start.17 = (bf16[512,1024]{1,0:T(8,128)(2,1)S(1)}, bf16[512,1024]{1,0:T(8,128)(2,1)S(1)}, u32[]{:S(2)}, u32[]{:S(2)}) collective-permute-start(bf16[512,1024]{1,0:T(8,128)(2,1)S(1)} %shard_map.28), channel_id=1, source_target_pairs={{0,0},{1,2},{2,1},{3,3},{4,4},{5,6},{6,5},{7,7},{8,8},{9,10},{10,9... | collective-permute-start | bytes 3145736 | tf_op jit(solution)/shard_map/ppermute | solution.py:142
Sparse Core Ops, SparseCore 0:
  29.6 75.1 all-gather.1

commit v2 on v1

v2 whole, which is shorter than its diff:
```python
import jax
import jax.numpy as jnp
from jax import lax
from jax.experimental import pallas as pl
from jax.experimental.pallas import tpu as pltpu
from jax.sharding import Mesh
from jax.sharding import PartitionSpec as P

AX = ("y", "xl", "z", "a", "xh")
N = 8
SUB = 64
HALF = N * SUB
SHIFT = ((0, 4), (1, -1), (2, -2), (3, -3))


def index(y, xl, z, a, xh):
    return (((y % N * 2 + xl) * N + z % N) * 2 + a) * 2 + xh


def pairs(target):
    every = [
        (y, xl, z, a, xh)
        for y in range(N)
        for xl in range(2)
        for z in range(N)
        for a in range(2)
        for xh in range(2)
    ]
    return [(index(*d), index(*target(*d))) for d in every]


def col_pairs(stage):
    def target(y, xl, z, a, half):
        part = z // 4
        return y + SHIFT[z % 4][a], half ^ part ^ stage, y, xl, part

    return pairs(target)


def shift_z(step):
    return pairs(lambda y, xl, z, a, xh: (y, xl, z + step, a, xh))


def swap_core():
    return pairs(lambda y, xl, z, a, xh: (y, xl, z, 1 - a, xh))


def swap_lag():
    return pairs(lambda y, xl, z, a, xh: (y, xl, z, a, 1 - xh))


def chunks(own, mate):
    for d in range(-3, 5):
        step, first = abs(d), SUB if d < 0 else 0
        yield own[step], first, d, 0
        if step == 0:
            yield mate[0], 0, d, 1
        elif step < 3:
            yield mate[0], SUB + (step - 1) * 2 * SUB + first, d, 1
        else:
            yield mate[step - 2], first, d, 1


def gram_kernel(where_ref, cols_hbm, *refs):
    own, mate = refs[0:5], refs[5:8]
    out_ref, rows, cols, row_norm, sem_rows, sem_cols = refs[8:]
    y, z, a, half, live = (where_ref[i] for i in range(5))
    col_copies = []
    for there in range(N):
        o = (there - z) & (N - 1)
        j = jnp.where(o < 4, 2 * o, (17 - 2 * o) & (N - 1))
        copy = pltpu.make_async_copy(
            cols_hbm.at[pl.ds(there * SUB, SUB), :],
            cols.at[pl.ds(pl.multiple_of(j * SUB, SUB), SUB), :],
            sem_cols.at[there],
        )
        copy.start()
        col_copies.append(copy)
    row_copies = []
    for n, (ref, first, d, other) in enumerate(chunks(own, mate)):
        there = (z - d) & (N - 1)
        core = a if other == 0 else 1 - a
        at = (2 * there + core) & (N - 1)
        copy = pltpu.make_async_copy(
            ref.at[pl.ds(first, SUB), :],
            rows.at[pl.ds(pl.multiple_of(at * SUB, SUB), SUB), :],
            sem_rows.at[n],
        )
        mine = there // 4 == half
        pl.when(mine)(copy.start)
        row_copies.append((mine, copy))
    for mine, copy in row_copies:
        pl.when(mine)(copy.wait)

    @pl.loop(0, HALF // 32)
    def _(i):
        at = pl.ds(pl.multiple_of(i * 32, 32), 32)
        total = jnp.zeros((32, 128), jnp.float32)
        for c in range(rows.shape[1] // 128):
            x = rows[at, c * 128 : (c + 1) * 128].astype(jnp.float32)
            total += x * x
        row_norm[at, :] = jnp.broadcast_to(
            jnp.sum(total, axis=1, keepdims=True), (32, 128)
        )

    for copy in col_copies:
        copy.wait()
    scale = live.astype(jnp.float32)
    samples = rows.shape[1]

    @pl.loop(0, HALF // 256)
    def _(i):
        at = pl.ds(pl.multiple_of(i * 256, 256), 256)
        b = cols[at, :]
        inner = lax.dot_general(
            rows[...], b, (((1,), (1,)), ((), ())), preferred_element_type=jnp.float32
        )
        total = jnp.zeros((256, 128), jnp.float32)
        for c in range(samples // 128):
            x = b[:, c * 128 : (c + 1) * 128].astype(jnp.float32)
            total += x * x
        col_norm = jnp.sum(total.T, axis=0, keepdims=True)
        dist = row_norm[:, :1] + col_norm - 2.0 * inner
        gram = jnp.exp(dist * (-2.0 / samples)) * scale
        out_ref[:, at] = gram.astype(jnp.bfloat16)


def gram_tile(where, cols, own, mate):
    samples = cols.shape[1]
    anywhere = pl.BlockSpec(memory_space=pl.ANY)
    return pl.pallas_call(
        gram_kernel,
        out_shape=jax.ShapeDtypeStruct((HALF, HALF), jnp.bfloat16),
        in_specs=[pl.BlockSpec(memory_space=pltpu.SMEM)] + [anywhere] * 9,
        out_specs=pl.BlockSpec(memory_space=pltpu.VMEM),
        scratch_shapes=[
            pltpu.VMEM((HALF, samples), jnp.bfloat16),
            pltpu.VMEM((HALF, samples), jnp.bfloat16),
            pltpu.VMEM((HALF, 128), jnp.float32),
            pltpu.SemaphoreType.DMA((2 * N,)),
            pltpu.SemaphoreType.DMA((N,)),
        ],
        compiler_params=pltpu.CompilerParams(vmem_limit_bytes=48 * 1024 * 1024),
        cost_estimate=pl.CostEstimate(
            flops=2 * HALF * HALF * samples,
            bytes_accessed=9 * 1024 * 1024,
            transcendentals=HALF * HALF,
        ),
    )(where, cols, *own, *mate)


def on_device(trajectories, pair_live):
    y, xl, z, a, xh = (lax.axis_index(name) for name in AX)
    live = pair_live[y * 2 + xl, z * 2 + a]

    def send(value, to):
        return lax.ppermute(value, AX, to)

    early = send(trajectories, col_pairs(0))
    late = send(trajectories, col_pairs(1))
    other = send(trajectories, swap_lag())
    early, late, other = lax.optimization_barrier((early, late, other))
    cols = lax.all_gather(
        jnp.concatenate([early, late], axis=1), "y", axis=0, tiled=True
    )
    rows = jnp.where(
        xl == 0,
        jnp.concatenate([trajectories, other], axis=1),
        jnp.concatenate([other, trajectories], axis=1),
    )

    own, steps = [rows], []
    up = down = rows
    for step in range(4):
        if step == 3:
            up, down = up[: SUB // 2], down[SUB // 2 :]
        up, down = send(up, shift_z(1)), send(down, shift_z(-1))
        own.append(jnp.concatenate([up, down], axis=0))
    mate = [send(jnp.concatenate(own[:3], axis=0), swap_core())]
    mate += [send(chunk, swap_core()) for chunk in own[3:]]

    def tile(half):
        where = jnp.stack([y, z, a, half, live]).astype(jnp.int32)
        return gram_tile(where, cols, own, mate)

    given = send(tile(1 - xh), swap_lag())
    kept = tile(xh)
    return jnp.where(
        xh == 0,
        jnp.concatenate([kept, given], axis=1),
        jnp.concatenate([given, kept], axis=1),
    )


def solution(mesh):
    fine = Mesh(mesh.devices.reshape(N, 2, N, 2, 2), AX)
    return jax.shard_map(
        on_device,
        mesh=fine,
        in_specs=(P(("y", "xl", "z", "a"), "xh"), P()),
        out_specs=P(("y", "xl", "xh"), ("z", "a")),
        check_vma=False,
    )
```

time: 178 us -> 162 us (0.910)
  the two profiles are of different devices: /device:TPU:35 before, /device:TPU:16 now
where the time goes in v2:
time: 162 us
  starting transfers between devices  65.9 us (41%)
  waiting for transfers between devices  48.5 us (30%)
  Pallas kernels  18.2 us (11%)
  between operations  13.6 us (8%)
  local copies, waits for them, and re-layouts  10.2 us (6%)
  other arithmetic  5.3 us (3%)
    ppermute x15, starting transfers between devices, send(): return lax.ppermute(value, AX, to)  65.9 us
    ppermute x15, waiting for transfers between devices, send(): return lax.ppermute(value, AX, to)  48.5 us
    pallas_call x2, Pallas kernels, gram_tile(): pl.pallas_call(gram_kernel, out_shape=jax.ShapeDtypeStruct((HALF, HALF),...  18.2 us
    unnamed x11, local copies, waits for them, and re-layouts  5.65 us
  transfers between devices with their start and end apart: 16, of which 9 were waited for; matrix products, arithmetic and copies ran while one was open for 6% of the time, Pallas kernels for 5%

profile of v2, /device:TPU:16, one launch (start us, length us, event | category | flops | bytes accessed | tf_op | source)
XLA Modules:
  0.0 161.8 jit_solution(17291746014779993450)
XLA Ops:
  6.5 0.0 all-gather.2.cloned.1.call-start
  6.5 6.1 %collective-permute-start = (bf16[64,2048]{1,0:T(8,128)(2,1)}, bf16[64,2048]{1,0:T(8,128)(2,1)S(1)}, u32[]{:S(2)}, u32[]{:S(2)}) collective-permute-start(bf16[64,2048]{1,0:T(8,128)(2,1)} %param.2), channel_id=1, source_target_pairs={{0,0},{1,32},{2,256},{3,288},{4,64},{5,96},{6,448},{7,480},{8,128}... | collective-permute-start | bytes 786440 | tf_op jit(solution)/shard_map/ppermute | solution.py:157
  12.6 6.0 %collective-permute-start.1 = (bf16[64,2048]{1,0:T(8,128)(2,1)}, bf16[64,2048]{1,0:T(8,128)(2,1)S(1)}, u32[]{:S(2)}, u32[]{:S(2)}) collective-permute-start(bf16[64,2048]{1,0:T(8,128)(2,1)} %param.2), channel_id=1, source_target_pairs={{0,32},{1,0},{2,288},{3,256},{4,96},{5,64},{6,480},{7,448},{8,160}... | collective-permute-start | bytes 786440 | tf_op jit(solution)/shard_map/ppermute | solution.py:157
  18.7 4.5 %collective-permute-start.2 = (bf16[64,2048]{1,0:T(8,128)(2,1)}, bf16[64,2048]{1,0:T(8,128)(2,1)S(1)}, u32[]{:S(2)}, u32[]{:S(2)}) collective-permute-start(bf16[64,2048]{1,0:T(8,128)(2,1)} %param.2), channel_id=1, source_target_pairs={{0,1},{1,0},{2,3},{3,2},{4,5},{5,4},{6,7},{7,6},{8,9},{9,8},{10,11... | collective-permute-start | bytes 786440 | tf_op jit(solution)/shard_map/ppermute | solution.py:157
  23.2 0.0 collective-permute-done
  23.2 5.4 %collective-permute-done.1 = bf16[64,2048]{1,0:T(8,128)(2,1)S(1)} collective-permute-done((bf16[64,2048]{1,0:T(8,128)(2,1)}, bf16[64,2048]{1,0:T(8,128)(2,1)S(1)}, u32[]{:S(2)}, u32[]{:S(2)}) %collective-permute-start.1) | collective-permute-done | bytes 262176 | tf_op jit(solution)/shard_map/ppermute | solution.py:157
  28.6 6.4 %collective-permute-done.2 = bf16[64,2048]{1,0:T(8,128)(2,1)S(1)} collective-permute-done((bf16[64,2048]{1,0:T(8,128)(2,1)}, bf16[64,2048]{1,0:T(8,128)(2,1)S(1)}, u32[]{:S(2)}, u32[]{:S(2)}) %collective-permute-start.2) | collective-permute-done | bytes 262176 | tf_op jit(solution)/shard_map/ppermute | solution.py:157
  35.1 0.8 pad_maximum_fusion
  35.9 0.0 all-gather.2.cloned.1.call-update
  35.9 2.0 %constant_dynamic-update-slice_fusion.12 = (bf16[320,4096]{1,0:T(8,128)(2,1)}, bf16[64,4096]{1,0:T(8,128)(2,1)S(1)}) fusion(bf16[64,2048]{1,0:T(8,128)(2,1)} %param.2, bf16[64,2048]{1,0:T(8,128)(2,1)S(1)} %collective-permute-done.2, pred[]{:T(512)S(6)} %eq.7), kind=kLoop, calls=%fused_computation.15 | loop fusion | flops 2359295 | bytes 1572865
  37.9 0.0 copy-start
  37.9 1.9 %collective-permute-start.3 = (bf16[64,4096]{1,0:T(8,128)(2,1)S(1)}, bf16[64,4096]{1,0:T(8,128)(2,1)S(1)}, u32[]{:S(2)}, u32[]{:S(2)}) collective-permute-start(bf16[64,4096]{1,0:T(8,128)(2,1)S(1)} %get-tuple-element.12.refs_0_), channel_id=1, source_target_pairs={{0,4},{1,5},{2,6},{3,7},{4,8},{5,9},{6,10},{7,11},{8,12},{9,13},{1... | collective-permute-start | bytes 1572872 | tf_op jit(solution)/shard_map/ppermute | solution.py:157
  39.8 17.3 %collective-permute-start.4 = (bf16[64,4096]{1,0:T(8,128)(2,1)S(1)}, bf16[64,4096]{1,0:T(8,128)(2,1)S(1)}, u32[]{:S(2)}, u32[]{:S(2)}) collective-permute-start(bf16[64,4096]{1,0:T(8,128)(2,1)S(1)} %get-tuple-element.12.refs_0_), channel_id=1, source_target_pairs={{0,28},{1,29},{2,30},{3,31},{4,0},{5,1},{6,2},{7,3},{8,4},{9,5},{1... | collective-permute-start | bytes 1572872 | tf_op jit(solution)/shard_map/ppermute | solution.py:157
  57.1 9.6 %collective-permute-done.3 = bf16[64,4096]{1,0:T(8,128)(2,1)S(1)} collective-permute-done((bf16[64,4096]{1,0:T(8,128)(2,1)S(1)}, bf16[64,4096]{1,0:T(8,128)(2,1)S(1)}, u32[]{:S(2)}, u32[]{:S(2)}) %collective-permute-start.3) | collective-permute-done | bytes 524320 | tf_op jit(solution)/shard_map/ppermute | solution.py:157
  66.7 1.9 %collective-permute-start.5 = (bf16[64,4096]{1,0:T(8,128)(2,1)S(1)}, bf16[64,4096]{1,0:T(8,128)(2,1)S(1)}, u32[]{:S(2)}, u32[]{:S(2)}) collective-permute-start(bf16[64,4096]{1,0:T(8,128)(2,1)S(1)} %collective-permute-done.3), channel_id=1, source_target_pairs={{0,4},{1,5},{2,6},{3,7},{4,8},{5,9},{6,10},{7,11},{8,12},{9,13},{1... | collective-permute-start | bytes 1572872 | tf_op jit(solution)/shard_map/ppermute | solution.py:157
  68.6 0.9 constant_dynamic-update-slice_fusion.11
  69.5 0.0 collective-permute-done.4
  69.5 5.1 %collective-permute-start.6 = (bf16[64,4096]{1,0:T(8,128)(2,1)S(1)}, bf16[64,4096]{1,0:T(8,128)(2,1)S(1)}, u32[]{:S(2)}, u32[]{:S(2)}) collective-permute-start(bf16[64,4096]{1,0:T(8,128)(2,1)S(1)} %collective-permute-done.4), channel_id=1, source_target_pairs={{0,28},{1,29},{2,30},{3,31},{4,0},{5,1},{6,2},{7,3},{8,4},{9,5},{1... | collective-permute-start | bytes 1572872 | tf_op jit(solution)/shard_map/ppermute | solution.py:157
  74.6 1.0 constant_dynamic-update-slice_fusion.10
  75.6 6.8 %collective-permute-done.5 = bf16[64,4096]{1,0:T(8,128)(2,1)S(1)} collective-permute-done((bf16[64,4096]{1,0:T(8,128)(2,1)S(1)}, bf16[64,4096]{1,0:T(8,128)(2,1)S(1)}, u32[]{:S(2)}, u32[]{:S(2)}) %collective-permute-start.5) | collective-permute-done | bytes 524320 | tf_op jit(solution)/shard_map/ppermute | solution.py:157
  82.4 1.9 %collective-permute-start.7 = (bf16[64,4096]{1,0:T(8,128)(2,1)S(1)}, bf16[64,4096]{1,0:T(8,128)(2,1)S(1)}, u32[]{:S(2)}, u32[]{:S(2)}) collective-permute-start(bf16[64,4096]{1,0:T(8,128)(2,1)S(1)} %collective-permute-done.5), channel_id=1, source_target_pairs={{0,4},{1,5},{2,6},{3,7},{4,8},{5,9},{6,10},{7,11},{8,12},{9,13},{1... | collective-permute-start | bytes 1572872 | tf_op jit(solution)/shard_map/ppermute | solution.py:157
  84.4 1.0 constant_dynamic-update-slice_fusion.9
  85.3 0.0 collective-permute-done.6
  85.3 0.9 constant_dynamic-update-slice_fusion.8
  86.2 0.0 copy-done
  86.2 1.9 %collective-permute-start.11 = (bf16[320,4096]{1,0:T(8,128)(2,1)}, bf16[320,4096]{1,0:T(8,128)(2,1)}, u32[]{:S(2)}, u32[]{:S(2)}) collective-permute-start(bf16[320,4096]{1,0:T(8,128)(2,1)} %get-tuple-element.13), channel_id=1, source_target_pairs={{0,2},{1,3},{2,0},{3,1},{4,6},{5,7},{6,4},{7,5},{8,10},{9,11},{10,... | collective-permute-start | bytes 7864328 | tf_op jit(solution)/shard_map/ppermute | solution.py:157
  88.2 5.1 %collective-permute-start.8 = (bf16[64,4096]{1,0:T(8,128)(2,1)S(1)}, bf16[64,4096]{1,0:T(8,128)(2,1)S(1)}, u32[]{:S(2)}, u32[]{:S(2)}) collective-permute-start(bf16[64,4096]{1,0:T(8,128)(2,1)S(1)} %collective-permute-done.6), channel_id=1, source_target_pairs={{0,28},{1,29},{2,30},{3,31},{4,0},{5,1},{6,2},{7,3},{8,4},{9,5},{1... | collective-permute-start | bytes 1572872 | tf_op jit(solution)/shard_map/ppermute | solution.py:157
  93.3 4.0 %collective-permute-done.7 = bf16[64,4096]{1,0:T(8,128)(2,1)S(1)} collective-permute-done((bf16[64,4096]{1,0:T(8,128)(2,1)S(1)}, bf16[64,4096]{1,0:T(8,128)(2,1)S(1)}, u32[]{:S(2)}, u32[]{:S(2)}) %collective-permute-start.7) | collective-permute-done | bytes 524320 | tf_op jit(solution)/shard_map/ppermute | solution.py:157
  97.3 1.9 %collective-permute-start.9 = (bf16[32,4096]{1,0:T(8,128)(2,1)S(1)}, bf16[32,4096]{1,0:T(8,128)(2,1)S(1)}, u32[]{:S(2)}, u32[]{:S(2)}) collective-permute-start(bf16[32,4096]{1,0:T(8,128)(2,1)S(1)} %slice.8), channel_id=1, source_target_pairs={{0,4},{1,5},{2,6},{3,7},{4,8},{5,9},{6,10},{7,11},{8,12},{9,13},{1... | collective-permute-start | bytes 786440 | tf_op jit(solution)/shard_map/ppermute | solution.py:157
  99.3 5.9 %collective-permute-done.8 = bf16[64,4096]{1,0:T(8,128)(2,1)S(1)} collective-permute-done((bf16[64,4096]{1,0:T(8,128)(2,1)S(1)}, bf16[64,4096]{1,0:T(8,128)(2,1)S(1)}, u32[]{:S(2)}, u32[]{:S(2)}) %collective-permute-start.8) | collective-permute-done | bytes 524320 | tf_op jit(solution)/shard_map/ppermute | solution.py:157
  105.2 1.9 %collective-permute-start.12 = (bf16[128,4096]{1,0:T(8,128)(2,1)S(1)}, bf16[128,4096]{1,0:T(8,128)(2,1)}, u32[]{:S(2)}, u32[]{:S(2)}) collective-permute-start(bf16[128,4096]{1,0:T(8,128)(2,1)S(1)} %constant_dynamic-update-slice_fusion.4.refs_3_), channel_id=1, source_target_pairs={{0,2},{1,3},{2,0},{3,1},{4,6},{5,7},{6,4},{7,5},{8,10},{9,11},{10,... | collective-permute-start | bytes 3145736 | tf_op jit(solution)/shard_map/ppermute | solution.py:157
  107.1 5.6 %collective-permute-start.10 = (bf16[32,4096]{1,0:T(8,128)(2,1)S(1)}, bf16[32,4096]{1,0:T(8,128)(2,1)S(1)}, u32[]{:S(2)}, u32[]{:S(2)}) collective-permute-start(bf16[32,4096]{1,0:T(8,128)(2,1)S(1)} %slice.9), channel_id=1, source_target_pairs={{0,28},{1,29},{2,30},{3,31},{4,0},{5,1},{6,2},{7,3},{8,4},{9,5},{1... | collective-permute-start | bytes 786440 | tf_op jit(solution)/shard_map/ppermute | solution.py:157
  112.7 0.0 collective-permute-done.9
  112.7 0.7 constant_dynamic-update-slice_fusion.7
  113.5 5.5 %collective-permute-done.10 = bf16[32,4096]{1,0:T(8,128)(2,1)S(1)} collective-permute-done((bf16[32,4096]{1,0:T(8,128)(2,1)S(1)}, bf16[32,4096]{1,0:T(8,128)(2,1)S(1)}, u32[]{:S(2)}, u32[]{:S(2)}) %collective-permute-start.10) | collective-permute-done | bytes 262176 | tf_op jit(solution)/shard_map/ppermute | solution.py:157
  118.9 0.7 constant_dynamic-update-slice_fusion.6.refs_4_
  119.6 1.9 %collective-permute-start.13 = (bf16[64,4096]{1,0:T(8,128)(2,1)}, bf16[64,4096]{1,0:T(8,128)(2,1)}, u32[]{:S(2)}, u32[]{:S(2)}) collective-permute-start(bf16[64,4096]{1,0:T(8,128)(2,1)} %constant_dynamic-update-slice_fusion.6.refs_4_), channel_id=1, source_target_pairs={{0,2},{1,3},{2,0},{3,1},{4,6},{5,7},{6,4},{7,5},{8,10},{9,11},{10,... | collective-permute-start | bytes 1572872 | tf_op jit(solution)/shard_map/ppermute | solution.py:157
  121.6 1.4 dynamic_slice.3
  122.9 0.8 stack.30.where_ref
  123.7 0.1 collective-permute-done.13.refs_7_
  123.8 0.0 collective-permute-done.12.refs_6_
  123.8 0.0 collective-permute-done.11.refs_5_
  123.8 0.0 all-gather.2.cloned.1.call-done.cols_hbm
  123.8 0.0 copy-start.1
  123.8 1.0 copy-done.1
  124.8 9.6 %shard_map.29 = bf16[512,512]{1,0:T(8,128)(2,1)} custom-call(s32[5]{0:T(128)S(1)} %stack.30.where_ref, bf16[512,4096]{1,0:T(8,128)(2,1)} %all-gather.2.cloned.1.call-done.cols_hbm, bf16[64,4096]{1,0:T(8,128)(2,1)S(1)} %copy-done.1, bf16[128,4096]{1,0:T(8,128)(2,1)S(1)} %get-tuple-element.18.refs_1_, bf16[128,4096]{1,0:T(8,128)(2,1)S(1)} %get-tuple-element.14.refs_2_, ...), custom_call_target="tpu_custom_call" | custom-call | flops 2147483648 | bytes 9437184 | tf_op jit(solution)/shard_map/pallas_call | solution.py:131
  134.4 2.7 %collective-permute-start.14 = (bf16[512,512]{1,0:T(8,128)(2,1)}, bf16[512,512]{1,0:T(8,128)(2,1)}, u32[]{:S(2)}, u32[]{:S(2)}) collective-permute-start(bf16[512,512]{1,0:T(8,128)(2,1)} %shard_map.29), channel_id=1, source_target_pairs={{0,1},{1,0},{2,3},{3,2},{4,5},{5,4},{6,7},{7,6},{8,9},{9,8},{10,11... | collective-permute-start | bytes 1572872 | tf_op jit(solution)/shard_map/ppermute | solution.py:157
  137.1 0.8 stack.28.where_ref
  137.9 0.0 copy-start.2
  137.9 1.0 copy-done.2
  138.9 8.6 %shard_map.28 = bf16[512,512]{1,0:T(8,128)(2,1)S(1)} custom-call(s32[5]{0:T(128)S(1)} %stack.28.where_ref, bf16[512,4096]{1,0:T(8,128)(2,1)} %all-gather.2.cloned.1.call-done.cols_hbm, bf16[64,4096]{1,0:T(8,128)(2,1)S(1)} %copy-done.2, bf16[128,4096]{1,0:T(8,128)(2,1)S(1)} %get-tuple-element.18.refs_1_, bf16[128,4096]{1,0:T(8,128)(2,1)S(1)} %get-tuple-element.14.refs_2_, ...), custom_call_target="tpu_custom_call" | custom-call | flops 2147483648 | bytes 9437184 | tf_op jit(solution)/shard_map/pallas_call | solution.py:131
  147.6 4.8 %collective-permute-done.14 = bf16[512,512]{1,0:T(8,128)(2,1)} collective-permute-done((bf16[512,512]{1,0:T(8,128)(2,1)}, bf16[512,512]{1,0:T(8,128)(2,1)}, u32[]{:S(2)}, u32[]{:S(2)}) %collective-permute-start.14) | collective-permute-done | bytes 524320 | tf_op jit(solution)/shard_map/ppermute | solution.py:157
  152.4 2.5 %maximum_select_fusion = bf16[512,1024]{1,0:T(8,128)(2,1)} fusion(bf16[512,512]{1,0:T(8,128)(2,1)} %collective-permute-done.14, bf16[512,512]{1,0:T(8,128)(2,1)S(1)} %shard_map.28, pred[]{:T(512)S(6)} %eq.6), kind=kLoop, calls=%fused_computation | loop fusion | flops 4718592 | bytes 2097153 | tf_op jit(solution)/shard_map/jit(_where)/select_n | solution.py:188
  (4 shorter events, 0.1 us)
Async XLA Ops:
  6.5 117.3 %all-gather.2.cloned.1.call-start = ((), (), s32[]{:S(2)}) async-start(), calls=%async_computation | async-start | bytes 4718592 | tf_op jit(solution)/shard_map/all_gather | solution.py:163
  6.5 16.7 %collective-permute-start = (bf16[64,2048]{1,0:T(8,128)(2,1)}, bf16[64,2048]{1,0:T(8,128)(2,1)S(1)}, u32[]{:S(2)}, u32[]{:S(2)}) collective-permute-start(bf16[64,2048]{1,0:T(8,128)(2,1)} %param.2), channel_id=1, source_target_pairs={{0,0},{1,32},{2,256},{3,288},{4,64},{5,96},{6,448},{7,480},{8,128}... | collective-permute-start | bytes 786440 | tf_op jit(solution)/shard_map/ppermute | solution.py:157
  12.6 16.0 %collective-permute-start.1 = (bf16[64,2048]{1,0:T(8,128)(2,1)}, bf16[64,2048]{1,0:T(8,128)(2,1)S(1)}, u32[]{:S(2)}, u32[]{:S(2)}) collective-permute-start(bf16[64,2048]{1,0:T(8,128)(2,1)} %param.2), channel_id=1, source_target_pairs={{0,32},{1,0},{2,288},{3,256},{4,96},{5,64},{6,480},{7,448},{8,160}... | collective-permute-start | bytes 786440 | tf_op jit(solution)/shard_map/ppermute | solution.py:157
  18.7 16.4 %collective-permute-start.2 = (bf16[64,2048]{1,0:T(8,128)(2,1)}, bf16[64,2048]{1,0:T(8,128)(2,1)S(1)}, u32[]{:S(2)}, u32[]{:S(2)}) collective-permute-start(bf16[64,2048]{1,0:T(8,128)(2,1)} %param.2), channel_id=1, source_target_pairs={{0,1},{1,0},{2,3},{3,2},{4,5},{5,4},{6,7},{7,6},{8,9},{9,8},{10,11... | collective-permute-start | bytes 786440 | tf_op jit(solution)/shard_map/ppermute | solution.py:157
  37.9 48.3 %copy-start = (bf16[64,4096]{1,0:T(8,128)(2,1)}, bf16[64,4096]{1,0:T(8,128)(2,1)S(1)}, u32[]{:S(2)}) copy-start(bf16[64,4096]{1,0:T(8,128)(2,1)S(1)} %get-tuple-element.12.refs_0_) | copy-start | bytes 1572868
  37.9 28.8 %collective-permute-start.3 = (bf16[64,4096]{1,0:T(8,128)(2,1)S(1)}, bf16[64,4096]{1,0:T(8,128)(2,1)S(1)}, u32[]{:S(2)}, u32[]{:S(2)}) collective-permute-start(bf16[64,4096]{1,0:T(8,128)(2,1)S(1)} %get-tuple-element.12.refs_0_), channel_id=1, source_target_pairs={{0,4},{1,5},{2,6},{3,7},{4,8},{5,9},{6,10},{7,11},{8,12},{9,13},{1... | collective-permute-start | bytes 1572872 | tf_op jit(solution)/shard_map/ppermute | solution.py:157
  39.8 29.7 %collective-permute-start.4 = (bf16[64,4096]{1,0:T(8,128)(2,1)S(1)}, bf16[64,4096]{1,0:T(8,128)(2,1)S(1)}, u32[]{:S(2)}, u32[]{:S(2)}) collective-permute-start(bf16[64,4096]{1,0:T(8,128)(2,1)S(1)} %get-tuple-element.12.refs_0_), channel_id=1, source_target_pairs={{0,28},{1,29},{2,30},{3,31},{4,0},{5,1},{6,2},{7,3},{8,4},{9,5},{1... | collective-permute-start | bytes 1572872 | tf_op jit(solution)/shard_map/ppermute | solution.py:157
  66.7 15.7 %collective-permute-start.5 = (bf16[64,4096]{1,0:T(8,128)(2,1)S(1)}, bf16[64,4096]{1,0:T(8,128)(2,1)S(1)}, u32[]{:S(2)}, u32[]{:S(2)}) collective-permute-start(bf16[64,4096]{1,0:T(8,128)(2,1)S(1)} %collective-permute-done.3), channel_id=1, source_target_pairs={{0,4},{1,5},{2,6},{3,7},{4,8},{5,9},{6,10},{7,11},{8,12},{9,13},{1... | collective-permute-start | bytes 1572872 | tf_op jit(solution)/shard_map/ppermute | solution.py:157
  69.5 15.8 %collective-permute-start.6 = (bf16[64,4096]{1,0:T(8,128)(2,1)S(1)}, bf16[64,4096]{1,0:T(8,128)(2,1)S(1)}, u32[]{:S(2)}, u32[]{:S(2)}) collective-permute-start(bf16[64,4096]{1,0:T(8,128)(2,1)S(1)} %collective-permute-done.4), channel_id=1, source_target_pairs={{0,28},{1,29},{2,30},{3,31},{4,0},{5,1},{6,2},{7,3},{8,4},{9,5},{1... | collective-permute-start | bytes 1572872 | tf_op jit(solution)/shard_map/ppermute | solution.py:157
  82.4 14.8 %collective-permute-start.7 = (bf16[64,4096]{1,0:T(8,128)(2,1)S(1)}, bf16[64,4096]{1,0:T(8,128)(2,1)S(1)}, u32[]{:S(2)}, u32[]{:S(2)}) collective-permute-start(bf16[64,4096]{1,0:T(8,128)(2,1)S(1)} %collective-permute-done.5), channel_id=1, source_target_pairs={{0,4},{1,5},{2,6},{3,7},{4,8},{5,9},{6,10},{7,11},{8,12},{9,13},{1... | collective-permute-start | bytes 1572872 | tf_op jit(solution)/shard_map/ppermute | solution.py:157
  86.2 37.5 %collective-permute-start.11 = (bf16[320,4096]{1,0:T(8,128)(2,1)}, bf16[320,4096]{1,0:T(8,128)(2,1)}, u32[]{:S(2)}, u32[]{:S(2)}) collective-permute-start(bf16[320,4096]{1,0:T(8,128)(2,1)} %get-tuple-element.13), channel_id=1, source_target_pairs={{0,2},{1,3},{2,0},{3,1},{4,6},{5,7},{6,4},{7,5},{8,10},{9,11},{10,... | collective-permute-start | bytes 7864328 | tf_op jit(solution)/shard_map/ppermute | solution.py:157
  88.2 17.0 %collective-permute-start.8 = (bf16[64,4096]{1,0:T(8,128)(2,1)S(1)}, bf16[64,4096]{1,0:T(8,128)(2,1)S(1)}, u32[]{:S(2)}, u32[]{:S(2)}) collective-permute-start(bf16[64,4096]{1,0:T(8,128)(2,1)S(1)} %collective-permute-done.6), channel_id=1, source_target_pairs={{0,28},{1,29},{2,30},{3,31},{4,0},{5,1},{6,2},{7,3},{8,4},{9,5},{1... | collective-permute-start | bytes 1572872 | tf_op jit(solution)/shard_map/ppermute | solution.py:157
  97.3 15.4 %collective-permute-start.9 = (bf16[32,4096]{1,0:T(8,128)(2,1)S(1)}, bf16[32,4096]{1,0:T(8,128)(2,1)S(1)}, u32[]{:S(2)}, u32[]{:S(2)}) collective-permute-start(bf16[32,4096]{1,0:T(8,128)(2,1)S(1)} %slice.8), channel_id=1, source_target_pairs={{0,4},{1,5},{2,6},{3,7},{4,8},{5,9},{6,10},{7,11},{8,12},{9,13},{1... | collective-permute-start | bytes 786440 | tf_op jit(solution)/shard_map/ppermute | solution.py:157
  105.2 18.6 %collective-permute-start.12 = (bf16[128,4096]{1,0:T(8,128)(2,1)S(1)}, bf16[128,4096]{1,0:T(8,128)(2,1)}, u32[]{:S(2)}, u32[]{:S(2)}) collective-permute-start(bf16[128,4096]{1,0:T(8,128)(2,1)S(1)} %constant_dynamic-update-slice_fusion.4.refs_3_), channel_id=1, source_target_pairs={{0,2},{1,3},{2,0},{3,1},{4,6},{5,7},{6,4},{7,5},{8,10},{9,11},{10,... | collective-permute-start | bytes 3145736 | tf_op jit(solution)/shard_map/ppermute | solution.py:157
  107.1 11.8 %collective-permute-start.10 = (bf16[32,4096]{1,0:T(8,128)(2,1)S(1)}, bf16[32,4096]{1,0:T(8,128)(2,1)S(1)}, u32[]{:S(2)}, u32[]{:S(2)}) collective-permute-start(bf16[32,4096]{1,0:T(8,128)(2,1)S(1)} %slice.9), channel_id=1, source_target_pairs={{0,28},{1,29},{2,30},{3,31},{4,0},{5,1},{6,2},{7,3},{8,4},{9,5},{1... | collective-permute-start | bytes 786440 | tf_op jit(solution)/shard_map/ppermute | solution.py:157
  119.6 4.1 %collective-permute-start.13 = (bf16[64,4096]{1,0:T(8,128)(2,1)}, bf16[64,4096]{1,0:T(8,128)(2,1)}, u32[]{:S(2)}, u32[]{:S(2)}) collective-permute-start(bf16[64,4096]{1,0:T(8,128)(2,1)} %constant_dynamic-update-slice_fusion.6.refs_4_), channel_id=1, source_target_pairs={{0,2},{1,3},{2,0},{3,1},{4,6},{5,7},{6,4},{7,5},{8,10},{9,11},{10,... | collective-permute-start | bytes 1572872 | tf_op jit(solution)/shard_map/ppermute | solution.py:157
  123.8 1.0 copy-start.1
  134.4 18.0 %collective-permute-start.14 = (bf16[512,512]{1,0:T(8,128)(2,1)}, bf16[512,512]{1,0:T(8,128)(2,1)}, u32[]{:S(2)}, u32[]{:S(2)}) collective-permute-start(bf16[512,512]{1,0:T(8,128)(2,1)} %shard_map.29), channel_id=1, source_target_pairs={{0,1},{1,0},{2,3},{3,2},{4,5},{5,4},{6,7},{7,6},{8,9},{9,8},{10,11... | collective-permute-start | bytes 1572872 | tf_op jit(solution)/shard_map/ppermute | solution.py:157
  137.9 1.0 copy-start.2
Sparse Core Ops, SparseCore 0:
  36.0 61.9 all-gather.1

commit v3 on v2

v3 whole, which is shorter than its diff:
```python
import functools

import jax
import jax.numpy as jnp
from jax import lax
from jax.experimental import pallas as pl
from jax.experimental.pallas import tpu as pltpu
from jax.sharding import Mesh
from jax.sharding import PartitionSpec as P

AX = ("y", "xl", "z", "a", "xh")
N = 8
SUB = 64
HALF = N * SUB
SHIFT = ((0, 4), (1, -1), (2, -2), (3, -3))


def index(y, xl, z, a, xh):
    return (((y % N * 2 + xl) * N + z % N) * 2 + a) * 2 + xh


def pairs(target):
    every = [
        (y, xl, z, a, xh)
        for y in range(N)
        for xl in range(2)
        for z in range(N)
        for a in range(2)
        for xh in range(2)
    ]
    return [(index(*d), index(*target(*d))) for d in every]


def col_pairs(stage):
    def target(y, xl, z, a, half):
        part = z // 4
        return y + SHIFT[z % 4][a], half ^ part ^ stage, y, xl, part

    return pairs(target)


def shift_z(step):
    return pairs(lambda y, xl, z, a, xh: (y, xl, z + step, a, xh))


def swap_core():
    return pairs(lambda y, xl, z, a, xh: (y, xl, z, 1 - a, xh))


def swap_lag():
    return pairs(lambda y, xl, z, a, xh: (y, xl, z, a, 1 - xh))


def chunks(own, mate):
    for d in range(-3, 5):
        step, first = abs(d), SUB if d < 0 else 0
        yield own[step], first, d, 0
        if step == 0:
            yield mate[0], 0, d, 1
        elif step < 3:
            yield mate[0], SUB + (step - 1) * 2 * SUB + first, d, 1
        else:
            yield mate[step - 2], first, d, 1


def square_sums(ref, first):
    total = jnp.zeros((SUB, 128), jnp.float32)
    for c in range(ref.shape[1] // 128):
        x = ref[pl.ds(first, SUB), c * 128 : (c + 1) * 128].astype(jnp.float32)
        total += x * x
    return total


def gram_kernel(keep, live_ref, cols_hbm, *refs):
    own, mate = refs[0:5], refs[5:8]
    out_ref, rows, cols, row_norm, col_norm, sem_rows, sem_cols = refs[8:]
    y, xl, z, a, xh = (lax.axis_index(name) for name in AX)
    half = xh if keep else 1 - xh
    samples = rows.shape[1]
    col_copies = []
    for there in range(N):
        o = (there - z) & (N - 1)
        j = jnp.where(o < 4, 2 * o, (17 - 2 * o) & (N - 1))
        first = pl.multiple_of(j * SUB, SUB)
        copy = pltpu.make_async_copy(
            cols_hbm.at[pl.ds(there * SUB, SUB), :],
            cols.at[pl.ds(first, SUB), :],
            sem_cols.at[there],
        )
        copy.start()
        col_copies.append((first, copy))
    row_copies = []
    for n, (ref, start, d, other) in enumerate(chunks(own, mate)):
        there = (z - d) & (N - 1)
        core = a if other == 0 else 1 - a
        first = pl.multiple_of(((2 * there + core) & (N - 1)) * SUB, SUB)
        copy = pltpu.make_async_copy(
            ref.at[pl.ds(start, SUB), :],
            rows.at[pl.ds(first, SUB), :],
            sem_rows.at[n],
        )
        mine = there // 4 == half
        pl.when(mine)(copy.start)
        row_copies.append((mine, first, copy))

    for first, copy in col_copies:
        copy.wait()
        col_norm[pl.ds(first, SUB), :] = square_sums(cols, first)
    for mine, first, copy in row_copies:

        @pl.when(mine)
        def _(first=first, copy=copy):
            copy.wait()
            total = jnp.sum(square_sums(rows, first), axis=1, keepdims=True)
            row_norm[pl.ds(first, SUB), :] = jnp.broadcast_to(total, (SUB, 128))

    scale = live_ref[2 * y + xl, 2 * z + a].astype(jnp.float32)
    base = xh * HALF if keep else 0

    @pl.loop(0, HALF // 256)
    def _(i):
        at = pl.ds(pl.multiple_of(i * 256, 256), 256)
        inner = lax.dot_general(
            rows[...],
            cols[at, :],
            (((1,), (1,)), ((), ())),
            preferred_element_type=jnp.float32,
        )
        across = jnp.sum(col_norm[at, :].T, axis=0, keepdims=True)
        dist = row_norm[:, :1] + across - 2.0 * inner
        gram = jnp.exp(dist * (-2.0 / samples)) * scale
        to = pl.ds(pl.multiple_of(base + i * 256, 256), 256)
        out_ref[:, to] = gram.astype(jnp.bfloat16)


def gram_tile(keep, pair_live, cols, own, mate):
    samples = cols.shape[1]
    anywhere = pl.BlockSpec(memory_space=pl.ANY)
    width = 2 * HALF if keep else HALF
    return pl.pallas_call(
        functools.partial(gram_kernel, keep),
        out_shape=jax.ShapeDtypeStruct((HALF, width), jnp.bfloat16),
        in_specs=[pl.BlockSpec(memory_space=pltpu.SMEM)] + [anywhere] * 9,
        out_specs=pl.BlockSpec(memory_space=pltpu.VMEM),
        scratch_shapes=[
            pltpu.VMEM((HALF, samples), jnp.bfloat16),
            pltpu.VMEM((HALF, samples), jnp.bfloat16),
            pltpu.VMEM((HALF, 128), jnp.float32),
            pltpu.VMEM((HALF, 128), jnp.float32),
            pltpu.SemaphoreType.DMA((2 * N,)),
            pltpu.SemaphoreType.DMA((N,)),
        ],
        compiler_params=pltpu.CompilerParams(vmem_limit_bytes=56 * 1024 * 1024),
        cost_estimate=pl.CostEstimate(
            flops=2 * HALF * HALF * samples,
            bytes_accessed=9 * 1024 * 1024,
            transcendentals=HALF * HALF,
        ),
    )(pair_live, cols, *own, *mate)


def on_device(trajectories, pair_live):
    xl, xh = lax.axis_index("xl"), lax.axis_index("xh")

    def send(value, to):
        return lax.ppermute(value, AX, to)

    other = send(trajectories, swap_lag())
    early = send(trajectories, col_pairs(0))
    late = send(trajectories, col_pairs(1))
    rows = jnp.where(
        xl == 0,
        jnp.concatenate([trajectories, other], axis=1),
        jnp.concatenate([other, trajectories], axis=1),
    )
    early, late, rows = lax.optimization_barrier((early, late, rows))
    cols = lax.all_gather(
        jnp.concatenate([early, late], axis=1), "y", axis=0, tiled=True
    )

    own = [rows]
    up = down = rows
    for step in range(4):
        if step == 3:
            up, down = up[: SUB // 2], down[SUB // 2 :]
        up, down = send(up, shift_z(1)), send(down, shift_z(-1))
        own.append(jnp.concatenate([up, down], axis=0))
    mate = [send(jnp.concatenate(own[:3], axis=0), swap_core())]
    mate += [send(chunk, swap_core()) for chunk in own[3:]]

    given = send(gram_tile(False, pair_live, cols, own, mate), swap_lag())
    kept = gram_tile(True, pair_live, cols, own, mate)
    return lax.dynamic_update_slice(kept, given, (0, (1 - xh) * HALF))


def solution(mesh):
    fine = Mesh(mesh.devices.reshape(N, 2, N, 2, 2), AX)
    return jax.shard_map(
        on_device,
        mesh=fine,
        in_specs=(P(("y", "xl", "z", "a"), "xh"), P()),
        out_specs=P(("y", "xl", "xh"), ("z", "a")),
        check_vma=False,
    )
```

time: 162 us -> 161 us (level)
  local copies, waits for them, and re-layouts: 10.2 us -> 4.74 us
  starting transfers between devices: 65.9 us -> 71.1 us
  other arithmetic: 5.3 us -> 2.01 us
    ppermute x15, starting transfers between devices: 65.9 us -> 71.1 us  [send(): return lax.ppermute(value, AX, to)]
    unnamed x1 -> x0, other arithmetic: 1.98 us -> none
    unnamed x11 -> x22, local copies, waits for them, and re-layouts: 5.65 us -> 3.72 us
  transfers between devices with their start and end apart: 16 -> 16, of which waited for: 9 -> 8; matrix products, arithmetic and copies ran while one was open for 6% -> 1% of each run, Pallas kernels for 5% -> 6%
where the time goes in v3:
time: 161 us; the launch traced here: 160 us
  starting transfers between devices  71.1 us (44%)
  waiting for transfers between devices  49.7 us (31%)
  Pallas kernels  19 us (12%)
  between operations  13.7 us (9%)
  local copies, waits for them, and re-layouts  4.74 us (3%)
  other arithmetic  2.01 us (1%)
    ppermute x15, starting transfers between devices, send(): return lax.ppermute(value, AX, to)  71.1 us
    ppermute x15, waiting for transfers between devices, send(): return lax.ppermute(value, AX, to)  49.7 us
    pallas_call x2, Pallas kernels, gram_tile(): pl.pallas_call(functools.partial(gram_kernel, keep), out_shape=jax.ShapeD...  19 us
    unnamed x22, local copies, waits for them, and re-layouts  3.72 us
  transfers between devices with their start and end apart: 16, of which 8 were waited for; matrix products, arithmetic and copies ran while one was open for 1% of the time, Pallas kernels for 6%

profile of v3, /device:TPU:16, one launch (start us, length us, event | category | flops | bytes accessed | tf_op | source)
XLA Modules:
  0.0 160.3 jit_solution(16936137467354247877)
XLA Ops:
  6.5 0.0 all-gather.2.cloned.1.call-start
  6.5 4.9 %collective-permute-start.2 = (bf16[64,2048]{1,0:T(8,128)(2,1)}, bf16[64,2048]{1,0:T(8,128)(2,1)S(1)}, u32[]{:S(2)}, u32[]{:S(2)}) collective-permute-start(bf16[64,2048]{1,0:T(8,128)(2,1)} %param.2), channel_id=1, source_target_pairs={{0,1},{1,0},{2,3},{3,2},{4,5},{5,4},{6,7},{7,6},{8,9},{9,8},{10,11... | collective-permute-start | bytes 786440 | tf_op jit(solution)/shard_map/ppermute | solution.py:166
  11.5 6.1 %collective-permute-start = (bf16[64,2048]{1,0:T(8,128)(2,1)}, bf16[64,2048]{1,0:T(8,128)(2,1)S(1)}, u32[]{:S(2)}, u32[]{:S(2)}) collective-permute-start(bf16[64,2048]{1,0:T(8,128)(2,1)} %param.2), channel_id=1, source_target_pairs={{0,0},{1,32},{2,256},{3,288},{4,64},{5,96},{6,448},{7,480},{8,128}... | collective-permute-start | bytes 786440 | tf_op jit(solution)/shard_map/ppermute | solution.py:166
  17.6 5.8 %collective-permute-start.1 = (bf16[64,2048]{1,0:T(8,128)(2,1)}, bf16[64,2048]{1,0:T(8,128)(2,1)S(1)}, u32[]{:S(2)}, u32[]{:S(2)}) collective-permute-start(bf16[64,2048]{1,0:T(8,128)(2,1)} %param.2), channel_id=1, source_target_pairs={{0,32},{1,0},{2,288},{3,256},{4,96},{5,64},{6,480},{7,448},{8,160}... | collective-permute-start | bytes 786440 | tf_op jit(solution)/shard_map/ppermute | solution.py:166
  23.3 0.0 collective-permute-done.2
  23.4 1.2 maximum_select_fusion.refs_0_
  24.5 0.0 copy-start.1
  24.5 0.0 collective-permute-done
  24.6 9.0 %collective-permute-done.1 = bf16[64,2048]{1,0:T(8,128)(2,1)S(1)} collective-permute-done((bf16[64,2048]{1,0:T(8,128)(2,1)}, bf16[64,2048]{1,0:T(8,128)(2,1)S(1)}, u32[]{:S(2)}, u32[]{:S(2)}) %collective-permute-start.1) | collective-permute-done | bytes 262176 | tf_op jit(solution)/shard_map/ppermute | solution.py:166
  33.6 0.8 pad_maximum_fusion
  34.4 0.0 all-gather.2.cloned.1.call-update
  34.5 1.9 %collective-permute-start.3 = (bf16[64,4096]{1,0:T(8,128)(2,1)S(1)}, bf16[64,4096]{1,0:T(8,128)(2,1)S(1)}, u32[]{:S(2)}, u32[]{:S(2)}) collective-permute-start(bf16[64,4096]{1,0:T(8,128)(2,1)S(1)} %maximum_select_fusion.refs_0_), channel_id=1, source_target_pairs={{0,4},{1,5},{2,6},{3,7},{4,8},{5,9},{6,10},{7,11},{8,12},{9,13},{1... | collective-permute-start | bytes 1572872 | tf_op jit(solution)/shard_map/ppermute | solution.py:166
  36.4 23.1 %collective-permute-start.4 = (bf16[64,4096]{1,0:T(8,128)(2,1)S(1)}, bf16[64,4096]{1,0:T(8,128)(2,1)S(1)}, u32[]{:S(2)}, u32[]{:S(2)}) collective-permute-start(bf16[64,4096]{1,0:T(8,128)(2,1)S(1)} %maximum_select_fusion.refs_0_), channel_id=1, source_target_pairs={{0,28},{1,29},{2,30},{3,31},{4,0},{5,1},{6,2},{7,3},{8,4},{9,5},{1... | collective-permute-start | bytes 1572872 | tf_op jit(solution)/shard_map/ppermute | solution.py:166
  59.6 8.9 %collective-permute-done.3 = bf16[64,4096]{1,0:T(8,128)(2,1)S(1)} collective-permute-done((bf16[64,4096]{1,0:T(8,128)(2,1)S(1)}, bf16[64,4096]{1,0:T(8,128)(2,1)S(1)}, u32[]{:S(2)}, u32[]{:S(2)}) %collective-permute-start.3) | collective-permute-done | bytes 524320 | tf_op jit(solution)/shard_map/ppermute | solution.py:166
  68.5 1.9 %collective-permute-start.5 = (bf16[64,4096]{1,0:T(8,128)(2,1)S(1)}, bf16[64,4096]{1,0:T(8,128)(2,1)S(1)}, u32[]{:S(2)}, u32[]{:S(2)}) collective-permute-start(bf16[64,4096]{1,0:T(8,128)(2,1)S(1)} %collective-permute-done.3), channel_id=1, source_target_pairs={{0,4},{1,5},{2,6},{3,7},{4,8},{5,9},{6,10},{7,11},{8,12},{9,13},{1... | collective-permute-start | bytes 1572872 | tf_op jit(solution)/shard_map/ppermute | solution.py:166
  70.4 0.1 constant_dynamic-update-slice_fusion.11
  70.5 0.0 collective-permute-done.4
  70.6 5.1 %collective-permute-start.6 = (bf16[64,4096]{1,0:T(8,128)(2,1)S(1)}, bf16[64,4096]{1,0:T(8,128)(2,1)S(1)}, u32[]{:S(2)}, u32[]{:S(2)}) collective-permute-start(bf16[64,4096]{1,0:T(8,128)(2,1)S(1)} %collective-permute-done.4), channel_id=1, source_target_pairs={{0,28},{1,29},{2,30},{3,31},{4,0},{5,1},{6,2},{7,3},{8,4},{9,5},{1... | collective-permute-start | bytes 1572872 | tf_op jit(solution)/shard_map/ppermute | solution.py:166
  75.7 0.1 constant_dynamic-update-slice_fusion.10
  75.8 0.0 copy-done.1
  75.8 0.0 copy-start.2
  75.8 7.8 %collective-permute-done.5 = bf16[64,4096]{1,0:T(8,128)(2,1)S(1)} collective-permute-done((bf16[64,4096]{1,0:T(8,128)(2,1)S(1)}, bf16[64,4096]{1,0:T(8,128)(2,1)S(1)}, u32[]{:S(2)}, u32[]{:S(2)}) %collective-permute-start.5) | collective-permute-done | bytes 524320 | tf_op jit(solution)/shard_map/ppermute | solution.py:166
  83.6 1.9 %collective-permute-start.7 = (bf16[64,4096]{1,0:T(8,128)(2,1)S(1)}, bf16[64,4096]{1,0:T(8,128)(2,1)S(1)}, u32[]{:S(2)}, u32[]{:S(2)}) collective-permute-start(bf16[64,4096]{1,0:T(8,128)(2,1)S(1)} %collective-permute-done.5), channel_id=1, source_target_pairs={{0,4},{1,5},{2,6},{3,7},{4,8},{5,9},{6,10},{7,11},{8,12},{9,13},{1... | collective-permute-start | bytes 1572872 | tf_op jit(solution)/shard_map/ppermute | solution.py:166
  85.5 0.1 constant_dynamic-update-slice_fusion.9
  85.7 0.0 collective-permute-done.6
  85.7 0.1 constant_dynamic-update-slice_fusion.8
  85.8 0.0 copy-start.3
  85.8 1.9 %collective-permute-start.11 = (bf16[320,4096]{1,0:T(8,128)(2,1)S(1)}, bf16[320,4096]{1,0:T(8,128)(2,1)S(1)}, u32[]{:S(2)}, u32[]{:S(2)}) collective-permute-start(bf16[320,4096]{1,0:T(8,128)(2,1)S(1)} %get-tuple-element.11), channel_id=1, source_target_pairs={{0,2},{1,3},{2,0},{3,1},{4,6},{5,7},{6,4},{7,5},{8,10},{9,11},{10,... | collective-permute-start | bytes 7864328 | tf_op jit(solution)/shard_map/ppermute | solution.py:166
  87.7 5.1 %collective-permute-start.8 = (bf16[64,4096]{1,0:T(8,128)(2,1)S(1)}, bf16[64,4096]{1,0:T(8,128)(2,1)S(1)}, u32[]{:S(2)}, u32[]{:S(2)}) collective-permute-start(bf16[64,4096]{1,0:T(8,128)(2,1)S(1)} %collective-permute-done.6), channel_id=1, source_target_pairs={{0,28},{1,29},{2,30},{3,31},{4,0},{5,1},{6,2},{7,3},{8,4},{9,5},{1... | collective-permute-start | bytes 1572872 | tf_op jit(solution)/shard_map/ppermute | solution.py:166
  92.9 5.0 %collective-permute-done.7 = bf16[64,4096]{1,0:T(8,128)(2,1)S(1)} collective-permute-done((bf16[64,4096]{1,0:T(8,128)(2,1)S(1)}, bf16[64,4096]{1,0:T(8,128)(2,1)S(1)}, u32[]{:S(2)}, u32[]{:S(2)}) %collective-permute-start.7) | collective-permute-done | bytes 524320 | tf_op jit(solution)/shard_map/ppermute | solution.py:166
  97.8 1.9 %collective-permute-start.9 = (bf16[32,4096]{1,0:T(8,128)(2,1)S(1)}, bf16[32,4096]{1,0:T(8,128)(2,1)S(1)}, u32[]{:S(2)}, u32[]{:S(2)}) collective-permute-start(bf16[32,4096]{1,0:T(8,128)(2,1)S(1)} %slice.8), channel_id=1, source_target_pairs={{0,4},{1,5},{2,6},{3,7},{4,8},{5,9},{6,10},{7,11},{8,12},{9,13},{1... | collective-permute-start | bytes 786440 | tf_op jit(solution)/shard_map/ppermute | solution.py:166
  99.8 4.9 %collective-permute-done.8 = bf16[64,4096]{1,0:T(8,128)(2,1)S(1)} collective-permute-done((bf16[64,4096]{1,0:T(8,128)(2,1)S(1)}, bf16[64,4096]{1,0:T(8,128)(2,1)S(1)}, u32[]{:S(2)}, u32[]{:S(2)}) %collective-permute-start.8) | collective-permute-done | bytes 524320 | tf_op jit(solution)/shard_map/ppermute | solution.py:166
  104.7 0.0 copy-done.2
  104.7 0.0 copy-start.4
  104.7 1.9 %collective-permute-start.12 = (bf16[128,4096]{1,0:T(8,128)(2,1)S(1)}, bf16[128,4096]{1,0:T(8,128)(2,1)S(1)}, u32[]{:S(2)}, u32[]{:S(2)}) collective-permute-start(bf16[128,4096]{1,0:T(8,128)(2,1)S(1)} %constant_dynamic-update-slice_fusion.4.refs_3_), channel_id=1, source_target_pairs={{0,2},{1,3},{2,0},{3,1},{4,6},{5,7},{6,4},{7,5},{8,10},{9,11},{10,... | collective-permute-start | bytes 3145736 | tf_op jit(solution)/shard_map/ppermute | solution.py:166
  106.7 5.6 %collective-permute-start.10 = (bf16[32,4096]{1,0:T(8,128)(2,1)S(1)}, bf16[32,4096]{1,0:T(8,128)(2,1)S(1)}, u32[]{:S(2)}, u32[]{:S(2)}) collective-permute-start(bf16[32,4096]{1,0:T(8,128)(2,1)S(1)} %slice.9), channel_id=1, source_target_pairs={{0,28},{1,29},{2,30},{3,31},{4,0},{5,1},{6,2},{7,3},{8,4},{9,5},{1... | collective-permute-start | bytes 786440 | tf_op jit(solution)/shard_map/ppermute | solution.py:166
  112.3 0.0 collective-permute-done.9
  112.3 6.2 %collective-permute-done.10 = bf16[32,4096]{1,0:T(8,128)(2,1)S(1)} collective-permute-done((bf16[32,4096]{1,0:T(8,128)(2,1)S(1)}, bf16[32,4096]{1,0:T(8,128)(2,1)S(1)}, u32[]{:S(2)}, u32[]{:S(2)}) %collective-permute-start.10) | collective-permute-done | bytes 262176 | tf_op jit(solution)/shard_map/ppermute | solution.py:166
  118.5 0.0 copy-start.6
  118.5 1.9 %collective-permute-start.13 = (bf16[64,4096]{1,0:T(8,128)(2,1)S(1)}, bf16[64,4096]{1,0:T(8,128)(2,1)S(1)}, u32[]{:S(2)}, u32[]{:S(2)}) collective-permute-start(bf16[64,4096]{1,0:T(8,128)(2,1)S(1)} %constant_dynamic-update-slice_fusion.6.refs_4_), channel_id=1, source_target_pairs={{0,2},{1,3},{2,0},{3,1},{4,6},{5,7},{6,4},{7,5},{8,10},{9,11},{10,... | collective-permute-start | bytes 1572872 | tf_op jit(solution)/shard_map/ppermute | solution.py:166
  120.5 1.9 %collective-permute-done.13.refs_7_ = bf16[64,4096]{1,0:T(8,128)(2,1)S(1)} collective-permute-done((bf16[64,4096]{1,0:T(8,128)(2,1)S(1)}, bf16[64,4096]{1,0:T(8,128)(2,1)S(1)}, u32[]{:S(2)}, u32[]{:S(2)}) %collective-permute-start.13) | collective-permute-done | bytes 524320 | tf_op jit(solution)/shard_map/ppermute | solution.py:166
  122.3 0.0 copy-done.3
  122.3 0.0 copy-start.7
  122.3 0.0 collective-permute-done.12.refs_6_
  122.3 0.0 copy-done.4
  122.4 0.8 copy-done.7
  123.2 0.0 copy-start.5
  123.2 1.0 copy-done.5
  124.1 0.0 collective-permute-done.11.refs_5_
  124.2 0.0 copy-start
  124.2 0.0 all-gather.2.cloned.1.call-done.cols_hbm
  124.2 0.0 copy-done.6
  124.2 1.5 copy-done
  125.7 9.4 %shard_map.29 = bf16[512,512]{1,0:T(8,128)(2,1)} custom-call(s32[16,16]{1,0:T(8,128)} %live_ref.3, bf16[512,4096]{1,0:T(8,128)(2,1)} %all-gather.2.cloned.1.call-done.cols_hbm, bf16[64,4096]{1,0:T(8,128)(2,1)} %copy-done.1, bf16[128,4096]{1,0:T(8,128)(2,1)} %copy-done.2, bf16[128,4096]{1,0:T(8,128)(2,1)} %copy-done.3, bf16[128,4096]{1,0:T(8,128)(2,1)} %copy-done.4, ...), custom_call_target="tpu_custom_call" | custom-call | flops 2147483648 | bytes 9437184 | tf_op jit(solution)/shard_map/pallas_call | solution.py:140
  135.1 1.9 %collective-permute-start.14 = (bf16[512,512]{1,0:T(8,128)(2,1)}, bf16[512,512]{1,0:T(8,128)(2,1)S(1)}, u32[]{:S(2)}, u32[]{:S(2)}) collective-permute-start(bf16[512,512]{1,0:T(8,128)(2,1)} %shard_map.29), channel_id=1, source_target_pairs={{0,1},{1,0},{2,3},{3,2},{4,5},{5,4},{6,7},{7,6},{8,9},{9,8},{10,11... | collective-permute-start | bytes 1572872 | tf_op jit(solution)/shard_map/ppermute | solution.py:166
  137.0 9.6 %shard_map.28 = bf16[512,1024]{1,0:T(8,128)(2,1)} custom-call(s32[16,16]{1,0:T(8,128)} %live_ref.3, bf16[512,4096]{1,0:T(8,128)(2,1)} %all-gather.2.cloned.1.call-done.cols_hbm, bf16[64,4096]{1,0:T(8,128)(2,1)} %copy-done.1, bf16[128,4096]{1,0:T(8,128)(2,1)} %copy-done.2, bf16[128,4096]{1,0:T(8,128)(2,1)} %copy-done.3, bf16[128,4096]{1,0:T(8,128)(2,1)} %copy-done.4, ...), custom_call_target="tpu_custom_call" | custom-call | flops 2147483648 | bytes 9437184 | tf_op jit(solution)/shard_map/pallas_call | solution.py:140
  146.6 6.0 %collective-permute-done.14 = bf16[512,512]{1,0:T(8,128)(2,1)S(1)} collective-permute-done((bf16[512,512]{1,0:T(8,128)(2,1)}, bf16[512,512]{1,0:T(8,128)(2,1)S(1)}, u32[]{:S(2)}, u32[]{:S(2)}) %collective-permute-start.14) | collective-permute-done | bytes 524320 | tf_op jit(solution)/shard_map/ppermute | solution.py:166
  152.6 0.8 constant_dynamic-update-slice_fusion.13
  (7 shorter events, 0.2 us)
Async XLA Ops:
  6.5 117.6 %all-gather.2.cloned.1.call-start = ((), (), s32[]{:S(2)}) async-start(), calls=%async_computation | async-start | bytes 4718592 | tf_op jit(solution)/shard_map/all_gather | solution.py:177
  6.5 16.8 %collective-permute-start.2 = (bf16[64,2048]{1,0:T(8,128)(2,1)}, bf16[64,2048]{1,0:T(8,128)(2,1)S(1)}, u32[]{:S(2)}, u32[]{:S(2)}) collective-permute-start(bf16[64,2048]{1,0:T(8,128)(2,1)} %param.2), channel_id=1, source_target_pairs={{0,1},{1,0},{2,3},{3,2},{4,5},{5,4},{6,7},{7,6},{8,9},{9,8},{10,11... | collective-permute-start | bytes 786440 | tf_op jit(solution)/shard_map/ppermute | solution.py:166
  11.5 13.1 %collective-permute-start = (bf16[64,2048]{1,0:T(8,128)(2,1)}, bf16[64,2048]{1,0:T(8,128)(2,1)S(1)}, u32[]{:S(2)}, u32[]{:S(2)}) collective-permute-start(bf16[64,2048]{1,0:T(8,128)(2,1)} %param.2), channel_id=1, source_target_pairs={{0,0},{1,32},{2,256},{3,288},{4,64},{5,96},{6,448},{7,480},{8,128}... | collective-permute-start | bytes 786440 | tf_op jit(solution)/shard_map/ppermute | solution.py:166
  17.6 16.0 %collective-permute-start.1 = (bf16[64,2048]{1,0:T(8,128)(2,1)}, bf16[64,2048]{1,0:T(8,128)(2,1)S(1)}, u32[]{:S(2)}, u32[]{:S(2)}) collective-permute-start(bf16[64,2048]{1,0:T(8,128)(2,1)} %param.2), channel_id=1, source_target_pairs={{0,32},{1,0},{2,288},{3,256},{4,96},{5,64},{6,480},{7,448},{8,160}... | collective-permute-start | bytes 786440 | tf_op jit(solution)/shard_map/ppermute | solution.py:166
  24.5 51.3 %copy-start.1 = (bf16[64,4096]{1,0:T(8,128)(2,1)}, bf16[64,4096]{1,0:T(8,128)(2,1)S(1)}, u32[]{:S(2)}) copy-start(bf16[64,4096]{1,0:T(8,128)(2,1)S(1)} %maximum_select_fusion.refs_0_) | copy-start | bytes 1572868
  34.5 34.1 %collective-permute-start.3 = (bf16[64,4096]{1,0:T(8,128)(2,1)S(1)}, bf16[64,4096]{1,0:T(8,128)(2,1)S(1)}, u32[]{:S(2)}, u32[]{:S(2)}) collective-permute-start(bf16[64,4096]{1,0:T(8,128)(2,1)S(1)} %maximum_select_fusion.refs_0_), channel_id=1, source_target_pairs={{0,4},{1,5},{2,6},{3,7},{4,8},{5,9},{6,10},{7,11},{8,12},{9,13},{1... | collective-permute-start | bytes 1572872 | tf_op jit(solution)/shard_map/ppermute | solution.py:166
  36.4 34.2 %collective-permute-start.4 = (bf16[64,4096]{1,0:T(8,128)(2,1)S(1)}, bf16[64,4096]{1,0:T(8,128)(2,1)S(1)}, u32[]{:S(2)}, u32[]{:S(2)}) collective-permute-start(bf16[64,4096]{1,0:T(8,128)(2,1)S(1)} %maximum_select_fusion.refs_0_), channel_id=1, source_target_pairs={{0,28},{1,29},{2,30},{3,31},{4,0},{5,1},{6,2},{7,3},{8,4},{9,5},{1... | collective-permute-start | bytes 1572872 | tf_op jit(solution)/shard_map/ppermute | solution.py:166
  68.5 15.1 %collective-permute-start.5 = (bf16[64,4096]{1,0:T(8,128)(2,1)S(1)}, bf16[64,4096]{1,0:T(8,128)(2,1)S(1)}, u32[]{:S(2)}, u32[]{:S(2)}) collective-permute-start(bf16[64,4096]{1,0:T(8,128)(2,1)S(1)} %collective-permute-done.3), channel_id=1, source_target_pairs={{0,4},{1,5},{2,6},{3,7},{4,8},{5,9},{6,10},{7,11},{8,12},{9,13},{1... | collective-permute-start | bytes 1572872 | tf_op jit(solution)/shard_map/ppermute | solution.py:166
  70.6 15.1 %collective-permute-start.6 = (bf16[64,4096]{1,0:T(8,128)(2,1)S(1)}, bf16[64,4096]{1,0:T(8,128)(2,1)S(1)}, u32[]{:S(2)}, u32[]{:S(2)}) collective-permute-start(bf16[64,4096]{1,0:T(8,128)(2,1)S(1)} %collective-permute-done.4), channel_id=1, source_target_pairs={{0,28},{1,29},{2,30},{3,31},{4,0},{5,1},{6,2},{7,3},{8,4},{9,5},{1... | collective-permute-start | bytes 1572872 | tf_op jit(solution)/shard_map/ppermute | solution.py:166
  75.8 28.9 %copy-start.2 = (bf16[128,4096]{1,0:T(8,128)(2,1)}, bf16[128,4096]{1,0:T(8,128)(2,1)S(1)}, u32[]{:S(2)}) copy-start(bf16[128,4096]{1,0:T(8,128)(2,1)S(1)} %get-tuple-element.16.refs_1_) | copy-start | bytes 3145732
  83.6 14.2 %collective-permute-start.7 = (bf16[64,4096]{1,0:T(8,128)(2,1)S(1)}, bf16[64,4096]{1,0:T(8,128)(2,1)S(1)}, u32[]{:S(2)}, u32[]{:S(2)}) collective-permute-start(bf16[64,4096]{1,0:T(8,128)(2,1)S(1)} %collective-permute-done.5), channel_id=1, source_target_pairs={{0,4},{1,5},{2,6},{3,7},{4,8},{5,9},{6,10},{7,11},{8,12},{9,13},{1... | collective-permute-start | bytes 1572872 | tf_op jit(solution)/shard_map/ppermute | solution.py:166
  85.8 36.6 %copy-start.3 = (bf16[128,4096]{1,0:T(8,128)(2,1)}, bf16[128,4096]{1,0:T(8,128)(2,1)S(1)}, u32[]{:S(2)}) copy-start(bf16[128,4096]{1,0:T(8,128)(2,1)S(1)} %get-tuple-element.12.refs_2_) | copy-start | bytes 3145732
  85.8 38.4 %collective-permute-start.11 = (bf16[320,4096]{1,0:T(8,128)(2,1)S(1)}, bf16[320,4096]{1,0:T(8,128)(2,1)S(1)}, u32[]{:S(2)}, u32[]{:S(2)}) collective-permute-start(bf16[320,4096]{1,0:T(8,128)(2,1)S(1)} %get-tuple-element.11), channel_id=1, source_target_pairs={{0,2},{1,3},{2,0},{3,1},{4,6},{5,7},{6,4},{7,5},{8,10},{9,11},{10,... | collective-permute-start | bytes 7864328 | tf_op jit(solution)/shard_map/ppermute | solution.py:166
  87.7 17.0 %collective-permute-start.8 = (bf16[64,4096]{1,0:T(8,128)(2,1)S(1)}, bf16[64,4096]{1,0:T(8,128)(2,1)S(1)}, u32[]{:S(2)}, u32[]{:S(2)}) collective-permute-start(bf16[64,4096]{1,0:T(8,128)(2,1)S(1)} %collective-permute-done.6), channel_id=1, source_target_pairs={{0,28},{1,29},{2,30},{3,31},{4,0},{5,1},{6,2},{7,3},{8,4},{9,5},{1... | collective-permute-start | bytes 1572872 | tf_op jit(solution)/shard_map/ppermute | solution.py:166
  97.8 14.5 %collective-permute-start.9 = (bf16[32,4096]{1,0:T(8,128)(2,1)S(1)}, bf16[32,4096]{1,0:T(8,128)(2,1)S(1)}, u32[]{:S(2)}, u32[]{:S(2)}) collective-permute-start(bf16[32,4096]{1,0:T(8,128)(2,1)S(1)} %slice.8), channel_id=1, source_target_pairs={{0,4},{1,5},{2,6},{3,7},{4,8},{5,9},{6,10},{7,11},{8,12},{9,13},{1... | collective-permute-start | bytes 786440 | tf_op jit(solution)/shard_map/ppermute | solution.py:166
  104.7 17.6 %copy-start.4 = (bf16[128,4096]{1,0:T(8,128)(2,1)}, bf16[128,4096]{1,0:T(8,128)(2,1)S(1)}, u32[]{:S(2)}) copy-start(bf16[128,4096]{1,0:T(8,128)(2,1)S(1)} %constant_dynamic-update-slice_fusion.4.refs_3_) | copy-start | bytes 3145732
  104.7 17.6 %collective-permute-start.12 = (bf16[128,4096]{1,0:T(8,128)(2,1)S(1)}, bf16[128,4096]{1,0:T(8,128)(2,1)S(1)}, u32[]{:S(2)}, u32[]{:S(2)}) collective-permute-start(bf16[128,4096]{1,0:T(8,128)(2,1)S(1)} %constant_dynamic-update-slice_fusion.4.refs_3_), channel_id=1, source_target_pairs={{0,2},{1,3},{2,0},{3,1},{4,6},{5,7},{6,4},{7,5},{8,10},{9,11},{10,... | collective-permute-start | bytes 3145736 | tf_op jit(solution)/shard_map/ppermute | solution.py:166
  106.7 11.8 %collective-permute-start.10 = (bf16[32,4096]{1,0:T(8,128)(2,1)S(1)}, bf16[32,4096]{1,0:T(8,128)(2,1)S(1)}, u32[]{:S(2)}, u32[]{:S(2)}) collective-permute-start(bf16[32,4096]{1,0:T(8,128)(2,1)S(1)} %slice.9), channel_id=1, source_target_pairs={{0,28},{1,29},{2,30},{3,31},{4,0},{5,1},{6,2},{7,3},{8,4},{9,5},{1... | collective-permute-start | bytes 786440 | tf_op jit(solution)/shard_map/ppermute | solution.py:166
  118.5 5.6 %copy-start.6 = (bf16[64,4096]{1,0:T(8,128)(2,1)}, bf16[64,4096]{1,0:T(8,128)(2,1)S(1)}, u32[]{:S(2)}) copy-start(bf16[64,4096]{1,0:T(8,128)(2,1)S(1)} %constant_dynamic-update-slice_fusion.6.refs_4_) | copy-start | bytes 1572868
  118.5 3.8 %collective-permute-start.13 = (bf16[64,4096]{1,0:T(8,128)(2,1)S(1)}, bf16[64,4096]{1,0:T(8,128)(2,1)S(1)}, u32[]{:S(2)}, u32[]{:S(2)}) collective-permute-start(bf16[64,4096]{1,0:T(8,128)(2,1)S(1)} %constant_dynamic-update-slice_fusion.6.refs_4_), channel_id=1, source_target_pairs={{0,2},{1,3},{2,0},{3,1},{4,6},{5,7},{6,4},{7,5},{8,10},{9,11},{10,... | collective-permute-start | bytes 1572872 | tf_op jit(solution)/shard_map/ppermute | solution.py:166
  122.3 0.8 copy-start.7
  123.2 1.0 copy-start.5
  124.2 1.5 copy-start
  135.1 17.6 %collective-permute-start.14 = (bf16[512,512]{1,0:T(8,128)(2,1)}, bf16[512,512]{1,0:T(8,128)(2,1)S(1)}, u32[]{:S(2)}, u32[]{:S(2)}) collective-permute-start(bf16[512,512]{1,0:T(8,128)(2,1)} %shard_map.29), channel_id=1, source_target_pairs={{0,1},{1,0},{2,3},{3,2},{4,5},{5,4},{6,7},{7,6},{8,9},{9,8},{10,11... | collective-permute-start | bytes 1572872 | tf_op jit(solution)/shard_map/ppermute | solution.py:166
Sparse Core Ops, SparseCore 0:
  34.6 66.8 all-gather.1

commit v4 on v0

v4 whole, which is shorter than its diff:
```python
import functools

import jax
import jax.numpy as jnp
from jax import lax
from jax.experimental import pallas as pl
from jax.experimental.pallas import tpu as pltpu
from jax.sharding import Mesh
from jax.sharding import PartitionSpec as P

AX = ("y", "xl", "z", "a", "xh")
N = 8
SUB = 64
HALF = N * SUB
DEPTH = 1024
SHIFT = ((0, 4), (1, -1), (2, -2), (3, -3))
MIB = 1024 * 1024


def index(y, xl, z, a, xh):
    return (((y % N * 2 + xl) * N + z % N) * 2 + a) * 2 + xh


def pairs(target):
    every = [
        (y, xl, z, a, xh)
        for y in range(N)
        for xl in range(2)
        for z in range(N)
        for a in range(2)
        for xh in range(2)
    ]
    return [(index(*d), index(*target(*d))) for d in every]


def col_pairs(stage):
    def target(y, xl, z, a, half):
        part = z // 4
        return y + SHIFT[z % 4][a], half ^ part ^ stage, y, xl, part

    return pairs(target)


def shift_y(step):
    return pairs(lambda y, xl, z, a, xh: (y + step, xl, z, a, xh))


def swap_lag():
    return pairs(lambda y, xl, z, a, xh: (y, xl, z, a, 1 - xh))


def square_sums(x):
    total = jnp.zeros((x.shape[0], 128), jnp.float32)
    for c in range(x.shape[1] // 128):
        part = x[:, c * 128 : (c + 1) * 128].astype(jnp.float32)
        total += part * part
    return total


def place(d):
    o = (lax.axis_index("y") - d - lax.axis_index("z")) & (N - 1)
    j = jnp.where(o < 4, 2 * o, (17 - 2 * o) & (N - 1))
    return pl.multiple_of(j * SUB, SUB)


def order_kernel(chunks, *refs):
    count = len(chunks)
    sources = refs[:count]
    cols, norm, held, sums, sem = refs[-5:]
    copies = []
    for i, (source, (d, first, size)) in enumerate(zip(sources, chunks)):
        at = pl.ds(i * SUB, size)
        load = pltpu.make_async_copy(source, held.at[at, :], sem.at[0, i])
        load.start()
        copies.append((load, at, pl.ds(place(d) + first, size)))
    stores = []
    for i, (load, at, to) in enumerate(copies):
        load.wait()
        stores.append(
            pltpu.make_async_copy(held.at[at, :], cols.at[to, :], sem.at[1, i])
        )
        stores[-1].start()
        sums[at, :] = square_sums(held[at, :])
        stores.append(
            pltpu.make_async_copy(sums.at[at, :], norm.at[to, :], sem.at[2, i])
        )
        stores[-1].start()
    for store in stores:
        store.wait()


def in_order(chunks, sources, held=()):
    samples = sources[0].shape[1]
    count = len(chunks)
    return pl.pallas_call(
        functools.partial(order_kernel, chunks),
        out_shape=(
            jax.ShapeDtypeStruct((HALF, samples), jnp.bfloat16),
            jax.ShapeDtypeStruct((HALF, 128), jnp.float32),
        ),
        in_specs=[pl.BlockSpec(memory_space=pl.ANY)] * (count + len(held)),
        out_specs=[pl.BlockSpec(memory_space=pl.ANY)] * 2,
        input_output_aliases={count + i: i for i in range(len(held))},
        scratch_shapes=[
            pltpu.VMEM((count * SUB, samples), jnp.bfloat16),
            pltpu.VMEM((count * SUB, 128), jnp.float32),
            pltpu.SemaphoreType.DMA((3, count)),
        ],
        compiler_params=pltpu.CompilerParams(vmem_limit_bytes=16 * MIB),
        cost_estimate=pl.CostEstimate(
            flops=2 * count * SUB * samples,
            bytes_accessed=count * MIB,
            transcendentals=0,
        ),
    )(*sources, *held)


def gram_kernel(keep, live_ref, rows_hbm, cols_hbm, col_norm, out_ref, *scratch):
    rows, cols, inner, row_norm, sem = scratch
    y, xl, z, a, xh = (lax.axis_index(name) for name in AX)
    half = xh if keep else 1 - xh
    first = pl.multiple_of(half * HALF, HALF)
    blocks = rows.shape[0]
    samples = blocks * DEPTH
    copies = []
    for k in range(blocks):
        deep = pl.ds(k * DEPTH, DEPTH)
        copies.append(
            (
                pltpu.make_async_copy(cols_hbm.at[:, deep], cols.at[k], sem.at[0, k]),
                pltpu.make_async_copy(
                    rows_hbm.at[pl.ds(first, HALF), deep], rows.at[k], sem.at[1, k]
                ),
            )
        )
        for copy in copies[-1]:
            copy.start()
    for k in range(blocks):
        for copy in copies[k]:
            copy.wait()
        part = lax.dot_general(
            rows[k], cols[k], (((1,), (1,)), ((), ())), preferred_element_type=jnp.float32
        )
        norm = square_sums(rows[k])
        if k == 0:
            inner[...] = part
            row_norm[...] = norm
        else:
            inner[...] += part
            row_norm[...] += norm
    scale = live_ref[2 * y + xl, 2 * z + a].astype(jnp.float32)
    down = jnp.sum(row_norm[...], axis=1, keepdims=True)
    across = jnp.sum(col_norm[...].T, axis=0, keepdims=True)
    dist = down + across - 2.0 * inner[...]
    gram = jnp.exp(dist * (-2.0 / samples)) * scale
    base = pl.multiple_of(xh * HALF, HALF) if keep else 0
    out_ref[:, pl.ds(base, HALF)] = gram.astype(jnp.bfloat16)


def gram_tile(keep, pair_live, rows, cols, col_norm):
    samples = cols.shape[1]
    width = 2 * HALF if keep else HALF
    operand = pltpu.VMEM((samples // DEPTH, HALF, DEPTH), jnp.bfloat16)
    return pl.pallas_call(
        functools.partial(gram_kernel, keep),
        out_shape=jax.ShapeDtypeStruct((HALF, width), jnp.bfloat16),
        in_specs=[
            pl.BlockSpec(memory_space=pltpu.SMEM),
            pl.BlockSpec(memory_space=pl.ANY),
            pl.BlockSpec(memory_space=pl.ANY),
            pl.BlockSpec(memory_space=pltpu.VMEM),
        ],
        out_specs=pl.BlockSpec(memory_space=pltpu.VMEM),
        scratch_shapes=[
            operand,
            operand,
            pltpu.VMEM((HALF, HALF), jnp.float32),
            pltpu.VMEM((HALF, 128), jnp.float32),
            pltpu.SemaphoreType.DMA((2, samples // DEPTH)),
        ],
        compiler_params=pltpu.CompilerParams(vmem_limit_bytes=56 * MIB),
        cost_estimate=pl.CostEstimate(
            flops=2 * HALF * HALF * samples,
            bytes_accessed=9 * MIB,
            transcendentals=HALF * HALF,
        ),
    )(pair_live, rows, cols, col_norm)


def on_device(trajectories, pair_live):
    xl, xh = lax.axis_index("xl"), lax.axis_index("xh")

    def send(value, to):
        return lax.ppermute(value, AX, to)

    other = send(trajectories, swap_lag())
    early = send(trajectories, col_pairs(0))
    late = send(trajectories, col_pairs(1))
    rows = jnp.where(
        xl == 0,
        jnp.concatenate([trajectories, other], axis=1),
        jnp.concatenate([other, trajectories], axis=1),
    )
    rows = lax.all_gather(rows, ("z", "a"), axis=0, tiled=True)
    cols = jnp.concatenate([early, late], axis=1)

    chunks, sources = [(0, 0, SUB)], [cols]
    up = down = cols
    for step in range(1, N // 2):
        up, down = send(up, shift_y(1)), send(down, shift_y(-1))
        chunks += [(step, 0, SUB), (-step, 0, SUB)]
        sources += [up, down]
    most = in_order(chunks, sources)
    part = SUB // 2
    last = [send(up[:part], shift_y(1)), send(down[part:], shift_y(-1))]
    chunks = [(N // 2, 0, part), (N // 2, part, part)]
    cols, col_norm = in_order(chunks, last, most)

    given = send(gram_tile(False, pair_live, rows, cols, col_norm), swap_lag())
    kept = gram_tile(True, pair_live, rows, cols, col_norm)
    return lax.dynamic_update_slice(kept, given, (0, (1 - xh) * HALF))


def solution(mesh):
    fine = Mesh(mesh.devices.reshape(N, 2, N, 2, 2), AX)
    return jax.shard_map(
        on_device,
        mesh=fine,
        in_specs=(P(("y", "xl", "z", "a"), "xh"), P()),
        out_specs=P(("y", "xl", "xh"), ("z", "a")),
        check_vma=False,
    )
```

time: 354 us -> 148 us (0.42)
  waiting for transfers between devices: 316 us -> 67.2 us
  starting transfers between devices: 0.08 us -> 46.8 us
  Pallas kernels: 0 us -> 14.6 us
  other arithmetic: 10.5 us -> 1.94 us
  matrix products: 8.28 us -> 0 us
    psum x1 -> x0, waiting for transfers between devices: 201 us -> none  [from_root(): return lax.psum(kept, axis)]
    ppermute x0 -> x12, waiting for transfers between devices: none -> 67.2 us  [send(): return lax.ppermute(value, AX, to)]
    reduce_scatter x1 -> x0, waiting for transfers between devices: 61.6 us -> none  [on_device(): lax.psum_scatter(pair_distance(row_block, col_block, row_norm, col_norm),...]
    all_gather x1, waiting for transfers between devices: 52.5 us -> 0.01 us  [on_device(): rows = lax.all_gather(rows, ('z', 'a'), axis=0, tiled=True)]
    ppermute x0 -> x12, starting transfers between devices: none -> 46.8 us  [send(): return lax.ppermute(value, AX, to)]
    pallas_call x0 -> x4, Pallas kernels: none -> 14.6 us  [the longest x2 12.5 us: gram_tile(): pl.pallas_call(functools.partial(gram_kernel, keep), out_shape=jax.ShapeD...]
    dot_general x1 -> x0, matrix products: 8.28 us -> none  [pair_distance(): lax.dot_general(left, right, (((1,), (1,)), ((), ())), preferred_element_...]
    reduce_sum x2 -> x0, other arithmetic: 6.29 us -> none  [squares(): return jnp.sum(jnp.square(block.astype(jnp.float32)), axis=1)]
  transfers between devices with their start and end apart: 3 -> 13, of which waited for: 3 -> 9; matrix products, arithmetic and copies ran while one was open for 1% -> 0% of each run, Pallas kernels for 0% -> 6%
where the time goes in v4:
time: 148 us
  waiting for transfers between devices  67.2 us (45%)
  starting transfers between devices  46.8 us (32%)
  Pallas kernels  14.6 us (10%)
  between operations  13.6 us (9%)
  local copies, waits for them, and re-layouts  3.56 us (2%)
  other arithmetic  1.94 us (1%)
    ppermute x12, waiting for transfers between devices, send(): return lax.ppermute(value, AX, to)  67.2 us
    ppermute x12, starting transfers between devices, send(): return lax.ppermute(value, AX, to)  46.8 us
    pallas_call x2, Pallas kernels, gram_tile(): pl.pallas_call(functools.partial(gram_kernel, keep), out_shape=jax.ShapeD...  12.5 us
  transfers between devices with their start and end apart: 13, of which 9 were waited for; matrix products, arithmetic and copies ran while one was open for 0% of the time, Pallas kernels for 6%

profile of v4, /device:TPU:6, one launch (start us, length us, event | category | flops | bytes accessed | tf_op | source)
XLA Modules:
  0.0 147.7 jit_solution(8596878775684618452)
XLA Ops:
  6.5 0.0 all-gather.2.cloned.1.call-start
  6.5 3.3 %collective-permute-start = (bf16[64,2048]{1,0:T(8,128)(2,1)}, bf16[64,2048]{1,0:T(8,128)(2,1)S(1)}, u32[]{:S(2)}, u32[]{:S(2)}) collective-permute-start(bf16[64,2048]{1,0:T(8,128)(2,1)} %param.2), channel_id=1, source_target_pairs={{0,1},{1,0},{2,3},{3,2},{4,5},{5,4},{6,7},{7,6},{8,9},{9,8},{10,11... | collective-permute-start | bytes 786440 | tf_op jit(solution)/shard_map/ppermute | solution.py:194
  9.9 8.3 %collective-permute-done = bf16[64,2048]{1,0:T(8,128)(2,1)S(1)} collective-permute-done((bf16[64,2048]{1,0:T(8,128)(2,1)}, bf16[64,2048]{1,0:T(8,128)(2,1)S(1)}, u32[]{:S(2)}, u32[]{:S(2)}) %collective-permute-start) | collective-permute-done | bytes 262176 | tf_op jit(solution)/shard_map/ppermute | solution.py:194
  18.2 1.9 %maximum_select_fusion = bf16[64,4096]{1,0:T(8,128)(2,1)} fusion(bf16[64,2048]{1,0:T(8,128)(2,1)S(1)} %collective-permute-done, bf16[64,2048]{1,0:T(8,128)(2,1)} %param.2, pred[]{:T(512)S(6)} %eq.3), kind=kLoop, calls=%fused_computation | loop fusion | flops 2359296 | bytes 1048577 | tf_op jit(solution)/shard_map/jit(_where)/select_n | solution.py:199
  20.1 0.0 all-gather.2.cloned.1.call-update
  20.2 1.9 %collective-permute-start.1 = (bf16[64,2048]{1,0:T(8,128)(2,1)}, bf16[64,2048]{1,0:T(8,128)(2,1)S(1)}, u32[]{:S(2)}, u32[]{:S(2)}) collective-permute-start(bf16[64,2048]{1,0:T(8,128)(2,1)} %param.2), channel_id=1, source_target_pairs={{0,0},{1,32},{2,256},{3,288},{4,64},{5,96},{6,448},{7,480},{8,128}... | collective-permute-start | bytes 786440 | tf_op jit(solution)/shard_map/ppermute | solution.py:194
  22.1 7.9 %collective-permute-start.2 = (bf16[64,2048]{1,0:T(8,128)(2,1)}, bf16[64,2048]{1,0:T(8,128)(2,1)S(1)}, u32[]{:S(2)}, u32[]{:S(2)}) collective-permute-start(bf16[64,2048]{1,0:T(8,128)(2,1)} %param.2), channel_id=1, source_target_pairs={{0,32},{1,0},{2,288},{3,256},{4,96},{5,64},{6,480},{7,448},{8,160}... | collective-permute-start | bytes 786440 | tf_op jit(solution)/shard_map/ppermute | solution.py:194
  30.0 7.1 %collective-permute-done.1 = bf16[64,2048]{1,0:T(8,128)(2,1)S(1)} collective-permute-done((bf16[64,2048]{1,0:T(8,128)(2,1)}, bf16[64,2048]{1,0:T(8,128)(2,1)S(1)}, u32[]{:S(2)}, u32[]{:S(2)}) %collective-permute-start.1) | collective-permute-done | bytes 262176 | tf_op jit(solution)/shard_map/ppermute | solution.py:194
  37.1 11.4 %collective-permute-done.2 = bf16[64,2048]{1,0:T(8,128)(2,1)S(1)} collective-permute-done((bf16[64,2048]{1,0:T(8,128)(2,1)}, bf16[64,2048]{1,0:T(8,128)(2,1)S(1)}, u32[]{:S(2)}, u32[]{:S(2)}) %collective-permute-start.2) | collective-permute-done | bytes 262176 | tf_op jit(solution)/shard_map/ppermute | solution.py:194
  48.6 7.2 %collective-permute-start.7 = (bf16[64,4096]{1,0:T(8,128)(2,1)S(1)}, bf16[64,4096]{1,0:T(8,128)(2,1)S(1)}, u32[]{:S(2)}, u32[]{:S(2)}) collective-permute-start(bf16[64,4096]{1,0:T(8,128)(2,1)S(1)} %constant_dynamic-update-slice_fusion.refs_0_), channel_id=1, source_target_pairs={{0,448},{1,449},{2,450},{3,451},{4,452},{5,453},{6,454},{7,455},{8... | collective-permute-start | bytes 1572872 | tf_op jit(solution)/shard_map/ppermute | solution.py:194
  55.8 1.9 %collective-permute-start.3 = (bf16[64,4096]{1,0:T(8,128)(2,1)S(1)}, bf16[64,4096]{1,0:T(8,128)(2,1)S(1)}, u32[]{:S(2)}, u32[]{:S(2)}) collective-permute-start(bf16[64,4096]{1,0:T(8,128)(2,1)S(1)} %constant_dynamic-update-slice_fusion.refs_0_), channel_id=1, source_target_pairs={{0,64},{1,65},{2,66},{3,67},{4,68},{5,69},{6,70},{7,71},{8,72},{9,... | collective-permute-start | bytes 1572872 | tf_op jit(solution)/shard_map/ppermute | solution.py:194
  57.7 10.2 %collective-permute-done.7.refs_2_ = bf16[64,4096]{1,0:T(8,128)(2,1)S(1)} collective-permute-done((bf16[64,4096]{1,0:T(8,128)(2,1)S(1)}, bf16[64,4096]{1,0:T(8,128)(2,1)S(1)}, u32[]{:S(2)}, u32[]{:S(2)}) %collective-permute-start.7) | collective-permute-done | bytes 524320 | tf_op jit(solution)/shard_map/ppermute | solution.py:194
  68.0 5.6 %collective-permute-start.8 = (bf16[64,4096]{1,0:T(8,128)(2,1)S(1)}, bf16[64,4096]{1,0:T(8,128)(2,1)S(1)}, u32[]{:S(2)}, u32[]{:S(2)}) collective-permute-start(bf16[64,4096]{1,0:T(8,128)(2,1)S(1)} %collective-permute-done.7.refs_2_), channel_id=1, source_target_pairs={{0,448},{1,449},{2,450},{3,451},{4,452},{5,453},{6,454},{7,455},{8... | collective-permute-start | bytes 1572872 | tf_op jit(solution)/shard_map/ppermute | solution.py:194
  73.6 0.0 collective-permute-done.3.refs_1_
  73.6 1.9 %collective-permute-start.4 = (bf16[64,4096]{1,0:T(8,128)(2,1)S(1)}, bf16[64,4096]{1,0:T(8,128)(2,1)S(1)}, u32[]{:S(2)}, u32[]{:S(2)}) collective-permute-start(bf16[64,4096]{1,0:T(8,128)(2,1)S(1)} %collective-permute-done.3.refs_1_), channel_id=1, source_target_pairs={{0,64},{1,65},{2,66},{3,67},{4,68},{5,69},{6,70},{7,71},{8,72},{9,... | collective-permute-start | bytes 1572872 | tf_op jit(solution)/shard_map/ppermute | solution.py:194
  75.5 9.5 %collective-permute-done.8.refs_4_ = bf16[64,4096]{1,0:T(8,128)(2,1)S(1)} collective-permute-done((bf16[64,4096]{1,0:T(8,128)(2,1)S(1)}, bf16[64,4096]{1,0:T(8,128)(2,1)S(1)}, u32[]{:S(2)}, u32[]{:S(2)}) %collective-permute-start.8) | collective-permute-done | bytes 524320 | tf_op jit(solution)/shard_map/ppermute | solution.py:194
  85.0 5.6 %collective-permute-start.9 = (bf16[64,4096]{1,0:T(8,128)(2,1)S(1)}, bf16[64,4096]{1,0:T(8,128)(2,1)S(1)}, u32[]{:S(2)}, u32[]{:S(2)}) collective-permute-start(bf16[64,4096]{1,0:T(8,128)(2,1)S(1)} %collective-permute-done.8.refs_4_), channel_id=1, source_target_pairs={{0,448},{1,449},{2,450},{3,451},{4,452},{5,453},{6,454},{7,455},{8... | collective-permute-start | bytes 1572872 | tf_op jit(solution)/shard_map/ppermute | solution.py:194
  90.6 0.0 collective-permute-done.4.refs_3_
  90.6 1.9 %collective-permute-start.5 = (bf16[64,4096]{1,0:T(8,128)(2,1)S(1)}, bf16[64,4096]{1,0:T(8,128)(2,1)S(1)}, u32[]{:S(2)}, u32[]{:S(2)}) collective-permute-start(bf16[64,4096]{1,0:T(8,128)(2,1)S(1)} %collective-permute-done.4.refs_3_), channel_id=1, source_target_pairs={{0,64},{1,65},{2,66},{3,67},{4,68},{5,69},{6,70},{7,71},{8,72},{9,... | collective-permute-start | bytes 1572872 | tf_op jit(solution)/shard_map/ppermute | solution.py:194
  92.5 8.7 %collective-permute-done.9.refs_6_ = bf16[64,4096]{1,0:T(8,128)(2,1)S(1)} collective-permute-done((bf16[64,4096]{1,0:T(8,128)(2,1)S(1)}, bf16[64,4096]{1,0:T(8,128)(2,1)S(1)}, u32[]{:S(2)}, u32[]{:S(2)}) %collective-permute-start.9) | collective-permute-done | bytes 524320 | tf_op jit(solution)/shard_map/ppermute | solution.py:194
  101.3 5.6 %collective-permute-start.10 = (bf16[32,4096]{1,0:T(8,128)(2,1)S(1)}, bf16[32,4096]{1,0:T(8,128)(2,1)S(1)}, u32[]{:S(2)}, u32[]{:S(2)}) collective-permute-start(bf16[32,4096]{1,0:T(8,128)(2,1)S(1)} %slice.9), channel_id=1, source_target_pairs={{0,448},{1,449},{2,450},{3,451},{4,452},{5,453},{6,454},{7,455},{8... | collective-permute-start | bytes 786440 | tf_op jit(solution)/shard_map/ppermute | solution.py:194
  106.9 0.0 collective-permute-done.5.refs_5_
  106.9 1.9 %collective-permute-start.6 = (bf16[32,4096]{1,0:T(8,128)(2,1)S(1)}, bf16[32,4096]{1,0:T(8,128)(2,1)S(1)}, u32[]{:S(2)}, u32[]{:S(2)}) collective-permute-start(bf16[32,4096]{1,0:T(8,128)(2,1)S(1)} %slice.8), channel_id=1, source_target_pairs={{0,64},{1,65},{2,66},{3,67},{4,68},{5,69},{6,70},{7,71},{8,72},{9,... | collective-permute-start | bytes 786440 | tf_op jit(solution)/shard_map/ppermute | solution.py:194
  108.8 1.8 %shard_map.28 = (bf16[512,4096]{1,0:T(8,128)(2,1)S(1)}, f32[512,128]{1,0:T(8,128)S(1)}) custom-call(bf16[64,4096]{1,0:T(8,128)(2,1)S(1)} %constant_dynamic-update-slice_fusion.refs_0_, bf16[64,4096]{1,0:T(8,128)(2,1)S(1)} %collective-permute-done.3.refs_1_, bf16[64,4096]{1,0:T(8,128)(2,1)S(1)} %collective-permute-done.7.refs_2_, ...), custom_call_target="tpu_custom_call" | custom-call | flops 3670016 | bytes 7340032 | tf_op jit(solution)/shard_map/pallas_call | solution.py:95
  110.7 0.4 collective-permute-done.10.refs_1_
  111.0 5.4 %collective-permute-done.6.refs_0_ = bf16[32,4096]{1,0:T(8,128)(2,1)S(1)} collective-permute-done((bf16[32,4096]{1,0:T(8,128)(2,1)S(1)}, bf16[32,4096]{1,0:T(8,128)(2,1)S(1)}, u32[]{:S(2)}, u32[]{:S(2)}) %collective-permute-start.6) | collective-permute-done | bytes 262176 | tf_op jit(solution)/shard_map/ppermute | solution.py:194
  116.4 0.3 shard_map.29
  116.7 0.0 copy-start
  116.7 2.0 %copy-done = bf16[512,4096]{1,0:T(8,128)(2,1)} copy-done((bf16[512,4096]{1,0:T(8,128)(2,1)}, bf16[512,4096]{1,0:T(8,128)(2,1)S(1)}, u32[]{:S(2)}) %copy-start) | copy-done | bytes 4194328
  118.7 0.0 copy-start.1
  118.7 0.7 copy-done.1
  119.4 0.0 all-gather.2.cloned.1.call-done.rows_hbm
  119.4 6.2 %shard_map.31 = bf16[512,512]{1,0:T(8,128)(2,1)} custom-call(s32[16,16]{1,0:T(8,128)} %live_ref.3, bf16[1024,4096]{1,0:T(8,128)(2,1)} %all-gather.2.cloned.1.call-done.rows_hbm, bf16[512,4096]{1,0:T(8,128)(2,1)} %copy-done, f32[512,128]{1,0:T(8,128)} %copy-done.1), custom_call_target="tpu_custom_call" | custom-call | flops 2147483648 | bytes 9437184 | tf_op jit(solution)/shard_map/pallas_call | solution.py:164
  125.6 1.9 %collective-permute-start.11 = (bf16[512,512]{1,0:T(8,128)(2,1)}, bf16[512,512]{1,0:T(8,128)(2,1)S(1)}, u32[]{:S(2)}, u32[]{:S(2)}) collective-permute-start(bf16[512,512]{1,0:T(8,128)(2,1)} %shard_map.31), channel_id=1, source_target_pairs={{0,1},{1,0},{2,3},{3,2},{4,5},{5,4},{6,7},{7,6},{8,9},{9,8},{10,11... | collective-permute-start | bytes 1572872 | tf_op jit(solution)/shard_map/ppermute | solution.py:194
  127.5 6.3 %shard_map.30 = bf16[512,1024]{1,0:T(8,128)(2,1)} custom-call(s32[16,16]{1,0:T(8,128)} %live_ref.3, bf16[1024,4096]{1,0:T(8,128)(2,1)} %all-gather.2.cloned.1.call-done.rows_hbm, bf16[512,4096]{1,0:T(8,128)(2,1)} %copy-done, f32[512,128]{1,0:T(8,128)} %copy-done.1), custom_call_target="tpu_custom_call" | custom-call | flops 2147483648 | bytes 9437184 | tf_op jit(solution)/shard_map/pallas_call | solution.py:164
  133.9 6.2 %collective-permute-done.11 = bf16[512,512]{1,0:T(8,128)(2,1)S(1)} collective-permute-done((bf16[512,512]{1,0:T(8,128)(2,1)}, bf16[512,512]{1,0:T(8,128)(2,1)S(1)}, u32[]{:S(2)}, u32[]{:S(2)}) %collective-permute-start.11) | collective-permute-done | bytes 524320 | tf_op jit(solution)/shard_map/ppermute | solution.py:194
  140.0 0.8 constant_dynamic-update-slice_fusion.2
  (4 shorter events, 0.1 us)
Async XLA Ops:
  6.5 112.8 %all-gather.2.cloned.1.call-start = ((), (), s32[]{:S(2)}) async-start(), calls=%async_computation | async-start | bytes 8912896 | tf_op jit(solution)/shard_map/all_gather | solution.py:204
  6.5 11.6 %collective-permute-start = (bf16[64,2048]{1,0:T(8,128)(2,1)}, bf16[64,2048]{1,0:T(8,128)(2,1)S(1)}, u32[]{:S(2)}, u32[]{:S(2)}) collective-permute-start(bf16[64,2048]{1,0:T(8,128)(2,1)} %param.2), channel_id=1, source_target_pairs={{0,1},{1,0},{2,3},{3,2},{4,5},{5,4},{6,7},{7,6},{8,9},{9,8},{10,11... | collective-permute-start | bytes 786440 | tf_op jit(solution)/shard_map/ppermute | solution.py:194
  20.2 17.0 %collective-permute-start.1 = (bf16[64,2048]{1,0:T(8,128)(2,1)}, bf16[64,2048]{1,0:T(8,128)(2,1)S(1)}, u32[]{:S(2)}, u32[]{:S(2)}) collective-permute-start(bf16[64,2048]{1,0:T(8,128)(2,1)} %param.2), channel_id=1, source_target_pairs={{0,0},{1,32},{2,256},{3,288},{4,64},{5,96},{6,448},{7,480},{8,128}... | collective-permute-start | bytes 786440 | tf_op jit(solution)/shard_map/ppermute | solution.py:194
  22.1 26.5 %collective-permute-start.2 = (bf16[64,2048]{1,0:T(8,128)(2,1)}, bf16[64,2048]{1,0:T(8,128)(2,1)S(1)}, u32[]{:S(2)}, u32[]{:S(2)}) collective-permute-start(bf16[64,2048]{1,0:T(8,128)(2,1)} %param.2), channel_id=1, source_target_pairs={{0,32},{1,0},{2,288},{3,256},{4,96},{5,64},{6,480},{7,448},{8,160}... | collective-permute-start | bytes 786440 | tf_op jit(solution)/shard_map/ppermute | solution.py:194
  48.6 19.4 %collective-permute-start.7 = (bf16[64,4096]{1,0:T(8,128)(2,1)S(1)}, bf16[64,4096]{1,0:T(8,128)(2,1)S(1)}, u32[]{:S(2)}, u32[]{:S(2)}) collective-permute-start(bf16[64,4096]{1,0:T(8,128)(2,1)S(1)} %constant_dynamic-update-slice_fusion.refs_0_), channel_id=1, source_target_pairs={{0,448},{1,449},{2,450},{3,451},{4,452},{5,453},{6,454},{7,455},{8... | collective-permute-start | bytes 1572872 | tf_op jit(solution)/shard_map/ppermute | solution.py:194
  55.8 17.8 %collective-permute-start.3 = (bf16[64,4096]{1,0:T(8,128)(2,1)S(1)}, bf16[64,4096]{1,0:T(8,128)(2,1)S(1)}, u32[]{:S(2)}, u32[]{:S(2)}) collective-permute-start(bf16[64,4096]{1,0:T(8,128)(2,1)S(1)} %constant_dynamic-update-slice_fusion.refs_0_), channel_id=1, source_target_pairs={{0,64},{1,65},{2,66},{3,67},{4,68},{5,69},{6,70},{7,71},{8,72},{9,... | collective-permute-start | bytes 1572872 | tf_op jit(solution)/shard_map/ppermute | solution.py:194
  68.0 17.0 %collective-permute-start.8 = (bf16[64,4096]{1,0:T(8,128)(2,1)S(1)}, bf16[64,4096]{1,0:T(8,128)(2,1)S(1)}, u32[]{:S(2)}, u32[]{:S(2)}) collective-permute-start(bf16[64,4096]{1,0:T(8,128)(2,1)S(1)} %collective-permute-done.7.refs_2_), channel_id=1, source_target_pairs={{0,448},{1,449},{2,450},{3,451},{4,452},{5,453},{6,454},{7,455},{8... | collective-permute-start | bytes 1572872 | tf_op jit(solution)/shard_map/ppermute | solution.py:194
  73.6 17.0 %collective-permute-start.4 = (bf16[64,4096]{1,0:T(8,128)(2,1)S(1)}, bf16[64,4096]{1,0:T(8,128)(2,1)S(1)}, u32[]{:S(2)}, u32[]{:S(2)}) collective-permute-start(bf16[64,4096]{1,0:T(8,128)(2,1)S(1)} %collective-permute-done.3.refs_1_), channel_id=1, source_target_pairs={{0,64},{1,65},{2,66},{3,67},{4,68},{5,69},{6,70},{7,71},{8,72},{9,... | collective-permute-start | bytes 1572872 | tf_op jit(solution)/shard_map/ppermute | solution.py:194
  85.0 16.3 %collective-permute-start.9 = (bf16[64,4096]{1,0:T(8,128)(2,1)S(1)}, bf16[64,4096]{1,0:T(8,128)(2,1)S(1)}, u32[]{:S(2)}, u32[]{:S(2)}) collective-permute-start(bf16[64,4096]{1,0:T(8,128)(2,1)S(1)} %collective-permute-done.8.refs_4_), channel_id=1, source_target_pairs={{0,448},{1,449},{2,450},{3,451},{4,452},{5,453},{6,454},{7,455},{8... | collective-permute-start | bytes 1572872 | tf_op jit(solution)/shard_map/ppermute | solution.py:194
  90.6 16.3 %collective-permute-start.5 = (bf16[64,4096]{1,0:T(8,128)(2,1)S(1)}, bf16[64,4096]{1,0:T(8,128)(2,1)S(1)}, u32[]{:S(2)}, u32[]{:S(2)}) collective-permute-start(bf16[64,4096]{1,0:T(8,128)(2,1)S(1)} %collective-permute-done.4.refs_3_), channel_id=1, source_target_pairs={{0,64},{1,65},{2,66},{3,67},{4,68},{5,69},{6,70},{7,71},{8,72},{9,... | collective-permute-start | bytes 1572872 | tf_op jit(solution)/shard_map/ppermute | solution.py:194
  101.3 9.7 %collective-permute-start.10 = (bf16[32,4096]{1,0:T(8,128)(2,1)S(1)}, bf16[32,4096]{1,0:T(8,128)(2,1)S(1)}, u32[]{:S(2)}, u32[]{:S(2)}) collective-permute-start(bf16[32,4096]{1,0:T(8,128)(2,1)S(1)} %slice.9), channel_id=1, source_target_pairs={{0,448},{1,449},{2,450},{3,451},{4,452},{5,453},{6,454},{7,455},{8... | collective-permute-start | bytes 786440 | tf_op jit(solution)/shard_map/ppermute | solution.py:194
  106.9 9.5 %collective-permute-start.6 = (bf16[32,4096]{1,0:T(8,128)(2,1)S(1)}, bf16[32,4096]{1,0:T(8,128)(2,1)S(1)}, u32[]{:S(2)}, u32[]{:S(2)}) collective-permute-start(bf16[32,4096]{1,0:T(8,128)(2,1)S(1)} %slice.8), channel_id=1, source_target_pairs={{0,64},{1,65},{2,66},{3,67},{4,68},{5,69},{6,70},{7,71},{8,72},{9,... | collective-permute-start | bytes 786440 | tf_op jit(solution)/shard_map/ppermute | solution.py:194
  116.7 2.0 %copy-start = (bf16[512,4096]{1,0:T(8,128)(2,1)}, bf16[512,4096]{1,0:T(8,128)(2,1)S(1)}, u32[]{:S(2)}) copy-start(bf16[512,4096]{1,0:T(8,128)(2,1)S(1)} %get-tuple-element.11.cols_hbm) | copy-start | bytes 12582916
  118.7 0.7 copy-start.1
  125.6 14.4 %collective-permute-start.11 = (bf16[512,512]{1,0:T(8,128)(2,1)}, bf16[512,512]{1,0:T(8,128)(2,1)S(1)}, u32[]{:S(2)}, u32[]{:S(2)}) collective-permute-start(bf16[512,512]{1,0:T(8,128)(2,1)} %shard_map.31), channel_id=1, source_target_pairs={{0,1},{1,0},{2,3},{3,2},{4,5},{5,4},{6,7},{7,6},{8,9},{9,8},{10,11... | collective-permute-start | bytes 1572872 | tf_op jit(solution)/shard_map/ppermute | solution.py:194
Sparse Core Ops, SparseCore 0:
  20.3 69.8 all-gather.1

commit v5 on v4

--- a/solution.py
+++ b/solution.py
@@ -33,9 +33,13 @@
     return [(index(*d), index(*target(*d))) for d in every]
 
 
+def col_half(z, xh):
+    return xh ^ (z >> 1 & 1)
+
+
 def col_pairs(stage):
     def target(y, xl, z, a, half):
-        part = z // 4
+        part = col_half(y, z // 4)
         return y + SHIFT[z % 4][a], half ^ part ^ stage, y, xl, part
 
     return pairs(target)
@@ -106,7 +110,7 @@
             pltpu.VMEM((count * SUB, 128), jnp.float32),
             pltpu.SemaphoreType.DMA((3, count)),
         ],
-        compiler_params=pltpu.CompilerParams(vmem_limit_bytes=16 * MIB),
+        compiler_params=pltpu.CompilerParams(vmem_limit_bytes=56 * MIB),
         cost_estimate=pl.CostEstimate(
             flops=2 * count * SUB * samples,
             bytes_accessed=count * MIB,
@@ -139,7 +143,10 @@
         for copy in copies[k]:
             copy.wait()
         part = lax.dot_general(
-            rows[k], cols[k], (((1,), (1,)), ((), ())), preferred_element_type=jnp.float32
+            rows[k],
+            cols[k],
+            (((1,), (1,)), ((), ())),
+            preferred_element_type=jnp.float32,
         )
         norm = square_sums(rows[k])
         if k == 0:
@@ -153,7 +160,7 @@
     across = jnp.sum(col_norm[...].T, axis=0, keepdims=True)
     dist = down + across - 2.0 * inner[...]
     gram = jnp.exp(dist * (-2.0 / samples)) * scale
-    base = pl.multiple_of(xh * HALF, HALF) if keep else 0
+    base = pl.multiple_of(col_half(z, xh) * HALF, HALF) if keep else 0
     out_ref[:, pl.ds(base, HALF)] = gram.astype(jnp.bfloat16)
 
 
@@ -188,7 +195,7 @@
 
 
 def on_device(trajectories, pair_live):
-    xl, xh = lax.axis_index("xl"), lax.axis_index("xh")
+    xl, z, xh = (lax.axis_index(name) for name in ("xl", "z", "xh"))
 
     def send(value, to):
         return lax.ppermute(value, AX, to)
@@ -196,6 +203,7 @@
     other = send(trajectories, swap_lag())
     early = send(trajectories, col_pairs(0))
     late = send(trajectories, col_pairs(1))
+    early, late, other = lax.optimization_barrier((early, late, other))
     rows = jnp.where(
         xl == 0,
         jnp.concatenate([trajectories, other], axis=1),
@@ -218,7 +226,7 @@
 
     given = send(gram_tile(False, pair_live, rows, cols, col_norm), swap_lag())
     kept = gram_tile(True, pair_live, rows, cols, col_norm)
-    return lax.dynamic_update_slice(kept, given, (0, (1 - xh) * HALF))
+    return lax.dynamic_update_slice(kept, given, (0, (1 - col_half(z, xh)) * HALF))
 
 
 def solution(mesh):

time: 148 us -> 142 us (0.959)
  the two profiles are of different devices: /device:TPU:6 before, /device:TPU:128 now
where the time goes in v5:
time: 142 us; the launch traced here: 141 us
  waiting for transfers between devices  57.5 us (40%)
  starting transfers between devices  48.7 us (34%)
  Pallas kernels  17.5 us (12%)
  between operations  13.7 us (10%)
  other arithmetic  1.98 us (1%)
  local copies, waits for them, and re-layouts  1.64 us (1%)
    ppermute x12, waiting for transfers between devices, send(): return lax.ppermute(value, AX, to)  57.4 us
    ppermute x12, starting transfers between devices, send(): return lax.ppermute(value, AX, to)  48.7 us
    pallas_call x2, Pallas kernels, gram_tile(): pl.pallas_call(functools.partial(gram_kernel, keep), out_shape=jax.ShapeD...  12.6 us
    pallas_call x2, Pallas kernels, in_order(): pl.pallas_call(functools.partial(order_kernel, chunks), out_shape=(jax.Sh...  4.93 us
  transfers between devices with their start and end apart: 13, of which 8 were waited for; matrix products, arithmetic and copies ran while one was open for 0% of the time, Pallas kernels for 8%

profile of v5, /device:TPU:128, one launch (start us, length us, event | category | flops | bytes accessed | tf_op | source)
XLA Modules:
  0.0 141.0 jit_solution(156351655387595992)
XLA Ops:
  6.5 0.0 all-gather.2.cloned.1.call-start
  6.5 2.7 %collective-permute-start = (bf16[64,2048]{1,0:T(8,128)(2,1)}, bf16[64,2048]{1,0:T(8,128)(2,1)S(1)}, u32[]{:S(2)}, u32[]{:S(2)}) collective-permute-start(bf16[64,2048]{1,0:T(8,128)(2,1)} %param.2), channel_id=1, source_target_pairs={{0,0},{1,32},{2,256},{3,288},{4,64},{5,96},{6,448},{7,480},{8,128}... | collective-permute-start | bytes 786440 | tf_op jit(solution)/shard_map/ppermute | solution.py:201
  9.2 8.0 %collective-permute-start.1 = (bf16[64,2048]{1,0:T(8,128)(2,1)}, bf16[64,2048]{1,0:T(8,128)(2,1)S(1)}, u32[]{:S(2)}, u32[]{:S(2)}) collective-permute-start(bf16[64,2048]{1,0:T(8,128)(2,1)} %param.2), channel_id=1, source_target_pairs={{0,32},{1,0},{2,288},{3,256},{4,96},{5,64},{6,480},{7,448},{8,160}... | collective-permute-start | bytes 786440 | tf_op jit(solution)/shard_map/ppermute | solution.py:201
  17.2 5.1 %collective-permute-start.2 = (bf16[64,2048]{1,0:T(8,128)(2,1)}, bf16[64,2048]{1,0:T(8,128)(2,1)S(1)}, u32[]{:S(2)}, u32[]{:S(2)}) collective-permute-start(bf16[64,2048]{1,0:T(8,128)(2,1)} %param.2), channel_id=1, source_target_pairs={{0,1},{1,0},{2,3},{3,2},{4,5},{5,4},{6,7},{7,6},{8,9},{9,8},{10,11... | collective-permute-start | bytes 786440 | tf_op jit(solution)/shard_map/ppermute | solution.py:201
  22.4 4.2 %collective-permute-done = bf16[64,2048]{1,0:T(8,128)(2,1)S(1)} collective-permute-done((bf16[64,2048]{1,0:T(8,128)(2,1)}, bf16[64,2048]{1,0:T(8,128)(2,1)S(1)}, u32[]{:S(2)}, u32[]{:S(2)}) %collective-permute-start) | collective-permute-done | bytes 262176 | tf_op jit(solution)/shard_map/ppermute | solution.py:201
  26.6 11.7 %collective-permute-done.1 = bf16[64,2048]{1,0:T(8,128)(2,1)S(1)} collective-permute-done((bf16[64,2048]{1,0:T(8,128)(2,1)}, bf16[64,2048]{1,0:T(8,128)(2,1)S(1)}, u32[]{:S(2)}, u32[]{:S(2)}) %collective-permute-start.1) | collective-permute-done | bytes 262176 | tf_op jit(solution)/shard_map/ppermute | solution.py:201
  38.3 0.0 collective-permute-done.2
  38.3 2.0 %maximum_select_fusion = bf16[64,4096]{1,0:T(8,128)(2,1)} fusion(bf16[64,2048]{1,0:T(8,128)(2,1)S(1)} %collective-permute-done.2, bf16[64,2048]{1,0:T(8,128)(2,1)} %param.2, pred[]{:T(512)S(6)} %eq.3), kind=kLoop, calls=%fused_computation | loop fusion | flops 2359296 | bytes 1048577 | tf_op jit(solution)/shard_map/jit(_where)/select_n | solution.py:207
  40.3 0.0 all-gather.2.cloned.1.call-update
  40.4 0.0 copy-start.2
  40.4 6.5 %collective-permute-start.7 = (bf16[64,4096]{1,0:T(8,128)(2,1)S(1)}, bf16[64,4096]{1,0:T(8,128)(2,1)S(1)}, u32[]{:S(2)}, u32[]{:S(2)}) collective-permute-start(bf16[64,4096]{1,0:T(8,128)(2,1)S(1)} %constant_dynamic-update-slice_fusion.refs_0_), channel_id=1, source_target_pairs={{0,448},{1,449},{2,450},{3,451},{4,452},{5,453},{6,454},{7,455},{8... | collective-permute-start | bytes 1572872 | tf_op jit(solution)/shard_map/ppermute | solution.py:201
  46.9 1.9 %collective-permute-start.3 = (bf16[64,4096]{1,0:T(8,128)(2,1)S(1)}, bf16[64,4096]{1,0:T(8,128)(2,1)S(1)}, u32[]{:S(2)}, u32[]{:S(2)}) collective-permute-start(bf16[64,4096]{1,0:T(8,128)(2,1)S(1)} %constant_dynamic-update-slice_fusion.refs_0_), channel_id=1, source_target_pairs={{0,64},{1,65},{2,66},{3,67},{4,68},{5,69},{6,70},{7,71},{8,72},{9,... | collective-permute-start | bytes 1572872 | tf_op jit(solution)/shard_map/ppermute | solution.py:201
  48.8 9.2 %collective-permute-done.7.refs_2_ = bf16[64,4096]{1,0:T(8,128)(2,1)S(1)} collective-permute-done((bf16[64,4096]{1,0:T(8,128)(2,1)S(1)}, bf16[64,4096]{1,0:T(8,128)(2,1)S(1)}, u32[]{:S(2)}, u32[]{:S(2)}) %collective-permute-start.7) | collective-permute-done | bytes 524320 | tf_op jit(solution)/shard_map/ppermute | solution.py:201
  58.1 0.0 copy-start.3
  58.1 5.6 %collective-permute-start.8 = (bf16[64,4096]{1,0:T(8,128)(2,1)S(1)}, bf16[64,4096]{1,0:T(8,128)(2,1)S(1)}, u32[]{:S(2)}, u32[]{:S(2)}) collective-permute-start(bf16[64,4096]{1,0:T(8,128)(2,1)S(1)} %collective-permute-done.7.refs_2_), channel_id=1, source_target_pairs={{0,448},{1,449},{2,450},{3,451},{4,452},{5,453},{6,454},{7,455},{8... | collective-permute-start | bytes 1572872 | tf_op jit(solution)/shard_map/ppermute | solution.py:201
  63.7 0.3 collective-permute-done.3.refs_1_
  64.0 0.0 copy-start.4
  64.0 1.9 %collective-permute-start.4 = (bf16[64,4096]{1,0:T(8,128)(2,1)S(1)}, bf16[64,4096]{1,0:T(8,128)(2,1)S(1)}, u32[]{:S(2)}, u32[]{:S(2)}) collective-permute-start(bf16[64,4096]{1,0:T(8,128)(2,1)S(1)} %collective-permute-done.3.refs_1_), channel_id=1, source_target_pairs={{0,64},{1,65},{2,66},{3,67},{4,68},{5,69},{6,70},{7,71},{8,72},{9,... | collective-permute-start | bytes 1572872 | tf_op jit(solution)/shard_map/ppermute | solution.py:201
  65.9 10.0 %collective-permute-done.8.refs_4_ = bf16[64,4096]{1,0:T(8,128)(2,1)S(1)} collective-permute-done((bf16[64,4096]{1,0:T(8,128)(2,1)S(1)}, bf16[64,4096]{1,0:T(8,128)(2,1)S(1)}, u32[]{:S(2)}, u32[]{:S(2)}) %collective-permute-start.8) | collective-permute-done | bytes 524320 | tf_op jit(solution)/shard_map/ppermute | solution.py:201
  75.9 0.0 copy-start.5
  76.0 5.6 %collective-permute-start.9 = (bf16[64,4096]{1,0:T(8,128)(2,1)S(1)}, bf16[64,4096]{1,0:T(8,128)(2,1)S(1)}, u32[]{:S(2)}, u32[]{:S(2)}) collective-permute-start(bf16[64,4096]{1,0:T(8,128)(2,1)S(1)} %collective-permute-done.8.refs_4_), channel_id=1, source_target_pairs={{0,448},{1,449},{2,450},{3,451},{4,452},{5,453},{6,454},{7,455},{8... | collective-permute-start | bytes 1572872 | tf_op jit(solution)/shard_map/ppermute | solution.py:201
  81.5 0.0 collective-permute-done.4.refs_3_
  81.6 0.0 copy-start.6
  81.6 1.9 %collective-permute-start.5 = (bf16[64,4096]{1,0:T(8,128)(2,1)S(1)}, bf16[64,4096]{1,0:T(8,128)(2,1)S(1)}, u32[]{:S(2)}, u32[]{:S(2)}) collective-permute-start(bf16[64,4096]{1,0:T(8,128)(2,1)S(1)} %collective-permute-done.4.refs_3_), channel_id=1, source_target_pairs={{0,64},{1,65},{2,66},{3,67},{4,68},{5,69},{6,70},{7,71},{8,72},{9,... | collective-permute-start | bytes 1572872 | tf_op jit(solution)/shard_map/ppermute | solution.py:201
  83.5 9.5 %collective-permute-done.9.refs_6_ = bf16[64,4096]{1,0:T(8,128)(2,1)S(1)} collective-permute-done((bf16[64,4096]{1,0:T(8,128)(2,1)S(1)}, bf16[64,4096]{1,0:T(8,128)(2,1)S(1)}, u32[]{:S(2)}, u32[]{:S(2)}) %collective-permute-start.9) | collective-permute-done | bytes 524320 | tf_op jit(solution)/shard_map/ppermute | solution.py:201
  93.0 0.0 copy-start
  93.0 5.6 %collective-permute-start.10 = (bf16[32,4096]{1,0:T(8,128)(2,1)S(1)}, bf16[32,4096]{1,0:T(8,128)(2,1)S(1)}, u32[]{:S(2)}, u32[]{:S(2)}) collective-permute-start(bf16[32,4096]{1,0:T(8,128)(2,1)S(1)} %slice.9), channel_id=1, source_target_pairs={{0,448},{1,449},{2,450},{3,451},{4,452},{5,453},{6,454},{7,455},{8... | collective-permute-start | bytes 786440 | tf_op jit(solution)/shard_map/ppermute | solution.py:201
  98.6 0.0 collective-permute-done.5.refs_5_
  98.6 0.0 copy-start.1
  98.7 1.9 %collective-permute-start.6 = (bf16[32,4096]{1,0:T(8,128)(2,1)S(1)}, bf16[32,4096]{1,0:T(8,128)(2,1)S(1)}, u32[]{:S(2)}, u32[]{:S(2)}) collective-permute-start(bf16[32,4096]{1,0:T(8,128)(2,1)S(1)} %slice.8), channel_id=1, source_target_pairs={{0,64},{1,65},{2,66},{3,67},{4,68},{5,69},{6,70},{7,71},{8,72},{9,... | collective-permute-start | bytes 786440 | tf_op jit(solution)/shard_map/ppermute | solution.py:201
  100.6 0.0 copy-done.2
  100.6 0.0 copy-done.3
  100.6 0.0 copy-done.4
  100.6 0.0 copy-done.5
  100.6 0.0 copy-done.6
  100.6 0.0 copy-done
  100.6 0.0 copy-done.1
  100.7 3.1 %shard_map.28 = (bf16[512,4096]{1,0:T(8,128)(2,1)}, f32[512,128]{1,0:T(8,128)}) custom-call(bf16[64,4096]{1,0:T(8,128)(2,1)} %copy-done.2, bf16[64,4096]{1,0:T(8,128)(2,1)} %copy-done.4, bf16[64,4096]{1,0:T(8,128)(2,1)} %copy-done.3, bf16[64,4096]{1,0:T(8,128)(2,1)} %copy-done.6, bf16[64,4096]{1,0:T(8,128)(2,1)} %copy-done.5, bf16[64,4096]{1,0:T(8,128)(2,1)} %copy-done.1, ...), custom_call_target="tpu_custom_call" | custom-call | flops 3670016 | bytes 7340032 | tf_op jit(solution)/shard_map/pallas_call | solution.py:99
  103.8 0.0 collective-permute-done.10.refs_1_
  103.8 0.0 copy-start.7
  103.8 5.2 %collective-permute-done.6.refs_0_ = bf16[32,4096]{1,0:T(8,128)(2,1)S(1)} collective-permute-done((bf16[32,4096]{1,0:T(8,128)(2,1)S(1)}, bf16[32,4096]{1,0:T(8,128)(2,1)S(1)}, u32[]{:S(2)}, u32[]{:S(2)}) %collective-permute-start.6) | collective-permute-done | bytes 262176 | tf_op jit(solution)/shard_map/ppermute | solution.py:201
  109.0 0.0 copy-start.8
  109.0 0.0 copy-done.7
  109.0 0.7 copy-done.8
  109.7 1.8 %shard_map.29 = (bf16[512,4096]{1,0:T(8,128)(2,1)}, f32[512,128]{1,0:T(8,128)}) custom-call(bf16[32,4096]{1,0:T(8,128)(2,1)} %copy-done.8, bf16[32,4096]{1,0:T(8,128)(2,1)} %copy-done.7, bf16[512,4096]{1,0:T(8,128)(2,1)} %get-tuple-element.15.refs_2_, f32[512,128]{1,0:T(8,128)} %get-tuple-element.16.refs_3_), custom_call_target="tpu_custom_call", output_to_operand_aliasing={{0}: (2, {}), {1}: (3, {})} | custom-call | flops 1048576 | bytes 2097152 | tf_op jit(solution)/shard_map/pallas_call | solution.py:99
  111.5 0.0 all-gather.2.cloned.1.call-done.rows_hbm
  111.5 6.2 %shard_map.31 = bf16[512,512]{1,0:T(8,128)(2,1)} custom-call(s32[16,16]{1,0:T(8,128)} %live_ref.3, bf16[1024,4096]{1,0:T(8,128)(2,1)} %all-gather.2.cloned.1.call-done.rows_hbm, bf16[512,4096]{1,0:T(8,128)(2,1)} %get-tuple-element.17.cols_hbm, f32[512,128]{1,0:T(8,128)} %get-tuple-element.18.col_norm), custom_call_target="tpu_custom_call" | custom-call | flops 2147483648 | bytes 9437184 | tf_op jit(solution)/shard_map/pallas_call | solution.py:171
  117.8 1.9 %collective-permute-start.11 = (bf16[512,512]{1,0:T(8,128)(2,1)}, bf16[512,512]{1,0:T(8,128)(2,1)S(1)}, u32[]{:S(2)}, u32[]{:S(2)}) collective-permute-start(bf16[512,512]{1,0:T(8,128)(2,1)} %shard_map.31), channel_id=1, source_target_pairs={{0,1},{1,0},{2,3},{3,2},{4,5},{5,4},{6,7},{7,6},{8,9},{9,8},{10,11... | collective-permute-start | bytes 1572872 | tf_op jit(solution)/shard_map/ppermute | solution.py:201
  119.7 6.3 %shard_map.30 = bf16[512,1024]{1,0:T(8,128)(2,1)} custom-call(s32[16,16]{1,0:T(8,128)} %live_ref.3, bf16[1024,4096]{1,0:T(8,128)(2,1)} %all-gather.2.cloned.1.call-done.rows_hbm, bf16[512,4096]{1,0:T(8,128)(2,1)} %get-tuple-element.17.cols_hbm, f32[512,128]{1,0:T(8,128)} %get-tuple-element.18.col_norm), custom_call_target="tpu_custom_call" | custom-call | flops 2147483648 | bytes 9437184 | tf_op jit(solution)/shard_map/pallas_call | solution.py:171
  126.1 7.2 %collective-permute-done.11 = bf16[512,512]{1,0:T(8,128)(2,1)S(1)} collective-permute-done((bf16[512,512]{1,0:T(8,128)(2,1)}, bf16[512,512]{1,0:T(8,128)(2,1)S(1)}, u32[]{:S(2)}, u32[]{:S(2)}) %collective-permute-start.11) | collective-permute-done | bytes 524320 | tf_op jit(solution)/shard_map/ppermute | solution.py:201
  133.3 0.8 constant_dynamic-update-slice_fusion.2
  (4 shorter events, 0.1 us)
Async XLA Ops:
  6.5 105.0 %all-gather.2.cloned.1.call-start = ((), (), s32[]{:S(2)}) async-start(), calls=%async_computation | async-start | bytes 8912896 | tf_op jit(solution)/shard_map/all_gather | solution.py:212
  6.5 20.1 %collective-permute-start = (bf16[64,2048]{1,0:T(8,128)(2,1)}, bf16[64,2048]{1,0:T(8,128)(2,1)S(1)}, u32[]{:S(2)}, u32[]{:S(2)}) collective-permute-start(bf16[64,2048]{1,0:T(8,128)(2,1)} %param.2), channel_id=1, source_target_pairs={{0,0},{1,32},{2,256},{3,288},{4,64},{5,96},{6,448},{7,480},{8,128}... | collective-permute-start | bytes 786440 | tf_op jit(solution)/shard_map/ppermute | solution.py:201
  9.2 29.1 %collective-permute-start.1 = (bf16[64,2048]{1,0:T(8,128)(2,1)}, bf16[64,2048]{1,0:T(8,128)(2,1)S(1)}, u32[]{:S(2)}, u32[]{:S(2)}) collective-permute-start(bf16[64,2048]{1,0:T(8,128)(2,1)} %param.2), channel_id=1, source_target_pairs={{0,32},{1,0},{2,288},{3,256},{4,96},{5,64},{6,480},{7,448},{8,160}... | collective-permute-start | bytes 786440 | tf_op jit(solution)/shard_map/ppermute | solution.py:201
  17.2 21.1 %collective-permute-start.2 = (bf16[64,2048]{1,0:T(8,128)(2,1)}, bf16[64,2048]{1,0:T(8,128)(2,1)S(1)}, u32[]{:S(2)}, u32[]{:S(2)}) collective-permute-start(bf16[64,2048]{1,0:T(8,128)(2,1)} %param.2), channel_id=1, source_target_pairs={{0,1},{1,0},{2,3},{3,2},{4,5},{5,4},{6,7},{7,6},{8,9},{9,8},{10,11... | collective-permute-start | bytes 786440 | tf_op jit(solution)/shard_map/ppermute | solution.py:201
  40.4 60.2 %copy-start.2 = (bf16[64,4096]{1,0:T(8,128)(2,1)}, bf16[64,4096]{1,0:T(8,128)(2,1)S(1)}, u32[]{:S(2)}) copy-start(bf16[64,4096]{1,0:T(8,128)(2,1)S(1)} %constant_dynamic-update-slice_fusion.refs_0_) | copy-start | bytes 1572868
  40.4 17.6 %collective-permute-start.7 = (bf16[64,4096]{1,0:T(8,128)(2,1)S(1)}, bf16[64,4096]{1,0:T(8,128)(2,1)S(1)}, u32[]{:S(2)}, u32[]{:S(2)}) collective-permute-start(bf16[64,4096]{1,0:T(8,128)(2,1)S(1)} %constant_dynamic-update-slice_fusion.refs_0_), channel_id=1, source_target_pairs={{0,448},{1,449},{2,450},{3,451},{4,452},{5,453},{6,454},{7,455},{8... | collective-permute-start | bytes 1572872 | tf_op jit(solution)/shard_map/ppermute | solution.py:201
  46.9 17.1 %collective-permute-start.3 = (bf16[64,4096]{1,0:T(8,128)(2,1)S(1)}, bf16[64,4096]{1,0:T(8,128)(2,1)S(1)}, u32[]{:S(2)}, u32[]{:S(2)}) collective-permute-start(bf16[64,4096]{1,0:T(8,128)(2,1)S(1)} %constant_dynamic-update-slice_fusion.refs_0_), channel_id=1, source_target_pairs={{0,64},{1,65},{2,66},{3,67},{4,68},{5,69},{6,70},{7,71},{8,72},{9,... | collective-permute-start | bytes 1572872 | tf_op jit(solution)/shard_map/ppermute | solution.py:201
  58.1 42.5 %copy-start.3 = (bf16[64,4096]{1,0:T(8,128)(2,1)}, bf16[64,4096]{1,0:T(8,128)(2,1)S(1)}, u32[]{:S(2)}) copy-start(bf16[64,4096]{1,0:T(8,128)(2,1)S(1)} %collective-permute-done.7.refs_2_) | copy-start | bytes 1572868
  58.1 17.9 %collective-permute-start.8 = (bf16[64,4096]{1,0:T(8,128)(2,1)S(1)}, bf16[64,4096]{1,0:T(8,128)(2,1)S(1)}, u32[]{:S(2)}, u32[]{:S(2)}) collective-permute-start(bf16[64,4096]{1,0:T(8,128)(2,1)S(1)} %collective-permute-done.7.refs_2_), channel_id=1, source_target_pairs={{0,448},{1,449},{2,450},{3,451},{4,452},{5,453},{6,454},{7,455},{8... | collective-permute-start | bytes 1572872 | tf_op jit(solution)/shard_map/ppermute | solution.py:201
  64.0 36.6 %copy-start.4 = (bf16[64,4096]{1,0:T(8,128)(2,1)}, bf16[64,4096]{1,0:T(8,128)(2,1)S(1)}, u32[]{:S(2)}) copy-start(bf16[64,4096]{1,0:T(8,128)(2,1)S(1)} %collective-permute-done.3.refs_1_) | copy-start | bytes 1572868
  64.0 17.6 %collective-permute-start.4 = (bf16[64,4096]{1,0:T(8,128)(2,1)S(1)}, bf16[64,4096]{1,0:T(8,128)(2,1)S(1)}, u32[]{:S(2)}, u32[]{:S(2)}) collective-permute-start(bf16[64,4096]{1,0:T(8,128)(2,1)S(1)} %collective-permute-done.3.refs_1_), channel_id=1, source_target_pairs={{0,64},{1,65},{2,66},{3,67},{4,68},{5,69},{6,70},{7,71},{8,72},{9,... | collective-permute-start | bytes 1572872 | tf_op jit(solution)/shard_map/ppermute | solution.py:201
  75.9 24.7 %copy-start.5 = (bf16[64,4096]{1,0:T(8,128)(2,1)}, bf16[64,4096]{1,0:T(8,128)(2,1)S(1)}, u32[]{:S(2)}) copy-start(bf16[64,4096]{1,0:T(8,128)(2,1)S(1)} %collective-permute-done.8.refs_4_) | copy-start | bytes 1572868
  76.0 17.0 %collective-permute-start.9 = (bf16[64,4096]{1,0:T(8,128)(2,1)S(1)}, bf16[64,4096]{1,0:T(8,128)(2,1)S(1)}, u32[]{:S(2)}, u32[]{:S(2)}) collective-permute-start(bf16[64,4096]{1,0:T(8,128)(2,1)S(1)} %collective-permute-done.8.refs_4_), channel_id=1, source_target_pairs={{0,448},{1,449},{2,450},{3,451},{4,452},{5,453},{6,454},{7,455},{8... | collective-permute-start | bytes 1572872 | tf_op jit(solution)/shard_map/ppermute | solution.py:201
  81.6 19.1 %copy-start.6 = (bf16[64,4096]{1,0:T(8,128)(2,1)}, bf16[64,4096]{1,0:T(8,128)(2,1)S(1)}, u32[]{:S(2)}) copy-start(bf16[64,4096]{1,0:T(8,128)(2,1)S(1)} %collective-permute-done.4.refs_3_) | copy-start | bytes 1572868
  81.6 17.0 %collective-permute-start.5 = (bf16[64,4096]{1,0:T(8,128)(2,1)S(1)}, bf16[64,4096]{1,0:T(8,128)(2,1)S(1)}, u32[]{:S(2)}, u32[]{:S(2)}) collective-permute-start(bf16[64,4096]{1,0:T(8,128)(2,1)S(1)} %collective-permute-done.4.refs_3_), channel_id=1, source_target_pairs={{0,64},{1,65},{2,66},{3,67},{4,68},{5,69},{6,70},{7,71},{8,72},{9,... | collective-permute-start | bytes 1572872 | tf_op jit(solution)/shard_map/ppermute | solution.py:201
  93.0 7.7 %copy-start = (bf16[64,4096]{1,0:T(8,128)(2,1)}, bf16[64,4096]{1,0:T(8,128)(2,1)S(1)}, u32[]{:S(2)}) copy-start(bf16[64,4096]{1,0:T(8,128)(2,1)S(1)} %collective-permute-done.9.refs_6_) | copy-start | bytes 1572868
  93.0 10.8 %collective-permute-start.10 = (bf16[32,4096]{1,0:T(8,128)(2,1)S(1)}, bf16[32,4096]{1,0:T(8,128)(2,1)S(1)}, u32[]{:S(2)}, u32[]{:S(2)}) collective-permute-start(bf16[32,4096]{1,0:T(8,128)(2,1)S(1)} %slice.9), channel_id=1, source_target_pairs={{0,448},{1,449},{2,450},{3,451},{4,452},{5,453},{6,454},{7,455},{8... | collective-permute-start | bytes 786440 | tf_op jit(solution)/shard_map/ppermute | solution.py:201
  98.6 2.0 %copy-start.1 = (bf16[64,4096]{1,0:T(8,128)(2,1)}, bf16[64,4096]{1,0:T(8,128)(2,1)S(1)}, u32[]{:S(2)}) copy-start(bf16[64,4096]{1,0:T(8,128)(2,1)S(1)} %collective-permute-done.5.refs_5_) | copy-start | bytes 1572868
  98.7 10.3 %collective-permute-start.6 = (bf16[32,4096]{1,0:T(8,128)(2,1)S(1)}, bf16[32,4096]{1,0:T(8,128)(2,1)S(1)}, u32[]{:S(2)}, u32[]{:S(2)}) collective-permute-start(bf16[32,4096]{1,0:T(8,128)(2,1)S(1)} %slice.8), channel_id=1, source_target_pairs={{0,64},{1,65},{2,66},{3,67},{4,68},{5,69},{6,70},{7,71},{8,72},{9,... | collective-permute-start | bytes 786440 | tf_op jit(solution)/shard_map/ppermute | solution.py:201
  103.8 5.2 %copy-start.7 = (bf16[32,4096]{1,0:T(8,128)(2,1)}, bf16[32,4096]{1,0:T(8,128)(2,1)S(1)}, u32[]{:S(2)}) copy-start(bf16[32,4096]{1,0:T(8,128)(2,1)S(1)} %collective-permute-done.10.refs_1_) | copy-start | bytes 786436
  109.0 0.7 copy-start.8
  117.8 15.5 %collective-permute-start.11 = (bf16[512,512]{1,0:T(8,128)(2,1)}, bf16[512,512]{1,0:T(8,128)(2,1)S(1)}, u32[]{:S(2)}, u32[]{:S(2)}) collective-permute-start(bf16[512,512]{1,0:T(8,128)(2,1)} %shard_map.31), channel_id=1, source_target_pairs={{0,1},{1,0},{2,3},{3,2},{4,5},{5,4},{6,7},{7,6},{8,9},{9,8},{10,11... | collective-permute-start | bytes 1572872 | tf_op jit(solution)/shard_map/ppermute | solution.py:201
Sparse Core Ops, SparseCore 0:
  40.5 58.5 all-gather.1

commit v6 on v5

--- a/solution.py
+++ b/solution.py
@@ -67,60 +67,61 @@
     return pl.multiple_of(j * SUB, SUB)
 
 
-def order_kernel(chunks, *refs):
-    count = len(chunks)
-    sources = refs[:count]
-    cols, norm, held, sums, sem = refs[-5:]
-    copies = []
-    for i, (source, (d, first, size)) in enumerate(zip(sources, chunks)):
-        at = pl.ds(i * SUB, size)
-        load = pltpu.make_async_copy(source, held.at[at, :], sem.at[0, i])
+def order_kernel(steps, *refs):
+    sources = refs[: 2 * len(steps)]
+    cols, norm, held, sums, sem = refs[2 * len(steps) :]
+    depth = held.shape[2]
+    loads = [
+        pltpu.make_async_copy(source, held.at[i], sem.at[0, i])
+        for i, source in enumerate(sources)
+    ]
+    for load in loads:
         load.start()
-        copies.append((load, at, pl.ds(place(d) + first, size)))
     stores = []
-    for i, (load, at, to) in enumerate(copies):
-        load.wait()
-        stores.append(
-            pltpu.make_async_copy(held.at[at, :], cols.at[to, :], sem.at[1, i])
-        )
-        stores[-1].start()
-        sums[at, :] = square_sums(held[at, :])
-        stores.append(
-            pltpu.make_async_copy(sums.at[at, :], norm.at[to, :], sem.at[2, i])
-        )
-        stores[-1].start()
+    for n, d in enumerate(steps):
+        to = pl.ds(place(d), SUB)
+        for i in (2 * n, 2 * n + 1):
+            loads[i].wait()
+            deep = pl.ds((i % 2) * depth, depth)
+            store = pltpu.make_async_copy(held.at[i], cols.at[to, deep], sem.at[1, i])
+            store.start()
+            stores.append(store)
+        sums[n] = square_sums(held[2 * n]) + square_sums(held[2 * n + 1])
+        store = pltpu.make_async_copy(sums.at[n], norm.at[to, :], sem.at[2, n])
+        store.start()
+        stores.append(store)
     for store in stores:
         store.wait()
 
 
-def in_order(chunks, sources, held=()):
-    samples = sources[0].shape[1]
-    count = len(chunks)
+def in_order(steps, sources):
+    depth = sources[0].shape[1]
+    count = len(sources)
     return pl.pallas_call(
-        functools.partial(order_kernel, chunks),
+        functools.partial(order_kernel, steps),
         out_shape=(
-            jax.ShapeDtypeStruct((HALF, samples), jnp.bfloat16),
+            jax.ShapeDtypeStruct((HALF, 2 * depth), jnp.bfloat16),
             jax.ShapeDtypeStruct((HALF, 128), jnp.float32),
         ),
-        in_specs=[pl.BlockSpec(memory_space=pl.ANY)] * (count + len(held)),
+        in_specs=[pl.BlockSpec(memory_space=pl.ANY)] * count,
         out_specs=[pl.BlockSpec(memory_space=pl.ANY)] * 2,
-        input_output_aliases={count + i: i for i in range(len(held))},
         scratch_shapes=[
-            pltpu.VMEM((count * SUB, samples), jnp.bfloat16),
-            pltpu.VMEM((count * SUB, 128), jnp.float32),
+            pltpu.VMEM((count, SUB, depth), jnp.bfloat16),
+            pltpu.VMEM((len(steps), SUB, 128), jnp.float32),
             pltpu.SemaphoreType.DMA((3, count)),
         ],
         compiler_params=pltpu.CompilerParams(vmem_limit_bytes=56 * MIB),
         cost_estimate=pl.CostEstimate(
-            flops=2 * count * SUB * samples,
-            bytes_accessed=count * MIB,
+            flops=2 * count * SUB * depth,
+            bytes_accessed=count * MIB // 2,
             transcendentals=0,
         ),
-    )(*sources, *held)
-
-
-def gram_kernel(keep, live_ref, rows_hbm, cols_hbm, col_norm, out_ref, *scratch):
-    rows, cols, inner, row_norm, sem = scratch
+    )(*sources)
+
+
+def gram_kernel(keep, live_ref, rows_hbm, cols_hbm, norm_ref, *refs):
+    last, out_ref = refs[:2], refs[2]
+    rows, cols, inner, row_norm, col_norm, sem = refs[3:]
     y, xl, z, a, xh = (lax.axis_index(name) for name in AX)
     half = xh if keep else 1 - xh
     first = pl.multiple_of(half * HALF, HALF)
@@ -139,9 +140,14 @@
         )
         for copy in copies[-1]:
             copy.start()
+    final = pl.ds(place(N // 2), SUB)
+    col_norm[...] = norm_ref[...]
+    col_norm[final, :] = square_sums(last[0]) + square_sums(last[1])
     for k in range(blocks):
         for copy in copies[k]:
             copy.wait()
+        source, start = divmod(k * DEPTH, samples // 2)
+        cols[k, final, :] = last[source][:, start : start + DEPTH]
         part = lax.dot_general(
             rows[k],
             cols[k],
@@ -164,7 +170,7 @@
     out_ref[:, pl.ds(base, HALF)] = gram.astype(jnp.bfloat16)
 
 
-def gram_tile(keep, pair_live, rows, cols, col_norm):
+def gram_tile(keep, pair_live, rows, cols, col_norm, last):
     samples = cols.shape[1]
     width = 2 * HALF if keep else HALF
     operand = pltpu.VMEM((samples // DEPTH, HALF, DEPTH), jnp.bfloat16)
@@ -176,12 +182,15 @@
             pl.BlockSpec(memory_space=pl.ANY),
             pl.BlockSpec(memory_space=pl.ANY),
             pl.BlockSpec(memory_space=pltpu.VMEM),
+            pl.BlockSpec(memory_space=pltpu.VMEM),
+            pl.BlockSpec(memory_space=pltpu.VMEM),
         ],
         out_specs=pl.BlockSpec(memory_space=pltpu.VMEM),
         scratch_shapes=[
             operand,
             operand,
             pltpu.VMEM((HALF, HALF), jnp.float32),
+            pltpu.VMEM((HALF, 128), jnp.float32),
             pltpu.VMEM((HALF, 128), jnp.float32),
             pltpu.SemaphoreType.DMA((2, samples // DEPTH)),
         ],
@@ -191,7 +200,7 @@
             bytes_accessed=9 * MIB,
             transcendentals=HALF * HALF,
         ),
-    )(pair_live, rows, cols, col_norm)
+    )(pair_live, rows, cols, col_norm, *last)
 
 
 def on_device(trajectories, pair_live):
@@ -203,29 +212,25 @@
     other = send(trajectories, swap_lag())
     early = send(trajectories, col_pairs(0))
     late = send(trajectories, col_pairs(1))
-    early, late, other = lax.optimization_barrier((early, late, other))
     rows = jnp.where(
         xl == 0,
         jnp.concatenate([trajectories, other], axis=1),
         jnp.concatenate([other, trajectories], axis=1),
     )
     rows = lax.all_gather(rows, ("z", "a"), axis=0, tiled=True)
-    cols = jnp.concatenate([early, late], axis=1)
-
-    chunks, sources = [(0, 0, SUB)], [cols]
-    up = down = cols
+
+    steps, sources = [0], [early, late]
+    up, down = [early, late], [early, late]
     for step in range(1, N // 2):
-        up, down = send(up, shift_y(1)), send(down, shift_y(-1))
-        chunks += [(step, 0, SUB), (-step, 0, SUB)]
-        sources += [up, down]
-    most = in_order(chunks, sources)
-    part = SUB // 2
-    last = [send(up[:part], shift_y(1)), send(down[part:], shift_y(-1))]
-    chunks = [(N // 2, 0, part), (N // 2, part, part)]
-    cols, col_norm = in_order(chunks, last, most)
-
-    given = send(gram_tile(False, pair_live, rows, cols, col_norm), swap_lag())
-    kept = gram_tile(True, pair_live, rows, cols, col_norm)
+        up = [send(part, shift_y(1)) for part in up]
+        down = [send(part, shift_y(-1)) for part in down]
+        steps += [step, -step]
+        sources += up + down
+    cols, col_norm = in_order(steps, sources)
+    last = [send(up[0], shift_y(1)), send(down[1], shift_y(-1))]
+
+    given = send(gram_tile(False, pair_live, rows, cols, col_norm, last), swap_lag())
+    kept = gram_tile(True, pair_live, rows, cols, col_norm, last)
     return lax.dynamic_update_slice(kept, given, (0, (1 - col_half(z, xh)) * HALF))
 
 

time: 142 us -> 141 us (level)
  the two profiles are of different devices: /device:TPU:128 before, /device:TPU:56 now
where the time goes in v6:
time: 141 us; the launch traced here: 140 us
  starting transfers between devices  78.8 us (56%)
  waiting for transfers between devices  26.5 us (19%)
  Pallas kernels  16.3 us (12%)
  between operations  13.8 us (10%)
  local copies, waits for them, and re-layouts  2.45 us (2%)
  other arithmetic  1.98 us (1%)
    ppermute x18, starting transfers between devices, send(): return lax.ppermute(value, AX, to)  78.8 us
    ppermute x18, waiting for transfers between devices, send(): return lax.ppermute(value, AX, to)  26.5 us
    pallas_call x2, Pallas kernels, gram_tile(): pl.pallas_call(functools.partial(gram_kernel, keep), out_shape=jax.ShapeD...  12.9 us
    pallas_call x1, Pallas kernels, in_order(): pl.pallas_call(functools.partial(order_kernel, steps), out_shape=(jax.Sha...  3.41 us
  transfers between devices with their start and end apart: 19, of which 6 were waited for; matrix products, arithmetic and copies ran while one was open for 0% of the time, Pallas kernels for 7%

profile of v6, /device:TPU:56, one launch (start us, length us, event | category | flops | bytes accessed | tf_op | source)
XLA Modules:
  0.0 139.9 jit_solution(7379842183883406990)
XLA Ops:
  6.5 0.0 all-gather.2.cloned.1.call-start
  6.5 4.9 %collective-permute-start = (bf16[64,2048]{1,0:T(8,128)(2,1)}, bf16[64,2048]{1,0:T(8,128)(2,1)S(1)}, u32[]{:S(2)}, u32[]{:S(2)}) collective-permute-start(bf16[64,2048]{1,0:T(8,128)(2,1)} %param.2), channel_id=1, source_target_pairs={{0,1},{1,0},{2,3},{3,2},{4,5},{5,4},{6,7},{7,6},{8,9},{9,8},{10,11... | collective-permute-start | bytes 786440 | tf_op jit(solution)/shard_map/ppermute | solution.py:210
  11.5 6.7 %collective-permute-done = bf16[64,2048]{1,0:T(8,128)(2,1)S(1)} collective-permute-done((bf16[64,2048]{1,0:T(8,128)(2,1)}, bf16[64,2048]{1,0:T(8,128)(2,1)S(1)}, u32[]{:S(2)}, u32[]{:S(2)}) %collective-permute-start) | collective-permute-done | bytes 262176 | tf_op jit(solution)/shard_map/ppermute | solution.py:210
  18.2 2.0 %maximum_select_fusion = bf16[64,4096]{1,0:T(8,128)(2,1)} fusion(bf16[64,2048]{1,0:T(8,128)(2,1)S(1)} %collective-permute-done, bf16[64,2048]{1,0:T(8,128)(2,1)} %param.2, pred[]{:T(512)S(6)} %eq.3), kind=kLoop, calls=%fused_computation | loop fusion | flops 2359296 | bytes 1048577 | tf_op jit(solution)/shard_map/jit(_where)/select_n | solution.py:215
  20.2 0.0 all-gather.2.cloned.1.call-update
  20.2 13.1 %collective-permute-start.1 = (bf16[64,2048]{1,0:T(8,128)(2,1)}, bf16[64,2048]{1,0:T(8,128)(2,1)S(1)}, u32[]{:S(2)}, u32[]{:S(2)}) collective-permute-start(bf16[64,2048]{1,0:T(8,128)(2,1)} %param.2), channel_id=1, source_target_pairs={{0,0},{1,32},{2,256},{3,288},{4,64},{5,96},{6,448},{7,480},{8,128}... | collective-permute-start | bytes 786440 | tf_op jit(solution)/shard_map/ppermute | solution.py:210
  33.3 3.9 %collective-permute-start.2 = (bf16[64,2048]{1,0:T(8,128)(2,1)}, bf16[64,2048]{1,0:T(8,128)(2,1)S(1)}, u32[]{:S(2)}, u32[]{:S(2)}) collective-permute-start(bf16[64,2048]{1,0:T(8,128)(2,1)} %param.2), channel_id=1, source_target_pairs={{0,32},{1,0},{2,288},{3,256},{4,96},{5,64},{6,480},{7,448},{8,160}... | collective-permute-start | bytes 786440 | tf_op jit(solution)/shard_map/ppermute | solution.py:210
  37.3 4.6 %collective-permute-done.1.refs_0_ = bf16[64,2048]{1,0:T(8,128)(2,1)S(1)} collective-permute-done((bf16[64,2048]{1,0:T(8,128)(2,1)}, bf16[64,2048]{1,0:T(8,128)(2,1)S(1)}, u32[]{:S(2)}, u32[]{:S(2)}) %collective-permute-start.1) | collective-permute-done | bytes 262176 | tf_op jit(solution)/shard_map/ppermute | solution.py:210
  41.9 1.9 %collective-permute-start.3 = (bf16[64,2048]{1,0:T(8,128)(2,1)S(1)}, bf16[64,2048]{1,0:T(8,128)(2,1)S(1)}, u32[]{:S(2)}, u32[]{:S(2)}) collective-permute-start(bf16[64,2048]{1,0:T(8,128)(2,1)S(1)} %collective-permute-done.1.refs_0_), channel_id=1, source_target_pairs={{0,64},{1,65},{2,66},{3,67},{4,68},{5,69},{6,70},{7,71},{8,72},{9,... | collective-permute-start | bytes 786440 | tf_op jit(solution)/shard_map/ppermute | solution.py:210
  43.8 7.7 %collective-permute-done.2.refs_1_ = bf16[64,2048]{1,0:T(8,128)(2,1)S(1)} collective-permute-done((bf16[64,2048]{1,0:T(8,128)(2,1)}, bf16[64,2048]{1,0:T(8,128)(2,1)S(1)}, u32[]{:S(2)}, u32[]{:S(2)}) %collective-permute-start.2) | collective-permute-done | bytes 262176 | tf_op jit(solution)/shard_map/ppermute | solution.py:210
  51.6 13.9 %collective-permute-start.6 = (bf16[64,2048]{1,0:T(8,128)(2,1)S(1)}, bf16[64,2048]{1,0:T(8,128)(2,1)S(1)}, u32[]{:S(2)}, u32[]{:S(2)}) collective-permute-start(bf16[64,2048]{1,0:T(8,128)(2,1)S(1)} %collective-permute-done.2.refs_1_), channel_id=1, source_target_pairs={{0,448},{1,449},{2,450},{3,451},{4,452},{5,453},{6,454},{7,455},{8... | collective-permute-start | bytes 786440 | tf_op jit(solution)/shard_map/ppermute | solution.py:210
  65.4 1.9 %collective-permute-start.4 = (bf16[64,2048]{1,0:T(8,128)(2,1)S(1)}, bf16[64,2048]{1,0:T(8,128)(2,1)S(1)}, u32[]{:S(2)}, u32[]{:S(2)}) collective-permute-start(bf16[64,2048]{1,0:T(8,128)(2,1)S(1)} %collective-permute-done.2.refs_1_), channel_id=1, source_target_pairs={{0,64},{1,65},{2,66},{3,67},{4,68},{5,69},{6,70},{7,71},{8,72},{9,... | collective-permute-start | bytes 786440 | tf_op jit(solution)/shard_map/ppermute | solution.py:210
  67.4 3.9 %collective-permute-start.5 = (bf16[64,2048]{1,0:T(8,128)(2,1)S(1)}, bf16[64,2048]{1,0:T(8,128)(2,1)S(1)}, u32[]{:S(2)}, u32[]{:S(2)}) collective-permute-start(bf16[64,2048]{1,0:T(8,128)(2,1)S(1)} %collective-permute-done.1.refs_0_), channel_id=1, source_target_pairs={{0,448},{1,449},{2,450},{3,451},{4,452},{5,453},{6,454},{7,455},{8... | collective-permute-start | bytes 786440 | tf_op jit(solution)/shard_map/ppermute | solution.py:210
  71.3 0.0 collective-permute-done.3.refs_2_
  71.3 0.0 copy-start.4
  71.3 3.1 %collective-permute-start.7 = (bf16[64,2048]{1,0:T(8,128)(2,1)S(1)}, bf16[64,2048]{1,0:T(8,128)(2,1)S(1)}, u32[]{:S(2)}, u32[]{:S(2)}) collective-permute-start(bf16[64,2048]{1,0:T(8,128)(2,1)S(1)} %collective-permute-done.3.refs_2_), channel_id=1, source_target_pairs={{0,64},{1,65},{2,66},{3,67},{4,68},{5,69},{6,70},{7,71},{8,72},{9,... | collective-permute-start | bytes 786440 | tf_op jit(solution)/shard_map/ppermute | solution.py:210
  74.5 0.0 collective-permute-done.6.refs_5_
  74.5 0.0 copy-start.5
  74.5 2.7 %collective-permute-start.10 = (bf16[64,2048]{1,0:T(8,128)(2,1)S(1)}, bf16[64,2048]{1,0:T(8,128)(2,1)S(1)}, u32[]{:S(2)}, u32[]{:S(2)}) collective-permute-start(bf16[64,2048]{1,0:T(8,128)(2,1)S(1)} %collective-permute-done.6.refs_5_), channel_id=1, source_target_pairs={{0,448},{1,449},{2,450},{3,451},{4,452},{5,453},{6,454},{7,455},{8... | collective-permute-start | bytes 786440 | tf_op jit(solution)/shard_map/ppermute | solution.py:210
  77.2 0.0 collective-permute-done.4.refs_3_
  77.2 0.0 copy-start.6
  77.2 4.3 %collective-permute-start.8 = (bf16[64,2048]{1,0:T(8,128)(2,1)S(1)}, bf16[64,2048]{1,0:T(8,128)(2,1)S(1)}, u32[]{:S(2)}, u32[]{:S(2)}) collective-permute-start(bf16[64,2048]{1,0:T(8,128)(2,1)S(1)} %collective-permute-done.4.refs_3_), channel_id=1, source_target_pairs={{0,64},{1,65},{2,66},{3,67},{4,68},{5,69},{6,70},{7,71},{8,72},{9,... | collective-permute-start | bytes 786440 | tf_op jit(solution)/shard_map/ppermute | solution.py:210
  81.6 0.0 collective-permute-done.5.refs_4_
  81.6 0.0 copy-start.7
  81.6 1.9 %collective-permute-start.9 = (bf16[64,2048]{1,0:T(8,128)(2,1)S(1)}, bf16[64,2048]{1,0:T(8,128)(2,1)S(1)}, u32[]{:S(2)}, u32[]{:S(2)}) collective-permute-start(bf16[64,2048]{1,0:T(8,128)(2,1)S(1)} %collective-permute-done.5.refs_4_), channel_id=1, source_target_pairs={{0,448},{1,449},{2,450},{3,451},{4,452},{5,453},{6,454},{7,455},{8... | collective-permute-start | bytes 786440 | tf_op jit(solution)/shard_map/ppermute | solution.py:210
  83.5 0.0 collective-permute-done.7.refs_6_
  83.5 0.0 copy-start.8
  83.5 5.1 %collective-permute-start.11 = (bf16[64,2048]{1,0:T(8,128)(2,1)S(1)}, bf16[64,2048]{1,0:T(8,128)(2,1)S(1)}, u32[]{:S(2)}, u32[]{:S(2)}) collective-permute-start(bf16[64,2048]{1,0:T(8,128)(2,1)S(1)} %collective-permute-done.7.refs_6_), channel_id=1, source_target_pairs={{0,64},{1,65},{2,66},{3,67},{4,68},{5,69},{6,70},{7,71},{8,72},{9,... | collective-permute-start | bytes 786440 | tf_op jit(solution)/shard_map/ppermute | solution.py:210
  88.7 0.0 collective-permute-done.10.refs_9_
  88.7 0.0 copy-start.9
  88.7 1.9 %collective-permute-start.14 = (bf16[64,2048]{1,0:T(8,128)(2,1)S(1)}, bf16[64,2048]{1,0:T(8,128)(2,1)S(1)}, u32[]{:S(2)}, u32[]{:S(2)}) collective-permute-start(bf16[64,2048]{1,0:T(8,128)(2,1)S(1)} %collective-permute-done.10.refs_9_), channel_id=1, source_target_pairs={{0,448},{1,449},{2,450},{3,451},{4,452},{5,453},{6,454},{7,455},{8... | collective-permute-start | bytes 786440 | tf_op jit(solution)/shard_map/ppermute | solution.py:210
  90.6 0.0 collective-permute-done.8.refs_7_
  90.6 0.0 copy-start.10
  90.7 5.1 %collective-permute-start.12 = (bf16[64,2048]{1,0:T(8,128)(2,1)S(1)}, bf16[64,2048]{1,0:T(8,128)(2,1)S(1)}, u32[]{:S(2)}, u32[]{:S(2)}) collective-permute-start(bf16[64,2048]{1,0:T(8,128)(2,1)S(1)} %collective-permute-done.8.refs_7_), channel_id=1, source_target_pairs={{0,64},{1,65},{2,66},{3,67},{4,68},{5,69},{6,70},{7,71},{8,72},{9,... | collective-permute-start | bytes 786440 | tf_op jit(solution)/shard_map/ppermute | solution.py:210
  95.8 0.0 collective-permute-done.9.refs_8_
  95.8 0.0 copy-start.11
  95.8 1.9 %collective-permute-start.13 = (bf16[64,2048]{1,0:T(8,128)(2,1)S(1)}, bf16[64,2048]{1,0:T(8,128)(2,1)S(1)}, u32[]{:S(2)}, u32[]{:S(2)}) collective-permute-start(bf16[64,2048]{1,0:T(8,128)(2,1)S(1)} %collective-permute-done.9.refs_8_), channel_id=1, source_target_pairs={{0,448},{1,449},{2,450},{3,451},{4,452},{5,453},{6,454},{7,455},{8... | collective-permute-start | bytes 786440 | tf_op jit(solution)/shard_map/ppermute | solution.py:210
  97.7 0.0 collective-permute-done.11.refs_10_
  97.8 0.0 copy-start.12
  97.8 5.1 %collective-permute-start.15 = (bf16[64,2048]{1,0:T(8,128)(2,1)S(1)}, bf16[64,2048]{1,0:T(8,128)(2,1)S(1)}, u32[]{:S(2)}, u32[]{:S(2)}) collective-permute-start(bf16[64,2048]{1,0:T(8,128)(2,1)S(1)} %collective-permute-done.11.refs_10_), channel_id=1, source_target_pairs={{0,64},{1,65},{2,66},{3,67},{4,68},{5,69},{6,70},{7,71},{8,72},{9,... | collective-permute-start | bytes 786440 | tf_op jit(solution)/shard_map/ppermute | solution.py:210
  102.9 0.0 collective-permute-done.14.refs_13_
  102.9 0.0 copy-start.13
  102.9 1.9 %collective-permute-start.16 = (bf16[64,2048]{1,0:T(8,128)(2,1)S(1)}, bf16[64,2048]{1,0:T(8,128)(2,1)S(1)}, u32[]{:S(2)}, u32[]{:S(2)}) collective-permute-start(bf16[64,2048]{1,0:T(8,128)(2,1)S(1)} %collective-permute-done.14.refs_13_), channel_id=1, source_target_pairs={{0,448},{1,449},{2,450},{3,451},{4,452},{5,453},{6,454},{7,455},{8... | collective-permute-start | bytes 786440 | tf_op jit(solution)/shard_map/ppermute | solution.py:210
  104.9 0.0 collective-permute-done.12.refs_11_
  104.9 0.0 copy-start.14
  104.9 0.4 collective-permute-done.13.refs_12_
  105.3 0.0 copy-done.2
  105.3 0.0 copy-done.3
  105.3 0.0 copy-done.4
  105.3 0.0 copy-done.5
  105.3 0.0 copy-done.6
  105.3 0.0 copy-done.7
  105.4 0.2 copy-done.14
  105.6 0.7 copy-done.15
  106.3 3.4 %shard_map.28 = (bf16[512,4096]{1,0:T(8,128)(2,1)}, f32[512,128]{1,0:T(8,128)}) custom-call(bf16[64,2048]{1,0:T(8,128)(2,1)} %copy-done.2, bf16[64,2048]{1,0:T(8,128)(2,1)} %copy-done.3, bf16[64,2048]{1,0:T(8,128)(2,1)} %copy-done.4, bf16[64,2048]{1,0:T(8,128)(2,1)} %copy-done.6, bf16[64,2048]{1,0:T(8,128)(2,1)} %copy-done.7, bf16[64,2048]{1,0:T(8,128)(2,1)} %copy-done.5, ...), custom_call_target="tpu_custom_call" | custom-call | flops 3670016 | bytes 7340032 | tf_op jit(solution)/shard_map/pallas_call | solution.py:100
  109.7 0.0 collective-permute-done.15.refs_0_
  109.7 0.0 copy-start
  109.7 2.7 %collective-permute-done.16.refs_1_ = bf16[64,2048]{1,0:T(8,128)(2,1)S(1)} collective-permute-done((bf16[64,2048]{1,0:T(8,128)(2,1)S(1)}, bf16[64,2048]{1,0:T(8,128)(2,1)S(1)}, u32[]{:S(2)}, u32[]{:S(2)}) %collective-permute-start.16) | collective-permute-done | bytes 262176 | tf_op jit(solution)/shard_map/ppermute | solution.py:210
  112.4 0.7 copy-done.1
  113.1 6.4 %shard_map.30 = bf16[512,512]{1,0:T(8,128)(2,1)} custom-call(s32[16,16]{1,0:T(8,128)} %live_ref.3, bf16[1024,4096]{1,0:T(8,128)(2,1)} %all-gather.2.cloned.1.call-done.rows_hbm, bf16[512,4096]{1,0:T(8,128)(2,1)} %get-tuple-element.7.cols_hbm, f32[512,128]{1,0:T(8,128)} %get-tuple-element.8.norm_ref, bf16[64,2048]{1,0:T(8,128)(2,1)} %copy-done, ...), custom_call_target="tpu_custom_call" | custom-call | flops 2147483648 | bytes 9437184 | tf_op jit(solution)/shard_map/pallas_call | solution.py:177
  119.5 1.9 %collective-permute-start.17 = (bf16[512,512]{1,0:T(8,128)(2,1)}, bf16[512,512]{1,0:T(8,128)(2,1)S(1)}, u32[]{:S(2)}, u32[]{:S(2)}) collective-permute-start(bf16[512,512]{1,0:T(8,128)(2,1)} %shard_map.30), channel_id=1, source_target_pairs={{0,1},{1,0},{2,3},{3,2},{4,5},{5,4},{6,7},{7,6},{8,9},{9,8},{10,11... | collective-permute-start | bytes 1572872 | tf_op jit(solution)/shard_map/ppermute | solution.py:210
  121.4 6.5 %shard_map.29 = bf16[512,1024]{1,0:T(8,128)(2,1)} custom-call(s32[16,16]{1,0:T(8,128)} %live_ref.3, bf16[1024,4096]{1,0:T(8,128)(2,1)} %all-gather.2.cloned.1.call-done.rows_hbm, bf16[512,4096]{1,0:T(8,128)(2,1)} %get-tuple-element.7.cols_hbm, f32[512,128]{1,0:T(8,128)} %get-tuple-element.8.norm_ref, bf16[64,2048]{1,0:T(8,128)(2,1)} %copy-done, ...), custom_call_target="tpu_custom_call" | custom-call | flops 2147483648 | bytes 9437184 | tf_op jit(solution)/shard_map/pallas_call | solution.py:177
  128.0 4.3 %collective-permute-done.17 = bf16[512,512]{1,0:T(8,128)(2,1)S(1)} collective-permute-done((bf16[512,512]{1,0:T(8,128)(2,1)}, bf16[512,512]{1,0:T(8,128)(2,1)S(1)}, u32[]{:S(2)}, u32[]{:S(2)}) %collective-permute-start.17) | collective-permute-done | bytes 524320 | tf_op jit(solution)/shard_map/ppermute | solution.py:210
  132.3 0.8 constant_dynamic-update-slice_fusion
  (12 shorter events, 0.0 us)
Async XLA Ops:
  6.5 105.9 %all-gather.2.cloned.1.call-start = ((), (), s32[]{:S(2)}) async-start(), calls=%async_computation | async-start | bytes 8912896 | tf_op jit(solution)/shard_map/all_gather | solution.py:220
  6.5 11.6 %collective-permute-start = (bf16[64,2048]{1,0:T(8,128)(2,1)}, bf16[64,2048]{1,0:T(8,128)(2,1)S(1)}, u32[]{:S(2)}, u32[]{:S(2)}) collective-permute-start(bf16[64,2048]{1,0:T(8,128)(2,1)} %param.2), channel_id=1, source_target_pairs={{0,1},{1,0},{2,3},{3,2},{4,5},{5,4},{6,7},{7,6},{8,9},{9,8},{10,11... | collective-permute-start | bytes 786440 | tf_op jit(solution)/shard_map/ppermute | solution.py:210
  20.2 21.7 %collective-permute-start.1 = (bf16[64,2048]{1,0:T(8,128)(2,1)}, bf16[64,2048]{1,0:T(8,128)(2,1)S(1)}, u32[]{:S(2)}, u32[]{:S(2)}) collective-permute-start(bf16[64,2048]{1,0:T(8,128)(2,1)} %param.2), channel_id=1, source_target_pairs={{0,0},{1,32},{2,256},{3,288},{4,64},{5,96},{6,448},{7,480},{8,128}... | collective-permute-start | bytes 786440 | tf_op jit(solution)/shard_map/ppermute | solution.py:210
  33.3 18.2 %collective-permute-start.2 = (bf16[64,2048]{1,0:T(8,128)(2,1)}, bf16[64,2048]{1,0:T(8,128)(2,1)S(1)}, u32[]{:S(2)}, u32[]{:S(2)}) collective-permute-start(bf16[64,2048]{1,0:T(8,128)(2,1)} %param.2), channel_id=1, source_target_pairs={{0,32},{1,0},{2,288},{3,256},{4,96},{5,64},{6,480},{7,448},{8,160}... | collective-permute-start | bytes 786440 | tf_op jit(solution)/shard_map/ppermute | solution.py:210
  41.9 63.4 %copy-start.2 = (bf16[64,2048]{1,0:T(8,128)(2,1)}, bf16[64,2048]{1,0:T(8,128)(2,1)S(1)}, u32[]{:S(2)}) copy-start(bf16[64,2048]{1,0:T(8,128)(2,1)S(1)} %collective-permute-done.1.refs_0_) | copy-start | bytes 786436
  41.9 29.4 %collective-permute-start.3 = (bf16[64,2048]{1,0:T(8,128)(2,1)S(1)}, bf16[64,2048]{1,0:T(8,128)(2,1)S(1)}, u32[]{:S(2)}, u32[]{:S(2)}) collective-permute-start(bf16[64,2048]{1,0:T(8,128)(2,1)S(1)} %collective-permute-done.1.refs_0_), channel_id=1, source_target_pairs={{0,64},{1,65},{2,66},{3,67},{4,68},{5,69},{6,70},{7,71},{8,72},{9,... | collective-permute-start | bytes 786440 | tf_op jit(solution)/shard_map/ppermute | solution.py:210
  51.6 53.7 %copy-start.3 = (bf16[64,2048]{1,0:T(8,128)(2,1)}, bf16[64,2048]{1,0:T(8,128)(2,1)S(1)}, u32[]{:S(2)}) copy-start(bf16[64,2048]{1,0:T(8,128)(2,1)S(1)} %collective-permute-done.2.refs_1_) | copy-start | bytes 786436
  51.6 22.9 %collective-permute-start.6 = (bf16[64,2048]{1,0:T(8,128)(2,1)S(1)}, bf16[64,2048]{1,0:T(8,128)(2,1)S(1)}, u32[]{:S(2)}, u32[]{:S(2)}) collective-permute-start(bf16[64,2048]{1,0:T(8,128)(2,1)S(1)} %collective-permute-done.2.refs_1_), channel_id=1, source_target_pairs={{0,448},{1,449},{2,450},{3,451},{4,452},{5,453},{6,454},{7,455},{8... | collective-permute-start | bytes 786440 | tf_op jit(solution)/shard_map/ppermute | solution.py:210
  65.4 11.8 %collective-permute-start.4 = (bf16[64,2048]{1,0:T(8,128)(2,1)S(1)}, bf16[64,2048]{1,0:T(8,128)(2,1)S(1)}, u32[]{:S(2)}, u32[]{:S(2)}) collective-permute-start(bf16[64,2048]{1,0:T(8,128)(2,1)S(1)} %collective-permute-done.2.refs_1_), channel_id=1, source_target_pairs={{0,64},{1,65},{2,66},{3,67},{4,68},{5,69},{6,70},{7,71},{8,72},{9,... | collective-permute-start | bytes 786440 | tf_op jit(solution)/shard_map/ppermute | solution.py:210
  67.4 14.2 %collective-permute-start.5 = (bf16[64,2048]{1,0:T(8,128)(2,1)S(1)}, bf16[64,2048]{1,0:T(8,128)(2,1)S(1)}, u32[]{:S(2)}, u32[]{:S(2)}) collective-permute-start(bf16[64,2048]{1,0:T(8,128)(2,1)S(1)} %collective-permute-done.1.refs_0_), channel_id=1, source_target_pairs={{0,448},{1,449},{2,450},{3,451},{4,452},{5,453},{6,454},{7,455},{8... | collective-permute-start | bytes 786440 | tf_op jit(solution)/shard_map/ppermute | solution.py:210
  71.3 34.0 %copy-start.4 = (bf16[64,2048]{1,0:T(8,128)(2,1)}, bf16[64,2048]{1,0:T(8,128)(2,1)S(1)}, u32[]{:S(2)}) copy-start(bf16[64,2048]{1,0:T(8,128)(2,1)S(1)} %collective-permute-done.3.refs_2_) | copy-start | bytes 786436
  71.3 12.2 %collective-permute-start.7 = (bf16[64,2048]{1,0:T(8,128)(2,1)S(1)}, bf16[64,2048]{1,0:T(8,128)(2,1)S(1)}, u32[]{:S(2)}, u32[]{:S(2)}) collective-permute-start(bf16[64,2048]{1,0:T(8,128)(2,1)S(1)} %collective-permute-done.3.refs_2_), channel_id=1, source_target_pairs={{0,64},{1,65},{2,66},{3,67},{4,68},{5,69},{6,70},{7,71},{8,72},{9,... | collective-permute-start | bytes 786440 | tf_op jit(solution)/shard_map/ppermute | solution.py:210
  74.5 30.8 %copy-start.5 = (bf16[64,2048]{1,0:T(8,128)(2,1)}, bf16[64,2048]{1,0:T(8,128)(2,1)S(1)}, u32[]{:S(2)}) copy-start(bf16[64,2048]{1,0:T(8,128)(2,1)S(1)} %collective-permute-done.6.refs_5_) | copy-start | bytes 786436
  74.5 14.2 %collective-permute-start.10 = (bf16[64,2048]{1,0:T(8,128)(2,1)S(1)}, bf16[64,2048]{1,0:T(8,128)(2,1)S(1)}, u32[]{:S(2)}, u32[]{:S(2)}) collective-permute-start(bf16[64,2048]{1,0:T(8,128)(2,1)S(1)} %collective-permute-done.6.refs_5_), channel_id=1, source_target_pairs={{0,448},{1,449},{2,450},{3,451},{4,452},{5,453},{6,454},{7,455},{8... | collective-permute-start | bytes 786440 | tf_op jit(solution)/shard_map/ppermute | solution.py:210
  77.2 28.1 %copy-start.6 = (bf16[64,2048]{1,0:T(8,128)(2,1)}, bf16[64,2048]{1,0:T(8,128)(2,1)S(1)}, u32[]{:S(2)}) copy-start(bf16[64,2048]{1,0:T(8,128)(2,1)S(1)} %collective-permute-done.4.refs_3_) | copy-start | bytes 786436
  77.2 13.4 %collective-permute-start.8 = (bf16[64,2048]{1,0:T(8,128)(2,1)S(1)}, bf16[64,2048]{1,0:T(8,128)(2,1)S(1)}, u32[]{:S(2)}, u32[]{:S(2)}) collective-permute-start(bf16[64,2048]{1,0:T(8,128)(2,1)S(1)} %collective-permute-done.4.refs_3_), channel_id=1, source_target_pairs={{0,64},{1,65},{2,66},{3,67},{4,68},{5,69},{6,70},{7,71},{8,72},{9,... | collective-permute-start | bytes 786440 | tf_op jit(solution)/shard_map/ppermute | solution.py:210
  81.6 23.7 %copy-start.7 = (bf16[64,2048]{1,0:T(8,128)(2,1)}, bf16[64,2048]{1,0:T(8,128)(2,1)S(1)}, u32[]{:S(2)}) copy-start(bf16[64,2048]{1,0:T(8,128)(2,1)S(1)} %collective-permute-done.5.refs_4_) | copy-start | bytes 786436
  81.6 14.2 %collective-permute-start.9 = (bf16[64,2048]{1,0:T(8,128)(2,1)S(1)}, bf16[64,2048]{1,0:T(8,128)(2,1)S(1)}, u32[]{:S(2)}, u32[]{:S(2)}) collective-permute-start(bf16[64,2048]{1,0:T(8,128)(2,1)S(1)} %collective-permute-done.5.refs_4_), channel_id=1, source_target_pairs={{0,448},{1,449},{2,450},{3,451},{4,452},{5,453},{6,454},{7,455},{8... | collective-permute-start | bytes 786440 | tf_op jit(solution)/shard_map/ppermute | solution.py:210
  83.5 21.8 %copy-start.8 = (bf16[64,2048]{1,0:T(8,128)(2,1)}, bf16[64,2048]{1,0:T(8,128)(2,1)S(1)}, u32[]{:S(2)}) copy-start(bf16[64,2048]{1,0:T(8,128)(2,1)S(1)} %collective-permute-done.7.refs_6_) | copy-start | bytes 786436
  83.5 14.2 %collective-permute-start.11 = (bf16[64,2048]{1,0:T(8,128)(2,1)S(1)}, bf16[64,2048]{1,0:T(8,128)(2,1)S(1)}, u32[]{:S(2)}, u32[]{:S(2)}) collective-permute-start(bf16[64,2048]{1,0:T(8,128)(2,1)S(1)} %collective-permute-done.7.refs_6_), channel_id=1, source_target_pairs={{0,64},{1,65},{2,66},{3,67},{4,68},{5,69},{6,70},{7,71},{8,72},{9,... | collective-permute-start | bytes 786440 | tf_op jit(solution)/shard_map/ppermute | solution.py:210
  88.7 16.6 %copy-start.9 = (bf16[64,2048]{1,0:T(8,128)(2,1)}, bf16[64,2048]{1,0:T(8,128)(2,1)S(1)}, u32[]{:S(2)}) copy-start(bf16[64,2048]{1,0:T(8,128)(2,1)S(1)} %collective-permute-done.10.refs_9_) | copy-start | bytes 786436
  88.7 14.2 %collective-permute-start.14 = (bf16[64,2048]{1,0:T(8,128)(2,1)S(1)}, bf16[64,2048]{1,0:T(8,128)(2,1)S(1)}, u32[]{:S(2)}, u32[]{:S(2)}) collective-permute-start(bf16[64,2048]{1,0:T(8,128)(2,1)S(1)} %collective-permute-done.10.refs_9_), channel_id=1, source_target_pairs={{0,448},{1,449},{2,450},{3,451},{4,452},{5,453},{6,454},{7,455},{8... | collective-permute-start | bytes 786440 | tf_op jit(solution)/shard_map/ppermute | solution.py:210
  90.6 14.7 %copy-start.10 = (bf16[64,2048]{1,0:T(8,128)(2,1)}, bf16[64,2048]{1,0:T(8,128)(2,1)S(1)}, u32[]{:S(2)}) copy-start(bf16[64,2048]{1,0:T(8,128)(2,1)S(1)} %collective-permute-done.8.refs_7_) | copy-start | bytes 786436
  90.7 14.2 %collective-permute-start.12 = (bf16[64,2048]{1,0:T(8,128)(2,1)S(1)}, bf16[64,2048]{1,0:T(8,128)(2,1)S(1)}, u32[]{:S(2)}, u32[]{:S(2)}) collective-permute-start(bf16[64,2048]{1,0:T(8,128)(2,1)S(1)} %collective-permute-done.8.refs_7_), channel_id=1, source_target_pairs={{0,64},{1,65},{2,66},{3,67},{4,68},{5,69},{6,70},{7,71},{8,72},{9,... | collective-permute-start | bytes 786440 | tf_op jit(solution)/shard_map/ppermute | solution.py:210
  95.8 9.6 %copy-start.11 = (bf16[64,2048]{1,0:T(8,128)(2,1)}, bf16[64,2048]{1,0:T(8,128)(2,1)S(1)}, u32[]{:S(2)}) copy-start(bf16[64,2048]{1,0:T(8,128)(2,1)S(1)} %collective-permute-done.9.refs_8_) | copy-start | bytes 786436
  95.8 9.5 %collective-permute-start.13 = (bf16[64,2048]{1,0:T(8,128)(2,1)S(1)}, bf16[64,2048]{1,0:T(8,128)(2,1)S(1)}, u32[]{:S(2)}, u32[]{:S(2)}) collective-permute-start(bf16[64,2048]{1,0:T(8,128)(2,1)S(1)} %collective-permute-done.9.refs_8_), channel_id=1, source_target_pairs={{0,448},{1,449},{2,450},{3,451},{4,452},{5,453},{6,454},{7,455},{8... | collective-permute-start | bytes 786440 | tf_op jit(solution)/shard_map/ppermute | solution.py:210
  97.8 7.6 %copy-start.12 = (bf16[64,2048]{1,0:T(8,128)(2,1)}, bf16[64,2048]{1,0:T(8,128)(2,1)S(1)}, u32[]{:S(2)}) copy-start(bf16[64,2048]{1,0:T(8,128)(2,1)S(1)} %collective-permute-done.11.refs_10_) | copy-start | bytes 786436
  97.8 11.9 %collective-permute-start.15 = (bf16[64,2048]{1,0:T(8,128)(2,1)S(1)}, bf16[64,2048]{1,0:T(8,128)(2,1)S(1)}, u32[]{:S(2)}, u32[]{:S(2)}) collective-permute-start(bf16[64,2048]{1,0:T(8,128)(2,1)S(1)} %collective-permute-done.11.refs_10_), channel_id=1, source_target_pairs={{0,64},{1,65},{2,66},{3,67},{4,68},{5,69},{6,70},{7,71},{8,72},{9,... | collective-permute-start | bytes 786440 | tf_op jit(solution)/shard_map/ppermute | solution.py:210
  102.9 2.5 %copy-start.13 = (bf16[64,2048]{1,0:T(8,128)(2,1)}, bf16[64,2048]{1,0:T(8,128)(2,1)S(1)}, u32[]{:S(2)}) copy-start(bf16[64,2048]{1,0:T(8,128)(2,1)S(1)} %collective-permute-done.14.refs_13_) | copy-start | bytes 786436
  102.9 9.5 %collective-permute-start.16 = (bf16[64,2048]{1,0:T(8,128)(2,1)S(1)}, bf16[64,2048]{1,0:T(8,128)(2,1)S(1)}, u32[]{:S(2)}, u32[]{:S(2)}) collective-permute-start(bf16[64,2048]{1,0:T(8,128)(2,1)S(1)} %collective-permute-done.14.refs_13_), channel_id=1, source_target_pairs={{0,448},{1,449},{2,450},{3,451},{4,452},{5,453},{6,454},{7,455},{8... | collective-permute-start | bytes 786440 | tf_op jit(solution)/shard_map/ppermute | solution.py:210
  104.9 0.7 copy-start.14
  105.6 0.7 copy-start.15
  109.7 2.7 %copy-start = (bf16[64,2048]{1,0:T(8,128)(2,1)}, bf16[64,2048]{1,0:T(8,128)(2,1)S(1)}, u32[]{:S(2)}) copy-start(bf16[64,2048]{1,0:T(8,128)(2,1)S(1)} %collective-permute-done.15.refs_0_) | copy-start | bytes 786436
  112.4 0.7 copy-start.1
  119.5 12.8 %collective-permute-start.17 = (bf16[512,512]{1,0:T(8,128)(2,1)}, bf16[512,512]{1,0:T(8,128)(2,1)S(1)}, u32[]{:S(2)}, u32[]{:S(2)}) collective-permute-start(bf16[512,512]{1,0:T(8,128)(2,1)} %shard_map.30), channel_id=1, source_target_pairs={{0,1},{1,0},{2,3},{3,2},{4,5},{5,4},{6,7},{7,6},{8,9},{9,8},{10,11... | collective-permute-start | bytes 1572872 | tf_op jit(solution)/shard_map/ppermute | solution.py:210
Sparse Core Ops, SparseCore 0:
  20.3 73.8 all-gather.1

commit v7 on v6

--- a/solution.py
+++ b/solution.py
@@ -212,6 +212,7 @@
     other = send(trajectories, swap_lag())
     early = send(trajectories, col_pairs(0))
     late = send(trajectories, col_pairs(1))
+    early, other = lax.optimization_barrier((early, other))
     rows = jnp.where(
         xl == 0,
         jnp.concatenate([trajectories, other], axis=1),

time: 141 us -> 137 us (0.972)
  the two profiles are of different devices: /device:TPU:56 before, /device:TPU:192 now
where the time goes in v7:
time: 137 us; the launch traced here: 136 us
  starting transfers between devices  85.7 us (63%)
  Pallas kernels  16.3 us (12%)
  waiting for transfers between devices  15.6 us (11%)
  between operations  13.9 us (10%)
  local copies, waits for them, and re-layouts  2.32 us (2%)
  other arithmetic  2.04 us (1%)
    ppermute x18, starting transfers between devices, send(): return lax.ppermute(value, AX, to)  85.7 us
    ppermute x18, waiting for transfers between devices, send(): return lax.ppermute(value, AX, to)  15.6 us
    pallas_call x2, Pallas kernels, gram_tile(): pl.pallas_call(functools.partial(gram_kernel, keep), out_shape=jax.ShapeD...  12.9 us
    pallas_call x1, Pallas kernels, in_order(): pl.pallas_call(functools.partial(order_kernel, steps), out_shape=(jax.Sha...  3.39 us
  transfers between devices with their start and end apart: 19, of which 5 were waited for; matrix products, arithmetic and copies ran while one was open for 0% of the time, Pallas kernels for 7%

profile of v7, /device:TPU:192, one launch (start us, length us, event | category | flops | bytes accessed | tf_op | source)
XLA Modules:
  0.0 135.9 jit_solution(1087828944468621505)
XLA Ops:
  6.5 0.0 all-gather.2.cloned.1.call-start
  6.5 2.8 %collective-permute-start = (bf16[64,2048]{1,0:T(8,128)(2,1)}, bf16[64,2048]{1,0:T(8,128)(2,1)S(1)}, u32[]{:S(2)}, u32[]{:S(2)}) collective-permute-start(bf16[64,2048]{1,0:T(8,128)(2,1)} %param.2), channel_id=1, source_target_pairs={{0,0},{1,32},{2,256},{3,288},{4,64},{5,96},{6,448},{7,480},{8,128}... | collective-permute-start | bytes 786440 | tf_op jit(solution)/shard_map/ppermute | solution.py:210
  9.3 4.9 %collective-permute-start.1 = (bf16[64,2048]{1,0:T(8,128)(2,1)}, bf16[64,2048]{1,0:T(8,128)(2,1)S(1)}, u32[]{:S(2)}, u32[]{:S(2)}) collective-permute-start(bf16[64,2048]{1,0:T(8,128)(2,1)} %param.2), channel_id=1, source_target_pairs={{0,1},{1,0},{2,3},{3,2},{4,5},{5,4},{6,7},{7,6},{8,9},{9,8},{10,11... | collective-permute-start | bytes 786440 | tf_op jit(solution)/shard_map/ppermute | solution.py:210
  14.2 7.4 %collective-permute-done.refs_0_ = bf16[64,2048]{1,0:T(8,128)(2,1)S(1)} collective-permute-done((bf16[64,2048]{1,0:T(8,128)(2,1)}, bf16[64,2048]{1,0:T(8,128)(2,1)S(1)}, u32[]{:S(2)}, u32[]{:S(2)}) %collective-permute-start) | collective-permute-done | bytes 262176 | tf_op jit(solution)/shard_map/ppermute | solution.py:210
  21.7 0.0 collective-permute-done.1
  21.7 2.0 %maximum_select_fusion = bf16[64,4096]{1,0:T(8,128)(2,1)} fusion(bf16[64,2048]{1,0:T(8,128)(2,1)S(1)} %collective-permute-done.1, bf16[64,2048]{1,0:T(8,128)(2,1)} %param.2, pred[]{:T(512)S(6)} %eq.3), kind=kLoop, calls=%fused_computation | loop fusion | flops 2359296 | bytes 1048577 | tf_op jit(solution)/shard_map/jit(_where)/select_n | solution.py:216
  23.7 0.0 all-gather.2.cloned.1.call-update
  23.8 12.1 %collective-permute-start.2 = (bf16[64,2048]{1,0:T(8,128)(2,1)}, bf16[64,2048]{1,0:T(8,128)(2,1)S(1)}, u32[]{:S(2)}, u32[]{:S(2)}) collective-permute-start(bf16[64,2048]{1,0:T(8,128)(2,1)} %param.2), channel_id=1, source_target_pairs={{0,32},{1,0},{2,288},{3,256},{4,96},{5,64},{6,480},{7,448},{8,160}... | collective-permute-start | bytes 786440 | tf_op jit(solution)/shard_map/ppermute | solution.py:210
  35.8 7.4 %collective-permute-start.3 = (bf16[64,2048]{1,0:T(8,128)(2,1)S(1)}, bf16[64,2048]{1,0:T(8,128)(2,1)S(1)}, u32[]{:S(2)}, u32[]{:S(2)}) collective-permute-start(bf16[64,2048]{1,0:T(8,128)(2,1)S(1)} %collective-permute-done.refs_0_), channel_id=1, source_target_pairs={{0,64},{1,65},{2,66},{3,67},{4,68},{5,69},{6,70},{7,71},{8,72},{9,... | collective-permute-start | bytes 786440 | tf_op jit(solution)/shard_map/ppermute | solution.py:210
  43.2 0.5 collective-permute-done.2.refs_1_
  43.7 12.9 %collective-permute-start.6 = (bf16[64,2048]{1,0:T(8,128)(2,1)S(1)}, bf16[64,2048]{1,0:T(8,128)(2,1)S(1)}, u32[]{:S(2)}, u32[]{:S(2)}) collective-permute-start(bf16[64,2048]{1,0:T(8,128)(2,1)S(1)} %collective-permute-done.2.refs_1_), channel_id=1, source_target_pairs={{0,448},{1,449},{2,450},{3,451},{4,452},{5,453},{6,454},{7,455},{8... | collective-permute-start | bytes 786440 | tf_op jit(solution)/shard_map/ppermute | solution.py:210
  56.6 9.0 %collective-permute-start.5 = (bf16[64,2048]{1,0:T(8,128)(2,1)S(1)}, bf16[64,2048]{1,0:T(8,128)(2,1)S(1)}, u32[]{:S(2)}, u32[]{:S(2)}) collective-permute-start(bf16[64,2048]{1,0:T(8,128)(2,1)S(1)} %collective-permute-done.refs_0_), channel_id=1, source_target_pairs={{0,448},{1,449},{2,450},{3,451},{4,452},{5,453},{6,454},{7,455},{8... | collective-permute-start | bytes 786440 | tf_op jit(solution)/shard_map/ppermute | solution.py:210
  65.6 1.9 %collective-permute-start.4 = (bf16[64,2048]{1,0:T(8,128)(2,1)S(1)}, bf16[64,2048]{1,0:T(8,128)(2,1)S(1)}, u32[]{:S(2)}, u32[]{:S(2)}) collective-permute-start(bf16[64,2048]{1,0:T(8,128)(2,1)S(1)} %collective-permute-done.2.refs_1_), channel_id=1, source_target_pairs={{0,64},{1,65},{2,66},{3,67},{4,68},{5,69},{6,70},{7,71},{8,72},{9,... | collective-permute-start | bytes 786440 | tf_op jit(solution)/shard_map/ppermute | solution.py:210
  67.6 0.0 collective-permute-done.3.refs_2_
  67.6 0.0 copy-start.4
  67.6 1.9 %collective-permute-start.7 = (bf16[64,2048]{1,0:T(8,128)(2,1)S(1)}, bf16[64,2048]{1,0:T(8,128)(2,1)S(1)}, u32[]{:S(2)}, u32[]{:S(2)}) collective-permute-start(bf16[64,2048]{1,0:T(8,128)(2,1)S(1)} %collective-permute-done.3.refs_2_), channel_id=1, source_target_pairs={{0,64},{1,65},{2,66},{3,67},{4,68},{5,69},{6,70},{7,71},{8,72},{9,... | collective-permute-start | bytes 786440 | tf_op jit(solution)/shard_map/ppermute | solution.py:210
  69.5 0.0 collective-permute-done.6.refs_5_
  69.5 0.0 copy-start.5
  69.5 5.1 %collective-permute-start.10 = (bf16[64,2048]{1,0:T(8,128)(2,1)S(1)}, bf16[64,2048]{1,0:T(8,128)(2,1)S(1)}, u32[]{:S(2)}, u32[]{:S(2)}) collective-permute-start(bf16[64,2048]{1,0:T(8,128)(2,1)S(1)} %collective-permute-done.6.refs_5_), channel_id=1, source_target_pairs={{0,448},{1,449},{2,450},{3,451},{4,452},{5,453},{6,454},{7,455},{8... | collective-permute-start | bytes 786440 | tf_op jit(solution)/shard_map/ppermute | solution.py:210
  74.7 0.0 collective-permute-done.5.refs_4_
  74.7 0.0 copy-start.6
  74.7 3.9 %collective-permute-start.9 = (bf16[64,2048]{1,0:T(8,128)(2,1)S(1)}, bf16[64,2048]{1,0:T(8,128)(2,1)S(1)}, u32[]{:S(2)}, u32[]{:S(2)}) collective-permute-start(bf16[64,2048]{1,0:T(8,128)(2,1)S(1)} %collective-permute-done.5.refs_4_), channel_id=1, source_target_pairs={{0,448},{1,449},{2,450},{3,451},{4,452},{5,453},{6,454},{7,455},{8... | collective-permute-start | bytes 786440 | tf_op jit(solution)/shard_map/ppermute | solution.py:210
  78.6 0.0 collective-permute-done.4.refs_3_
  78.6 1.9 %collective-permute-start.8 = (bf16[64,2048]{1,0:T(8,128)(2,1)S(1)}, bf16[64,2048]{1,0:T(8,128)(2,1)S(1)}, u32[]{:S(2)}, u32[]{:S(2)}) collective-permute-start(bf16[64,2048]{1,0:T(8,128)(2,1)S(1)} %collective-permute-done.4.refs_3_), channel_id=1, source_target_pairs={{0,64},{1,65},{2,66},{3,67},{4,68},{5,69},{6,70},{7,71},{8,72},{9,... | collective-permute-start | bytes 786440 | tf_op jit(solution)/shard_map/ppermute | solution.py:210
  80.6 1.3 collective-permute-done.7.refs_6_
  81.9 1.9 %collective-permute-start.11 = (bf16[64,2048]{1,0:T(8,128)(2,1)S(1)}, bf16[64,2048]{1,0:T(8,128)(2,1)S(1)}, u32[]{:S(2)}, u32[]{:S(2)}) collective-permute-start(bf16[64,2048]{1,0:T(8,128)(2,1)S(1)} %collective-permute-done.7.refs_6_), channel_id=1, source_target_pairs={{0,64},{1,65},{2,66},{3,67},{4,68},{5,69},{6,70},{7,71},{8,72},{9,... | collective-permute-start | bytes 786440 | tf_op jit(solution)/shard_map/ppermute | solution.py:210
  83.8 0.0 collective-permute-done.10.refs_9_
  83.8 5.1 %collective-permute-start.14 = (bf16[64,2048]{1,0:T(8,128)(2,1)S(1)}, bf16[64,2048]{1,0:T(8,128)(2,1)S(1)}, u32[]{:S(2)}, u32[]{:S(2)}) collective-permute-start(bf16[64,2048]{1,0:T(8,128)(2,1)S(1)} %collective-permute-done.10.refs_9_), channel_id=1, source_target_pairs={{0,448},{1,449},{2,450},{3,451},{4,452},{5,453},{6,454},{7,455},{8... | collective-permute-start | bytes 786440 | tf_op jit(solution)/shard_map/ppermute | solution.py:210
  89.0 0.0 collective-permute-done.9.refs_8_
  89.0 0.0 copy-start.10
  89.0 2.6 %collective-permute-start.13 = (bf16[64,2048]{1,0:T(8,128)(2,1)S(1)}, bf16[64,2048]{1,0:T(8,128)(2,1)S(1)}, u32[]{:S(2)}, u32[]{:S(2)}) collective-permute-start(bf16[64,2048]{1,0:T(8,128)(2,1)S(1)} %collective-permute-done.9.refs_8_), channel_id=1, source_target_pairs={{0,448},{1,449},{2,450},{3,451},{4,452},{5,453},{6,454},{7,455},{8... | collective-permute-start | bytes 786440 | tf_op jit(solution)/shard_map/ppermute | solution.py:210
  91.6 0.0 collective-permute-done.8.refs_7_
  91.7 3.2 %collective-permute-start.12 = (bf16[64,2048]{1,0:T(8,128)(2,1)S(1)}, bf16[64,2048]{1,0:T(8,128)(2,1)S(1)}, u32[]{:S(2)}, u32[]{:S(2)}) collective-permute-start(bf16[64,2048]{1,0:T(8,128)(2,1)S(1)} %collective-permute-done.8.refs_7_), channel_id=1, source_target_pairs={{0,64},{1,65},{2,66},{3,67},{4,68},{5,69},{6,70},{7,71},{8,72},{9,... | collective-permute-start | bytes 786440 | tf_op jit(solution)/shard_map/ppermute | solution.py:210
  94.9 0.0 collective-permute-done.11.refs_10_
  94.9 1.9 %collective-permute-start.15 = (bf16[64,2048]{1,0:T(8,128)(2,1)S(1)}, bf16[64,2048]{1,0:T(8,128)(2,1)S(1)}, u32[]{:S(2)}, u32[]{:S(2)}) collective-permute-start(bf16[64,2048]{1,0:T(8,128)(2,1)S(1)} %collective-permute-done.11.refs_10_), channel_id=1, source_target_pairs={{0,64},{1,65},{2,66},{3,67},{4,68},{5,69},{6,70},{7,71},{8,72},{9,... | collective-permute-start | bytes 786440 | tf_op jit(solution)/shard_map/ppermute | solution.py:210
  96.8 0.0 collective-permute-done.14.refs_13_
  96.8 0.0 copy-start.13
  96.9 5.1 %collective-permute-start.16 = (bf16[64,2048]{1,0:T(8,128)(2,1)S(1)}, bf16[64,2048]{1,0:T(8,128)(2,1)S(1)}, u32[]{:S(2)}, u32[]{:S(2)}) collective-permute-start(bf16[64,2048]{1,0:T(8,128)(2,1)S(1)} %collective-permute-done.14.refs_13_), channel_id=1, source_target_pairs={{0,448},{1,449},{2,450},{3,451},{4,452},{5,453},{6,454},{7,455},{8... | collective-permute-start | bytes 786440 | tf_op jit(solution)/shard_map/ppermute | solution.py:210
  102.0 0.0 collective-permute-done.13.refs_12_
  102.0 1.5 %collective-permute-done.12.refs_11_ = bf16[64,2048]{1,0:T(8,128)(2,1)S(1)} collective-permute-done((bf16[64,2048]{1,0:T(8,128)(2,1)S(1)}, bf16[64,2048]{1,0:T(8,128)(2,1)S(1)}, u32[]{:S(2)}, u32[]{:S(2)}) %collective-permute-start.12) | collective-permute-done | bytes 262176 | tf_op jit(solution)/shard_map/ppermute | solution.py:210
  103.5 0.0 copy-done.4
  103.5 0.0 copy-done.5
  103.5 0.0 copy-done.6
  103.5 0.0 copy-done.7
  103.6 0.0 copy-done.8
  103.6 0.0 copy-done.9
  103.6 0.0 copy-done.10
  103.6 0.0 copy-done.11
  103.6 0.0 copy-done.12
  103.6 0.0 copy-done.13
  103.6 0.0 copy-done.14
  103.6 0.0 copy-start.15
  103.6 0.7 copy-done.15
  104.3 3.4 %shard_map.28 = (bf16[512,4096]{1,0:T(8,128)(2,1)}, f32[512,128]{1,0:T(8,128)}) custom-call(bf16[64,2048]{1,0:T(8,128)(2,1)} %copy-done.2, bf16[64,2048]{1,0:T(8,128)(2,1)} %copy-done.3, bf16[64,2048]{1,0:T(8,128)(2,1)} %copy-done.4, bf16[64,2048]{1,0:T(8,128)(2,1)} %copy-done.7, bf16[64,2048]{1,0:T(8,128)(2,1)} %copy-done.6, bf16[64,2048]{1,0:T(8,128)(2,1)} %copy-done.5, ...), custom_call_target="tpu_custom_call" | custom-call | flops 3670016 | bytes 7340032 | tf_op jit(solution)/shard_map/pallas_call | solution.py:100
  107.7 0.0 collective-permute-done.15.refs_0_
  107.7 0.0 collective-permute-done.16.refs_1_
  107.8 0.0 all-gather.2.cloned.1.call-done.rows_hbm
  107.8 0.6 copy-done
  108.4 0.1 copy-done.1
  108.5 6.4 %shard_map.30 = bf16[512,512]{1,0:T(8,128)(2,1)} custom-call(s32[16,16]{1,0:T(8,128)} %live_ref.3, bf16[1024,4096]{1,0:T(8,128)(2,1)} %all-gather.2.cloned.1.call-done.rows_hbm, bf16[512,4096]{1,0:T(8,128)(2,1)} %get-tuple-element.11.cols_hbm, f32[512,128]{1,0:T(8,128)} %get-tuple-element.12.norm_ref, bf16[64,2048]{1,0:T(8,128)(2,1)} %copy-done, ...), custom_call_target="tpu_custom_call" | custom-call | flops 2147483648 | bytes 9437184 | tf_op jit(solution)/shard_map/pallas_call | solution.py:177
  114.9 1.9 %collective-permute-start.17 = (bf16[512,512]{1,0:T(8,128)(2,1)}, bf16[512,512]{1,0:T(8,128)(2,1)S(1)}, u32[]{:S(2)}, u32[]{:S(2)}) collective-permute-start(bf16[512,512]{1,0:T(8,128)(2,1)} %shard_map.30), channel_id=1, source_target_pairs={{0,1},{1,0},{2,3},{3,2},{4,5},{5,4},{6,7},{7,6},{8,9},{9,8},{10,11... | collective-permute-start | bytes 1572872 | tf_op jit(solution)/shard_map/ppermute | solution.py:210
  116.9 6.5 %shard_map.29 = bf16[512,1024]{1,0:T(8,128)(2,1)} custom-call(s32[16,16]{1,0:T(8,128)} %live_ref.3, bf16[1024,4096]{1,0:T(8,128)(2,1)} %all-gather.2.cloned.1.call-done.rows_hbm, bf16[512,4096]{1,0:T(8,128)(2,1)} %get-tuple-element.11.cols_hbm, f32[512,128]{1,0:T(8,128)} %get-tuple-element.12.norm_ref, bf16[64,2048]{1,0:T(8,128)(2,1)} %copy-done, ...), custom_call_target="tpu_custom_call" | custom-call | flops 2147483648 | bytes 9437184 | tf_op jit(solution)/shard_map/pallas_call | solution.py:177
  123.4 4.8 %collective-permute-done.17 = bf16[512,512]{1,0:T(8,128)(2,1)S(1)} collective-permute-done((bf16[512,512]{1,0:T(8,128)(2,1)}, bf16[512,512]{1,0:T(8,128)(2,1)S(1)}, u32[]{:S(2)}, u32[]{:S(2)}) %collective-permute-start.17) | collective-permute-done | bytes 524320 | tf_op jit(solution)/shard_map/ppermute | solution.py:210
  128.2 0.8 constant_dynamic-update-slice_fusion
  (12 shorter events, 0.0 us)
Async XLA Ops:
  6.5 101.2 %all-gather.2.cloned.1.call-start = ((), (), s32[]{:S(2)}) async-start(), calls=%async_computation | async-start | bytes 8912896 | tf_op jit(solution)/shard_map/all_gather | solution.py:221
  6.5 15.1 %collective-permute-start = (bf16[64,2048]{1,0:T(8,128)(2,1)}, bf16[64,2048]{1,0:T(8,128)(2,1)S(1)}, u32[]{:S(2)}, u32[]{:S(2)}) collective-permute-start(bf16[64,2048]{1,0:T(8,128)(2,1)} %param.2), channel_id=1, source_target_pairs={{0,0},{1,32},{2,256},{3,288},{4,64},{5,96},{6,448},{7,480},{8,128}... | collective-permute-start | bytes 786440 | tf_op jit(solution)/shard_map/ppermute | solution.py:210
  9.3 12.4 %collective-permute-start.1 = (bf16[64,2048]{1,0:T(8,128)(2,1)}, bf16[64,2048]{1,0:T(8,128)(2,1)S(1)}, u32[]{:S(2)}, u32[]{:S(2)}) collective-permute-start(bf16[64,2048]{1,0:T(8,128)(2,1)} %param.2), channel_id=1, source_target_pairs={{0,1},{1,0},{2,3},{3,2},{4,5},{5,4},{6,7},{7,6},{8,9},{9,8},{10,11... | collective-permute-start | bytes 786440 | tf_op jit(solution)/shard_map/ppermute | solution.py:210
  21.7 81.8 %copy-start.2 = (bf16[64,2048]{1,0:T(8,128)(2,1)}, bf16[64,2048]{1,0:T(8,128)(2,1)S(1)}, u32[]{:S(2)}) copy-start(bf16[64,2048]{1,0:T(8,128)(2,1)S(1)} %collective-permute-done.refs_0_) | copy-start | bytes 786436
  23.8 19.9 %collective-permute-start.2 = (bf16[64,2048]{1,0:T(8,128)(2,1)}, bf16[64,2048]{1,0:T(8,128)(2,1)S(1)}, u32[]{:S(2)}, u32[]{:S(2)}) collective-permute-start(bf16[64,2048]{1,0:T(8,128)(2,1)} %param.2), channel_id=1, source_target_pairs={{0,32},{1,0},{2,288},{3,256},{4,96},{5,64},{6,480},{7,448},{8,160}... | collective-permute-start | bytes 786440 | tf_op jit(solution)/shard_map/ppermute | solution.py:210
  35.8 31.7 %collective-permute-start.3 = (bf16[64,2048]{1,0:T(8,128)(2,1)S(1)}, bf16[64,2048]{1,0:T(8,128)(2,1)S(1)}, u32[]{:S(2)}, u32[]{:S(2)}) collective-permute-start(bf16[64,2048]{1,0:T(8,128)(2,1)S(1)} %collective-permute-done.refs_0_), channel_id=1, source_target_pairs={{0,64},{1,65},{2,66},{3,67},{4,68},{5,69},{6,70},{7,71},{8,72},{9,... | collective-permute-start | bytes 786440 | tf_op jit(solution)/shard_map/ppermute | solution.py:210
  43.7 59.8 %copy-start.3 = (bf16[64,2048]{1,0:T(8,128)(2,1)}, bf16[64,2048]{1,0:T(8,128)(2,1)S(1)}, u32[]{:S(2)}) copy-start(bf16[64,2048]{1,0:T(8,128)(2,1)S(1)} %collective-permute-done.2.refs_1_) | copy-start | bytes 786436
  43.7 25.8 %collective-permute-start.6 = (bf16[64,2048]{1,0:T(8,128)(2,1)S(1)}, bf16[64,2048]{1,0:T(8,128)(2,1)S(1)}, u32[]{:S(2)}, u32[]{:S(2)}) collective-permute-start(bf16[64,2048]{1,0:T(8,128)(2,1)S(1)} %collective-permute-done.2.refs_1_), channel_id=1, source_target_pairs={{0,448},{1,449},{2,450},{3,451},{4,452},{5,453},{6,454},{7,455},{8... | collective-permute-start | bytes 786440 | tf_op jit(solution)/shard_map/ppermute | solution.py:210
  56.6 18.0 %collective-permute-start.5 = (bf16[64,2048]{1,0:T(8,128)(2,1)S(1)}, bf16[64,2048]{1,0:T(8,128)(2,1)S(1)}, u32[]{:S(2)}, u32[]{:S(2)}) collective-permute-start(bf16[64,2048]{1,0:T(8,128)(2,1)S(1)} %collective-permute-done.refs_0_), channel_id=1, source_target_pairs={{0,448},{1,449},{2,450},{3,451},{4,452},{5,453},{6,454},{7,455},{8... | collective-permute-start | bytes 786440 | tf_op jit(solution)/shard_map/ppermute | solution.py:210
  65.6 13.0 %collective-permute-start.4 = (bf16[64,2048]{1,0:T(8,128)(2,1)S(1)}, bf16[64,2048]{1,0:T(8,128)(2,1)S(1)}, u32[]{:S(2)}, u32[]{:S(2)}) collective-permute-start(bf16[64,2048]{1,0:T(8,128)(2,1)S(1)} %collective-permute-done.2.refs_1_), channel_id=1, source_target_pairs={{0,64},{1,65},{2,66},{3,67},{4,68},{5,69},{6,70},{7,71},{8,72},{9,... | collective-permute-start | bytes 786440 | tf_op jit(solution)/shard_map/ppermute | solution.py:210
  67.6 35.9 %copy-start.4 = (bf16[64,2048]{1,0:T(8,128)(2,1)}, bf16[64,2048]{1,0:T(8,128)(2,1)S(1)}, u32[]{:S(2)}) copy-start(bf16[64,2048]{1,0:T(8,128)(2,1)S(1)} %collective-permute-done.3.refs_2_) | copy-start | bytes 786436
  67.6 14.3 %collective-permute-start.7 = (bf16[64,2048]{1,0:T(8,128)(2,1)S(1)}, bf16[64,2048]{1,0:T(8,128)(2,1)S(1)}, u32[]{:S(2)}, u32[]{:S(2)}) collective-permute-start(bf16[64,2048]{1,0:T(8,128)(2,1)S(1)} %collective-permute-done.3.refs_2_), channel_id=1, source_target_pairs={{0,64},{1,65},{2,66},{3,67},{4,68},{5,69},{6,70},{7,71},{8,72},{9,... | collective-permute-start | bytes 786440 | tf_op jit(solution)/shard_map/ppermute | solution.py:210
  69.5 34.0 %copy-start.5 = (bf16[64,2048]{1,0:T(8,128)(2,1)}, bf16[64,2048]{1,0:T(8,128)(2,1)S(1)}, u32[]{:S(2)}) copy-start(bf16[64,2048]{1,0:T(8,128)(2,1)S(1)} %collective-permute-done.6.refs_5_) | copy-start | bytes 786436
  69.5 14.3 %collective-permute-start.10 = (bf16[64,2048]{1,0:T(8,128)(2,1)S(1)}, bf16[64,2048]{1,0:T(8,128)(2,1)S(1)}, u32[]{:S(2)}, u32[]{:S(2)}) collective-permute-start(bf16[64,2048]{1,0:T(8,128)(2,1)S(1)} %collective-permute-done.6.refs_5_), channel_id=1, source_target_pairs={{0,448},{1,449},{2,450},{3,451},{4,452},{5,453},{6,454},{7,455},{8... | collective-permute-start | bytes 786440 | tf_op jit(solution)/shard_map/ppermute | solution.py:210
  74.7 28.9 %copy-start.6 = (bf16[64,2048]{1,0:T(8,128)(2,1)}, bf16[64,2048]{1,0:T(8,128)(2,1)S(1)}, u32[]{:S(2)}) copy-start(bf16[64,2048]{1,0:T(8,128)(2,1)S(1)} %collective-permute-done.5.refs_4_) | copy-start | bytes 786436
  74.7 14.3 %collective-permute-start.9 = (bf16[64,2048]{1,0:T(8,128)(2,1)S(1)}, bf16[64,2048]{1,0:T(8,128)(2,1)S(1)}, u32[]{:S(2)}, u32[]{:S(2)}) collective-permute-start(bf16[64,2048]{1,0:T(8,128)(2,1)S(1)} %collective-permute-done.5.refs_4_), channel_id=1, source_target_pairs={{0,448},{1,449},{2,450},{3,451},{4,452},{5,453},{6,454},{7,455},{8... | collective-permute-start | bytes 786440 | tf_op jit(solution)/shard_map/ppermute | solution.py:210
  78.6 24.9 %copy-start.7 = (bf16[64,2048]{1,0:T(8,128)(2,1)}, bf16[64,2048]{1,0:T(8,128)(2,1)S(1)}, u32[]{:S(2)}) copy-start(bf16[64,2048]{1,0:T(8,128)(2,1)S(1)} %collective-permute-done.4.refs_3_) | copy-start | bytes 786436
  78.6 13.0 %collective-permute-start.8 = (bf16[64,2048]{1,0:T(8,128)(2,1)S(1)}, bf16[64,2048]{1,0:T(8,128)(2,1)S(1)}, u32[]{:S(2)}, u32[]{:S(2)}) collective-permute-start(bf16[64,2048]{1,0:T(8,128)(2,1)S(1)} %collective-permute-done.4.refs_3_), channel_id=1, source_target_pairs={{0,64},{1,65},{2,66},{3,67},{4,68},{5,69},{6,70},{7,71},{8,72},{9,... | collective-permute-start | bytes 786440 | tf_op jit(solution)/shard_map/ppermute | solution.py:210
  81.9 21.7 %copy-start.8 = (bf16[64,2048]{1,0:T(8,128)(2,1)}, bf16[64,2048]{1,0:T(8,128)(2,1)S(1)}, u32[]{:S(2)}) copy-start(bf16[64,2048]{1,0:T(8,128)(2,1)S(1)} %collective-permute-done.7.refs_6_) | copy-start | bytes 786436
  81.9 13.0 %collective-permute-start.11 = (bf16[64,2048]{1,0:T(8,128)(2,1)S(1)}, bf16[64,2048]{1,0:T(8,128)(2,1)S(1)}, u32[]{:S(2)}, u32[]{:S(2)}) collective-permute-start(bf16[64,2048]{1,0:T(8,128)(2,1)S(1)} %collective-permute-done.7.refs_6_), channel_id=1, source_target_pairs={{0,64},{1,65},{2,66},{3,67},{4,68},{5,69},{6,70},{7,71},{8,72},{9,... | collective-permute-start | bytes 786440 | tf_op jit(solution)/shard_map/ppermute | solution.py:210
  83.8 19.7 %copy-start.9 = (bf16[64,2048]{1,0:T(8,128)(2,1)}, bf16[64,2048]{1,0:T(8,128)(2,1)S(1)}, u32[]{:S(2)}) copy-start(bf16[64,2048]{1,0:T(8,128)(2,1)S(1)} %collective-permute-done.10.refs_9_) | copy-start | bytes 786436
  83.8 13.0 %collective-permute-start.14 = (bf16[64,2048]{1,0:T(8,128)(2,1)S(1)}, bf16[64,2048]{1,0:T(8,128)(2,1)S(1)}, u32[]{:S(2)}, u32[]{:S(2)}) collective-permute-start(bf16[64,2048]{1,0:T(8,128)(2,1)S(1)} %collective-permute-done.10.refs_9_), channel_id=1, source_target_pairs={{0,448},{1,449},{2,450},{3,451},{4,452},{5,453},{6,454},{7,455},{8... | collective-permute-start | bytes 786440 | tf_op jit(solution)/shard_map/ppermute | solution.py:210
  89.0 14.6 %copy-start.10 = (bf16[64,2048]{1,0:T(8,128)(2,1)}, bf16[64,2048]{1,0:T(8,128)(2,1)S(1)}, u32[]{:S(2)}) copy-start(bf16[64,2048]{1,0:T(8,128)(2,1)S(1)} %collective-permute-done.9.refs_8_) | copy-start | bytes 786436
  89.0 13.0 %collective-permute-start.13 = (bf16[64,2048]{1,0:T(8,128)(2,1)S(1)}, bf16[64,2048]{1,0:T(8,128)(2,1)S(1)}, u32[]{:S(2)}, u32[]{:S(2)}) collective-permute-start(bf16[64,2048]{1,0:T(8,128)(2,1)S(1)} %collective-permute-done.9.refs_8_), channel_id=1, source_target_pairs={{0,448},{1,449},{2,450},{3,451},{4,452},{5,453},{6,454},{7,455},{8... | collective-permute-start | bytes 786440 | tf_op jit(solution)/shard_map/ppermute | solution.py:210
  91.6 11.9 %copy-start.11 = (bf16[64,2048]{1,0:T(8,128)(2,1)}, bf16[64,2048]{1,0:T(8,128)(2,1)S(1)}, u32[]{:S(2)}) copy-start(bf16[64,2048]{1,0:T(8,128)(2,1)S(1)} %collective-permute-done.8.refs_7_) | copy-start | bytes 786436
  91.7 11.9 %collective-permute-start.12 = (bf16[64,2048]{1,0:T(8,128)(2,1)S(1)}, bf16[64,2048]{1,0:T(8,128)(2,1)S(1)}, u32[]{:S(2)}, u32[]{:S(2)}) collective-permute-start(bf16[64,2048]{1,0:T(8,128)(2,1)S(1)} %collective-permute-done.8.refs_7_), channel_id=1, source_target_pairs={{0,64},{1,65},{2,66},{3,67},{4,68},{5,69},{6,70},{7,71},{8,72},{9,... | collective-permute-start | bytes 786440 | tf_op jit(solution)/shard_map/ppermute | solution.py:210
  94.9 8.7 %copy-start.12 = (bf16[64,2048]{1,0:T(8,128)(2,1)}, bf16[64,2048]{1,0:T(8,128)(2,1)S(1)}, u32[]{:S(2)}) copy-start(bf16[64,2048]{1,0:T(8,128)(2,1)S(1)} %collective-permute-done.11.refs_10_) | copy-start | bytes 786436
  94.9 12.8 %collective-permute-start.15 = (bf16[64,2048]{1,0:T(8,128)(2,1)S(1)}, bf16[64,2048]{1,0:T(8,128)(2,1)S(1)}, u32[]{:S(2)}, u32[]{:S(2)}) collective-permute-start(bf16[64,2048]{1,0:T(8,128)(2,1)S(1)} %collective-permute-done.11.refs_10_), channel_id=1, source_target_pairs={{0,64},{1,65},{2,66},{3,67},{4,68},{5,69},{6,70},{7,71},{8,72},{9,... | collective-permute-start | bytes 786440 | tf_op jit(solution)/shard_map/ppermute | solution.py:210
  96.8 6.8 %copy-start.13 = (bf16[64,2048]{1,0:T(8,128)(2,1)}, bf16[64,2048]{1,0:T(8,128)(2,1)S(1)}, u32[]{:S(2)}) copy-start(bf16[64,2048]{1,0:T(8,128)(2,1)S(1)} %collective-permute-done.14.refs_13_) | copy-start | bytes 786436
  96.9 10.9 %collective-permute-start.16 = (bf16[64,2048]{1,0:T(8,128)(2,1)S(1)}, bf16[64,2048]{1,0:T(8,128)(2,1)S(1)}, u32[]{:S(2)}, u32[]{:S(2)}) collective-permute-start(bf16[64,2048]{1,0:T(8,128)(2,1)S(1)} %collective-permute-done.14.refs_13_), channel_id=1, source_target_pairs={{0,448},{1,449},{2,450},{3,451},{4,452},{5,453},{6,454},{7,455},{8... | collective-permute-start | bytes 786440 | tf_op jit(solution)/shard_map/ppermute | solution.py:210
  102.0 1.6 %copy-start.14 = (bf16[64,2048]{1,0:T(8,128)(2,1)}, bf16[64,2048]{1,0:T(8,128)(2,1)S(1)}, u32[]{:S(2)}) copy-start(bf16[64,2048]{1,0:T(8,128)(2,1)S(1)} %collective-permute-done.13.refs_12_) | copy-start | bytes 786436
  103.6 0.7 copy-start.15
  107.7 0.7 copy-start
  107.8 0.8 copy-start.1
  114.9 13.3 %collective-permute-start.17 = (bf16[512,512]{1,0:T(8,128)(2,1)}, bf16[512,512]{1,0:T(8,128)(2,1)S(1)}, u32[]{:S(2)}, u32[]{:S(2)}) collective-permute-start(bf16[512,512]{1,0:T(8,128)(2,1)} %shard_map.30), channel_id=1, source_target_pairs={{0,1},{1,0},{2,3},{3,2},{4,5},{5,4},{6,7},{7,6},{8,9},{9,8},{10,11... | collective-permute-start | bytes 1572872 | tf_op jit(solution)/shard_map/ppermute | solution.py:210
Sparse Core Ops, SparseCore 0:
  23.9 67.5 all-gather.1

commit v8 on v7

--- a/solution.py
+++ b/solution.py
@@ -45,8 +45,8 @@
     return pairs(target)
 
 
-def shift_y(step):
-    return pairs(lambda y, xl, z, a, xh: (y + step, xl, z, a, xh))
+def turn(step):
+    return pairs(lambda y, xl, z, a, xh: (y + (-step if a else step), xl, z, a, xh))
 
 
 def swap_lag():
@@ -62,15 +62,16 @@
 
 
 def place(d):
-    o = (lax.axis_index("y") - d - lax.axis_index("z")) & (N - 1)
+    y, z, a = (lax.axis_index(name) for name in ("y", "z", "a"))
+    o = (y - d * (1 - 2 * a) - z) & (N - 1)
     j = jnp.where(o < 4, 2 * o, (17 - 2 * o) & (N - 1))
     return pl.multiple_of(j * SUB, SUB)
 
 
 def order_kernel(steps, *refs):
-    sources = refs[: 2 * len(steps)]
-    cols, norm, held, sums, sem = refs[2 * len(steps) :]
-    depth = held.shape[2]
+    count = len(steps)
+    sources = refs[:count]
+    cols, norm, held, sums, sem = refs[count:]
     loads = [
         pltpu.make_async_copy(source, held.at[i], sem.at[0, i])
         for i, source in enumerate(sources)
@@ -78,42 +79,38 @@
     for load in loads:
         load.start()
     stores = []
-    for n, d in enumerate(steps):
+    for i, d in enumerate(steps):
         to = pl.ds(place(d), SUB)
-        for i in (2 * n, 2 * n + 1):
-            loads[i].wait()
-            deep = pl.ds((i % 2) * depth, depth)
-            store = pltpu.make_async_copy(held.at[i], cols.at[to, deep], sem.at[1, i])
-            store.start()
-            stores.append(store)
-        sums[n] = square_sums(held[2 * n]) + square_sums(held[2 * n + 1])
-        store = pltpu.make_async_copy(sums.at[n], norm.at[to, :], sem.at[2, n])
-        store.start()
-        stores.append(store)
+        loads[i].wait()
+        stores.append(pltpu.make_async_copy(held.at[i], cols.at[to, :], sem.at[1, i]))
+        stores[-1].start()
+        sums[i] = square_sums(held[i])
+        stores.append(pltpu.make_async_copy(sums.at[i], norm.at[to, :], sem.at[2, i]))
+        stores[-1].start()
     for store in stores:
         store.wait()
 
 
 def in_order(steps, sources):
-    depth = sources[0].shape[1]
+    samples = sources[0].shape[1]
     count = len(sources)
     return pl.pallas_call(
         functools.partial(order_kernel, steps),
         out_shape=(
-            jax.ShapeDtypeStruct((HALF, 2 * depth), jnp.bfloat16),
+            jax.ShapeDtypeStruct((HALF, samples), jnp.bfloat16),
             jax.ShapeDtypeStruct((HALF, 128), jnp.float32),
         ),
         in_specs=[pl.BlockSpec(memory_space=pl.ANY)] * count,
         out_specs=[pl.BlockSpec(memory_space=pl.ANY)] * 2,
         scratch_shapes=[
-            pltpu.VMEM((count, SUB, depth), jnp.bfloat16),
-            pltpu.VMEM((len(steps), SUB, 128), jnp.float32),
+            pltpu.VMEM((count, SUB, samples), jnp.bfloat16),
+            pltpu.VMEM((count, SUB, 128), jnp.float32),
             pltpu.SemaphoreType.DMA((3, count)),
         ],
         compiler_params=pltpu.CompilerParams(vmem_limit_bytes=56 * MIB),
         cost_estimate=pl.CostEstimate(
-            flops=2 * count * SUB * depth,
-            bytes_accessed=count * MIB // 2,
+            flops=2 * count * SUB * samples,
+            bytes_accessed=count * MIB,
             transcendentals=0,
         ),
     )(*sources)
@@ -140,15 +137,18 @@
         )
         for copy in copies[-1]:
             copy.start()
-    final = pl.ds(place(N // 2), SUB)
+    part = SUB // 2
+    final = place(N // 2)
+    final = [pl.ds(pl.multiple_of(final + i * part, part), part) for i in range(2)]
     col_norm[...] = norm_ref[...]
-    col_norm[final, :] = square_sums(last[0]) + square_sums(last[1])
+    for to, source in zip(final, last):
+        col_norm[to, :] = square_sums(source)
     for k in range(blocks):
         for copy in copies[k]:
             copy.wait()
-        source, start = divmod(k * DEPTH, samples // 2)
-        cols[k, final, :] = last[source][:, start : start + DEPTH]
-        part = lax.dot_general(
+        for to, source in zip(final, last):
+            cols[k, to, :] = source[:, k * DEPTH : (k + 1) * DEPTH]
+        product = lax.dot_general(
             rows[k],
             cols[k],
             (((1,), (1,)), ((), ())),
@@ -156,10 +156,10 @@
         )
         norm = square_sums(rows[k])
         if k == 0:
-            inner[...] = part
+            inner[...] = product
             row_norm[...] = norm
         else:
-            inner[...] += part
+            inner[...] += product
             row_norm[...] += norm
     scale = live_ref[2 * y + xl, 2 * z + a].astype(jnp.float32)
     down = jnp.sum(row_norm[...], axis=1, keepdims=True)
@@ -220,15 +220,15 @@
     )
     rows = lax.all_gather(rows, ("z", "a"), axis=0, tiled=True)
 
-    steps, sources = [0], [early, late]
-    up, down = [early, late], [early, late]
+    first = second = jnp.concatenate([early, late], axis=1)
+    steps, sources = [0], [first]
     for step in range(1, N // 2):
-        up = [send(part, shift_y(1)) for part in up]
-        down = [send(part, shift_y(-1)) for part in down]
+        first, second = send(first, turn(1)), send(second, turn(-1))
         steps += [step, -step]
-        sources += up + down
+        sources += [first, second]
     cols, col_norm = in_order(steps, sources)
-    last = [send(up[0], shift_y(1)), send(down[1], shift_y(-1))]
+    part = SUB // 2
+    last = [send(first[:part], turn(1)), send(second[part:], turn(-1))]
 
     given = send(gram_tile(False, pair_live, rows, cols, col_norm, last), swap_lag())
     kept = gram_tile(True, pair_live, rows, cols, col_norm, last)

time: 137 us -> 150 us (1.095)
  the two profiles are of different devices: /device:TPU:192 before, /device:TPU:30 now
where the time goes in v8:
time: 150 us
  waiting for transfers between devices  64.3 us (43%)
  starting transfers between devices  52 us (35%)
  Pallas kernels  16.1 us (11%)
  between operations  13.7 us (9%)
  other arithmetic  1.98 us (1%)
  local copies, waits for them, and re-layouts  1.69 us (1%)
    ppermute x12, waiting for transfers between devices, send(): return lax.ppermute(value, AX, to)  64.3 us
    ppermute x12, starting transfers between devices, send(): return lax.ppermute(value, AX, to)  52 us
    pallas_call x2, Pallas kernels, gram_tile(): pl.pallas_call(functools.partial(gram_kernel, keep), out_shape=jax.ShapeD...  12.9 us
    pallas_call x1, Pallas kernels, in_order(): pl.pallas_call(functools.partial(order_kernel, steps), out_shape=(jax.Sha...  3.16 us
  transfers between devices with their start and end apart: 13, of which 8 were waited for; matrix products, arithmetic and copies ran while one was open for 0% of the time, Pallas kernels for 6%

profile of v8, /device:TPU:30, one launch (start us, length us, event | category | flops | bytes accessed | tf_op | source)
XLA Modules:
  0.0 149.8 jit_solution(17663047581078660420)
XLA Ops:
  6.5 0.0 all-gather.2.cloned.1.call-start
  6.5 7.6 %collective-permute-start = (bf16[64,2048]{1,0:T(8,128)(2,1)}, bf16[64,2048]{1,0:T(8,128)(2,1)S(1)}, u32[]{:S(2)}, u32[]{:S(2)}) collective-permute-start(bf16[64,2048]{1,0:T(8,128)(2,1)} %param.2), channel_id=1, source_target_pairs={{0,0},{1,32},{2,256},{3,288},{4,64},{5,96},{6,448},{7,480},{8,128}... | collective-permute-start | bytes 786440 | tf_op jit(solution)/shard_map/ppermute | solution.py:210
  14.1 4.6 %collective-permute-start.1 = (bf16[64,2048]{1,0:T(8,128)(2,1)}, bf16[64,2048]{1,0:T(8,128)(2,1)S(1)}, u32[]{:S(2)}, u32[]{:S(2)}) collective-permute-start(bf16[64,2048]{1,0:T(8,128)(2,1)} %param.2), channel_id=1, source_target_pairs={{0,1},{1,0},{2,3},{3,2},{4,5},{5,4},{6,7},{7,6},{8,9},{9,8},{10,11... | collective-permute-start | bytes 786440 | tf_op jit(solution)/shard_map/ppermute | solution.py:210
  18.8 3.9 %collective-permute-done = bf16[64,2048]{1,0:T(8,128)(2,1)S(1)} collective-permute-done((bf16[64,2048]{1,0:T(8,128)(2,1)}, bf16[64,2048]{1,0:T(8,128)(2,1)S(1)}, u32[]{:S(2)}, u32[]{:S(2)}) %collective-permute-start) | collective-permute-done | bytes 262176 | tf_op jit(solution)/shard_map/ppermute | solution.py:210
  22.7 7.3 %collective-permute-done.1 = bf16[64,2048]{1,0:T(8,128)(2,1)S(1)} collective-permute-done((bf16[64,2048]{1,0:T(8,128)(2,1)}, bf16[64,2048]{1,0:T(8,128)(2,1)S(1)}, u32[]{:S(2)}, u32[]{:S(2)}) %collective-permute-start.1) | collective-permute-done | bytes 262176 | tf_op jit(solution)/shard_map/ppermute | solution.py:210
  29.9 2.0 %maximum_select_fusion = bf16[64,4096]{1,0:T(8,128)(2,1)} fusion(bf16[64,2048]{1,0:T(8,128)(2,1)S(1)} %collective-permute-done.1, bf16[64,2048]{1,0:T(8,128)(2,1)} %param.2, pred[]{:T(512)S(6)} %eq.3), kind=kLoop, calls=%fused_computation | loop fusion | flops 2359296 | bytes 1048577 | tf_op jit(solution)/shard_map/jit(_where)/select_n | solution.py:216
  31.9 0.0 all-gather.2.cloned.1.call-update
  31.9 3.6 %collective-permute-start.2 = (bf16[64,2048]{1,0:T(8,128)(2,1)}, bf16[64,2048]{1,0:T(8,128)(2,1)S(1)}, u32[]{:S(2)}, u32[]{:S(2)}) collective-permute-start(bf16[64,2048]{1,0:T(8,128)(2,1)} %param.2), channel_id=1, source_target_pairs={{0,32},{1,0},{2,288},{3,256},{4,96},{5,64},{6,480},{7,448},{8,160}... | collective-permute-start | bytes 786440 | tf_op jit(solution)/shard_map/ppermute | solution.py:210
  35.6 15.5 %collective-permute-done.2 = bf16[64,2048]{1,0:T(8,128)(2,1)S(1)} collective-permute-done((bf16[64,2048]{1,0:T(8,128)(2,1)}, bf16[64,2048]{1,0:T(8,128)(2,1)S(1)}, u32[]{:S(2)}, u32[]{:S(2)}) %collective-permute-start.2) | collective-permute-done | bytes 262176 | tf_op jit(solution)/shard_map/ppermute | solution.py:210
  51.1 0.0 copy-start.2
  51.1 1.9 %collective-permute-start.4 = (bf16[64,4096]{1,0:T(8,128)(2,1)S(1)}, bf16[64,4096]{1,0:T(8,128)(2,1)S(1)}, u32[]{:S(2)}, u32[]{:S(2)}) collective-permute-start(bf16[64,4096]{1,0:T(8,128)(2,1)S(1)} %constant_dynamic-update-slice_fusion.refs_0_), channel_id=1, source_target_pairs={{0,448},{1,449},{2,66},{3,67},{4,452},{5,453},{6,70},{7,71},{8,456... | collective-permute-start | bytes 1572872 | tf_op jit(solution)/shard_map/ppermute | solution.py:210
  53.1 9.4 %collective-permute-start.3 = (bf16[64,4096]{1,0:T(8,128)(2,1)S(1)}, bf16[64,4096]{1,0:T(8,128)(2,1)S(1)}, u32[]{:S(2)}, u32[]{:S(2)}) collective-permute-start(bf16[64,4096]{1,0:T(8,128)(2,1)S(1)} %constant_dynamic-update-slice_fusion.refs_0_), channel_id=1, source_target_pairs={{0,64},{1,65},{2,450},{3,451},{4,68},{5,69},{6,454},{7,455},{8,72}... | collective-permute-start | bytes 1572872 | tf_op jit(solution)/shard_map/ppermute | solution.py:210
  62.5 7.5 %collective-permute-done.4.refs_2_ = bf16[64,4096]{1,0:T(8,128)(2,1)S(1)} collective-permute-done((bf16[64,4096]{1,0:T(8,128)(2,1)S(1)}, bf16[64,4096]{1,0:T(8,128)(2,1)S(1)}, u32[]{:S(2)}, u32[]{:S(2)}) %collective-permute-start.4) | collective-permute-done | bytes 524320 | tf_op jit(solution)/shard_map/ppermute | solution.py:210
  70.0 0.0 copy-start.5
  70.0 1.9 %collective-permute-start.6 = (bf16[64,4096]{1,0:T(8,128)(2,1)S(1)}, bf16[64,4096]{1,0:T(8,128)(2,1)S(1)}, u32[]{:S(2)}, u32[]{:S(2)}) collective-permute-start(bf16[64,4096]{1,0:T(8,128)(2,1)S(1)} %collective-permute-done.4.refs_2_), channel_id=1, source_target_pairs={{0,448},{1,449},{2,66},{3,67},{4,452},{5,453},{6,70},{7,71},{8,456... | collective-permute-start | bytes 1572872 | tf_op jit(solution)/shard_map/ppermute | solution.py:210
  71.9 0.0 collective-permute-done.3.refs_1_
  71.9 0.0 copy-start.6
  71.9 6.9 %collective-permute-start.5 = (bf16[64,4096]{1,0:T(8,128)(2,1)S(1)}, bf16[64,4096]{1,0:T(8,128)(2,1)S(1)}, u32[]{:S(2)}, u32[]{:S(2)}) collective-permute-start(bf16[64,4096]{1,0:T(8,128)(2,1)S(1)} %collective-permute-done.3.refs_1_), channel_id=1, source_target_pairs={{0,64},{1,65},{2,450},{3,451},{4,68},{5,69},{6,454},{7,455},{8,72}... | collective-permute-start | bytes 1572872 | tf_op jit(solution)/shard_map/ppermute | solution.py:210
  78.8 10.1 %collective-permute-done.6.refs_4_ = bf16[64,4096]{1,0:T(8,128)(2,1)S(1)} collective-permute-done((bf16[64,4096]{1,0:T(8,128)(2,1)S(1)}, bf16[64,4096]{1,0:T(8,128)(2,1)S(1)}, u32[]{:S(2)}, u32[]{:S(2)}) %collective-permute-start.6) | collective-permute-done | bytes 524320 | tf_op jit(solution)/shard_map/ppermute | solution.py:210
  88.9 0.0 copy-start.7
  88.9 1.9 %collective-permute-start.8 = (bf16[64,4096]{1,0:T(8,128)(2,1)S(1)}, bf16[64,4096]{1,0:T(8,128)(2,1)S(1)}, u32[]{:S(2)}, u32[]{:S(2)}) collective-permute-start(bf16[64,4096]{1,0:T(8,128)(2,1)S(1)} %collective-permute-done.6.refs_4_), channel_id=1, source_target_pairs={{0,448},{1,449},{2,66},{3,67},{4,452},{5,453},{6,70},{7,71},{8,456... | collective-permute-start | bytes 1572872 | tf_op jit(solution)/shard_map/ppermute | solution.py:210
  90.8 0.0 collective-permute-done.5.refs_3_
  90.8 0.0 copy-start.8
  90.8 5.1 %collective-permute-start.7 = (bf16[64,4096]{1,0:T(8,128)(2,1)S(1)}, bf16[64,4096]{1,0:T(8,128)(2,1)S(1)}, u32[]{:S(2)}, u32[]{:S(2)}) collective-permute-start(bf16[64,4096]{1,0:T(8,128)(2,1)S(1)} %collective-permute-done.5.refs_3_), channel_id=1, source_target_pairs={{0,64},{1,65},{2,450},{3,451},{4,68},{5,69},{6,454},{7,455},{8,72}... | collective-permute-start | bytes 1572872 | tf_op jit(solution)/shard_map/ppermute | solution.py:210
  96.0 10.8 %collective-permute-done.8.refs_6_ = bf16[64,4096]{1,0:T(8,128)(2,1)S(1)} collective-permute-done((bf16[64,4096]{1,0:T(8,128)(2,1)S(1)}, bf16[64,4096]{1,0:T(8,128)(2,1)S(1)}, u32[]{:S(2)}, u32[]{:S(2)}) %collective-permute-start.8) | collective-permute-done | bytes 524320 | tf_op jit(solution)/shard_map/ppermute | solution.py:210
  106.8 0.0 copy-start
  106.8 1.9 %collective-permute-start.10 = (bf16[32,4096]{1,0:T(8,128)(2,1)S(1)}, bf16[32,4096]{1,0:T(8,128)(2,1)S(1)}, u32[]{:S(2)}, u32[]{:S(2)}) collective-permute-start(bf16[32,4096]{1,0:T(8,128)(2,1)S(1)} %slice.9), channel_id=1, source_target_pairs={{0,448},{1,449},{2,66},{3,67},{4,452},{5,453},{6,70},{7,71},{8,456... | collective-permute-start | bytes 786440 | tf_op jit(solution)/shard_map/ppermute | solution.py:210
  108.7 0.0 collective-permute-done.7.refs_5_
  108.8 0.0 copy-start.1
  108.8 5.1 %collective-permute-start.9 = (bf16[32,4096]{1,0:T(8,128)(2,1)S(1)}, bf16[32,4096]{1,0:T(8,128)(2,1)S(1)}, u32[]{:S(2)}, u32[]{:S(2)}) collective-permute-start(bf16[32,4096]{1,0:T(8,128)(2,1)S(1)} %slice.8), channel_id=1, source_target_pairs={{0,64},{1,65},{2,450},{3,451},{4,68},{5,69},{6,454},{7,455},{8,72}... | collective-permute-start | bytes 786440 | tf_op jit(solution)/shard_map/ppermute | solution.py:210
  113.9 0.0 copy-done.2
  113.9 0.0 copy-done.5
  114.0 0.0 copy-done.6
  114.0 0.0 copy-done.7
  114.0 0.0 copy-done.8
  114.0 0.0 copy-done
  114.0 0.0 copy-done.1
  114.0 3.2 %shard_map.28 = (bf16[512,4096]{1,0:T(8,128)(2,1)}, f32[512,128]{1,0:T(8,128)}) custom-call(bf16[64,4096]{1,0:T(8,128)(2,1)} %copy-done.2, bf16[64,4096]{1,0:T(8,128)(2,1)} %copy-done.6, bf16[64,4096]{1,0:T(8,128)(2,1)} %copy-done.5, bf16[64,4096]{1,0:T(8,128)(2,1)} %copy-done.8, bf16[64,4096]{1,0:T(8,128)(2,1)} %copy-done.7, bf16[64,4096]{1,0:T(8,128)(2,1)} %copy-done.1, ...), custom_call_target="tpu_custom_call" | custom-call | flops 3670016 | bytes 7340032 | tf_op jit(solution)/shard_map/pallas_call | solution.py:97
  117.2 1.1 collective-permute-done.10.refs_1_
  118.2 0.0 copy-start.3
  118.2 0.0 collective-permute-done.9.refs_0_
  118.3 0.0 copy-start.4
  118.3 0.0 all-gather.2.cloned.1.call-done.rows_hbm
  118.3 0.7 copy-done.3
  118.9 0.1 copy-done.4
  119.0 6.4 %shard_map.30 = bf16[512,512]{1,0:T(8,128)(2,1)} custom-call(s32[16,16]{1,0:T(8,128)} %live_ref.3, bf16[1024,4096]{1,0:T(8,128)(2,1)} %all-gather.2.cloned.1.call-done.rows_hbm, bf16[512,4096]{1,0:T(8,128)(2,1)} %get-tuple-element.11.cols_hbm, f32[512,128]{1,0:T(8,128)} %get-tuple-element.12.norm_ref, bf16[32,4096]{1,0:T(8,128)(2,1)} %copy-done.4, ...), custom_call_target="tpu_custom_call" | custom-call | flops 2147483648 | bytes 9437184 | tf_op jit(solution)/shard_map/pallas_call | solution.py:177
  125.4 1.9 %collective-permute-start.11 = (bf16[512,512]{1,0:T(8,128)(2,1)}, bf16[512,512]{1,0:T(8,128)(2,1)S(1)}, u32[]{:S(2)}, u32[]{:S(2)}) collective-permute-start(bf16[512,512]{1,0:T(8,128)(2,1)} %shard_map.30), channel_id=1, source_target_pairs={{0,1},{1,0},{2,3},{3,2},{4,5},{5,4},{6,7},{7,6},{8,9},{9,8},{10,11... | collective-permute-start | bytes 1572872 | tf_op jit(solution)/shard_map/ppermute | solution.py:210
  127.4 6.5 %shard_map.29 = bf16[512,1024]{1,0:T(8,128)(2,1)} custom-call(s32[16,16]{1,0:T(8,128)} %live_ref.3, bf16[1024,4096]{1,0:T(8,128)(2,1)} %all-gather.2.cloned.1.call-done.rows_hbm, bf16[512,4096]{1,0:T(8,128)(2,1)} %get-tuple-element.11.cols_hbm, f32[512,128]{1,0:T(8,128)} %get-tuple-element.12.norm_ref, bf16[32,4096]{1,0:T(8,128)(2,1)} %copy-done.4, ...), custom_call_target="tpu_custom_call" | custom-call | flops 2147483648 | bytes 9437184 | tf_op jit(solution)/shard_map/pallas_call | solution.py:177
  133.9 8.2 %collective-permute-done.11 = bf16[512,512]{1,0:T(8,128)(2,1)S(1)} collective-permute-done((bf16[512,512]{1,0:T(8,128)(2,1)}, bf16[512,512]{1,0:T(8,128)(2,1)S(1)}, u32[]{:S(2)}, u32[]{:S(2)}) %collective-permute-start.11) | collective-permute-done | bytes 524320 | tf_op jit(solution)/shard_map/ppermute | solution.py:210
  142.1 0.8 constant_dynamic-update-slice_fusion.2
  (4 shorter events, 0.1 us)
Async XLA Ops:
  6.5 111.7 %all-gather.2.cloned.1.call-start = ((), (), s32[]{:S(2)}) async-start(), calls=%async_computation | async-start | bytes 8912896 | tf_op jit(solution)/shard_map/all_gather | solution.py:221
  6.5 16.1 %collective-permute-start = (bf16[64,2048]{1,0:T(8,128)(2,1)}, bf16[64,2048]{1,0:T(8,128)(2,1)S(1)}, u32[]{:S(2)}, u32[]{:S(2)}) collective-permute-start(bf16[64,2048]{1,0:T(8,128)(2,1)} %param.2), channel_id=1, source_target_pairs={{0,0},{1,32},{2,256},{3,288},{4,64},{5,96},{6,448},{7,480},{8,128}... | collective-permute-start | bytes 786440 | tf_op jit(solution)/shard_map/ppermute | solution.py:210
  14.1 15.8 %collective-permute-start.1 = (bf16[64,2048]{1,0:T(8,128)(2,1)}, bf16[64,2048]{1,0:T(8,128)(2,1)S(1)}, u32[]{:S(2)}, u32[]{:S(2)}) collective-permute-start(bf16[64,2048]{1,0:T(8,128)(2,1)} %param.2), channel_id=1, source_target_pairs={{0,1},{1,0},{2,3},{3,2},{4,5},{5,4},{6,7},{7,6},{8,9},{9,8},{10,11... | collective-permute-start | bytes 786440 | tf_op jit(solution)/shard_map/ppermute | solution.py:210
  31.9 19.2 %collective-permute-start.2 = (bf16[64,2048]{1,0:T(8,128)(2,1)}, bf16[64,2048]{1,0:T(8,128)(2,1)S(1)}, u32[]{:S(2)}, u32[]{:S(2)}) collective-permute-start(bf16[64,2048]{1,0:T(8,128)(2,1)} %param.2), channel_id=1, source_target_pairs={{0,32},{1,0},{2,288},{3,256},{4,96},{5,64},{6,480},{7,448},{8,160}... | collective-permute-start | bytes 786440 | tf_op jit(solution)/shard_map/ppermute | solution.py:210
  51.1 62.8 %copy-start.2 = (bf16[64,4096]{1,0:T(8,128)(2,1)}, bf16[64,4096]{1,0:T(8,128)(2,1)S(1)}, u32[]{:S(2)}) copy-start(bf16[64,4096]{1,0:T(8,128)(2,1)S(1)} %constant_dynamic-update-slice_fusion.refs_0_) | copy-start | bytes 1572868
  51.1 18.8 %collective-permute-start.4 = (bf16[64,4096]{1,0:T(8,128)(2,1)S(1)}, bf16[64,4096]{1,0:T(8,128)(2,1)S(1)}, u32[]{:S(2)}, u32[]{:S(2)}) collective-permute-start(bf16[64,4096]{1,0:T(8,128)(2,1)S(1)} %constant_dynamic-update-slice_fusion.refs_0_), channel_id=1, source_target_pairs={{0,448},{1,449},{2,66},{3,67},{4,452},{5,453},{6,70},{7,71},{8,456... | collective-permute-start | bytes 1572872 | tf_op jit(solution)/shard_map/ppermute | solution.py:210
  53.1 18.8 %collective-permute-start.3 = (bf16[64,4096]{1,0:T(8,128)(2,1)S(1)}, bf16[64,4096]{1,0:T(8,128)(2,1)S(1)}, u32[]{:S(2)}, u32[]{:S(2)}) collective-permute-start(bf16[64,4096]{1,0:T(8,128)(2,1)S(1)} %constant_dynamic-update-slice_fusion.refs_0_), channel_id=1, source_target_pairs={{0,64},{1,65},{2,450},{3,451},{4,68},{5,69},{6,454},{7,455},{8,72}... | collective-permute-start | bytes 1572872 | tf_op jit(solution)/shard_map/ppermute | solution.py:210
  70.0 44.0 %copy-start.5 = (bf16[64,4096]{1,0:T(8,128)(2,1)}, bf16[64,4096]{1,0:T(8,128)(2,1)S(1)}, u32[]{:S(2)}) copy-start(bf16[64,4096]{1,0:T(8,128)(2,1)S(1)} %collective-permute-done.4.refs_2_) | copy-start | bytes 1572868
  70.0 18.9 %collective-permute-start.6 = (bf16[64,4096]{1,0:T(8,128)(2,1)S(1)}, bf16[64,4096]{1,0:T(8,128)(2,1)S(1)}, u32[]{:S(2)}, u32[]{:S(2)}) collective-permute-start(bf16[64,4096]{1,0:T(8,128)(2,1)S(1)} %collective-permute-done.4.refs_2_), channel_id=1, source_target_pairs={{0,448},{1,449},{2,66},{3,67},{4,452},{5,453},{6,70},{7,71},{8,456... | collective-permute-start | bytes 1572872 | tf_op jit(solution)/shard_map/ppermute | solution.py:210
  71.9 42.0 %copy-start.6 = (bf16[64,4096]{1,0:T(8,128)(2,1)}, bf16[64,4096]{1,0:T(8,128)(2,1)S(1)}, u32[]{:S(2)}) copy-start(bf16[64,4096]{1,0:T(8,128)(2,1)S(1)} %collective-permute-done.3.refs_1_) | copy-start | bytes 1572868
  71.9 18.9 %collective-permute-start.5 = (bf16[64,4096]{1,0:T(8,128)(2,1)S(1)}, bf16[64,4096]{1,0:T(8,128)(2,1)S(1)}, u32[]{:S(2)}, u32[]{:S(2)}) collective-permute-start(bf16[64,4096]{1,0:T(8,128)(2,1)S(1)} %collective-permute-done.3.refs_1_), channel_id=1, source_target_pairs={{0,64},{1,65},{2,450},{3,451},{4,68},{5,69},{6,454},{7,455},{8,72}... | collective-permute-start | bytes 1572872 | tf_op jit(solution)/shard_map/ppermute | solution.py:210
  88.9 25.1 %copy-start.7 = (bf16[64,4096]{1,0:T(8,128)(2,1)}, bf16[64,4096]{1,0:T(8,128)(2,1)S(1)}, u32[]{:S(2)}) copy-start(bf16[64,4096]{1,0:T(8,128)(2,1)S(1)} %collective-permute-done.6.refs_4_) | copy-start | bytes 1572868
  88.9 17.9 %collective-permute-start.8 = (bf16[64,4096]{1,0:T(8,128)(2,1)S(1)}, bf16[64,4096]{1,0:T(8,128)(2,1)S(1)}, u32[]{:S(2)}, u32[]{:S(2)}) collective-permute-start(bf16[64,4096]{1,0:T(8,128)(2,1)S(1)} %collective-permute-done.6.refs_4_), channel_id=1, source_target_pairs={{0,448},{1,449},{2,66},{3,67},{4,452},{5,453},{6,70},{7,71},{8,456... | collective-permute-start | bytes 1572872 | tf_op jit(solution)/shard_map/ppermute | solution.py:210
  90.8 23.1 %copy-start.8 = (bf16[64,4096]{1,0:T(8,128)(2,1)}, bf16[64,4096]{1,0:T(8,128)(2,1)S(1)}, u32[]{:S(2)}) copy-start(bf16[64,4096]{1,0:T(8,128)(2,1)S(1)} %collective-permute-done.5.refs_3_) | copy-start | bytes 1572868
  90.8 17.9 %collective-permute-start.7 = (bf16[64,4096]{1,0:T(8,128)(2,1)S(1)}, bf16[64,4096]{1,0:T(8,128)(2,1)S(1)}, u32[]{:S(2)}, u32[]{:S(2)}) collective-permute-start(bf16[64,4096]{1,0:T(8,128)(2,1)S(1)} %collective-permute-done.5.refs_3_), channel_id=1, source_target_pairs={{0,64},{1,65},{2,450},{3,451},{4,68},{5,69},{6,454},{7,455},{8,72}... | collective-permute-start | bytes 1572872 | tf_op jit(solution)/shard_map/ppermute | solution.py:210
  106.8 7.2 %copy-start = (bf16[64,4096]{1,0:T(8,128)(2,1)}, bf16[64,4096]{1,0:T(8,128)(2,1)S(1)}, u32[]{:S(2)}) copy-start(bf16[64,4096]{1,0:T(8,128)(2,1)S(1)} %collective-permute-done.8.refs_6_) | copy-start | bytes 1572868
  106.8 11.4 %collective-permute-start.10 = (bf16[32,4096]{1,0:T(8,128)(2,1)S(1)}, bf16[32,4096]{1,0:T(8,128)(2,1)S(1)}, u32[]{:S(2)}, u32[]{:S(2)}) collective-permute-start(bf16[32,4096]{1,0:T(8,128)(2,1)S(1)} %slice.9), channel_id=1, source_target_pairs={{0,448},{1,449},{2,66},{3,67},{4,452},{5,453},{6,70},{7,71},{8,456... | collective-permute-start | bytes 786440 | tf_op jit(solution)/shard_map/ppermute | solution.py:210
  108.8 5.2 %copy-start.1 = (bf16[64,4096]{1,0:T(8,128)(2,1)}, bf16[64,4096]{1,0:T(8,128)(2,1)S(1)}, u32[]{:S(2)}) copy-start(bf16[64,4096]{1,0:T(8,128)(2,1)S(1)} %collective-permute-done.7.refs_5_) | copy-start | bytes 1572868
  108.8 9.5 %collective-permute-start.9 = (bf16[32,4096]{1,0:T(8,128)(2,1)S(1)}, bf16[32,4096]{1,0:T(8,128)(2,1)S(1)}, u32[]{:S(2)}, u32[]{:S(2)}) collective-permute-start(bf16[32,4096]{1,0:T(8,128)(2,1)S(1)} %slice.8), channel_id=1, source_target_pairs={{0,64},{1,65},{2,450},{3,451},{4,68},{5,69},{6,454},{7,455},{8,72}... | collective-permute-start | bytes 786440 | tf_op jit(solution)/shard_map/ppermute | solution.py:210
  118.2 0.7 copy-start.3
  118.3 0.8 copy-start.4
  125.4 16.6 %collective-permute-start.11 = (bf16[512,512]{1,0:T(8,128)(2,1)}, bf16[512,512]{1,0:T(8,128)(2,1)S(1)}, u32[]{:S(2)}, u32[]{:S(2)}) collective-permute-start(bf16[512,512]{1,0:T(8,128)(2,1)} %shard_map.30), channel_id=1, source_target_pairs={{0,1},{1,0},{2,3},{3,2},{4,5},{5,4},{6,7},{7,6},{8,9},{9,8},{10,11... | collective-permute-start | bytes 1572872 | tf_op jit(solution)/shard_map/ppermute | solution.py:210
Sparse Core Ops, SparseCore 0:
  32.1 62.0 all-gather.1

commit v9 on v7

v9 whole, which is shorter than its diff:
```python
import functools

import jax
import jax.numpy as jnp
from jax import lax
from jax.experimental import pallas as pl
from jax.experimental.pallas import tpu as pltpu
from jax.sharding import Mesh
from jax.sharding import PartitionSpec as P

AX = ("y", "xl", "z", "a", "xh")
N = 8
SUB = 64
HALF = N * SUB
DEPTH = 1024
SHIFT = ((0, 4), (1, -1), (2, -2), (3, -3))
MIB = 1024 * 1024


def index(y, xl, z, a, xh):
    return (((y % N * 2 + xl) * N + z % N) * 2 + a) * 2 + xh


def pairs(target):
    every = [
        (y, xl, z, a, xh)
        for y in range(N)
        for xl in range(2)
        for z in range(N)
        for a in range(2)
        for xh in range(2)
    ]
    return [(index(*d), index(*target(*d))) for d in every]


def col_half(z, xh):
    return xh ^ (z >> 1 & 1)


def col_pairs(stage):
    def target(y, xl, z, a, half):
        part = col_half(y, z // 4)
        return y + SHIFT[z % 4][a], half ^ part ^ stage, y, xl, part

    return pairs(target)


def shift_y(step):
    return pairs(lambda y, xl, z, a, xh: (y + step, xl, z, a, xh))


def swap_lag():
    return pairs(lambda y, xl, z, a, xh: (y, xl, z, a, 1 - xh))


def square_sums(x):
    total = jnp.zeros((x.shape[0], 128), jnp.float32)
    for c in range(x.shape[1] // 128):
        part = x[:, c * 128 : (c + 1) * 128].astype(jnp.float32)
        total += part * part
    return total


def place(d):
    o = (lax.axis_index("y") - d - lax.axis_index("z")) & (N - 1)
    j = jnp.where(o < 4, 2 * o, (17 - 2 * o) & (N - 1))
    return pl.multiple_of(j * SUB, SUB)


def gram_kernel(keep, steps, live_ref, rows_hbm, *refs):
    chunks, out_ref = refs[: 2 * len(steps)], refs[2 * len(steps)]
    rows, cols, inner, row_norm, col_norm, sem = refs[2 * len(steps) + 1 :]
    y, xl, z, a, xh = (lax.axis_index(name) for name in AX)
    half = xh if keep else 1 - xh
    first = pl.multiple_of(half * HALF, HALF)
    blocks = rows.shape[0]
    samples = blocks * DEPTH
    places = [pl.ds(place(d), SUB) for d in steps]
    copies = []
    for k in range(blocks):
        copies.append(
            [
                pltpu.make_async_copy(
                    rows_hbm.at[pl.ds(first, HALF), pl.ds(k * DEPTH, DEPTH)],
                    rows.at[k],
                    sem.at[k, len(steps)],
                )
            ]
        )
        part, start = divmod(k * DEPTH, samples // 2)
        for i, to in enumerate(places):
            copies[k].append(
                pltpu.make_async_copy(
                    chunks[2 * i + part].at[:, pl.ds(start, DEPTH)],
                    cols.at[k, to, :],
                    sem.at[k, i],
                )
            )
        for copy in copies[k]:
            copy.start()
    for k in range(blocks):
        for copy in copies[k]:
            copy.wait()
        product = lax.dot_general(
            rows[k], cols[k], (((1,), (1,)), ((), ())), preferred_element_type=jnp.float32
        )
        down, across = square_sums(rows[k]), square_sums(cols[k])
        if k == 0:
            inner[...] = product
            row_norm[...] = down
            col_norm[...] = across
        else:
            inner[...] += product
            row_norm[...] += down
            col_norm[...] += across
    scale = live_ref[2 * y + xl, 2 * z + a].astype(jnp.float32)
    down = jnp.sum(row_norm[...], axis=1, keepdims=True)
    across = jnp.sum(col_norm[...].T, axis=0, keepdims=True)
    dist = down + across - 2.0 * inner[...]
    gram = jnp.exp(dist * (-2.0 / samples)) * scale
    base = pl.multiple_of(col_half(z, xh) * HALF, HALF) if keep else 0
    out_ref[:, pl.ds(base, HALF)] = gram.astype(jnp.bfloat16)


def gram_tile(keep, pair_live, rows, steps, chunks):
    samples = rows.shape[1]
    width = 2 * HALF if keep else HALF
    operand = pltpu.VMEM((samples // DEPTH, HALF, DEPTH), jnp.bfloat16)
    return pl.pallas_call(
        functools.partial(gram_kernel, keep, steps),
        out_shape=jax.ShapeDtypeStruct((HALF, width), jnp.bfloat16),
        in_specs=[pl.BlockSpec(memory_space=pltpu.SMEM)]
        + [pl.BlockSpec(memory_space=pl.ANY)] * (1 + len(chunks)),
        out_specs=pl.BlockSpec(memory_space=pltpu.VMEM),
        scratch_shapes=[
            operand,
            operand,
            pltpu.VMEM((HALF, HALF), jnp.float32),
            pltpu.VMEM((HALF, 128), jnp.float32),
            pltpu.VMEM((HALF, 128), jnp.float32),
            pltpu.SemaphoreType.DMA((samples // DEPTH, N + 1)),
        ],
        compiler_params=pltpu.CompilerParams(vmem_limit_bytes=56 * MIB),
        cost_estimate=pl.CostEstimate(
            flops=2 * HALF * HALF * samples,
            bytes_accessed=9 * MIB,
            transcendentals=HALF * HALF,
        ),
    )(pair_live, rows, *chunks)


def on_device(trajectories, pair_live):
    xl, z, xh = (lax.axis_index(name) for name in ("xl", "z", "xh"))

    def send(value, to):
        return lax.ppermute(value, AX, to)

    other = send(trajectories, swap_lag())
    early = send(trajectories, col_pairs(0))
    late = send(trajectories, col_pairs(1))
    early, other = lax.optimization_barrier((early, other))
    rows = jnp.where(
        xl == 0,
        jnp.concatenate([trajectories, other], axis=1),
        jnp.concatenate([other, trajectories], axis=1),
    )
    rows = lax.all_gather(rows, ("z", "a"), axis=0, tiled=True)

    steps, chunks = [0], [early, late]
    up, down = [early, late], [early, late]
    for step in range(1, N // 2):
        up = [send(part, shift_y(1)) for part in up]
        down = [send(part, shift_y(-1)) for part in down]
        steps += [step, -step]
        chunks += up + down
    steps.append(N // 2)
    chunks += [send(up[0], shift_y(1)), send(down[1], shift_y(-1))]

    given = send(gram_tile(False, pair_live, rows, steps, chunks), swap_lag())
    kept = gram_tile(True, pair_live, rows, steps, chunks)
    return lax.dynamic_update_slice(kept, given, (0, (1 - col_half(z, xh)) * HALF))


def solution(mesh):
    fine = Mesh(mesh.devices.reshape(N, 2, N, 2, 2), AX)
    return jax.shard_map(
        on_device,
        mesh=fine,
        in_specs=(P(("y", "xl", "z", "a"), "xh"), P()),
        out_specs=P(("y", "xl", "xh"), ("z", "a")),
        check_vma=False,
    )
```

time: 137 us -> 137 us (level)
  waiting for transfers between devices: 15.6 us -> 28.3 us
  starting transfers between devices: 85.7 us -> 77.4 us
  Pallas kernels: 16.3 us -> 13.1 us
    ppermute x18, waiting for transfers between devices: 15.6 us -> 28.3 us  [send(): return lax.ppermute(value, AX, to)]
    ppermute x18, starting transfers between devices: 85.7 us -> 77.4 us  [send(): return lax.ppermute(value, AX, to)]
    pallas_call x3 -> x2, Pallas kernels: 16.3 us -> 13.1 us  [gram_tile(): pl.pallas_call(functools.partial(gram_kernel, keep, steps), out_shape=jax...]
  transfers between devices with their start and end apart: 19 -> 19, of which waited for: 5 -> 7; matrix products, arithmetic and copies ran while one was open for 0% -> 0% of each run, Pallas kernels for 7% -> 5%
where the time goes in v9:
time: 137 us; the launch traced here: 136 us
  starting transfers between devices  77.4 us (56%)
  waiting for transfers between devices  28.3 us (21%)
  between operations  13.8 us (10%)
  Pallas kernels  13.1 us (10%)
  other arithmetic  2.04 us (1%)
  local copies, waits for them, and re-layouts  1.61 us (1%)
    ppermute x18, starting transfers between devices, send(): return lax.ppermute(value, AX, to)  77.4 us
    ppermute x18, waiting for transfers between devices, send(): return lax.ppermute(value, AX, to)  28.3 us
    pallas_call x2, Pallas kernels, gram_tile(): pl.pallas_call(functools.partial(gram_kernel, keep, steps), out_shape=jax...  13.1 us
  transfers between devices with their start and end apart: 19, of which 7 were waited for; matrix products, arithmetic and copies ran while one was open for 0% of the time, Pallas kernels for 5%

profile of v9, /device:TPU:192, one launch (start us, length us, event | category | flops | bytes accessed | tf_op | source)
XLA Modules:
  0.0 136.2 jit_solution(15252203742596698719)
XLA Ops:
  6.5 0.0 all-gather.2.cloned.1.call-start
  6.5 4.9 %collective-permute-start.1 = (bf16[64,2048]{1,0:T(8,128)(2,1)}, bf16[64,2048]{1,0:T(8,128)(2,1)S(1)}, u32[]{:S(2)}, u32[]{:S(2)}) collective-permute-start(bf16[64,2048]{1,0:T(8,128)(2,1)} %param.2), channel_id=1, source_target_pairs={{0,1},{1,0},{2,3},{3,2},{4,5},{5,4},{6,7},{7,6},{8,9},{9,8},{10,11... | collective-permute-start | bytes 786440 | tf_op jit(solution)/shard_map/ppermute | solution.py:156
  11.5 2.8 %collective-permute-start = (bf16[64,2048]{1,0:T(8,128)(2,1)}, bf16[64,2048]{1,0:T(8,128)(2,1)S(1)}, u32[]{:S(2)}, u32[]{:S(2)}) collective-permute-start(bf16[64,2048]{1,0:T(8,128)(2,1)} %param.2), channel_id=1, source_target_pairs={{0,0},{1,32},{2,256},{3,288},{4,64},{5,96},{6,448},{7,480},{8,128}... | collective-permute-start | bytes 786440 | tf_op jit(solution)/shard_map/ppermute | solution.py:156
  14.3 3.9 %collective-permute-done.1 = bf16[64,2048]{1,0:T(8,128)(2,1)S(1)} collective-permute-done((bf16[64,2048]{1,0:T(8,128)(2,1)}, bf16[64,2048]{1,0:T(8,128)(2,1)S(1)}, u32[]{:S(2)}, u32[]{:S(2)}) %collective-permute-start.1) | collective-permute-done | bytes 262176 | tf_op jit(solution)/shard_map/ppermute | solution.py:156
  18.2 8.2 %collective-permute-done.refs_0_ = bf16[64,2048]{1,0:T(8,128)(2,1)S(1)} collective-permute-done((bf16[64,2048]{1,0:T(8,128)(2,1)}, bf16[64,2048]{1,0:T(8,128)(2,1)S(1)}, u32[]{:S(2)}, u32[]{:S(2)}) %collective-permute-start) | collective-permute-done | bytes 262176 | tf_op jit(solution)/shard_map/ppermute | solution.py:156
  26.3 2.0 %maximum_select_fusion = bf16[64,4096]{1,0:T(8,128)(2,1)} fusion(bf16[64,2048]{1,0:T(8,128)(2,1)S(1)} %collective-permute-done.1, bf16[64,2048]{1,0:T(8,128)(2,1)} %param.2, pred[]{:T(512)S(6)} %eq.3), kind=kLoop, calls=%fused_computation | loop fusion | flops 2359296 | bytes 1048577 | tf_op jit(solution)/shard_map/jit(_where)/select_n | solution.py:162
  28.4 0.0 all-gather.2.cloned.1.call-update
  28.4 4.0 %collective-permute-start.2 = (bf16[64,2048]{1,0:T(8,128)(2,1)}, bf16[64,2048]{1,0:T(8,128)(2,1)S(1)}, u32[]{:S(2)}, u32[]{:S(2)}) collective-permute-start(bf16[64,2048]{1,0:T(8,128)(2,1)} %param.2), channel_id=1, source_target_pairs={{0,32},{1,0},{2,288},{3,256},{4,96},{5,64},{6,480},{7,448},{8,160}... | collective-permute-start | bytes 786440 | tf_op jit(solution)/shard_map/ppermute | solution.py:156
  32.5 6.6 %collective-permute-start.3 = (bf16[64,2048]{1,0:T(8,128)(2,1)S(1)}, bf16[64,2048]{1,0:T(8,128)(2,1)S(1)}, u32[]{:S(2)}, u32[]{:S(2)}) collective-permute-start(bf16[64,2048]{1,0:T(8,128)(2,1)S(1)} %collective-permute-done.refs_0_), channel_id=1, source_target_pairs={{0,64},{1,65},{2,66},{3,67},{4,68},{5,69},{6,70},{7,71},{8,72},{9,... | collective-permute-start | bytes 786440 | tf_op jit(solution)/shard_map/ppermute | solution.py:156
  39.1 7.4 %collective-permute-done.2.refs_1_ = bf16[64,2048]{1,0:T(8,128)(2,1)S(1)} collective-permute-done((bf16[64,2048]{1,0:T(8,128)(2,1)}, bf16[64,2048]{1,0:T(8,128)(2,1)S(1)}, u32[]{:S(2)}, u32[]{:S(2)}) %collective-permute-start.2) | collective-permute-done | bytes 262176 | tf_op jit(solution)/shard_map/ppermute | solution.py:156
  46.5 13.4 %collective-permute-start.6 = (bf16[64,2048]{1,0:T(8,128)(2,1)S(1)}, bf16[64,2048]{1,0:T(8,128)(2,1)S(1)}, u32[]{:S(2)}, u32[]{:S(2)}) collective-permute-start(bf16[64,2048]{1,0:T(8,128)(2,1)S(1)} %collective-permute-done.2.refs_1_), channel_id=1, source_target_pairs={{0,448},{1,449},{2,450},{3,451},{4,452},{5,453},{6,454},{7,455},{8... | collective-permute-start | bytes 786440 | tf_op jit(solution)/shard_map/ppermute | solution.py:156
  59.9 9.0 %collective-permute-start.5 = (bf16[64,2048]{1,0:T(8,128)(2,1)S(1)}, bf16[64,2048]{1,0:T(8,128)(2,1)S(1)}, u32[]{:S(2)}, u32[]{:S(2)}) collective-permute-start(bf16[64,2048]{1,0:T(8,128)(2,1)S(1)} %collective-permute-done.refs_0_), channel_id=1, source_target_pairs={{0,448},{1,449},{2,450},{3,451},{4,452},{5,453},{6,454},{7,455},{8... | collective-permute-start | bytes 786440 | tf_op jit(solution)/shard_map/ppermute | solution.py:156
  68.9 1.9 %collective-permute-start.4 = (bf16[64,2048]{1,0:T(8,128)(2,1)S(1)}, bf16[64,2048]{1,0:T(8,128)(2,1)S(1)}, u32[]{:S(2)}, u32[]{:S(2)}) collective-permute-start(bf16[64,2048]{1,0:T(8,128)(2,1)S(1)} %collective-permute-done.2.refs_1_), channel_id=1, source_target_pairs={{0,64},{1,65},{2,66},{3,67},{4,68},{5,69},{6,70},{7,71},{8,72},{9,... | collective-permute-start | bytes 786440 | tf_op jit(solution)/shard_map/ppermute | solution.py:156
  70.8 0.0 collective-permute-done.3.refs_2_
  70.8 0.0 copy-start.2
  70.8 1.9 %collective-permute-start.7 = (bf16[64,2048]{1,0:T(8,128)(2,1)S(1)}, bf16[64,2048]{1,0:T(8,128)(2,1)S(1)}, u32[]{:S(2)}, u32[]{:S(2)}) collective-permute-start(bf16[64,2048]{1,0:T(8,128)(2,1)S(1)} %collective-permute-done.3.refs_2_), channel_id=1, source_target_pairs={{0,64},{1,65},{2,66},{3,67},{4,68},{5,69},{6,70},{7,71},{8,72},{9,... | collective-permute-start | bytes 786440 | tf_op jit(solution)/shard_map/ppermute | solution.py:156
  72.8 0.0 collective-permute-done.6.refs_5_
  72.8 0.0 copy-start.3
  72.8 5.1 %collective-permute-start.10 = (bf16[64,2048]{1,0:T(8,128)(2,1)S(1)}, bf16[64,2048]{1,0:T(8,128)(2,1)S(1)}, u32[]{:S(2)}, u32[]{:S(2)}) collective-permute-start(bf16[64,2048]{1,0:T(8,128)(2,1)S(1)} %collective-permute-done.6.refs_5_), channel_id=1, source_target_pairs={{0,448},{1,449},{2,450},{3,451},{4,452},{5,453},{6,454},{7,455},{8... | collective-permute-start | bytes 786440 | tf_op jit(solution)/shard_map/ppermute | solution.py:156
  77.9 0.0 collective-permute-done.5.refs_4_
  77.9 0.0 copy-start.4
  78.0 3.9 %collective-permute-start.9 = (bf16[64,2048]{1,0:T(8,128)(2,1)S(1)}, bf16[64,2048]{1,0:T(8,128)(2,1)S(1)}, u32[]{:S(2)}, u32[]{:S(2)}) collective-permute-start(bf16[64,2048]{1,0:T(8,128)(2,1)S(1)} %collective-permute-done.5.refs_4_), channel_id=1, source_target_pairs={{0,448},{1,449},{2,450},{3,451},{4,452},{5,453},{6,454},{7,455},{8... | collective-permute-start | bytes 786440 | tf_op jit(solution)/shard_map/ppermute | solution.py:156
  81.9 0.0 collective-permute-done.4.refs_3_
  81.9 0.0 copy-start.5
  81.9 1.9 %collective-permute-start.8 = (bf16[64,2048]{1,0:T(8,128)(2,1)S(1)}, bf16[64,2048]{1,0:T(8,128)(2,1)S(1)}, u32[]{:S(2)}, u32[]{:S(2)}) collective-permute-start(bf16[64,2048]{1,0:T(8,128)(2,1)S(1)} %collective-permute-done.4.refs_3_), channel_id=1, source_target_pairs={{0,64},{1,65},{2,66},{3,67},{4,68},{5,69},{6,70},{7,71},{8,72},{9,... | collective-permute-start | bytes 786440 | tf_op jit(solution)/shard_map/ppermute | solution.py:156
  83.8 0.6 collective-permute-done.7.refs_6_
  84.5 1.9 %collective-permute-start.11 = (bf16[64,2048]{1,0:T(8,128)(2,1)S(1)}, bf16[64,2048]{1,0:T(8,128)(2,1)S(1)}, u32[]{:S(2)}, u32[]{:S(2)}) collective-permute-start(bf16[64,2048]{1,0:T(8,128)(2,1)S(1)} %collective-permute-done.7.refs_6_), channel_id=1, source_target_pairs={{0,64},{1,65},{2,66},{3,67},{4,68},{5,69},{6,70},{7,71},{8,72},{9,... | collective-permute-start | bytes 786440 | tf_op jit(solution)/shard_map/ppermute | solution.py:156
  86.4 0.0 collective-permute-done.10.refs_9_
  86.4 0.0 copy-start.7
  86.4 5.1 %collective-permute-start.14 = (bf16[64,2048]{1,0:T(8,128)(2,1)S(1)}, bf16[64,2048]{1,0:T(8,128)(2,1)S(1)}, u32[]{:S(2)}, u32[]{:S(2)}) collective-permute-start(bf16[64,2048]{1,0:T(8,128)(2,1)S(1)} %collective-permute-done.10.refs_9_), channel_id=1, source_target_pairs={{0,448},{1,449},{2,450},{3,451},{4,452},{5,453},{6,454},{7,455},{8... | collective-permute-start | bytes 786440 | tf_op jit(solution)/shard_map/ppermute | solution.py:156
  91.5 0.0 collective-permute-done.9.refs_8_
  91.6 0.0 copy-start.8
  91.6 3.3 %collective-permute-start.13 = (bf16[64,2048]{1,0:T(8,128)(2,1)S(1)}, bf16[64,2048]{1,0:T(8,128)(2,1)S(1)}, u32[]{:S(2)}, u32[]{:S(2)}) collective-permute-start(bf16[64,2048]{1,0:T(8,128)(2,1)S(1)} %collective-permute-done.9.refs_8_), channel_id=1, source_target_pairs={{0,448},{1,449},{2,450},{3,451},{4,452},{5,453},{6,454},{7,455},{8... | collective-permute-start | bytes 786440 | tf_op jit(solution)/shard_map/ppermute | solution.py:156
  94.9 0.0 collective-permute-done.8.refs_7_
  94.9 0.0 copy-start.9
  94.9 2.5 %collective-permute-start.12 = (bf16[64,2048]{1,0:T(8,128)(2,1)S(1)}, bf16[64,2048]{1,0:T(8,128)(2,1)S(1)}, u32[]{:S(2)}, u32[]{:S(2)}) collective-permute-start(bf16[64,2048]{1,0:T(8,128)(2,1)S(1)} %collective-permute-done.8.refs_7_), channel_id=1, source_target_pairs={{0,64},{1,65},{2,66},{3,67},{4,68},{5,69},{6,70},{7,71},{8,72},{9,... | collective-permute-start | bytes 786440 | tf_op jit(solution)/shard_map/ppermute | solution.py:156
  97.4 0.0 collective-permute-done.11.refs_10_
  97.5 0.0 copy-start.10
  97.5 1.9 %collective-permute-start.15 = (bf16[64,2048]{1,0:T(8,128)(2,1)S(1)}, bf16[64,2048]{1,0:T(8,128)(2,1)S(1)}, u32[]{:S(2)}, u32[]{:S(2)}) collective-permute-start(bf16[64,2048]{1,0:T(8,128)(2,1)S(1)} %collective-permute-done.11.refs_10_), channel_id=1, source_target_pairs={{0,64},{1,65},{2,66},{3,67},{4,68},{5,69},{6,70},{7,71},{8,72},{9,... | collective-permute-start | bytes 786440 | tf_op jit(solution)/shard_map/ppermute | solution.py:156
  99.4 0.0 collective-permute-done.14.refs_13_
  99.4 0.0 copy-start.11
  99.4 5.1 %collective-permute-start.16 = (bf16[64,2048]{1,0:T(8,128)(2,1)S(1)}, bf16[64,2048]{1,0:T(8,128)(2,1)}, u32[]{:S(2)}, u32[]{:S(2)}) collective-permute-start(bf16[64,2048]{1,0:T(8,128)(2,1)S(1)} %collective-permute-done.14.refs_13_), channel_id=1, source_target_pairs={{0,448},{1,449},{2,450},{3,451},{4,452},{5,453},{6,454},{7,455},{8... | collective-permute-start | bytes 786440 | tf_op jit(solution)/shard_map/ppermute | solution.py:156
  104.6 0.0 collective-permute-done.13.refs_12_
  104.6 0.0 copy-start.12
  104.6 0.9 collective-permute-done.12.refs_11_
  105.5 2.8 %collective-permute-done.15.refs_14_ = bf16[64,2048]{1,0:T(8,128)(2,1)S(1)} collective-permute-done((bf16[64,2048]{1,0:T(8,128)(2,1)S(1)}, bf16[64,2048]{1,0:T(8,128)(2,1)S(1)}, u32[]{:S(2)}, u32[]{:S(2)}) %collective-permute-start.15) | collective-permute-done | bytes 262176 | tf_op jit(solution)/shard_map/ppermute | solution.py:156
  108.3 0.0 copy-done.13
  108.3 0.7 copy-done.14
  109.0 0.0 collective-permute-done.16.refs_15_
  109.0 0.0 copy-done
  109.0 0.0 copy-done.1
  109.0 0.0 copy-done.2
  109.0 0.0 copy-done.3
  109.1 0.0 copy-done.4
  109.1 0.0 copy-done.5
  109.1 0.0 copy-done.6
  109.1 0.0 copy-done.7
  109.1 0.0 copy-done.8
  109.1 0.0 copy-done.9
  109.1 6.5 %shard_map.29 = bf16[512,512]{1,0:T(8,128)(2,1)} custom-call(s32[16,16]{1,0:T(8,128)} %live_ref.3, bf16[1024,4096]{1,0:T(8,128)(2,1)} %all-gather.2.cloned.1.call-done.rows_hbm, bf16[64,2048]{1,0:T(8,128)(2,1)} %copy-done, bf16[64,2048]{1,0:T(8,128)(2,1)} %copy-done.1, bf16[64,2048]{1,0:T(8,128)(2,1)} %copy-done.2, bf16[64,2048]{1,0:T(8,128)(2,1)} %copy-done.5, ...), custom_call_target="tpu_custom_call" | custom-call | flops 2147483648 | bytes 9437184 | tf_op jit(solution)/shard_map/pallas_call | solution.py:129
  115.6 1.9 %collective-permute-start.17 = (bf16[512,512]{1,0:T(8,128)(2,1)}, bf16[512,512]{1,0:T(8,128)(2,1)S(1)}, u32[]{:S(2)}, u32[]{:S(2)}) collective-permute-start(bf16[512,512]{1,0:T(8,128)(2,1)} %shard_map.29), channel_id=1, source_target_pairs={{0,1},{1,0},{2,3},{3,2},{4,5},{5,4},{6,7},{7,6},{8,9},{9,8},{10,11... | collective-permute-start | bytes 1572872 | tf_op jit(solution)/shard_map/ppermute | solution.py:156
  117.6 6.6 %shard_map.28 = bf16[512,1024]{1,0:T(8,128)(2,1)} custom-call(s32[16,16]{1,0:T(8,128)} %live_ref.3, bf16[1024,4096]{1,0:T(8,128)(2,1)} %all-gather.2.cloned.1.call-done.rows_hbm, bf16[64,2048]{1,0:T(8,128)(2,1)} %copy-done, bf16[64,2048]{1,0:T(8,128)(2,1)} %copy-done.1, bf16[64,2048]{1,0:T(8,128)(2,1)} %copy-done.2, bf16[64,2048]{1,0:T(8,128)(2,1)} %copy-done.5, ...), custom_call_target="tpu_custom_call" | custom-call | flops 2147483648 | bytes 9437184 | tf_op jit(solution)/shard_map/pallas_call | solution.py:129
  124.2 4.4 %collective-permute-done.17 = bf16[512,512]{1,0:T(8,128)(2,1)S(1)} collective-permute-done((bf16[512,512]{1,0:T(8,128)(2,1)}, bf16[512,512]{1,0:T(8,128)(2,1)S(1)}, u32[]{:S(2)}, u32[]{:S(2)}) %collective-permute-start.17) | collective-permute-done | bytes 524320 | tf_op jit(solution)/shard_map/ppermute | solution.py:156
  128.6 0.8 constant_dynamic-update-slice_fusion
  (9 shorter events, 0.0 us)
Async XLA Ops:
  6.5 102.5 %all-gather.2.cloned.1.call-start = ((), (), s32[]{:S(2)}) async-start(), calls=%async_computation | async-start | bytes 8912896 | tf_op jit(solution)/shard_map/all_gather | solution.py:167
  6.5 11.6 %collective-permute-start.1 = (bf16[64,2048]{1,0:T(8,128)(2,1)}, bf16[64,2048]{1,0:T(8,128)(2,1)S(1)}, u32[]{:S(2)}, u32[]{:S(2)}) collective-permute-start(bf16[64,2048]{1,0:T(8,128)(2,1)} %param.2), channel_id=1, source_target_pairs={{0,1},{1,0},{2,3},{3,2},{4,5},{5,4},{6,7},{7,6},{8,9},{9,8},{10,11... | collective-permute-start | bytes 786440 | tf_op jit(solution)/shard_map/ppermute | solution.py:156
  11.5 14.9 %collective-permute-start = (bf16[64,2048]{1,0:T(8,128)(2,1)}, bf16[64,2048]{1,0:T(8,128)(2,1)S(1)}, u32[]{:S(2)}, u32[]{:S(2)}) collective-permute-start(bf16[64,2048]{1,0:T(8,128)(2,1)} %param.2), channel_id=1, source_target_pairs={{0,0},{1,32},{2,256},{3,288},{4,64},{5,96},{6,448},{7,480},{8,128}... | collective-permute-start | bytes 786440 | tf_op jit(solution)/shard_map/ppermute | solution.py:156
  26.3 82.7 %copy-start = (bf16[64,2048]{1,0:T(8,128)(2,1)}, bf16[64,2048]{1,0:T(8,128)(2,1)S(1)}, u32[]{:S(2)}) copy-start(bf16[64,2048]{1,0:T(8,128)(2,1)S(1)} %collective-permute-done.refs_0_) | copy-start | bytes 786436
  28.4 18.1 %collective-permute-start.2 = (bf16[64,2048]{1,0:T(8,128)(2,1)}, bf16[64,2048]{1,0:T(8,128)(2,1)S(1)}, u32[]{:S(2)}, u32[]{:S(2)}) collective-permute-start(bf16[64,2048]{1,0:T(8,128)(2,1)} %param.2), channel_id=1, source_target_pairs={{0,32},{1,0},{2,288},{3,256},{4,96},{5,64},{6,480},{7,448},{8,160}... | collective-permute-start | bytes 786440 | tf_op jit(solution)/shard_map/ppermute | solution.py:156
  32.5 38.4 %collective-permute-start.3 = (bf16[64,2048]{1,0:T(8,128)(2,1)S(1)}, bf16[64,2048]{1,0:T(8,128)(2,1)S(1)}, u32[]{:S(2)}, u32[]{:S(2)}) collective-permute-start(bf16[64,2048]{1,0:T(8,128)(2,1)S(1)} %collective-permute-done.refs_0_), channel_id=1, source_target_pairs={{0,64},{1,65},{2,66},{3,67},{4,68},{5,69},{6,70},{7,71},{8,72},{9,... | collective-permute-start | bytes 786440 | tf_op jit(solution)/shard_map/ppermute | solution.py:156
  46.5 62.5 %copy-start.1 = (bf16[64,2048]{1,0:T(8,128)(2,1)}, bf16[64,2048]{1,0:T(8,128)(2,1)S(1)}, u32[]{:S(2)}) copy-start(bf16[64,2048]{1,0:T(8,128)(2,1)S(1)} %collective-permute-done.2.refs_1_) | copy-start | bytes 786436
  46.5 26.3 %collective-permute-start.6 = (bf16[64,2048]{1,0:T(8,128)(2,1)S(1)}, bf16[64,2048]{1,0:T(8,128)(2,1)S(1)}, u32[]{:S(2)}, u32[]{:S(2)}) collective-permute-start(bf16[64,2048]{1,0:T(8,128)(2,1)S(1)} %collective-permute-done.2.refs_1_), channel_id=1, source_target_pairs={{0,448},{1,449},{2,450},{3,451},{4,452},{5,453},{6,454},{7,455},{8... | collective-permute-start | bytes 786440 | tf_op jit(solution)/shard_map/ppermute | solution.py:156
  59.9 18.1 %collective-permute-start.5 = (bf16[64,2048]{1,0:T(8,128)(2,1)S(1)}, bf16[64,2048]{1,0:T(8,128)(2,1)S(1)}, u32[]{:S(2)}, u32[]{:S(2)}) collective-permute-start(bf16[64,2048]{1,0:T(8,128)(2,1)S(1)} %collective-permute-done.refs_0_), channel_id=1, source_target_pairs={{0,448},{1,449},{2,450},{3,451},{4,452},{5,453},{6,454},{7,455},{8... | collective-permute-start | bytes 786440 | tf_op jit(solution)/shard_map/ppermute | solution.py:156
  68.9 13.0 %collective-permute-start.4 = (bf16[64,2048]{1,0:T(8,128)(2,1)S(1)}, bf16[64,2048]{1,0:T(8,128)(2,1)S(1)}, u32[]{:S(2)}, u32[]{:S(2)}) collective-permute-start(bf16[64,2048]{1,0:T(8,128)(2,1)S(1)} %collective-permute-done.2.refs_1_), channel_id=1, source_target_pairs={{0,64},{1,65},{2,66},{3,67},{4,68},{5,69},{6,70},{7,71},{8,72},{9,... | collective-permute-start | bytes 786440 | tf_op jit(solution)/shard_map/ppermute | solution.py:156
  70.8 38.2 %copy-start.2 = (bf16[64,2048]{1,0:T(8,128)(2,1)}, bf16[64,2048]{1,0:T(8,128)(2,1)S(1)}, u32[]{:S(2)}) copy-start(bf16[64,2048]{1,0:T(8,128)(2,1)S(1)} %collective-permute-done.3.refs_2_) | copy-start | bytes 786436
  70.8 13.6 %collective-permute-start.7 = (bf16[64,2048]{1,0:T(8,128)(2,1)S(1)}, bf16[64,2048]{1,0:T(8,128)(2,1)S(1)}, u32[]{:S(2)}, u32[]{:S(2)}) collective-permute-start(bf16[64,2048]{1,0:T(8,128)(2,1)S(1)} %collective-permute-done.3.refs_2_), channel_id=1, source_target_pairs={{0,64},{1,65},{2,66},{3,67},{4,68},{5,69},{6,70},{7,71},{8,72},{9,... | collective-permute-start | bytes 786440 | tf_op jit(solution)/shard_map/ppermute | solution.py:156
  72.8 36.3 %copy-start.3 = (bf16[64,2048]{1,0:T(8,128)(2,1)}, bf16[64,2048]{1,0:T(8,128)(2,1)S(1)}, u32[]{:S(2)}) copy-start(bf16[64,2048]{1,0:T(8,128)(2,1)S(1)} %collective-permute-done.6.refs_5_) | copy-start | bytes 786436
  72.8 13.6 %collective-permute-start.10 = (bf16[64,2048]{1,0:T(8,128)(2,1)S(1)}, bf16[64,2048]{1,0:T(8,128)(2,1)S(1)}, u32[]{:S(2)}, u32[]{:S(2)}) collective-permute-start(bf16[64,2048]{1,0:T(8,128)(2,1)S(1)} %collective-permute-done.6.refs_5_), channel_id=1, source_target_pairs={{0,448},{1,449},{2,450},{3,451},{4,452},{5,453},{6,454},{7,455},{8... | collective-permute-start | bytes 786440 | tf_op jit(solution)/shard_map/ppermute | solution.py:156
  77.9 31.1 %copy-start.4 = (bf16[64,2048]{1,0:T(8,128)(2,1)}, bf16[64,2048]{1,0:T(8,128)(2,1)S(1)}, u32[]{:S(2)}) copy-start(bf16[64,2048]{1,0:T(8,128)(2,1)S(1)} %collective-permute-done.5.refs_4_) | copy-start | bytes 786436
  78.0 13.6 %collective-permute-start.9 = (bf16[64,2048]{1,0:T(8,128)(2,1)S(1)}, bf16[64,2048]{1,0:T(8,128)(2,1)S(1)}, u32[]{:S(2)}, u32[]{:S(2)}) collective-permute-start(bf16[64,2048]{1,0:T(8,128)(2,1)S(1)} %collective-permute-done.5.refs_4_), channel_id=1, source_target_pairs={{0,448},{1,449},{2,450},{3,451},{4,452},{5,453},{6,454},{7,455},{8... | collective-permute-start | bytes 786440 | tf_op jit(solution)/shard_map/ppermute | solution.py:156
  81.9 27.2 %copy-start.5 = (bf16[64,2048]{1,0:T(8,128)(2,1)}, bf16[64,2048]{1,0:T(8,128)(2,1)S(1)}, u32[]{:S(2)}) copy-start(bf16[64,2048]{1,0:T(8,128)(2,1)S(1)} %collective-permute-done.4.refs_3_) | copy-start | bytes 786436
  81.9 13.0 %collective-permute-start.8 = (bf16[64,2048]{1,0:T(8,128)(2,1)S(1)}, bf16[64,2048]{1,0:T(8,128)(2,1)S(1)}, u32[]{:S(2)}, u32[]{:S(2)}) collective-permute-start(bf16[64,2048]{1,0:T(8,128)(2,1)S(1)} %collective-permute-done.4.refs_3_), channel_id=1, source_target_pairs={{0,64},{1,65},{2,66},{3,67},{4,68},{5,69},{6,70},{7,71},{8,72},{9,... | collective-permute-start | bytes 786440 | tf_op jit(solution)/shard_map/ppermute | solution.py:156
  84.5 24.6 %copy-start.6 = (bf16[64,2048]{1,0:T(8,128)(2,1)}, bf16[64,2048]{1,0:T(8,128)(2,1)S(1)}, u32[]{:S(2)}) copy-start(bf16[64,2048]{1,0:T(8,128)(2,1)S(1)} %collective-permute-done.7.refs_6_) | copy-start | bytes 786436
  84.5 13.0 %collective-permute-start.11 = (bf16[64,2048]{1,0:T(8,128)(2,1)S(1)}, bf16[64,2048]{1,0:T(8,128)(2,1)S(1)}, u32[]{:S(2)}, u32[]{:S(2)}) collective-permute-start(bf16[64,2048]{1,0:T(8,128)(2,1)S(1)} %collective-permute-done.7.refs_6_), channel_id=1, source_target_pairs={{0,64},{1,65},{2,66},{3,67},{4,68},{5,69},{6,70},{7,71},{8,72},{9,... | collective-permute-start | bytes 786440 | tf_op jit(solution)/shard_map/ppermute | solution.py:156
  86.4 22.7 %copy-start.7 = (bf16[64,2048]{1,0:T(8,128)(2,1)}, bf16[64,2048]{1,0:T(8,128)(2,1)S(1)}, u32[]{:S(2)}) copy-start(bf16[64,2048]{1,0:T(8,128)(2,1)S(1)} %collective-permute-done.10.refs_9_) | copy-start | bytes 786436
  86.4 13.0 %collective-permute-start.14 = (bf16[64,2048]{1,0:T(8,128)(2,1)S(1)}, bf16[64,2048]{1,0:T(8,128)(2,1)S(1)}, u32[]{:S(2)}, u32[]{:S(2)}) collective-permute-start(bf16[64,2048]{1,0:T(8,128)(2,1)S(1)} %collective-permute-done.10.refs_9_), channel_id=1, source_target_pairs={{0,448},{1,449},{2,450},{3,451},{4,452},{5,453},{6,454},{7,455},{8... | collective-permute-start | bytes 786440 | tf_op jit(solution)/shard_map/ppermute | solution.py:156
  91.6 17.5 %copy-start.8 = (bf16[64,2048]{1,0:T(8,128)(2,1)}, bf16[64,2048]{1,0:T(8,128)(2,1)S(1)}, u32[]{:S(2)}) copy-start(bf16[64,2048]{1,0:T(8,128)(2,1)S(1)} %collective-permute-done.9.refs_8_) | copy-start | bytes 786436
  91.6 13.0 %collective-permute-start.13 = (bf16[64,2048]{1,0:T(8,128)(2,1)S(1)}, bf16[64,2048]{1,0:T(8,128)(2,1)S(1)}, u32[]{:S(2)}, u32[]{:S(2)}) collective-permute-start(bf16[64,2048]{1,0:T(8,128)(2,1)S(1)} %collective-permute-done.9.refs_8_), channel_id=1, source_target_pairs={{0,448},{1,449},{2,450},{3,451},{4,452},{5,453},{6,454},{7,455},{8... | collective-permute-start | bytes 786440 | tf_op jit(solution)/shard_map/ppermute | solution.py:156
  94.9 14.2 %copy-start.9 = (bf16[64,2048]{1,0:T(8,128)(2,1)}, bf16[64,2048]{1,0:T(8,128)(2,1)S(1)}, u32[]{:S(2)}) copy-start(bf16[64,2048]{1,0:T(8,128)(2,1)S(1)} %collective-permute-done.8.refs_7_) | copy-start | bytes 786436
  94.9 10.5 %collective-permute-start.12 = (bf16[64,2048]{1,0:T(8,128)(2,1)S(1)}, bf16[64,2048]{1,0:T(8,128)(2,1)S(1)}, u32[]{:S(2)}, u32[]{:S(2)}) collective-permute-start(bf16[64,2048]{1,0:T(8,128)(2,1)S(1)} %collective-permute-done.8.refs_7_), channel_id=1, source_target_pairs={{0,64},{1,65},{2,66},{3,67},{4,68},{5,69},{6,70},{7,71},{8,72},{9,... | collective-permute-start | bytes 786440 | tf_op jit(solution)/shard_map/ppermute | solution.py:156
  97.5 11.7 %copy-start.10 = (bf16[64,2048]{1,0:T(8,128)(2,1)}, bf16[64,2048]{1,0:T(8,128)(2,1)S(1)}, u32[]{:S(2)}) copy-start(bf16[64,2048]{1,0:T(8,128)(2,1)S(1)} %collective-permute-done.11.refs_10_) | copy-start | bytes 786436
  97.5 10.8 %collective-permute-start.15 = (bf16[64,2048]{1,0:T(8,128)(2,1)S(1)}, bf16[64,2048]{1,0:T(8,128)(2,1)S(1)}, u32[]{:S(2)}, u32[]{:S(2)}) collective-permute-start(bf16[64,2048]{1,0:T(8,128)(2,1)S(1)} %collective-permute-done.11.refs_10_), channel_id=1, source_target_pairs={{0,64},{1,65},{2,66},{3,67},{4,68},{5,69},{6,70},{7,71},{8,72},{9,... | collective-permute-start | bytes 786440 | tf_op jit(solution)/shard_map/ppermute | solution.py:156
  99.4 9.7 %copy-start.11 = (bf16[64,2048]{1,0:T(8,128)(2,1)}, bf16[64,2048]{1,0:T(8,128)(2,1)S(1)}, u32[]{:S(2)}) copy-start(bf16[64,2048]{1,0:T(8,128)(2,1)S(1)} %collective-permute-done.14.refs_13_) | copy-start | bytes 786436
  99.4 9.6 %collective-permute-start.16 = (bf16[64,2048]{1,0:T(8,128)(2,1)S(1)}, bf16[64,2048]{1,0:T(8,128)(2,1)}, u32[]{:S(2)}, u32[]{:S(2)}) collective-permute-start(bf16[64,2048]{1,0:T(8,128)(2,1)S(1)} %collective-permute-done.14.refs_13_), channel_id=1, source_target_pairs={{0,448},{1,449},{2,450},{3,451},{4,452},{5,453},{6,454},{7,455},{8... | collective-permute-start | bytes 786440 | tf_op jit(solution)/shard_map/ppermute | solution.py:156
  104.6 4.6 %copy-start.12 = (bf16[64,2048]{1,0:T(8,128)(2,1)}, bf16[64,2048]{1,0:T(8,128)(2,1)S(1)}, u32[]{:S(2)}) copy-start(bf16[64,2048]{1,0:T(8,128)(2,1)S(1)} %collective-permute-done.13.refs_12_) | copy-start | bytes 786436
  105.5 2.8 %copy-start.13 = (bf16[64,2048]{1,0:T(8,128)(2,1)}, bf16[64,2048]{1,0:T(8,128)(2,1)S(1)}, u32[]{:S(2)}) copy-start(bf16[64,2048]{1,0:T(8,128)(2,1)S(1)} %collective-permute-done.12.refs_11_) | copy-start | bytes 786436
  108.3 0.7 copy-start.14
  115.6 12.9 %collective-permute-start.17 = (bf16[512,512]{1,0:T(8,128)(2,1)}, bf16[512,512]{1,0:T(8,128)(2,1)S(1)}, u32[]{:S(2)}, u32[]{:S(2)}) collective-permute-start(bf16[512,512]{1,0:T(8,128)(2,1)} %shard_map.29), channel_id=1, source_target_pairs={{0,1},{1,0},{2,3},{3,2},{4,5},{5,4},{6,7},{7,6},{8,9},{9,8},{10,11... | collective-permute-start | bytes 1572872 | tf_op jit(solution)/shard_map/ppermute | solution.py:156
Sparse Core Ops, SparseCore 0:
  28.5 66.3 all-gather.1

commit v10 on v9

--- a/solution.py
+++ b/solution.py
@@ -166,9 +166,12 @@
     )
     rows = lax.all_gather(rows, ("z", "a"), axis=0, tiled=True)
 
-    steps, chunks = [0], [early, late]
-    up, down = [early, late], [early, late]
-    for step in range(1, N // 2):
+    above, below = send(early, shift_y(1)), send(early, shift_y(-1))
+    above, below, late = lax.optimization_barrier((above, below, late))
+    up = [above, send(late, shift_y(1))]
+    down = [below, send(late, shift_y(-1))]
+    steps, chunks = [0, 1, -1], [early, late, *up, *down]
+    for step in range(2, N // 2):
         up = [send(part, shift_y(1)) for part in up]
         down = [send(part, shift_y(-1)) for part in down]
         steps += [step, -step]

time: 137 us -> 140 us (1.022)
  the two profiles are of different devices: /device:TPU:192 before, /device:TPU:4 now
where the time goes in v10:
time: 140 us; the launch traced here: 139 us
  starting transfers between devices  64.6 us (46%)
  waiting for transfers between devices  44.1 us (32%)
  between operations  13.8 us (10%)
  Pallas kernels  13.1 us (9%)
  other arithmetic  2.04 us (1%)
  local copies, waits for them, and re-layouts  1.58 us (1%)
    ppermute x18, starting transfers between devices, send(): return lax.ppermute(value, AX, to)  64.6 us
    ppermute x18, waiting for transfers between devices, send(): return lax.ppermute(value, AX, to)  44.1 us
    pallas_call x2, Pallas kernels, gram_tile(): pl.pallas_call(functools.partial(gram_kernel, keep, steps), out_shape=jax...  13.1 us
  transfers between devices with their start and end apart: 19, of which 8 were waited for; matrix products, arithmetic and copies ran while one was open for 0% of the time, Pallas kernels for 5%

profile of v10, /device:TPU:4, one launch (start us, length us, event | category | flops | bytes accessed | tf_op | source)
XLA Modules:
  0.0 139.2 jit_solution(339923857601584251)
XLA Ops:
  6.5 0.0 all-gather.2.cloned.1.call-start
  6.5 7.8 %collective-permute-start.1 = (bf16[64,2048]{1,0:T(8,128)(2,1)}, bf16[64,2048]{1,0:T(8,128)(2,1)S(1)}, u32[]{:S(2)}, u32[]{:S(2)}) collective-permute-start(bf16[64,2048]{1,0:T(8,128)(2,1)} %param.2), channel_id=1, source_target_pairs={{0,1},{1,0},{2,3},{3,2},{4,5},{5,4},{6,7},{7,6},{8,9},{9,8},{10,11... | collective-permute-start | bytes 786440 | tf_op jit(solution)/shard_map/ppermute | solution.py:156
  14.3 1.9 %collective-permute-start = (bf16[64,2048]{1,0:T(8,128)(2,1)}, bf16[64,2048]{1,0:T(8,128)(2,1)S(1)}, u32[]{:S(2)}, u32[]{:S(2)}) collective-permute-start(bf16[64,2048]{1,0:T(8,128)(2,1)} %param.2), channel_id=1, source_target_pairs={{0,0},{1,32},{2,256},{3,288},{4,64},{5,96},{6,448},{7,480},{8,128}... | collective-permute-start | bytes 786440 | tf_op jit(solution)/shard_map/ppermute | solution.py:156
  16.3 2.6 %collective-permute-done.1 = bf16[64,2048]{1,0:T(8,128)(2,1)S(1)} collective-permute-done((bf16[64,2048]{1,0:T(8,128)(2,1)}, bf16[64,2048]{1,0:T(8,128)(2,1)S(1)}, u32[]{:S(2)}, u32[]{:S(2)}) %collective-permute-start.1) | collective-permute-done | bytes 262176 | tf_op jit(solution)/shard_map/ppermute | solution.py:156
  18.9 10.0 %collective-permute-done.refs_0_ = bf16[64,2048]{1,0:T(8,128)(2,1)S(1)} collective-permute-done((bf16[64,2048]{1,0:T(8,128)(2,1)}, bf16[64,2048]{1,0:T(8,128)(2,1)S(1)}, u32[]{:S(2)}, u32[]{:S(2)}) %collective-permute-start) | collective-permute-done | bytes 262176 | tf_op jit(solution)/shard_map/ppermute | solution.py:156
  28.9 2.0 %maximum_select_fusion = bf16[64,4096]{1,0:T(8,128)(2,1)} fusion(bf16[64,2048]{1,0:T(8,128)(2,1)S(1)} %collective-permute-done.1, bf16[64,2048]{1,0:T(8,128)(2,1)} %param.2, pred[]{:T(512)S(6)} %eq.3), kind=kLoop, calls=%fused_computation | loop fusion | flops 2359296 | bytes 1048577 | tf_op jit(solution)/shard_map/jit(_where)/select_n | solution.py:162
  30.9 0.0 all-gather.2.cloned.1.call-update
  30.9 1.9 %collective-permute-start.4 = (bf16[64,2048]{1,0:T(8,128)(2,1)}, bf16[64,2048]{1,0:T(8,128)(2,1)S(1)}, u32[]{:S(2)}, u32[]{:S(2)}) collective-permute-start(bf16[64,2048]{1,0:T(8,128)(2,1)} %param.2), channel_id=1, source_target_pairs={{0,32},{1,0},{2,288},{3,256},{4,96},{5,64},{6,480},{7,448},{8,160}... | collective-permute-start | bytes 786440 | tf_op jit(solution)/shard_map/ppermute | solution.py:156
  32.9 11.2 %collective-permute-start.3 = (bf16[64,2048]{1,0:T(8,128)(2,1)S(1)}, bf16[64,2048]{1,0:T(8,128)(2,1)S(1)}, u32[]{:S(2)}, u32[]{:S(2)}) collective-permute-start(bf16[64,2048]{1,0:T(8,128)(2,1)S(1)} %collective-permute-done.refs_0_), channel_id=1, source_target_pairs={{0,448},{1,449},{2,450},{3,451},{4,452},{5,453},{6,454},{7,455},{8... | collective-permute-start | bytes 786440 | tf_op jit(solution)/shard_map/ppermute | solution.py:156
  44.0 1.9 %collective-permute-start.2 = (bf16[64,2048]{1,0:T(8,128)(2,1)S(1)}, bf16[64,2048]{1,0:T(8,128)(2,1)S(1)}, u32[]{:S(2)}, u32[]{:S(2)}) collective-permute-start(bf16[64,2048]{1,0:T(8,128)(2,1)S(1)} %collective-permute-done.refs_0_), channel_id=1, source_target_pairs={{0,64},{1,65},{2,66},{3,67},{4,68},{5,69},{6,70},{7,71},{8,72},{9,... | collective-permute-start | bytes 786440 | tf_op jit(solution)/shard_map/ppermute | solution.py:156
  46.0 11.0 %collective-permute-done.4.refs_1_ = bf16[64,2048]{1,0:T(8,128)(2,1)S(1)} collective-permute-done((bf16[64,2048]{1,0:T(8,128)(2,1)}, bf16[64,2048]{1,0:T(8,128)(2,1)S(1)}, u32[]{:S(2)}, u32[]{:S(2)}) %collective-permute-start.4) | collective-permute-done | bytes 262176 | tf_op jit(solution)/shard_map/ppermute | solution.py:156
  57.0 0.0 collective-permute-done.3.refs_4_
  57.0 3.9 %collective-permute-done.2.refs_2_ = bf16[64,2048]{1,0:T(8,128)(2,1)S(1)} collective-permute-done((bf16[64,2048]{1,0:T(8,128)(2,1)S(1)}, bf16[64,2048]{1,0:T(8,128)(2,1)S(1)}, u32[]{:S(2)}, u32[]{:S(2)}) %collective-permute-start.2) | collective-permute-done | bytes 262176 | tf_op jit(solution)/shard_map/ppermute | solution.py:156
  60.9 3.0 %collective-permute-start.6 = (bf16[64,2048]{1,0:T(8,128)(2,1)S(1)}, bf16[64,2048]{1,0:T(8,128)(2,1)S(1)}, u32[]{:S(2)}, u32[]{:S(2)}) collective-permute-start(bf16[64,2048]{1,0:T(8,128)(2,1)S(1)} %collective-permute-done.4.refs_1_), channel_id=1, source_target_pairs={{0,448},{1,449},{2,450},{3,451},{4,452},{5,453},{6,454},{7,455},{8... | collective-permute-start | bytes 786440 | tf_op jit(solution)/shard_map/ppermute | solution.py:156
  63.9 2.8 %collective-permute-start.7 = (bf16[64,2048]{1,0:T(8,128)(2,1)S(1)}, bf16[64,2048]{1,0:T(8,128)(2,1)S(1)}, u32[]{:S(2)}, u32[]{:S(2)}) collective-permute-start(bf16[64,2048]{1,0:T(8,128)(2,1)S(1)} %collective-permute-done.2.refs_2_), channel_id=1, source_target_pairs={{0,64},{1,65},{2,66},{3,67},{4,68},{5,69},{6,70},{7,71},{8,72},{9,... | collective-permute-start | bytes 786440 | tf_op jit(solution)/shard_map/ppermute | solution.py:156
  66.8 1.9 %collective-permute-start.5 = (bf16[64,2048]{1,0:T(8,128)(2,1)S(1)}, bf16[64,2048]{1,0:T(8,128)(2,1)S(1)}, u32[]{:S(2)}, u32[]{:S(2)}) collective-permute-start(bf16[64,2048]{1,0:T(8,128)(2,1)S(1)} %collective-permute-done.4.refs_1_), channel_id=1, source_target_pairs={{0,64},{1,65},{2,66},{3,67},{4,68},{5,69},{6,70},{7,71},{8,72},{9,... | collective-permute-start | bytes 786440 | tf_op jit(solution)/shard_map/ppermute | solution.py:156
  68.7 3.2 %collective-permute-done.6.refs_5_ = bf16[64,2048]{1,0:T(8,128)(2,1)S(1)} collective-permute-done((bf16[64,2048]{1,0:T(8,128)(2,1)S(1)}, bf16[64,2048]{1,0:T(8,128)(2,1)S(1)}, u32[]{:S(2)}, u32[]{:S(2)}) %collective-permute-start.6) | collective-permute-done | bytes 262176 | tf_op jit(solution)/shard_map/ppermute | solution.py:156
  71.9 4.0 %collective-permute-start.10 = (bf16[64,2048]{1,0:T(8,128)(2,1)S(1)}, bf16[64,2048]{1,0:T(8,128)(2,1)S(1)}, u32[]{:S(2)}, u32[]{:S(2)}) collective-permute-start(bf16[64,2048]{1,0:T(8,128)(2,1)S(1)} %collective-permute-done.6.refs_5_), channel_id=1, source_target_pairs={{0,448},{1,449},{2,450},{3,451},{4,452},{5,453},{6,454},{7,455},{8... | collective-permute-start | bytes 786440 | tf_op jit(solution)/shard_map/ppermute | solution.py:156
  76.0 1.9 %collective-permute-start.9 = (bf16[64,2048]{1,0:T(8,128)(2,1)S(1)}, bf16[64,2048]{1,0:T(8,128)(2,1)S(1)}, u32[]{:S(2)}, u32[]{:S(2)}) collective-permute-start(bf16[64,2048]{1,0:T(8,128)(2,1)S(1)} %collective-permute-done.3.refs_4_), channel_id=1, source_target_pairs={{0,448},{1,449},{2,450},{3,451},{4,452},{5,453},{6,454},{7,455},{8... | collective-permute-start | bytes 786440 | tf_op jit(solution)/shard_map/ppermute | solution.py:156
  77.9 0.0 collective-permute-done.7.refs_6_
  77.9 0.0 copy-start.5
  77.9 3.9 %collective-permute-start.11 = (bf16[64,2048]{1,0:T(8,128)(2,1)S(1)}, bf16[64,2048]{1,0:T(8,128)(2,1)S(1)}, u32[]{:S(2)}, u32[]{:S(2)}) collective-permute-start(bf16[64,2048]{1,0:T(8,128)(2,1)S(1)} %collective-permute-done.7.refs_6_), channel_id=1, source_target_pairs={{0,64},{1,65},{2,66},{3,67},{4,68},{5,69},{6,70},{7,71},{8,72},{9,... | collective-permute-start | bytes 786440 | tf_op jit(solution)/shard_map/ppermute | solution.py:156
  81.8 0.0 collective-permute-done.5.refs_3_
  81.8 0.0 copy-start.6
  81.9 1.9 %collective-permute-start.8 = (bf16[64,2048]{1,0:T(8,128)(2,1)S(1)}, bf16[64,2048]{1,0:T(8,128)(2,1)S(1)}, u32[]{:S(2)}, u32[]{:S(2)}) collective-permute-start(bf16[64,2048]{1,0:T(8,128)(2,1)S(1)} %collective-permute-done.5.refs_3_), channel_id=1, source_target_pairs={{0,64},{1,65},{2,66},{3,67},{4,68},{5,69},{6,70},{7,71},{8,72},{9,... | collective-permute-start | bytes 786440 | tf_op jit(solution)/shard_map/ppermute | solution.py:156
  83.8 0.0 collective-permute-done.10.refs_9_
  83.8 0.0 copy-start.7
  83.8 5.1 %collective-permute-start.14 = (bf16[64,2048]{1,0:T(8,128)(2,1)S(1)}, bf16[64,2048]{1,0:T(8,128)(2,1)S(1)}, u32[]{:S(2)}, u32[]{:S(2)}) collective-permute-start(bf16[64,2048]{1,0:T(8,128)(2,1)S(1)} %collective-permute-done.10.refs_9_), channel_id=1, source_target_pairs={{0,448},{1,449},{2,450},{3,451},{4,452},{5,453},{6,454},{7,455},{8... | collective-permute-start | bytes 786440 | tf_op jit(solution)/shard_map/ppermute | solution.py:156
  88.9 0.0 collective-permute-done.9.refs_8_
  89.0 0.0 copy-start.8
  89.0 3.9 %collective-permute-start.13 = (bf16[64,2048]{1,0:T(8,128)(2,1)S(1)}, bf16[64,2048]{1,0:T(8,128)(2,1)S(1)}, u32[]{:S(2)}, u32[]{:S(2)}) collective-permute-start(bf16[64,2048]{1,0:T(8,128)(2,1)S(1)} %collective-permute-done.9.refs_8_), channel_id=1, source_target_pairs={{0,448},{1,449},{2,450},{3,451},{4,452},{5,453},{6,454},{7,455},{8... | collective-permute-start | bytes 786440 | tf_op jit(solution)/shard_map/ppermute | solution.py:156
  92.9 0.0 collective-permute-done.11.refs_10_
  92.9 0.0 copy-start.9
  92.9 2.0 %collective-permute-start.15 = (bf16[64,2048]{1,0:T(8,128)(2,1)S(1)}, bf16[64,2048]{1,0:T(8,128)(2,1)S(1)}, u32[]{:S(2)}, u32[]{:S(2)}) collective-permute-start(bf16[64,2048]{1,0:T(8,128)(2,1)S(1)} %collective-permute-done.11.refs_10_), channel_id=1, source_target_pairs={{0,64},{1,65},{2,66},{3,67},{4,68},{5,69},{6,70},{7,71},{8,72},{9,... | collective-permute-start | bytes 786440 | tf_op jit(solution)/shard_map/ppermute | solution.py:156
  94.8 0.0 collective-permute-done.8.refs_7_
  94.9 0.0 copy-start.10
  94.9 2.1 %collective-permute-start.12 = (bf16[64,2048]{1,0:T(8,128)(2,1)S(1)}, bf16[64,2048]{1,0:T(8,128)(2,1)S(1)}, u32[]{:S(2)}, u32[]{:S(2)}) collective-permute-start(bf16[64,2048]{1,0:T(8,128)(2,1)S(1)} %collective-permute-done.8.refs_7_), channel_id=1, source_target_pairs={{0,64},{1,65},{2,66},{3,67},{4,68},{5,69},{6,70},{7,71},{8,72},{9,... | collective-permute-start | bytes 786440 | tf_op jit(solution)/shard_map/ppermute | solution.py:156
  97.0 0.0 collective-permute-done.14.refs_13_
  97.0 0.0 copy-start.11
  97.0 5.0 %collective-permute-start.16 = (bf16[64,2048]{1,0:T(8,128)(2,1)S(1)}, bf16[64,2048]{1,0:T(8,128)(2,1)}, u32[]{:S(2)}, u32[]{:S(2)}) collective-permute-start(bf16[64,2048]{1,0:T(8,128)(2,1)S(1)} %collective-permute-done.14.refs_13_), channel_id=1, source_target_pairs={{0,448},{1,449},{2,450},{3,451},{4,452},{5,453},{6,454},{7,455},{8... | collective-permute-start | bytes 786440 | tf_op jit(solution)/shard_map/ppermute | solution.py:156
  102.0 0.0 collective-permute-done.13.refs_12_
  102.0 0.0 copy-start.12
  102.0 3.3 %collective-permute-done.15.refs_14_ = bf16[64,2048]{1,0:T(8,128)(2,1)S(1)} collective-permute-done((bf16[64,2048]{1,0:T(8,128)(2,1)S(1)}, bf16[64,2048]{1,0:T(8,128)(2,1)S(1)}, u32[]{:S(2)}, u32[]{:S(2)}) %collective-permute-start.15) | collective-permute-done | bytes 262176 | tf_op jit(solution)/shard_map/ppermute | solution.py:156
  105.2 3.5 %collective-permute-done.12.refs_11_ = bf16[64,2048]{1,0:T(8,128)(2,1)S(1)} collective-permute-done((bf16[64,2048]{1,0:T(8,128)(2,1)S(1)}, bf16[64,2048]{1,0:T(8,128)(2,1)S(1)}, u32[]{:S(2)}, u32[]{:S(2)}) %collective-permute-start.12) | collective-permute-done | bytes 262176 | tf_op jit(solution)/shard_map/ppermute | solution.py:156
  108.8 0.0 copy-done.13
  108.8 0.7 copy-done.14
  109.5 0.0 collective-permute-done.16.refs_15_
  109.5 0.0 copy-done.1
  109.5 0.0 copy-done.2
  109.5 0.0 copy-done.3
  109.5 0.0 copy-done.4
  109.5 0.0 copy-done.5
  109.5 0.0 copy-done.6
  109.5 0.0 copy-done.7
  109.5 0.0 copy-done.8
  109.5 0.0 copy-done.9
  109.6 0.0 copy-done.10
  109.6 0.0 copy-done.11
  109.6 0.0 copy-done.12
  109.6 6.5 %shard_map.29 = bf16[512,512]{1,0:T(8,128)(2,1)} custom-call(s32[16,16]{1,0:T(8,128)} %live_ref.3, bf16[1024,4096]{1,0:T(8,128)(2,1)} %all-gather.2.cloned.1.call-done.rows_hbm, bf16[64,2048]{1,0:T(8,128)(2,1)} %copy-done, bf16[64,2048]{1,0:T(8,128)(2,1)} %copy-done.1, bf16[64,2048]{1,0:T(8,128)(2,1)} %copy-done.3, bf16[64,2048]{1,0:T(8,128)(2,1)} %copy-done.6, ...), custom_call_target="tpu_custom_call" | custom-call | flops 2147483648 | bytes 9437184 | tf_op jit(solution)/shard_map/pallas_call | solution.py:129
  116.1 2.3 %collective-permute-start.17 = (bf16[512,512]{1,0:T(8,128)(2,1)}, bf16[512,512]{1,0:T(8,128)(2,1)S(1)}, u32[]{:S(2)}, u32[]{:S(2)}) collective-permute-start(bf16[512,512]{1,0:T(8,128)(2,1)} %shard_map.29), channel_id=1, source_target_pairs={{0,1},{1,0},{2,3},{3,2},{4,5},{5,4},{6,7},{7,6},{8,9},{9,8},{10,11... | collective-permute-start | bytes 1572872 | tf_op jit(solution)/shard_map/ppermute | solution.py:156
  118.4 6.6 %shard_map.28 = bf16[512,1024]{1,0:T(8,128)(2,1)} custom-call(s32[16,16]{1,0:T(8,128)} %live_ref.3, bf16[1024,4096]{1,0:T(8,128)(2,1)} %all-gather.2.cloned.1.call-done.rows_hbm, bf16[64,2048]{1,0:T(8,128)(2,1)} %copy-done, bf16[64,2048]{1,0:T(8,128)(2,1)} %copy-done.1, bf16[64,2048]{1,0:T(8,128)(2,1)} %copy-done.3, bf16[64,2048]{1,0:T(8,128)(2,1)} %copy-done.6, ...), custom_call_target="tpu_custom_call" | custom-call | flops 2147483648 | bytes 9437184 | tf_op jit(solution)/shard_map/pallas_call | solution.py:129
  125.0 6.5 %collective-permute-done.17 = bf16[512,512]{1,0:T(8,128)(2,1)S(1)} collective-permute-done((bf16[512,512]{1,0:T(8,128)(2,1)}, bf16[512,512]{1,0:T(8,128)(2,1)S(1)}, u32[]{:S(2)}, u32[]{:S(2)}) %collective-permute-start.17) | collective-permute-done | bytes 524320 | tf_op jit(solution)/shard_map/ppermute | solution.py:156
  131.5 0.8 constant_dynamic-update-slice_fusion
  (9 shorter events, 0.0 us)
Async XLA Ops:
  6.5 102.9 %all-gather.2.cloned.1.call-start = ((), (), s32[]{:S(2)}) async-start(), calls=%async_computation | async-start | bytes 8912896 | tf_op jit(solution)/shard_map/all_gather | solution.py:167
  6.5 12.3 %collective-permute-start.1 = (bf16[64,2048]{1,0:T(8,128)(2,1)}, bf16[64,2048]{1,0:T(8,128)(2,1)S(1)}, u32[]{:S(2)}, u32[]{:S(2)}) collective-permute-start(bf16[64,2048]{1,0:T(8,128)(2,1)} %param.2), channel_id=1, source_target_pairs={{0,1},{1,0},{2,3},{3,2},{4,5},{5,4},{6,7},{7,6},{8,9},{9,8},{10,11... | collective-permute-start | bytes 786440 | tf_op jit(solution)/shard_map/ppermute | solution.py:156
  14.3 14.6 %collective-permute-start = (bf16[64,2048]{1,0:T(8,128)(2,1)}, bf16[64,2048]{1,0:T(8,128)(2,1)S(1)}, u32[]{:S(2)}, u32[]{:S(2)}) collective-permute-start(bf16[64,2048]{1,0:T(8,128)(2,1)} %param.2), channel_id=1, source_target_pairs={{0,0},{1,32},{2,256},{3,288},{4,64},{5,96},{6,448},{7,480},{8,128}... | collective-permute-start | bytes 786440 | tf_op jit(solution)/shard_map/ppermute | solution.py:156
  28.9 80.6 %copy-start = (bf16[64,2048]{1,0:T(8,128)(2,1)}, bf16[64,2048]{1,0:T(8,128)(2,1)S(1)}, u32[]{:S(2)}) copy-start(bf16[64,2048]{1,0:T(8,128)(2,1)S(1)} %collective-permute-done.refs_0_) | copy-start | bytes 786436
  30.9 26.0 %collective-permute-start.4 = (bf16[64,2048]{1,0:T(8,128)(2,1)}, bf16[64,2048]{1,0:T(8,128)(2,1)S(1)}, u32[]{:S(2)}, u32[]{:S(2)}) collective-permute-start(bf16[64,2048]{1,0:T(8,128)(2,1)} %param.2), channel_id=1, source_target_pairs={{0,32},{1,0},{2,288},{3,256},{4,96},{5,64},{6,480},{7,448},{8,160}... | collective-permute-start | bytes 786440 | tf_op jit(solution)/shard_map/ppermute | solution.py:156
  32.9 24.1 %collective-permute-start.3 = (bf16[64,2048]{1,0:T(8,128)(2,1)S(1)}, bf16[64,2048]{1,0:T(8,128)(2,1)S(1)}, u32[]{:S(2)}, u32[]{:S(2)}) collective-permute-start(bf16[64,2048]{1,0:T(8,128)(2,1)S(1)} %collective-permute-done.refs_0_), channel_id=1, source_target_pairs={{0,448},{1,449},{2,450},{3,451},{4,452},{5,453},{6,454},{7,455},{8... | collective-permute-start | bytes 786440 | tf_op jit(solution)/shard_map/ppermute | solution.py:156
  44.0 16.9 %collective-permute-start.2 = (bf16[64,2048]{1,0:T(8,128)(2,1)S(1)}, bf16[64,2048]{1,0:T(8,128)(2,1)S(1)}, u32[]{:S(2)}, u32[]{:S(2)}) collective-permute-start(bf16[64,2048]{1,0:T(8,128)(2,1)S(1)} %collective-permute-done.refs_0_), channel_id=1, source_target_pairs={{0,64},{1,65},{2,66},{3,67},{4,68},{5,69},{6,70},{7,71},{8,72},{9,... | collective-permute-start | bytes 786440 | tf_op jit(solution)/shard_map/ppermute | solution.py:156
  57.0 52.5 %copy-start.1 = (bf16[64,2048]{1,0:T(8,128)(2,1)}, bf16[64,2048]{1,0:T(8,128)(2,1)S(1)}, u32[]{:S(2)}) copy-start(bf16[64,2048]{1,0:T(8,128)(2,1)S(1)} %collective-permute-done.4.refs_1_) | copy-start | bytes 786436
  57.0 52.5 %copy-start.2 = (bf16[64,2048]{1,0:T(8,128)(2,1)}, bf16[64,2048]{1,0:T(8,128)(2,1)S(1)}, u32[]{:S(2)}) copy-start(bf16[64,2048]{1,0:T(8,128)(2,1)S(1)} %collective-permute-done.3.refs_4_) | copy-start | bytes 786436
  60.9 48.6 %copy-start.3 = (bf16[64,2048]{1,0:T(8,128)(2,1)}, bf16[64,2048]{1,0:T(8,128)(2,1)S(1)}, u32[]{:S(2)}) copy-start(bf16[64,2048]{1,0:T(8,128)(2,1)S(1)} %collective-permute-done.2.refs_2_) | copy-start | bytes 786436
  60.9 11.0 %collective-permute-start.6 = (bf16[64,2048]{1,0:T(8,128)(2,1)S(1)}, bf16[64,2048]{1,0:T(8,128)(2,1)S(1)}, u32[]{:S(2)}, u32[]{:S(2)}) collective-permute-start(bf16[64,2048]{1,0:T(8,128)(2,1)S(1)} %collective-permute-done.4.refs_1_), channel_id=1, source_target_pairs={{0,448},{1,449},{2,450},{3,451},{4,452},{5,453},{6,454},{7,455},{8... | collective-permute-start | bytes 786440 | tf_op jit(solution)/shard_map/ppermute | solution.py:156
  63.9 14.0 %collective-permute-start.7 = (bf16[64,2048]{1,0:T(8,128)(2,1)S(1)}, bf16[64,2048]{1,0:T(8,128)(2,1)S(1)}, u32[]{:S(2)}, u32[]{:S(2)}) collective-permute-start(bf16[64,2048]{1,0:T(8,128)(2,1)S(1)} %collective-permute-done.2.refs_2_), channel_id=1, source_target_pairs={{0,64},{1,65},{2,66},{3,67},{4,68},{5,69},{6,70},{7,71},{8,72},{9,... | collective-permute-start | bytes 786440 | tf_op jit(solution)/shard_map/ppermute | solution.py:156
  66.8 15.1 %collective-permute-start.5 = (bf16[64,2048]{1,0:T(8,128)(2,1)S(1)}, bf16[64,2048]{1,0:T(8,128)(2,1)S(1)}, u32[]{:S(2)}, u32[]{:S(2)}) collective-permute-start(bf16[64,2048]{1,0:T(8,128)(2,1)S(1)} %collective-permute-done.4.refs_1_), channel_id=1, source_target_pairs={{0,64},{1,65},{2,66},{3,67},{4,68},{5,69},{6,70},{7,71},{8,72},{9,... | collective-permute-start | bytes 786440 | tf_op jit(solution)/shard_map/ppermute | solution.py:156
  71.9 37.6 %copy-start.4 = (bf16[64,2048]{1,0:T(8,128)(2,1)}, bf16[64,2048]{1,0:T(8,128)(2,1)S(1)}, u32[]{:S(2)}) copy-start(bf16[64,2048]{1,0:T(8,128)(2,1)S(1)} %collective-permute-done.6.refs_5_) | copy-start | bytes 786436
  71.9 11.9 %collective-permute-start.10 = (bf16[64,2048]{1,0:T(8,128)(2,1)S(1)}, bf16[64,2048]{1,0:T(8,128)(2,1)S(1)}, u32[]{:S(2)}, u32[]{:S(2)}) collective-permute-start(bf16[64,2048]{1,0:T(8,128)(2,1)S(1)} %collective-permute-done.6.refs_5_), channel_id=1, source_target_pairs={{0,448},{1,449},{2,450},{3,451},{4,452},{5,453},{6,454},{7,455},{8... | collective-permute-start | bytes 786440 | tf_op jit(solution)/shard_map/ppermute | solution.py:156
  76.0 13.0 %collective-permute-start.9 = (bf16[64,2048]{1,0:T(8,128)(2,1)S(1)}, bf16[64,2048]{1,0:T(8,128)(2,1)S(1)}, u32[]{:S(2)}, u32[]{:S(2)}) collective-permute-start(bf16[64,2048]{1,0:T(8,128)(2,1)S(1)} %collective-permute-done.3.refs_4_), channel_id=1, source_target_pairs={{0,448},{1,449},{2,450},{3,451},{4,452},{5,453},{6,454},{7,455},{8... | collective-permute-start | bytes 786440 | tf_op jit(solution)/shard_map/ppermute | solution.py:156
  77.9 31.6 %copy-start.5 = (bf16[64,2048]{1,0:T(8,128)(2,1)}, bf16[64,2048]{1,0:T(8,128)(2,1)S(1)}, u32[]{:S(2)}) copy-start(bf16[64,2048]{1,0:T(8,128)(2,1)S(1)} %collective-permute-done.7.refs_6_) | copy-start | bytes 786436
  77.9 15.0 %collective-permute-start.11 = (bf16[64,2048]{1,0:T(8,128)(2,1)S(1)}, bf16[64,2048]{1,0:T(8,128)(2,1)S(1)}, u32[]{:S(2)}, u32[]{:S(2)}) collective-permute-start(bf16[64,2048]{1,0:T(8,128)(2,1)S(1)} %collective-permute-done.7.refs_6_), channel_id=1, source_target_pairs={{0,64},{1,65},{2,66},{3,67},{4,68},{5,69},{6,70},{7,71},{8,72},{9,... | collective-permute-start | bytes 786440 | tf_op jit(solution)/shard_map/ppermute | solution.py:156
  81.8 27.7 %copy-start.6 = (bf16[64,2048]{1,0:T(8,128)(2,1)}, bf16[64,2048]{1,0:T(8,128)(2,1)S(1)}, u32[]{:S(2)}) copy-start(bf16[64,2048]{1,0:T(8,128)(2,1)S(1)} %collective-permute-done.5.refs_3_) | copy-start | bytes 786436
  81.9 13.0 %collective-permute-start.8 = (bf16[64,2048]{1,0:T(8,128)(2,1)S(1)}, bf16[64,2048]{1,0:T(8,128)(2,1)S(1)}, u32[]{:S(2)}, u32[]{:S(2)}) collective-permute-start(bf16[64,2048]{1,0:T(8,128)(2,1)S(1)} %collective-permute-done.5.refs_3_), channel_id=1, source_target_pairs={{0,64},{1,65},{2,66},{3,67},{4,68},{5,69},{6,70},{7,71},{8,72},{9,... | collective-permute-start | bytes 786440 | tf_op jit(solution)/shard_map/ppermute | solution.py:156
  83.8 25.7 %copy-start.7 = (bf16[64,2048]{1,0:T(8,128)(2,1)}, bf16[64,2048]{1,0:T(8,128)(2,1)S(1)}, u32[]{:S(2)}) copy-start(bf16[64,2048]{1,0:T(8,128)(2,1)S(1)} %collective-permute-done.10.refs_9_) | copy-start | bytes 786436
  83.8 13.2 %collective-permute-start.14 = (bf16[64,2048]{1,0:T(8,128)(2,1)S(1)}, bf16[64,2048]{1,0:T(8,128)(2,1)S(1)}, u32[]{:S(2)}, u32[]{:S(2)}) collective-permute-start(bf16[64,2048]{1,0:T(8,128)(2,1)S(1)} %collective-permute-done.10.refs_9_), channel_id=1, source_target_pairs={{0,448},{1,449},{2,450},{3,451},{4,452},{5,453},{6,454},{7,455},{8... | collective-permute-start | bytes 786440 | tf_op jit(solution)/shard_map/ppermute | solution.py:156
  89.0 20.6 %copy-start.8 = (bf16[64,2048]{1,0:T(8,128)(2,1)}, bf16[64,2048]{1,0:T(8,128)(2,1)S(1)}, u32[]{:S(2)}) copy-start(bf16[64,2048]{1,0:T(8,128)(2,1)S(1)} %collective-permute-done.9.refs_8_) | copy-start | bytes 786436
  89.0 13.0 %collective-permute-start.13 = (bf16[64,2048]{1,0:T(8,128)(2,1)S(1)}, bf16[64,2048]{1,0:T(8,128)(2,1)S(1)}, u32[]{:S(2)}, u32[]{:S(2)}) collective-permute-start(bf16[64,2048]{1,0:T(8,128)(2,1)S(1)} %collective-permute-done.9.refs_8_), channel_id=1, source_target_pairs={{0,448},{1,449},{2,450},{3,451},{4,452},{5,453},{6,454},{7,455},{8... | collective-permute-start | bytes 786440 | tf_op jit(solution)/shard_map/ppermute | solution.py:156
  92.9 16.7 %copy-start.9 = (bf16[64,2048]{1,0:T(8,128)(2,1)}, bf16[64,2048]{1,0:T(8,128)(2,1)S(1)}, u32[]{:S(2)}) copy-start(bf16[64,2048]{1,0:T(8,128)(2,1)S(1)} %collective-permute-done.11.refs_10_) | copy-start | bytes 786436
  92.9 12.3 %collective-permute-start.15 = (bf16[64,2048]{1,0:T(8,128)(2,1)S(1)}, bf16[64,2048]{1,0:T(8,128)(2,1)S(1)}, u32[]{:S(2)}, u32[]{:S(2)}) collective-permute-start(bf16[64,2048]{1,0:T(8,128)(2,1)S(1)} %collective-permute-done.11.refs_10_), channel_id=1, source_target_pairs={{0,64},{1,65},{2,66},{3,67},{4,68},{5,69},{6,70},{7,71},{8,72},{9,... | collective-permute-start | bytes 786440 | tf_op jit(solution)/shard_map/ppermute | solution.py:156
  94.9 14.7 %copy-start.10 = (bf16[64,2048]{1,0:T(8,128)(2,1)}, bf16[64,2048]{1,0:T(8,128)(2,1)S(1)}, u32[]{:S(2)}) copy-start(bf16[64,2048]{1,0:T(8,128)(2,1)S(1)} %collective-permute-done.8.refs_7_) | copy-start | bytes 786436
  94.9 13.9 %collective-permute-start.12 = (bf16[64,2048]{1,0:T(8,128)(2,1)S(1)}, bf16[64,2048]{1,0:T(8,128)(2,1)S(1)}, u32[]{:S(2)}, u32[]{:S(2)}) collective-permute-start(bf16[64,2048]{1,0:T(8,128)(2,1)S(1)} %collective-permute-done.8.refs_7_), channel_id=1, source_target_pairs={{0,64},{1,65},{2,66},{3,67},{4,68},{5,69},{6,70},{7,71},{8,72},{9,... | collective-permute-start | bytes 786440 | tf_op jit(solution)/shard_map/ppermute | solution.py:156
  97.0 12.6 %copy-start.11 = (bf16[64,2048]{1,0:T(8,128)(2,1)}, bf16[64,2048]{1,0:T(8,128)(2,1)S(1)}, u32[]{:S(2)}) copy-start(bf16[64,2048]{1,0:T(8,128)(2,1)S(1)} %collective-permute-done.14.refs_13_) | copy-start | bytes 786436
  97.0 12.5 %collective-permute-start.16 = (bf16[64,2048]{1,0:T(8,128)(2,1)S(1)}, bf16[64,2048]{1,0:T(8,128)(2,1)}, u32[]{:S(2)}, u32[]{:S(2)}) collective-permute-start(bf16[64,2048]{1,0:T(8,128)(2,1)S(1)} %collective-permute-done.14.refs_13_), channel_id=1, source_target_pairs={{0,448},{1,449},{2,450},{3,451},{4,452},{5,453},{6,454},{7,455},{8... | collective-permute-start | bytes 786440 | tf_op jit(solution)/shard_map/ppermute | solution.py:156
  102.0 7.6 %copy-start.12 = (bf16[64,2048]{1,0:T(8,128)(2,1)}, bf16[64,2048]{1,0:T(8,128)(2,1)S(1)}, u32[]{:S(2)}) copy-start(bf16[64,2048]{1,0:T(8,128)(2,1)S(1)} %collective-permute-done.13.refs_12_) | copy-start | bytes 786436
  105.2 3.5 %copy-start.13 = (bf16[64,2048]{1,0:T(8,128)(2,1)}, bf16[64,2048]{1,0:T(8,128)(2,1)S(1)}, u32[]{:S(2)}) copy-start(bf16[64,2048]{1,0:T(8,128)(2,1)S(1)} %collective-permute-done.15.refs_14_) | copy-start | bytes 786436
  108.8 0.7 copy-start.14
  116.1 15.5 %collective-permute-start.17 = (bf16[512,512]{1,0:T(8,128)(2,1)}, bf16[512,512]{1,0:T(8,128)(2,1)S(1)}, u32[]{:S(2)}, u32[]{:S(2)}) collective-permute-start(bf16[512,512]{1,0:T(8,128)(2,1)} %shard_map.29), channel_id=1, source_target_pairs={{0,1},{1,0},{2,3},{3,2},{4,5},{5,4},{6,7},{7,6},{8,9},{9,8},{10,11... | collective-permute-start | bytes 1572872 | tf_op jit(solution)/shard_map/ppermute | solution.py:156
Sparse Core Ops, SparseCore 0:
  31.1 66.1 all-gather.1

commit v11 on v9

--- a/solution.py
+++ b/solution.py
@@ -158,7 +158,7 @@
     other = send(trajectories, swap_lag())
     early = send(trajectories, col_pairs(0))
     late = send(trajectories, col_pairs(1))
-    early, other = lax.optimization_barrier((early, other))
+    early, late, other = lax.optimization_barrier((early, late, other))
     rows = jnp.where(
         xl == 0,
         jnp.concatenate([trajectories, other], axis=1),

time: 137 us -> 137 us (level)
  the two profiles are of different devices: /device:TPU:192 before, /device:TPU:6 now
where the time goes in v11:
time: 137 us; the launch traced here: 136 us
  starting transfers between devices  72.8 us (53%)
  waiting for transfers between devices  32.4 us (24%)
  between operations  13.8 us (10%)
  Pallas kernels  13.1 us (10%)
  other arithmetic  2.04 us (1%)
  local copies, waits for them, and re-layouts  1.61 us (1%)
    ppermute x18, starting transfers between devices, send(): return lax.ppermute(value, AX, to)  72.8 us
    ppermute x18, waiting for transfers between devices, send(): return lax.ppermute(value, AX, to)  23.6 us
    pallas_call x2, Pallas kernels, gram_tile(): pl.pallas_call(functools.partial(gram_kernel, keep, steps), out_shape=jax...  13.1 us
    all_gather x1, waiting for transfers between devices, on_device(): rows = lax.all_gather(rows, ('z', 'a'), axis=0, tiled=True)  8.87 us
  transfers between devices with their start and end apart: 19, of which 7 were waited for; matrix products, arithmetic and copies ran while one was open for 0% of the time, Pallas kernels for 5%

profile of v11, /device:TPU:6, one launch (start us, length us, event | category | flops | bytes accessed | tf_op | source)
XLA Modules:
  0.0 135.8 jit_solution(6059042173890639900)
XLA Ops:
  6.5 0.0 all-gather.2.cloned.1.call-start
  6.5 1.9 %collective-permute-start.1 = (bf16[64,2048]{1,0:T(8,128)(2,1)}, bf16[64,2048]{1,0:T(8,128)(2,1)S(1)}, u32[]{:S(2)}, u32[]{:S(2)}) collective-permute-start(bf16[64,2048]{1,0:T(8,128)(2,1)} %param.2), channel_id=1, source_target_pairs={{0,32},{1,0},{2,288},{3,256},{4,96},{5,64},{6,480},{7,448},{8,160}... | collective-permute-start | bytes 786440 | tf_op jit(solution)/shard_map/ppermute | solution.py:156
  8.5 8.3 %collective-permute-start = (bf16[64,2048]{1,0:T(8,128)(2,1)}, bf16[64,2048]{1,0:T(8,128)(2,1)S(1)}, u32[]{:S(2)}, u32[]{:S(2)}) collective-permute-start(bf16[64,2048]{1,0:T(8,128)(2,1)} %param.2), channel_id=1, source_target_pairs={{0,0},{1,32},{2,256},{3,288},{4,64},{5,96},{6,448},{7,480},{8,128}... | collective-permute-start | bytes 786440 | tf_op jit(solution)/shard_map/ppermute | solution.py:156
  16.7 3.9 %collective-permute-start.2 = (bf16[64,2048]{1,0:T(8,128)(2,1)}, bf16[64,2048]{1,0:T(8,128)(2,1)S(1)}, u32[]{:S(2)}, u32[]{:S(2)}) collective-permute-start(bf16[64,2048]{1,0:T(8,128)(2,1)} %param.2), channel_id=1, source_target_pairs={{0,1},{1,0},{2,3},{3,2},{4,5},{5,4},{6,7},{7,6},{8,9},{9,8},{10,11... | collective-permute-start | bytes 786440 | tf_op jit(solution)/shard_map/ppermute | solution.py:156
  20.7 2.6 %collective-permute-done.1.refs_1_ = bf16[64,2048]{1,0:T(8,128)(2,1)S(1)} collective-permute-done((bf16[64,2048]{1,0:T(8,128)(2,1)}, bf16[64,2048]{1,0:T(8,128)(2,1)S(1)}, u32[]{:S(2)}, u32[]{:S(2)}) %collective-permute-start.1) | collective-permute-done | bytes 262176 | tf_op jit(solution)/shard_map/ppermute | solution.py:156
  23.3 7.7 %collective-permute-done.refs_0_ = bf16[64,2048]{1,0:T(8,128)(2,1)S(1)} collective-permute-done((bf16[64,2048]{1,0:T(8,128)(2,1)}, bf16[64,2048]{1,0:T(8,128)(2,1)S(1)}, u32[]{:S(2)}, u32[]{:S(2)}) %collective-permute-start) | collective-permute-done | bytes 262176 | tf_op jit(solution)/shard_map/ppermute | solution.py:156
  31.0 0.0 collective-permute-done.2
  31.0 2.0 %maximum_select_fusion = bf16[64,4096]{1,0:T(8,128)(2,1)} fusion(bf16[64,2048]{1,0:T(8,128)(2,1)S(1)} %collective-permute-done.2, bf16[64,2048]{1,0:T(8,128)(2,1)} %param.2, pred[]{:T(512)S(6)} %eq.3), kind=kLoop, calls=%fused_computation | loop fusion | flops 2359296 | bytes 1048577 | tf_op jit(solution)/shard_map/jit(_where)/select_n | solution.py:162
  33.1 0.0 all-gather.2.cloned.1.call-update
  33.1 1.9 %collective-permute-start.3 = (bf16[64,2048]{1,0:T(8,128)(2,1)S(1)}, bf16[64,2048]{1,0:T(8,128)(2,1)S(1)}, u32[]{:S(2)}, u32[]{:S(2)}) collective-permute-start(bf16[64,2048]{1,0:T(8,128)(2,1)S(1)} %collective-permute-done.refs_0_), channel_id=1, source_target_pairs={{0,64},{1,65},{2,66},{3,67},{4,68},{5,69},{6,70},{7,71},{8,72},{9,... | collective-permute-start | bytes 786440 | tf_op jit(solution)/shard_map/ppermute | solution.py:156
  35.0 14.7 %collective-permute-start.6 = (bf16[64,2048]{1,0:T(8,128)(2,1)S(1)}, bf16[64,2048]{1,0:T(8,128)(2,1)S(1)}, u32[]{:S(2)}, u32[]{:S(2)}) collective-permute-start(bf16[64,2048]{1,0:T(8,128)(2,1)S(1)} %collective-permute-done.1.refs_1_), channel_id=1, source_target_pairs={{0,448},{1,449},{2,450},{3,451},{4,452},{5,453},{6,454},{7,455},{8... | collective-permute-start | bytes 786440 | tf_op jit(solution)/shard_map/ppermute | solution.py:156
  49.8 3.9 %collective-permute-start.5 = (bf16[64,2048]{1,0:T(8,128)(2,1)S(1)}, bf16[64,2048]{1,0:T(8,128)(2,1)S(1)}, u32[]{:S(2)}, u32[]{:S(2)}) collective-permute-start(bf16[64,2048]{1,0:T(8,128)(2,1)S(1)} %collective-permute-done.refs_0_), channel_id=1, source_target_pairs={{0,448},{1,449},{2,450},{3,451},{4,452},{5,453},{6,454},{7,455},{8... | collective-permute-start | bytes 786440 | tf_op jit(solution)/shard_map/ppermute | solution.py:156
  53.7 1.9 %collective-permute-start.4 = (bf16[64,2048]{1,0:T(8,128)(2,1)S(1)}, bf16[64,2048]{1,0:T(8,128)(2,1)S(1)}, u32[]{:S(2)}, u32[]{:S(2)}) collective-permute-start(bf16[64,2048]{1,0:T(8,128)(2,1)S(1)} %collective-permute-done.1.refs_1_), channel_id=1, source_target_pairs={{0,64},{1,65},{2,66},{3,67},{4,68},{5,69},{6,70},{7,71},{8,72},{9,... | collective-permute-start | bytes 786440 | tf_op jit(solution)/shard_map/ppermute | solution.py:156
  55.6 0.0 collective-permute-done.3.refs_2_
  55.6 0.0 copy-start.2
  55.6 1.9 %collective-permute-start.7 = (bf16[64,2048]{1,0:T(8,128)(2,1)S(1)}, bf16[64,2048]{1,0:T(8,128)(2,1)S(1)}, u32[]{:S(2)}, u32[]{:S(2)}) collective-permute-start(bf16[64,2048]{1,0:T(8,128)(2,1)S(1)} %collective-permute-done.3.refs_2_), channel_id=1, source_target_pairs={{0,64},{1,65},{2,66},{3,67},{4,68},{5,69},{6,70},{7,71},{8,72},{9,... | collective-permute-start | bytes 786440 | tf_op jit(solution)/shard_map/ppermute | solution.py:156
  57.6 0.0 collective-permute-done.6.refs_5_
  57.6 0.0 copy-start.3
  57.6 5.1 %collective-permute-start.10 = (bf16[64,2048]{1,0:T(8,128)(2,1)S(1)}, bf16[64,2048]{1,0:T(8,128)(2,1)S(1)}, u32[]{:S(2)}, u32[]{:S(2)}) collective-permute-start(bf16[64,2048]{1,0:T(8,128)(2,1)S(1)} %collective-permute-done.6.refs_5_), channel_id=1, source_target_pairs={{0,448},{1,449},{2,450},{3,451},{4,452},{5,453},{6,454},{7,455},{8... | collective-permute-start | bytes 786440 | tf_op jit(solution)/shard_map/ppermute | solution.py:156
  62.7 0.0 collective-permute-done.5.refs_4_
  62.7 0.0 copy-start.4
  62.7 3.9 %collective-permute-start.9 = (bf16[64,2048]{1,0:T(8,128)(2,1)S(1)}, bf16[64,2048]{1,0:T(8,128)(2,1)S(1)}, u32[]{:S(2)}, u32[]{:S(2)}) collective-permute-start(bf16[64,2048]{1,0:T(8,128)(2,1)S(1)} %collective-permute-done.5.refs_4_), channel_id=1, source_target_pairs={{0,448},{1,449},{2,450},{3,451},{4,452},{5,453},{6,454},{7,455},{8... | collective-permute-start | bytes 786440 | tf_op jit(solution)/shard_map/ppermute | solution.py:156
  66.7 0.0 collective-permute-done.4.refs_3_
  66.7 0.0 copy-start.5
  66.7 1.9 %collective-permute-start.8 = (bf16[64,2048]{1,0:T(8,128)(2,1)S(1)}, bf16[64,2048]{1,0:T(8,128)(2,1)S(1)}, u32[]{:S(2)}, u32[]{:S(2)}) collective-permute-start(bf16[64,2048]{1,0:T(8,128)(2,1)S(1)} %collective-permute-done.4.refs_3_), channel_id=1, source_target_pairs={{0,64},{1,65},{2,66},{3,67},{4,68},{5,69},{6,70},{7,71},{8,72},{9,... | collective-permute-start | bytes 786440 | tf_op jit(solution)/shard_map/ppermute | solution.py:156
  68.6 0.0 collective-permute-done.7.refs_6_
  68.6 0.0 copy-start.6
  68.6 4.0 %collective-permute-start.11 = (bf16[64,2048]{1,0:T(8,128)(2,1)S(1)}, bf16[64,2048]{1,0:T(8,128)(2,1)S(1)}, u32[]{:S(2)}, u32[]{:S(2)}) collective-permute-start(bf16[64,2048]{1,0:T(8,128)(2,1)S(1)} %collective-permute-done.7.refs_6_), channel_id=1, source_target_pairs={{0,64},{1,65},{2,66},{3,67},{4,68},{5,69},{6,70},{7,71},{8,72},{9,... | collective-permute-start | bytes 786440 | tf_op jit(solution)/shard_map/ppermute | solution.py:156
  72.7 0.0 collective-permute-done.10.refs_9_
  72.7 0.0 copy-start.7
  72.7 3.1 %collective-permute-start.14 = (bf16[64,2048]{1,0:T(8,128)(2,1)S(1)}, bf16[64,2048]{1,0:T(8,128)(2,1)S(1)}, u32[]{:S(2)}, u32[]{:S(2)}) collective-permute-start(bf16[64,2048]{1,0:T(8,128)(2,1)S(1)} %collective-permute-done.10.refs_9_), channel_id=1, source_target_pairs={{0,448},{1,449},{2,450},{3,451},{4,452},{5,453},{6,454},{7,455},{8... | collective-permute-start | bytes 786440 | tf_op jit(solution)/shard_map/ppermute | solution.py:156
  75.7 0.0 collective-permute-done.9.refs_8_
  75.7 0.0 copy-start.8
  75.8 3.9 %collective-permute-start.13 = (bf16[64,2048]{1,0:T(8,128)(2,1)S(1)}, bf16[64,2048]{1,0:T(8,128)(2,1)S(1)}, u32[]{:S(2)}, u32[]{:S(2)}) collective-permute-start(bf16[64,2048]{1,0:T(8,128)(2,1)S(1)} %collective-permute-done.9.refs_8_), channel_id=1, source_target_pairs={{0,448},{1,449},{2,450},{3,451},{4,452},{5,453},{6,454},{7,455},{8... | collective-permute-start | bytes 786440 | tf_op jit(solution)/shard_map/ppermute | solution.py:156
  79.7 0.0 collective-permute-done.8.refs_7_
  79.7 0.0 copy-start.9
  79.7 1.9 %collective-permute-start.12 = (bf16[64,2048]{1,0:T(8,128)(2,1)S(1)}, bf16[64,2048]{1,0:T(8,128)(2,1)S(1)}, u32[]{:S(2)}, u32[]{:S(2)}) collective-permute-start(bf16[64,2048]{1,0:T(8,128)(2,1)S(1)} %collective-permute-done.8.refs_7_), channel_id=1, source_target_pairs={{0,64},{1,65},{2,66},{3,67},{4,68},{5,69},{6,70},{7,71},{8,72},{9,... | collective-permute-start | bytes 786440 | tf_op jit(solution)/shard_map/ppermute | solution.py:156
  81.6 0.0 collective-permute-done.11.refs_10_
  81.6 0.0 copy-start.10
  81.7 4.9 %collective-permute-start.15 = (bf16[64,2048]{1,0:T(8,128)(2,1)S(1)}, bf16[64,2048]{1,0:T(8,128)(2,1)S(1)}, u32[]{:S(2)}, u32[]{:S(2)}) collective-permute-start(bf16[64,2048]{1,0:T(8,128)(2,1)S(1)} %collective-permute-done.11.refs_10_), channel_id=1, source_target_pairs={{0,64},{1,65},{2,66},{3,67},{4,68},{5,69},{6,70},{7,71},{8,72},{9,... | collective-permute-start | bytes 786440 | tf_op jit(solution)/shard_map/ppermute | solution.py:156
  86.6 0.0 collective-permute-done.14.refs_13_
  86.6 2.1 %collective-permute-start.16 = (bf16[64,2048]{1,0:T(8,128)(2,1)S(1)}, bf16[64,2048]{1,0:T(8,128)(2,1)}, u32[]{:S(2)}, u32[]{:S(2)}) collective-permute-start(bf16[64,2048]{1,0:T(8,128)(2,1)S(1)} %collective-permute-done.14.refs_13_), channel_id=1, source_target_pairs={{0,448},{1,449},{2,450},{3,451},{4,452},{5,453},{6,454},{7,455},{8... | collective-permute-start | bytes 786440 | tf_op jit(solution)/shard_map/ppermute | solution.py:156
  88.7 0.0 collective-permute-done.13.refs_12_
  88.8 2.0 %collective-permute-done.12.refs_11_ = bf16[64,2048]{1,0:T(8,128)(2,1)S(1)} collective-permute-done((bf16[64,2048]{1,0:T(8,128)(2,1)S(1)}, bf16[64,2048]{1,0:T(8,128)(2,1)S(1)}, u32[]{:S(2)}, u32[]{:S(2)}) %collective-permute-start.12) | collective-permute-done | bytes 262176 | tf_op jit(solution)/shard_map/ppermute | solution.py:156
  90.8 2.8 %collective-permute-done.15.refs_14_ = bf16[64,2048]{1,0:T(8,128)(2,1)S(1)} collective-permute-done((bf16[64,2048]{1,0:T(8,128)(2,1)S(1)}, bf16[64,2048]{1,0:T(8,128)(2,1)S(1)}, u32[]{:S(2)}, u32[]{:S(2)}) %collective-permute-start.15) | collective-permute-done | bytes 262176 | tf_op jit(solution)/shard_map/ppermute | solution.py:156
  93.6 0.0 copy-done.13
  93.6 0.7 copy-done.14
  94.3 0.7 collective-permute-done.16.refs_15_
  95.0 8.9 %all-gather.2.cloned.1.call-done.rows_hbm = bf16[1024,4096]{1,0:T(8,128)(2,1)} async-done(((bf16[64,4096]{1,0:T(8,128)(2,1)}), bf16[1024,4096]{1,0:T(8,128)(2,1)}) %all-gather.2.cloned.1.call-update) | async-done | bytes 8388624 | tf_op jit(solution)/shard_map/all_gather | solution.py:167
  103.9 0.0 copy-done
  103.9 0.0 copy-done.4
  103.9 0.0 copy-done.5
  103.9 0.0 copy-done.6
  103.9 0.0 copy-done.7
  103.9 0.0 copy-done.8
  103.9 0.0 copy-done.9
  103.9 0.0 copy-done.10
  103.9 0.0 copy-done.11
  103.9 0.0 copy-done.12
  104.0 6.5 %shard_map.29 = bf16[512,512]{1,0:T(8,128)(2,1)} custom-call(s32[16,16]{1,0:T(8,128)} %live_ref.3, bf16[1024,4096]{1,0:T(8,128)(2,1)} %all-gather.2.cloned.1.call-done.rows_hbm, bf16[64,2048]{1,0:T(8,128)(2,1)} %copy-done.1, bf16[64,2048]{1,0:T(8,128)(2,1)} %copy-done, bf16[64,2048]{1,0:T(8,128)(2,1)} %copy-done.2, bf16[64,2048]{1,0:T(8,128)(2,1)} %copy-done.5, ...), custom_call_target="tpu_custom_call" | custom-call | flops 2147483648 | bytes 9437184 | tf_op jit(solution)/shard_map/pallas_call | solution.py:129
  110.4 3.4 %collective-permute-start.17 = (bf16[512,512]{1,0:T(8,128)(2,1)}, bf16[512,512]{1,0:T(8,128)(2,1)S(1)}, u32[]{:S(2)}, u32[]{:S(2)}) collective-permute-start(bf16[512,512]{1,0:T(8,128)(2,1)} %shard_map.29), channel_id=1, source_target_pairs={{0,1},{1,0},{2,3},{3,2},{4,5},{5,4},{6,7},{7,6},{8,9},{9,8},{10,11... | collective-permute-start | bytes 1572872 | tf_op jit(solution)/shard_map/ppermute | solution.py:156
  113.8 6.6 %shard_map.28 = bf16[512,1024]{1,0:T(8,128)(2,1)} custom-call(s32[16,16]{1,0:T(8,128)} %live_ref.3, bf16[1024,4096]{1,0:T(8,128)(2,1)} %all-gather.2.cloned.1.call-done.rows_hbm, bf16[64,2048]{1,0:T(8,128)(2,1)} %copy-done.1, bf16[64,2048]{1,0:T(8,128)(2,1)} %copy-done, bf16[64,2048]{1,0:T(8,128)(2,1)} %copy-done.2, bf16[64,2048]{1,0:T(8,128)(2,1)} %copy-done.5, ...), custom_call_target="tpu_custom_call" | custom-call | flops 2147483648 | bytes 9437184 | tf_op jit(solution)/shard_map/pallas_call | solution.py:129
  120.4 7.7 %collective-permute-done.17 = bf16[512,512]{1,0:T(8,128)(2,1)S(1)} collective-permute-done((bf16[512,512]{1,0:T(8,128)(2,1)}, bf16[512,512]{1,0:T(8,128)(2,1)S(1)}, u32[]{:S(2)}, u32[]{:S(2)}) %collective-permute-start.17) | collective-permute-done | bytes 524320 | tf_op jit(solution)/shard_map/ppermute | solution.py:156
  128.1 0.8 constant_dynamic-update-slice_fusion
  (9 shorter events, 0.0 us)
Async XLA Ops:
  6.5 97.3 %all-gather.2.cloned.1.call-start = ((), (), s32[]{:S(2)}) async-start(), calls=%async_computation | async-start | bytes 8912896 | tf_op jit(solution)/shard_map/all_gather | solution.py:167
  6.5 16.8 %collective-permute-start.1 = (bf16[64,2048]{1,0:T(8,128)(2,1)}, bf16[64,2048]{1,0:T(8,128)(2,1)S(1)}, u32[]{:S(2)}, u32[]{:S(2)}) collective-permute-start(bf16[64,2048]{1,0:T(8,128)(2,1)} %param.2), channel_id=1, source_target_pairs={{0,32},{1,0},{2,288},{3,256},{4,96},{5,64},{6,480},{7,448},{8,160}... | collective-permute-start | bytes 786440 | tf_op jit(solution)/shard_map/ppermute | solution.py:156
  8.5 22.6 %collective-permute-start = (bf16[64,2048]{1,0:T(8,128)(2,1)}, bf16[64,2048]{1,0:T(8,128)(2,1)S(1)}, u32[]{:S(2)}, u32[]{:S(2)}) collective-permute-start(bf16[64,2048]{1,0:T(8,128)(2,1)} %param.2), channel_id=1, source_target_pairs={{0,0},{1,32},{2,256},{3,288},{4,64},{5,96},{6,448},{7,480},{8,128}... | collective-permute-start | bytes 786440 | tf_op jit(solution)/shard_map/ppermute | solution.py:156
  16.7 14.3 %collective-permute-start.2 = (bf16[64,2048]{1,0:T(8,128)(2,1)}, bf16[64,2048]{1,0:T(8,128)(2,1)S(1)}, u32[]{:S(2)}, u32[]{:S(2)}) collective-permute-start(bf16[64,2048]{1,0:T(8,128)(2,1)} %param.2), channel_id=1, source_target_pairs={{0,1},{1,0},{2,3},{3,2},{4,5},{5,4},{6,7},{7,6},{8,9},{9,8},{10,11... | collective-permute-start | bytes 786440 | tf_op jit(solution)/shard_map/ppermute | solution.py:156
  23.3 80.5 %copy-start = (bf16[64,2048]{1,0:T(8,128)(2,1)}, bf16[64,2048]{1,0:T(8,128)(2,1)S(1)}, u32[]{:S(2)}) copy-start(bf16[64,2048]{1,0:T(8,128)(2,1)S(1)} %collective-permute-done.1.refs_1_) | copy-start | bytes 786436
  31.0 72.8 %copy-start.1 = (bf16[64,2048]{1,0:T(8,128)(2,1)}, bf16[64,2048]{1,0:T(8,128)(2,1)S(1)}, u32[]{:S(2)}) copy-start(bf16[64,2048]{1,0:T(8,128)(2,1)S(1)} %collective-permute-done.refs_0_) | copy-start | bytes 786436
  33.1 22.5 %collective-permute-start.3 = (bf16[64,2048]{1,0:T(8,128)(2,1)S(1)}, bf16[64,2048]{1,0:T(8,128)(2,1)S(1)}, u32[]{:S(2)}, u32[]{:S(2)}) collective-permute-start(bf16[64,2048]{1,0:T(8,128)(2,1)S(1)} %collective-permute-done.refs_0_), channel_id=1, source_target_pairs={{0,64},{1,65},{2,66},{3,67},{4,68},{5,69},{6,70},{7,71},{8,72},{9,... | collective-permute-start | bytes 786440 | tf_op jit(solution)/shard_map/ppermute | solution.py:156
  35.0 22.5 %collective-permute-start.6 = (bf16[64,2048]{1,0:T(8,128)(2,1)S(1)}, bf16[64,2048]{1,0:T(8,128)(2,1)S(1)}, u32[]{:S(2)}, u32[]{:S(2)}) collective-permute-start(bf16[64,2048]{1,0:T(8,128)(2,1)S(1)} %collective-permute-done.1.refs_1_), channel_id=1, source_target_pairs={{0,448},{1,449},{2,450},{3,451},{4,452},{5,453},{6,454},{7,455},{8... | collective-permute-start | bytes 786440 | tf_op jit(solution)/shard_map/ppermute | solution.py:156
  49.8 13.0 %collective-permute-start.5 = (bf16[64,2048]{1,0:T(8,128)(2,1)S(1)}, bf16[64,2048]{1,0:T(8,128)(2,1)S(1)}, u32[]{:S(2)}, u32[]{:S(2)}) collective-permute-start(bf16[64,2048]{1,0:T(8,128)(2,1)S(1)} %collective-permute-done.refs_0_), channel_id=1, source_target_pairs={{0,448},{1,449},{2,450},{3,451},{4,452},{5,453},{6,454},{7,455},{8... | collective-permute-start | bytes 786440 | tf_op jit(solution)/shard_map/ppermute | solution.py:156
  53.7 13.0 %collective-permute-start.4 = (bf16[64,2048]{1,0:T(8,128)(2,1)S(1)}, bf16[64,2048]{1,0:T(8,128)(2,1)S(1)}, u32[]{:S(2)}, u32[]{:S(2)}) collective-permute-start(bf16[64,2048]{1,0:T(8,128)(2,1)S(1)} %collective-permute-done.1.refs_1_), channel_id=1, source_target_pairs={{0,64},{1,65},{2,66},{3,67},{4,68},{5,69},{6,70},{7,71},{8,72},{9,... | collective-permute-start | bytes 786440 | tf_op jit(solution)/shard_map/ppermute | solution.py:156
  55.6 48.2 %copy-start.2 = (bf16[64,2048]{1,0:T(8,128)(2,1)}, bf16[64,2048]{1,0:T(8,128)(2,1)S(1)}, u32[]{:S(2)}) copy-start(bf16[64,2048]{1,0:T(8,128)(2,1)S(1)} %collective-permute-done.3.refs_2_) | copy-start | bytes 786436
  55.6 13.0 %collective-permute-start.7 = (bf16[64,2048]{1,0:T(8,128)(2,1)S(1)}, bf16[64,2048]{1,0:T(8,128)(2,1)S(1)}, u32[]{:S(2)}, u32[]{:S(2)}) collective-permute-start(bf16[64,2048]{1,0:T(8,128)(2,1)S(1)} %collective-permute-done.3.refs_2_), channel_id=1, source_target_pairs={{0,64},{1,65},{2,66},{3,67},{4,68},{5,69},{6,70},{7,71},{8,72},{9,... | collective-permute-start | bytes 786440 | tf_op jit(solution)/shard_map/ppermute | solution.py:156
  57.6 46.3 %copy-start.3 = (bf16[64,2048]{1,0:T(8,128)(2,1)}, bf16[64,2048]{1,0:T(8,128)(2,1)S(1)}, u32[]{:S(2)}) copy-start(bf16[64,2048]{1,0:T(8,128)(2,1)S(1)} %collective-permute-done.6.refs_5_) | copy-start | bytes 786436
  57.6 15.1 %collective-permute-start.10 = (bf16[64,2048]{1,0:T(8,128)(2,1)S(1)}, bf16[64,2048]{1,0:T(8,128)(2,1)S(1)}, u32[]{:S(2)}, u32[]{:S(2)}) collective-permute-start(bf16[64,2048]{1,0:T(8,128)(2,1)S(1)} %collective-permute-done.6.refs_5_), channel_id=1, source_target_pairs={{0,448},{1,449},{2,450},{3,451},{4,452},{5,453},{6,454},{7,455},{8... | collective-permute-start | bytes 786440 | tf_op jit(solution)/shard_map/ppermute | solution.py:156
  62.7 41.1 %copy-start.4 = (bf16[64,2048]{1,0:T(8,128)(2,1)}, bf16[64,2048]{1,0:T(8,128)(2,1)S(1)}, u32[]{:S(2)}) copy-start(bf16[64,2048]{1,0:T(8,128)(2,1)S(1)} %collective-permute-done.5.refs_4_) | copy-start | bytes 786436
  62.7 13.0 %collective-permute-start.9 = (bf16[64,2048]{1,0:T(8,128)(2,1)S(1)}, bf16[64,2048]{1,0:T(8,128)(2,1)S(1)}, u32[]{:S(2)}, u32[]{:S(2)}) collective-permute-start(bf16[64,2048]{1,0:T(8,128)(2,1)S(1)} %collective-permute-done.5.refs_4_), channel_id=1, source_target_pairs={{0,448},{1,449},{2,450},{3,451},{4,452},{5,453},{6,454},{7,455},{8... | collective-permute-start | bytes 786440 | tf_op jit(solution)/shard_map/ppermute | solution.py:156
  66.7 37.2 %copy-start.5 = (bf16[64,2048]{1,0:T(8,128)(2,1)}, bf16[64,2048]{1,0:T(8,128)(2,1)S(1)}, u32[]{:S(2)}) copy-start(bf16[64,2048]{1,0:T(8,128)(2,1)S(1)} %collective-permute-done.4.refs_3_) | copy-start | bytes 786436
  66.7 13.0 %collective-permute-start.8 = (bf16[64,2048]{1,0:T(8,128)(2,1)S(1)}, bf16[64,2048]{1,0:T(8,128)(2,1)S(1)}, u32[]{:S(2)}, u32[]{:S(2)}) collective-permute-start(bf16[64,2048]{1,0:T(8,128)(2,1)S(1)} %collective-permute-done.4.refs_3_), channel_id=1, source_target_pairs={{0,64},{1,65},{2,66},{3,67},{4,68},{5,69},{6,70},{7,71},{8,72},{9,... | collective-permute-start | bytes 786440 | tf_op jit(solution)/shard_map/ppermute | solution.py:156
  68.6 35.3 %copy-start.6 = (bf16[64,2048]{1,0:T(8,128)(2,1)}, bf16[64,2048]{1,0:T(8,128)(2,1)S(1)}, u32[]{:S(2)}) copy-start(bf16[64,2048]{1,0:T(8,128)(2,1)S(1)} %collective-permute-done.7.refs_6_) | copy-start | bytes 786436
  68.6 13.0 %collective-permute-start.11 = (bf16[64,2048]{1,0:T(8,128)(2,1)S(1)}, bf16[64,2048]{1,0:T(8,128)(2,1)S(1)}, u32[]{:S(2)}, u32[]{:S(2)}) collective-permute-start(bf16[64,2048]{1,0:T(8,128)(2,1)S(1)} %collective-permute-done.7.refs_6_), channel_id=1, source_target_pairs={{0,64},{1,65},{2,66},{3,67},{4,68},{5,69},{6,70},{7,71},{8,72},{9,... | collective-permute-start | bytes 786440 | tf_op jit(solution)/shard_map/ppermute | solution.py:156
  72.7 31.2 %copy-start.7 = (bf16[64,2048]{1,0:T(8,128)(2,1)}, bf16[64,2048]{1,0:T(8,128)(2,1)S(1)}, u32[]{:S(2)}) copy-start(bf16[64,2048]{1,0:T(8,128)(2,1)S(1)} %collective-permute-done.10.refs_9_) | copy-start | bytes 786436
  72.7 13.9 %collective-permute-start.14 = (bf16[64,2048]{1,0:T(8,128)(2,1)S(1)}, bf16[64,2048]{1,0:T(8,128)(2,1)S(1)}, u32[]{:S(2)}, u32[]{:S(2)}) collective-permute-start(bf16[64,2048]{1,0:T(8,128)(2,1)S(1)} %collective-permute-done.10.refs_9_), channel_id=1, source_target_pairs={{0,448},{1,449},{2,450},{3,451},{4,452},{5,453},{6,454},{7,455},{8... | collective-permute-start | bytes 786440 | tf_op jit(solution)/shard_map/ppermute | solution.py:156
  75.7 28.2 %copy-start.8 = (bf16[64,2048]{1,0:T(8,128)(2,1)}, bf16[64,2048]{1,0:T(8,128)(2,1)S(1)}, u32[]{:S(2)}) copy-start(bf16[64,2048]{1,0:T(8,128)(2,1)S(1)} %collective-permute-done.9.refs_8_) | copy-start | bytes 786436
  75.8 13.0 %collective-permute-start.13 = (bf16[64,2048]{1,0:T(8,128)(2,1)S(1)}, bf16[64,2048]{1,0:T(8,128)(2,1)S(1)}, u32[]{:S(2)}, u32[]{:S(2)}) collective-permute-start(bf16[64,2048]{1,0:T(8,128)(2,1)S(1)} %collective-permute-done.9.refs_8_), channel_id=1, source_target_pairs={{0,448},{1,449},{2,450},{3,451},{4,452},{5,453},{6,454},{7,455},{8... | collective-permute-start | bytes 786440 | tf_op jit(solution)/shard_map/ppermute | solution.py:156
  79.7 24.2 %copy-start.9 = (bf16[64,2048]{1,0:T(8,128)(2,1)}, bf16[64,2048]{1,0:T(8,128)(2,1)S(1)}, u32[]{:S(2)}) copy-start(bf16[64,2048]{1,0:T(8,128)(2,1)S(1)} %collective-permute-done.8.refs_7_) | copy-start | bytes 786436
  79.7 11.1 %collective-permute-start.12 = (bf16[64,2048]{1,0:T(8,128)(2,1)S(1)}, bf16[64,2048]{1,0:T(8,128)(2,1)S(1)}, u32[]{:S(2)}, u32[]{:S(2)}) collective-permute-start(bf16[64,2048]{1,0:T(8,128)(2,1)S(1)} %collective-permute-done.8.refs_7_), channel_id=1, source_target_pairs={{0,64},{1,65},{2,66},{3,67},{4,68},{5,69},{6,70},{7,71},{8,72},{9,... | collective-permute-start | bytes 786440 | tf_op jit(solution)/shard_map/ppermute | solution.py:156
  81.6 22.3 %copy-start.10 = (bf16[64,2048]{1,0:T(8,128)(2,1)}, bf16[64,2048]{1,0:T(8,128)(2,1)S(1)}, u32[]{:S(2)}) copy-start(bf16[64,2048]{1,0:T(8,128)(2,1)S(1)} %collective-permute-done.11.refs_10_) | copy-start | bytes 786436
  81.7 11.9 %collective-permute-start.15 = (bf16[64,2048]{1,0:T(8,128)(2,1)S(1)}, bf16[64,2048]{1,0:T(8,128)(2,1)S(1)}, u32[]{:S(2)}, u32[]{:S(2)}) collective-permute-start(bf16[64,2048]{1,0:T(8,128)(2,1)S(1)} %collective-permute-done.11.refs_10_), channel_id=1, source_target_pairs={{0,64},{1,65},{2,66},{3,67},{4,68},{5,69},{6,70},{7,71},{8,72},{9,... | collective-permute-start | bytes 786440 | tf_op jit(solution)/shard_map/ppermute | solution.py:156
  86.6 17.3 %copy-start.11 = (bf16[64,2048]{1,0:T(8,128)(2,1)}, bf16[64,2048]{1,0:T(8,128)(2,1)S(1)}, u32[]{:S(2)}) copy-start(bf16[64,2048]{1,0:T(8,128)(2,1)S(1)} %collective-permute-done.14.refs_13_) | copy-start | bytes 786436
  86.6 8.4 %collective-permute-start.16 = (bf16[64,2048]{1,0:T(8,128)(2,1)S(1)}, bf16[64,2048]{1,0:T(8,128)(2,1)}, u32[]{:S(2)}, u32[]{:S(2)}) collective-permute-start(bf16[64,2048]{1,0:T(8,128)(2,1)S(1)} %collective-permute-done.14.refs_13_), channel_id=1, source_target_pairs={{0,448},{1,449},{2,450},{3,451},{4,452},{5,453},{6,454},{7,455},{8... | collective-permute-start | bytes 786440 | tf_op jit(solution)/shard_map/ppermute | solution.py:156
  88.8 15.2 %copy-start.12 = (bf16[64,2048]{1,0:T(8,128)(2,1)}, bf16[64,2048]{1,0:T(8,128)(2,1)S(1)}, u32[]{:S(2)}) copy-start(bf16[64,2048]{1,0:T(8,128)(2,1)S(1)} %collective-permute-done.13.refs_12_) | copy-start | bytes 786436
  90.8 2.8 %copy-start.13 = (bf16[64,2048]{1,0:T(8,128)(2,1)}, bf16[64,2048]{1,0:T(8,128)(2,1)S(1)}, u32[]{:S(2)}) copy-start(bf16[64,2048]{1,0:T(8,128)(2,1)S(1)} %collective-permute-done.12.refs_11_) | copy-start | bytes 786436
  93.6 0.7 copy-start.14
  110.4 17.7 %collective-permute-start.17 = (bf16[512,512]{1,0:T(8,128)(2,1)}, bf16[512,512]{1,0:T(8,128)(2,1)S(1)}, u32[]{:S(2)}, u32[]{:S(2)}) collective-permute-start(bf16[512,512]{1,0:T(8,128)(2,1)} %shard_map.29), channel_id=1, source_target_pairs={{0,1},{1,0},{2,3},{3,2},{4,5},{5,4},{6,7},{7,6},{8,9},{9,8},{10,11... | collective-permute-start | bytes 1572872 | tf_op jit(solution)/shard_map/ppermute | solution.py:156
Sparse Core Ops, SparseCore 0:
  33.2 70.5 all-gather.1

commit v12 on v11

--- a/solution.py
+++ b/solution.py
@@ -78,16 +78,17 @@
     places = [pl.ds(place(d), SUB) for d in steps]
     copies = []
     for k in range(blocks):
+        part, start = divmod(k * DEPTH, samples // 2)
+        deep = pl.multiple_of((part ^ xl) * (samples // 2) + start, DEPTH)
         copies.append(
             [
                 pltpu.make_async_copy(
-                    rows_hbm.at[pl.ds(first, HALF), pl.ds(k * DEPTH, DEPTH)],
+                    rows_hbm.at[pl.ds(first, HALF), pl.ds(deep, DEPTH)],
                     rows.at[k],
                     sem.at[k, len(steps)],
                 )
             ]
         )
-        part, start = divmod(k * DEPTH, samples // 2)
         for i, to in enumerate(places):
             copies[k].append(
                 pltpu.make_async_copy(
@@ -150,7 +151,7 @@
 
 
 def on_device(trajectories, pair_live):
-    xl, z, xh = (lax.axis_index(name) for name in ("xl", "z", "xh"))
+    z, xh = lax.axis_index("z"), lax.axis_index("xh")
 
     def send(value, to):
         return lax.ppermute(value, AX, to)
@@ -159,11 +160,7 @@
     early = send(trajectories, col_pairs(0))
     late = send(trajectories, col_pairs(1))
     early, late, other = lax.optimization_barrier((early, late, other))
-    rows = jnp.where(
-        xl == 0,
-        jnp.concatenate([trajectories, other], axis=1),
-        jnp.concatenate([other, trajectories], axis=1),
-    )
+    rows = jnp.concatenate([trajectories, other], axis=1)
     rows = lax.all_gather(rows, ("z", "a"), axis=0, tiled=True)
 
     steps, chunks = [0], [early, late]

time: 137 us -> 136 us (level)
  starting transfers between devices: 72.8 us -> 69.1 us
  waiting for transfers between devices: 32.4 us -> 35.2 us
    ppermute x18, starting transfers between devices: 72.8 us -> 69.1 us  [send(): return lax.ppermute(value, AX, to)]
    ppermute x18, waiting for transfers between devices: 23.6 us -> 26.5 us  [send(): return lax.ppermute(value, AX, to)]
    select_n x1 -> x0, other arithmetic: 2.04 us -> none  [on_device(): jnp.where(xl == 0, jnp.concatenate([trajectories, other], axis=1), jnp.co...]
    concatenate x0 -> x1, other arithmetic: none -> 1.87 us  [on_device(): rows = jnp.concatenate([trajectories, other], axis=1)]
where the time goes in v12:
time: 136 us; the launch traced here: 135 us
  starting transfers between devices  69.1 us (51%)
  waiting for transfers between devices  35.2 us (26%)
  between operations  13.8 us (10%)
  Pallas kernels  13.1 us (10%)
  other arithmetic  1.87 us (1%)
  local copies, waits for them, and re-layouts  1.61 us (1%)
    ppermute x18, starting transfers between devices, send(): return lax.ppermute(value, AX, to)  69.1 us
    ppermute x18, waiting for transfers between devices, send(): return lax.ppermute(value, AX, to)  26.5 us
    pallas_call x2, Pallas kernels, gram_tile(): pl.pallas_call(functools.partial(gram_kernel, keep, steps), out_shape=jax...  13.1 us
    all_gather x1, waiting for transfers between devices, on_device(): rows = lax.all_gather(rows, ('z', 'a'), axis=0, tiled=True)  8.7 us
  transfers between devices with their start and end apart: 19, of which 7 were waited for; matrix products, arithmetic and copies ran while one was open for 0% of the time, Pallas kernels for 5%

profile of v12, /device:TPU:6, one launch (start us, length us, event | category | flops | bytes accessed | tf_op | source)
XLA Modules:
  0.0 134.7 jit_solution(10546885354226879156)
XLA Ops:
  6.5 0.0 all-gather.2.cloned.1.call-start
  6.5 2.7 %collective-permute-start = (bf16[64,2048]{1,0:T(8,128)(2,1)}, bf16[64,2048]{1,0:T(8,128)(2,1)S(1)}, u32[]{:S(2)}, u32[]{:S(2)}) collective-permute-start(bf16[64,2048]{1,0:T(8,128)(2,1)} %param.2), channel_id=1, source_target_pairs={{0,0},{1,32},{2,256},{3,288},{4,64},{5,96},{6,448},{7,480},{8,128}... | collective-permute-start | bytes 786440 | tf_op jit(solution)/shard_map/ppermute | solution.py:157
  9.3 7.1 %collective-permute-start.1 = (bf16[64,2048]{1,0:T(8,128)(2,1)}, bf16[64,2048]{1,0:T(8,128)(2,1)S(1)}, u32[]{:S(2)}, u32[]{:S(2)}) collective-permute-start(bf16[64,2048]{1,0:T(8,128)(2,1)} %param.2), channel_id=1, source_target_pairs={{0,32},{1,0},{2,288},{3,256},{4,96},{5,64},{6,480},{7,448},{8,160}... | collective-permute-start | bytes 786440 | tf_op jit(solution)/shard_map/ppermute | solution.py:157
  16.4 2.6 %collective-permute-start.2 = (bf16[64,2048]{1,0:T(8,128)(2,1)}, bf16[64,2048]{1,0:T(8,128)(2,1)S(1)}, u32[]{:S(2)}, u32[]{:S(2)}) collective-permute-start(bf16[64,2048]{1,0:T(8,128)(2,1)} %param.2), channel_id=1, source_target_pairs={{0,1},{1,0},{2,3},{3,2},{4,5},{5,4},{6,7},{7,6},{8,9},{9,8},{10,11... | collective-permute-start | bytes 786440 | tf_op jit(solution)/shard_map/ppermute | solution.py:157
  19.0 4.9 %collective-permute-done.refs_0_ = bf16[64,2048]{1,0:T(8,128)(2,1)S(1)} collective-permute-done((bf16[64,2048]{1,0:T(8,128)(2,1)}, bf16[64,2048]{1,0:T(8,128)(2,1)S(1)}, u32[]{:S(2)}, u32[]{:S(2)}) %collective-permute-start) | collective-permute-done | bytes 262176 | tf_op jit(solution)/shard_map/ppermute | solution.py:157
  23.9 8.8 %collective-permute-done.1.refs_1_ = bf16[64,2048]{1,0:T(8,128)(2,1)S(1)} collective-permute-done((bf16[64,2048]{1,0:T(8,128)(2,1)}, bf16[64,2048]{1,0:T(8,128)(2,1)S(1)}, u32[]{:S(2)}, u32[]{:S(2)}) %collective-permute-start.1) | collective-permute-done | bytes 262176 | tf_op jit(solution)/shard_map/ppermute | solution.py:157
  32.7 0.0 collective-permute-done.2
  32.7 1.9 %pad_maximum_fusion = bf16[64,4096]{1,0:T(8,128)(2,1)} fusion(bf16[64,2048]{1,0:T(8,128)(2,1)S(1)} %collective-permute-done.2, bf16[64,2048]{1,0:T(8,128)(2,1)} %param.2), kind=kLoop, calls=%fused_computation | loop fusion | flops 1048576 | bytes 1048576 | tf_op jit(solution)/shard_map/concatenate | solution.py:163
  34.6 0.0 all-gather.2.cloned.1.call-update
  34.6 1.9 %collective-permute-start.3 = (bf16[64,2048]{1,0:T(8,128)(2,1)S(1)}, bf16[64,2048]{1,0:T(8,128)(2,1)S(1)}, u32[]{:S(2)}, u32[]{:S(2)}) collective-permute-start(bf16[64,2048]{1,0:T(8,128)(2,1)S(1)} %collective-permute-done.refs_0_), channel_id=1, source_target_pairs={{0,64},{1,65},{2,66},{3,67},{4,68},{5,69},{6,70},{7,71},{8,72},{9,... | collective-permute-start | bytes 786440 | tf_op jit(solution)/shard_map/ppermute | solution.py:157
  36.6 9.0 %collective-permute-start.6 = (bf16[64,2048]{1,0:T(8,128)(2,1)S(1)}, bf16[64,2048]{1,0:T(8,128)(2,1)S(1)}, u32[]{:S(2)}, u32[]{:S(2)}) collective-permute-start(bf16[64,2048]{1,0:T(8,128)(2,1)S(1)} %collective-permute-done.1.refs_1_), channel_id=1, source_target_pairs={{0,448},{1,449},{2,450},{3,451},{4,452},{5,453},{6,454},{7,455},{8... | collective-permute-start | bytes 786440 | tf_op jit(solution)/shard_map/ppermute | solution.py:157
  45.6 1.9 %collective-permute-start.4 = (bf16[64,2048]{1,0:T(8,128)(2,1)S(1)}, bf16[64,2048]{1,0:T(8,128)(2,1)S(1)}, u32[]{:S(2)}, u32[]{:S(2)}) collective-permute-start(bf16[64,2048]{1,0:T(8,128)(2,1)S(1)} %collective-permute-done.1.refs_1_), channel_id=1, source_target_pairs={{0,64},{1,65},{2,66},{3,67},{4,68},{5,69},{6,70},{7,71},{8,72},{9,... | collective-permute-start | bytes 786440 | tf_op jit(solution)/shard_map/ppermute | solution.py:157
  47.5 5.1 %collective-permute-start.5 = (bf16[64,2048]{1,0:T(8,128)(2,1)S(1)}, bf16[64,2048]{1,0:T(8,128)(2,1)S(1)}, u32[]{:S(2)}, u32[]{:S(2)}) collective-permute-start(bf16[64,2048]{1,0:T(8,128)(2,1)S(1)} %collective-permute-done.refs_0_), channel_id=1, source_target_pairs={{0,448},{1,449},{2,450},{3,451},{4,452},{5,453},{6,454},{7,455},{8... | collective-permute-start | bytes 786440 | tf_op jit(solution)/shard_map/ppermute | solution.py:157
  52.6 0.0 collective-permute-done.3.refs_2_
  52.6 0.0 copy-start.2
  52.7 1.9 %collective-permute-start.7 = (bf16[64,2048]{1,0:T(8,128)(2,1)S(1)}, bf16[64,2048]{1,0:T(8,128)(2,1)S(1)}, u32[]{:S(2)}, u32[]{:S(2)}) collective-permute-start(bf16[64,2048]{1,0:T(8,128)(2,1)S(1)} %collective-permute-done.3.refs_2_), channel_id=1, source_target_pairs={{0,64},{1,65},{2,66},{3,67},{4,68},{5,69},{6,70},{7,71},{8,72},{9,... | collective-permute-start | bytes 786440 | tf_op jit(solution)/shard_map/ppermute | solution.py:157
  54.6 0.0 collective-permute-done.6.refs_5_
  54.6 0.0 copy-start.3
  54.6 5.1 %collective-permute-start.10 = (bf16[64,2048]{1,0:T(8,128)(2,1)S(1)}, bf16[64,2048]{1,0:T(8,128)(2,1)S(1)}, u32[]{:S(2)}, u32[]{:S(2)}) collective-permute-start(bf16[64,2048]{1,0:T(8,128)(2,1)S(1)} %collective-permute-done.6.refs_5_), channel_id=1, source_target_pairs={{0,448},{1,449},{2,450},{3,451},{4,452},{5,453},{6,454},{7,455},{8... | collective-permute-start | bytes 786440 | tf_op jit(solution)/shard_map/ppermute | solution.py:157
  59.7 0.0 collective-permute-done.4.refs_3_
  59.8 0.0 copy-start.4
  59.8 3.3 %collective-permute-start.8 = (bf16[64,2048]{1,0:T(8,128)(2,1)S(1)}, bf16[64,2048]{1,0:T(8,128)(2,1)S(1)}, u32[]{:S(2)}, u32[]{:S(2)}) collective-permute-start(bf16[64,2048]{1,0:T(8,128)(2,1)S(1)} %collective-permute-done.4.refs_3_), channel_id=1, source_target_pairs={{0,64},{1,65},{2,66},{3,67},{4,68},{5,69},{6,70},{7,71},{8,72},{9,... | collective-permute-start | bytes 786440 | tf_op jit(solution)/shard_map/ppermute | solution.py:157
  63.1 0.0 collective-permute-done.5.refs_4_
  63.1 0.0 copy-start.5
  63.1 3.7 %collective-permute-start.9 = (bf16[64,2048]{1,0:T(8,128)(2,1)S(1)}, bf16[64,2048]{1,0:T(8,128)(2,1)S(1)}, u32[]{:S(2)}, u32[]{:S(2)}) collective-permute-start(bf16[64,2048]{1,0:T(8,128)(2,1)S(1)} %collective-permute-done.5.refs_4_), channel_id=1, source_target_pairs={{0,448},{1,449},{2,450},{3,451},{4,452},{5,453},{6,454},{7,455},{8... | collective-permute-start | bytes 786440 | tf_op jit(solution)/shard_map/ppermute | solution.py:157
  66.9 0.0 collective-permute-done.7.refs_6_
  66.9 0.0 copy-start.6
  66.9 3.3 %collective-permute-start.11 = (bf16[64,2048]{1,0:T(8,128)(2,1)S(1)}, bf16[64,2048]{1,0:T(8,128)(2,1)S(1)}, u32[]{:S(2)}, u32[]{:S(2)}) collective-permute-start(bf16[64,2048]{1,0:T(8,128)(2,1)S(1)} %collective-permute-done.7.refs_6_), channel_id=1, source_target_pairs={{0,64},{1,65},{2,66},{3,67},{4,68},{5,69},{6,70},{7,71},{8,72},{9,... | collective-permute-start | bytes 786440 | tf_op jit(solution)/shard_map/ppermute | solution.py:157
  70.2 0.0 collective-permute-done.10.refs_9_
  70.2 0.0 copy-start.7
  70.2 3.7 %collective-permute-start.14 = (bf16[64,2048]{1,0:T(8,128)(2,1)S(1)}, bf16[64,2048]{1,0:T(8,128)(2,1)S(1)}, u32[]{:S(2)}, u32[]{:S(2)}) collective-permute-start(bf16[64,2048]{1,0:T(8,128)(2,1)S(1)} %collective-permute-done.10.refs_9_), channel_id=1, source_target_pairs={{0,448},{1,449},{2,450},{3,451},{4,452},{5,453},{6,454},{7,455},{8... | collective-permute-start | bytes 786440 | tf_op jit(solution)/shard_map/ppermute | solution.py:157
  74.0 0.0 collective-permute-done.8.refs_7_
  74.0 0.0 copy-start.8
  74.0 3.3 %collective-permute-start.12 = (bf16[64,2048]{1,0:T(8,128)(2,1)S(1)}, bf16[64,2048]{1,0:T(8,128)(2,1)S(1)}, u32[]{:S(2)}, u32[]{:S(2)}) collective-permute-start(bf16[64,2048]{1,0:T(8,128)(2,1)S(1)} %collective-permute-done.8.refs_7_), channel_id=1, source_target_pairs={{0,64},{1,65},{2,66},{3,67},{4,68},{5,69},{6,70},{7,71},{8,72},{9,... | collective-permute-start | bytes 786440 | tf_op jit(solution)/shard_map/ppermute | solution.py:157
  77.3 0.0 collective-permute-done.9.refs_8_
  77.3 0.0 copy-start.9
  77.3 3.7 %collective-permute-start.13 = (bf16[64,2048]{1,0:T(8,128)(2,1)S(1)}, bf16[64,2048]{1,0:T(8,128)(2,1)S(1)}, u32[]{:S(2)}, u32[]{:S(2)}) collective-permute-start(bf16[64,2048]{1,0:T(8,128)(2,1)S(1)} %collective-permute-done.9.refs_8_), channel_id=1, source_target_pairs={{0,448},{1,449},{2,450},{3,451},{4,452},{5,453},{6,454},{7,455},{8... | collective-permute-start | bytes 786440 | tf_op jit(solution)/shard_map/ppermute | solution.py:157
  81.1 0.0 collective-permute-done.11.refs_10_
  81.1 0.0 copy-start.10
  81.1 3.3 %collective-permute-start.15 = (bf16[64,2048]{1,0:T(8,128)(2,1)S(1)}, bf16[64,2048]{1,0:T(8,128)(2,1)S(1)}, u32[]{:S(2)}, u32[]{:S(2)}) collective-permute-start(bf16[64,2048]{1,0:T(8,128)(2,1)S(1)} %collective-permute-done.11.refs_10_), channel_id=1, source_target_pairs={{0,64},{1,65},{2,66},{3,67},{4,68},{5,69},{6,70},{7,71},{8,72},{9,... | collective-permute-start | bytes 786440 | tf_op jit(solution)/shard_map/ppermute | solution.py:157
  84.4 0.0 collective-permute-done.14.refs_13_
  84.4 0.0 copy-start.11
  84.4 3.7 %collective-permute-start.16 = (bf16[64,2048]{1,0:T(8,128)(2,1)S(1)}, bf16[64,2048]{1,0:T(8,128)(2,1)}, u32[]{:S(2)}, u32[]{:S(2)}) collective-permute-start(bf16[64,2048]{1,0:T(8,128)(2,1)S(1)} %collective-permute-done.14.refs_13_), channel_id=1, source_target_pairs={{0,448},{1,449},{2,450},{3,451},{4,452},{5,453},{6,454},{7,455},{8... | collective-permute-start | bytes 786440 | tf_op jit(solution)/shard_map/ppermute | solution.py:157
  88.2 0.0 collective-permute-done.12.refs_11_
  88.2 0.0 copy-start.12
  88.2 0.3 collective-permute-done.13.refs_12_
  88.5 2.0 %collective-permute-done.15.refs_14_ = bf16[64,2048]{1,0:T(8,128)(2,1)S(1)} collective-permute-done((bf16[64,2048]{1,0:T(8,128)(2,1)S(1)}, bf16[64,2048]{1,0:T(8,128)(2,1)S(1)}, u32[]{:S(2)}, u32[]{:S(2)}) %collective-permute-start.15) | collective-permute-done | bytes 262176 | tf_op jit(solution)/shard_map/ppermute | solution.py:157
  90.6 0.0 copy-done.13
  90.6 0.7 copy-done.14
  91.3 2.7 %collective-permute-done.16.refs_15_ = bf16[64,2048]{1,0:T(8,128)(2,1)} collective-permute-done((bf16[64,2048]{1,0:T(8,128)(2,1)S(1)}, bf16[64,2048]{1,0:T(8,128)(2,1)}, u32[]{:S(2)}, u32[]{:S(2)}) %collective-permute-start.16) | collective-permute-done | bytes 262176 | tf_op jit(solution)/shard_map/ppermute | solution.py:157
  94.0 8.7 %all-gather.2.cloned.1.call-done.rows_hbm = bf16[1024,4096]{1,0:T(8,128)(2,1)} async-done(((bf16[64,4096]{1,0:T(8,128)(2,1)}), bf16[1024,4096]{1,0:T(8,128)(2,1)}) %all-gather.2.cloned.1.call-update) | async-done | bytes 8388624 | tf_op jit(solution)/shard_map/all_gather | solution.py:164
  102.7 0.0 copy-done
  102.7 0.0 copy-done.1
  102.7 0.0 copy-done.2
  102.7 0.0 copy-done.3
  102.7 0.0 copy-done.4
  102.7 0.0 copy-done.5
  102.8 0.0 copy-done.6
  102.8 0.0 copy-done.7
  102.8 6.5 %shard_map.29 = bf16[512,512]{1,0:T(8,128)(2,1)} custom-call(s32[16,16]{1,0:T(8,128)} %live_ref.3, bf16[1024,4096]{1,0:T(8,128)(2,1)} %all-gather.2.cloned.1.call-done.rows_hbm, bf16[64,2048]{1,0:T(8,128)(2,1)} %copy-done, bf16[64,2048]{1,0:T(8,128)(2,1)} %copy-done.1, bf16[64,2048]{1,0:T(8,128)(2,1)} %copy-done.2, bf16[64,2048]{1,0:T(8,128)(2,1)} %copy-done.4, ...), custom_call_target="tpu_custom_call" | custom-call | flops 2147483648 | bytes 9437184 | tf_op jit(solution)/shard_map/pallas_call | solution.py:130
  109.3 3.4 %collective-permute-start.17 = (bf16[512,512]{1,0:T(8,128)(2,1)}, bf16[512,512]{1,0:T(8,128)(2,1)S(1)}, u32[]{:S(2)}, u32[]{:S(2)}) collective-permute-start(bf16[512,512]{1,0:T(8,128)(2,1)} %shard_map.29), channel_id=1, source_target_pairs={{0,1},{1,0},{2,3},{3,2},{4,5},{5,4},{6,7},{7,6},{8,9},{9,8},{10,11... | collective-permute-start | bytes 1572872 | tf_op jit(solution)/shard_map/ppermute | solution.py:157
  112.7 6.6 %shard_map.28 = bf16[512,1024]{1,0:T(8,128)(2,1)} custom-call(s32[16,16]{1,0:T(8,128)} %live_ref.3, bf16[1024,4096]{1,0:T(8,128)(2,1)} %all-gather.2.cloned.1.call-done.rows_hbm, bf16[64,2048]{1,0:T(8,128)(2,1)} %copy-done, bf16[64,2048]{1,0:T(8,128)(2,1)} %copy-done.1, bf16[64,2048]{1,0:T(8,128)(2,1)} %copy-done.2, bf16[64,2048]{1,0:T(8,128)(2,1)} %copy-done.4, ...), custom_call_target="tpu_custom_call" | custom-call | flops 2147483648 | bytes 9437184 | tf_op jit(solution)/shard_map/pallas_call | solution.py:130
  119.3 7.7 %collective-permute-done.17 = bf16[512,512]{1,0:T(8,128)(2,1)S(1)} collective-permute-done((bf16[512,512]{1,0:T(8,128)(2,1)}, bf16[512,512]{1,0:T(8,128)(2,1)S(1)}, u32[]{:S(2)}, u32[]{:S(2)}) %collective-permute-start.17) | collective-permute-done | bytes 524320 | tf_op jit(solution)/shard_map/ppermute | solution.py:157
  127.0 0.8 constant_dynamic-update-slice_fusion
  (9 shorter events, 0.0 us)
Async XLA Ops:
  6.5 96.2 %all-gather.2.cloned.1.call-start = ((), (), s32[]{:S(2)}) async-start(), calls=%async_computation | async-start | bytes 8912896 | tf_op jit(solution)/shard_map/all_gather | solution.py:164
  6.5 17.4 %collective-permute-start = (bf16[64,2048]{1,0:T(8,128)(2,1)}, bf16[64,2048]{1,0:T(8,128)(2,1)S(1)}, u32[]{:S(2)}, u32[]{:S(2)}) collective-permute-start(bf16[64,2048]{1,0:T(8,128)(2,1)} %param.2), channel_id=1, source_target_pairs={{0,0},{1,32},{2,256},{3,288},{4,64},{5,96},{6,448},{7,480},{8,128}... | collective-permute-start | bytes 786440 | tf_op jit(solution)/shard_map/ppermute | solution.py:157
  9.3 23.4 %collective-permute-start.1 = (bf16[64,2048]{1,0:T(8,128)(2,1)}, bf16[64,2048]{1,0:T(8,128)(2,1)S(1)}, u32[]{:S(2)}, u32[]{:S(2)}) collective-permute-start(bf16[64,2048]{1,0:T(8,128)(2,1)} %param.2), channel_id=1, source_target_pairs={{0,32},{1,0},{2,288},{3,256},{4,96},{5,64},{6,480},{7,448},{8,160}... | collective-permute-start | bytes 786440 | tf_op jit(solution)/shard_map/ppermute | solution.py:157
  16.4 16.4 %collective-permute-start.2 = (bf16[64,2048]{1,0:T(8,128)(2,1)}, bf16[64,2048]{1,0:T(8,128)(2,1)S(1)}, u32[]{:S(2)}, u32[]{:S(2)}) collective-permute-start(bf16[64,2048]{1,0:T(8,128)(2,1)} %param.2), channel_id=1, source_target_pairs={{0,1},{1,0},{2,3},{3,2},{4,5},{5,4},{6,7},{7,6},{8,9},{9,8},{10,11... | collective-permute-start | bytes 786440 | tf_op jit(solution)/shard_map/ppermute | solution.py:157
  23.9 78.8 %copy-start = (bf16[64,2048]{1,0:T(8,128)(2,1)}, bf16[64,2048]{1,0:T(8,128)(2,1)S(1)}, u32[]{:S(2)}) copy-start(bf16[64,2048]{1,0:T(8,128)(2,1)S(1)} %collective-permute-done.refs_0_) | copy-start | bytes 786436
  32.7 70.0 %copy-start.1 = (bf16[64,2048]{1,0:T(8,128)(2,1)}, bf16[64,2048]{1,0:T(8,128)(2,1)S(1)}, u32[]{:S(2)}) copy-start(bf16[64,2048]{1,0:T(8,128)(2,1)S(1)} %collective-permute-done.1.refs_1_) | copy-start | bytes 786436
  34.6 18.0 %collective-permute-start.3 = (bf16[64,2048]{1,0:T(8,128)(2,1)S(1)}, bf16[64,2048]{1,0:T(8,128)(2,1)S(1)}, u32[]{:S(2)}, u32[]{:S(2)}) collective-permute-start(bf16[64,2048]{1,0:T(8,128)(2,1)S(1)} %collective-permute-done.refs_0_), channel_id=1, source_target_pairs={{0,64},{1,65},{2,66},{3,67},{4,68},{5,69},{6,70},{7,71},{8,72},{9,... | collective-permute-start | bytes 786440 | tf_op jit(solution)/shard_map/ppermute | solution.py:157
  36.6 18.0 %collective-permute-start.6 = (bf16[64,2048]{1,0:T(8,128)(2,1)S(1)}, bf16[64,2048]{1,0:T(8,128)(2,1)S(1)}, u32[]{:S(2)}, u32[]{:S(2)}) collective-permute-start(bf16[64,2048]{1,0:T(8,128)(2,1)S(1)} %collective-permute-done.1.refs_1_), channel_id=1, source_target_pairs={{0,448},{1,449},{2,450},{3,451},{4,452},{5,453},{6,454},{7,455},{8... | collective-permute-start | bytes 786440 | tf_op jit(solution)/shard_map/ppermute | solution.py:157
  45.6 14.2 %collective-permute-start.4 = (bf16[64,2048]{1,0:T(8,128)(2,1)S(1)}, bf16[64,2048]{1,0:T(8,128)(2,1)S(1)}, u32[]{:S(2)}, u32[]{:S(2)}) collective-permute-start(bf16[64,2048]{1,0:T(8,128)(2,1)S(1)} %collective-permute-done.1.refs_1_), channel_id=1, source_target_pairs={{0,64},{1,65},{2,66},{3,67},{4,68},{5,69},{6,70},{7,71},{8,72},{9,... | collective-permute-start | bytes 786440 | tf_op jit(solution)/shard_map/ppermute | solution.py:157
  47.5 15.6 %collective-permute-start.5 = (bf16[64,2048]{1,0:T(8,128)(2,1)S(1)}, bf16[64,2048]{1,0:T(8,128)(2,1)S(1)}, u32[]{:S(2)}, u32[]{:S(2)}) collective-permute-start(bf16[64,2048]{1,0:T(8,128)(2,1)S(1)} %collective-permute-done.refs_0_), channel_id=1, source_target_pairs={{0,448},{1,449},{2,450},{3,451},{4,452},{5,453},{6,454},{7,455},{8... | collective-permute-start | bytes 786440 | tf_op jit(solution)/shard_map/ppermute | solution.py:157
  52.6 50.1 %copy-start.2 = (bf16[64,2048]{1,0:T(8,128)(2,1)}, bf16[64,2048]{1,0:T(8,128)(2,1)S(1)}, u32[]{:S(2)}) copy-start(bf16[64,2048]{1,0:T(8,128)(2,1)S(1)} %collective-permute-done.3.refs_2_) | copy-start | bytes 786436
  52.7 14.2 %collective-permute-start.7 = (bf16[64,2048]{1,0:T(8,128)(2,1)S(1)}, bf16[64,2048]{1,0:T(8,128)(2,1)S(1)}, u32[]{:S(2)}, u32[]{:S(2)}) collective-permute-start(bf16[64,2048]{1,0:T(8,128)(2,1)S(1)} %collective-permute-done.3.refs_2_), channel_id=1, source_target_pairs={{0,64},{1,65},{2,66},{3,67},{4,68},{5,69},{6,70},{7,71},{8,72},{9,... | collective-permute-start | bytes 786440 | tf_op jit(solution)/shard_map/ppermute | solution.py:157
  54.6 48.1 %copy-start.3 = (bf16[64,2048]{1,0:T(8,128)(2,1)}, bf16[64,2048]{1,0:T(8,128)(2,1)S(1)}, u32[]{:S(2)}) copy-start(bf16[64,2048]{1,0:T(8,128)(2,1)S(1)} %collective-permute-done.6.refs_5_) | copy-start | bytes 786436
  54.6 15.6 %collective-permute-start.10 = (bf16[64,2048]{1,0:T(8,128)(2,1)S(1)}, bf16[64,2048]{1,0:T(8,128)(2,1)S(1)}, u32[]{:S(2)}, u32[]{:S(2)}) collective-permute-start(bf16[64,2048]{1,0:T(8,128)(2,1)S(1)} %collective-permute-done.6.refs_5_), channel_id=1, source_target_pairs={{0,448},{1,449},{2,450},{3,451},{4,452},{5,453},{6,454},{7,455},{8... | collective-permute-start | bytes 786440 | tf_op jit(solution)/shard_map/ppermute | solution.py:157
  59.8 43.0 %copy-start.4 = (bf16[64,2048]{1,0:T(8,128)(2,1)}, bf16[64,2048]{1,0:T(8,128)(2,1)S(1)}, u32[]{:S(2)}) copy-start(bf16[64,2048]{1,0:T(8,128)(2,1)S(1)} %collective-permute-done.4.refs_3_) | copy-start | bytes 786436
  59.8 14.2 %collective-permute-start.8 = (bf16[64,2048]{1,0:T(8,128)(2,1)S(1)}, bf16[64,2048]{1,0:T(8,128)(2,1)S(1)}, u32[]{:S(2)}, u32[]{:S(2)}) collective-permute-start(bf16[64,2048]{1,0:T(8,128)(2,1)S(1)} %collective-permute-done.4.refs_3_), channel_id=1, source_target_pairs={{0,64},{1,65},{2,66},{3,67},{4,68},{5,69},{6,70},{7,71},{8,72},{9,... | collective-permute-start | bytes 786440 | tf_op jit(solution)/shard_map/ppermute | solution.py:157
  63.1 39.6 %copy-start.5 = (bf16[64,2048]{1,0:T(8,128)(2,1)}, bf16[64,2048]{1,0:T(8,128)(2,1)S(1)}, u32[]{:S(2)}) copy-start(bf16[64,2048]{1,0:T(8,128)(2,1)S(1)} %collective-permute-done.5.refs_4_) | copy-start | bytes 786436
  63.1 14.2 %collective-permute-start.9 = (bf16[64,2048]{1,0:T(8,128)(2,1)S(1)}, bf16[64,2048]{1,0:T(8,128)(2,1)S(1)}, u32[]{:S(2)}, u32[]{:S(2)}) collective-permute-start(bf16[64,2048]{1,0:T(8,128)(2,1)S(1)} %collective-permute-done.5.refs_4_), channel_id=1, source_target_pairs={{0,448},{1,449},{2,450},{3,451},{4,452},{5,453},{6,454},{7,455},{8... | collective-permute-start | bytes 786440 | tf_op jit(solution)/shard_map/ppermute | solution.py:157
  66.9 35.9 %copy-start.6 = (bf16[64,2048]{1,0:T(8,128)(2,1)}, bf16[64,2048]{1,0:T(8,128)(2,1)S(1)}, u32[]{:S(2)}) copy-start(bf16[64,2048]{1,0:T(8,128)(2,1)S(1)} %collective-permute-done.7.refs_6_) | copy-start | bytes 786436
  66.9 14.2 %collective-permute-start.11 = (bf16[64,2048]{1,0:T(8,128)(2,1)S(1)}, bf16[64,2048]{1,0:T(8,128)(2,1)S(1)}, u32[]{:S(2)}, u32[]{:S(2)}) collective-permute-start(bf16[64,2048]{1,0:T(8,128)(2,1)S(1)} %collective-permute-done.7.refs_6_), channel_id=1, source_target_pairs={{0,64},{1,65},{2,66},{3,67},{4,68},{5,69},{6,70},{7,71},{8,72},{9,... | collective-permute-start | bytes 786440 | tf_op jit(solution)/shard_map/ppermute | solution.py:157
  70.2 32.6 %copy-start.7 = (bf16[64,2048]{1,0:T(8,128)(2,1)}, bf16[64,2048]{1,0:T(8,128)(2,1)S(1)}, u32[]{:S(2)}) copy-start(bf16[64,2048]{1,0:T(8,128)(2,1)S(1)} %collective-permute-done.10.refs_9_) | copy-start | bytes 786436
  70.2 14.2 %collective-permute-start.14 = (bf16[64,2048]{1,0:T(8,128)(2,1)S(1)}, bf16[64,2048]{1,0:T(8,128)(2,1)S(1)}, u32[]{:S(2)}, u32[]{:S(2)}) collective-permute-start(bf16[64,2048]{1,0:T(8,128)(2,1)S(1)} %collective-permute-done.10.refs_9_), channel_id=1, source_target_pairs={{0,448},{1,449},{2,450},{3,451},{4,452},{5,453},{6,454},{7,455},{8... | collective-permute-start | bytes 786440 | tf_op jit(solution)/shard_map/ppermute | solution.py:157
  74.0 28.8 %copy-start.8 = (bf16[64,2048]{1,0:T(8,128)(2,1)}, bf16[64,2048]{1,0:T(8,128)(2,1)S(1)}, u32[]{:S(2)}) copy-start(bf16[64,2048]{1,0:T(8,128)(2,1)S(1)} %collective-permute-done.8.refs_7_) | copy-start | bytes 786436
  74.0 14.2 %collective-permute-start.12 = (bf16[64,2048]{1,0:T(8,128)(2,1)S(1)}, bf16[64,2048]{1,0:T(8,128)(2,1)S(1)}, u32[]{:S(2)}, u32[]{:S(2)}) collective-permute-start(bf16[64,2048]{1,0:T(8,128)(2,1)S(1)} %collective-permute-done.8.refs_7_), channel_id=1, source_target_pairs={{0,64},{1,65},{2,66},{3,67},{4,68},{5,69},{6,70},{7,71},{8,72},{9,... | collective-permute-start | bytes 786440 | tf_op jit(solution)/shard_map/ppermute | solution.py:157
  77.3 25.5 %copy-start.9 = (bf16[64,2048]{1,0:T(8,128)(2,1)}, bf16[64,2048]{1,0:T(8,128)(2,1)S(1)}, u32[]{:S(2)}) copy-start(bf16[64,2048]{1,0:T(8,128)(2,1)S(1)} %collective-permute-done.9.refs_8_) | copy-start | bytes 786436
  77.3 11.2 %collective-permute-start.13 = (bf16[64,2048]{1,0:T(8,128)(2,1)S(1)}, bf16[64,2048]{1,0:T(8,128)(2,1)S(1)}, u32[]{:S(2)}, u32[]{:S(2)}) collective-permute-start(bf16[64,2048]{1,0:T(8,128)(2,1)S(1)} %collective-permute-done.9.refs_8_), channel_id=1, source_target_pairs={{0,448},{1,449},{2,450},{3,451},{4,452},{5,453},{6,454},{7,455},{8... | collective-permute-start | bytes 786440 | tf_op jit(solution)/shard_map/ppermute | solution.py:157
  81.1 21.7 %copy-start.10 = (bf16[64,2048]{1,0:T(8,128)(2,1)}, bf16[64,2048]{1,0:T(8,128)(2,1)S(1)}, u32[]{:S(2)}) copy-start(bf16[64,2048]{1,0:T(8,128)(2,1)S(1)} %collective-permute-done.11.refs_10_) | copy-start | bytes 786436
  81.1 9.5 %collective-permute-start.15 = (bf16[64,2048]{1,0:T(8,128)(2,1)S(1)}, bf16[64,2048]{1,0:T(8,128)(2,1)S(1)}, u32[]{:S(2)}, u32[]{:S(2)}) collective-permute-start(bf16[64,2048]{1,0:T(8,128)(2,1)S(1)} %collective-permute-done.11.refs_10_), channel_id=1, source_target_pairs={{0,64},{1,65},{2,66},{3,67},{4,68},{5,69},{6,70},{7,71},{8,72},{9,... | collective-permute-start | bytes 786440 | tf_op jit(solution)/shard_map/ppermute | solution.py:157
  84.4 18.4 %copy-start.11 = (bf16[64,2048]{1,0:T(8,128)(2,1)}, bf16[64,2048]{1,0:T(8,128)(2,1)S(1)}, u32[]{:S(2)}) copy-start(bf16[64,2048]{1,0:T(8,128)(2,1)S(1)} %collective-permute-done.14.refs_13_) | copy-start | bytes 786436
  84.4 9.6 %collective-permute-start.16 = (bf16[64,2048]{1,0:T(8,128)(2,1)S(1)}, bf16[64,2048]{1,0:T(8,128)(2,1)}, u32[]{:S(2)}, u32[]{:S(2)}) collective-permute-start(bf16[64,2048]{1,0:T(8,128)(2,1)S(1)} %collective-permute-done.14.refs_13_), channel_id=1, source_target_pairs={{0,448},{1,449},{2,450},{3,451},{4,452},{5,453},{6,454},{7,455},{8... | collective-permute-start | bytes 786440 | tf_op jit(solution)/shard_map/ppermute | solution.py:157
  88.2 14.6 %copy-start.12 = (bf16[64,2048]{1,0:T(8,128)(2,1)}, bf16[64,2048]{1,0:T(8,128)(2,1)S(1)}, u32[]{:S(2)}) copy-start(bf16[64,2048]{1,0:T(8,128)(2,1)S(1)} %collective-permute-done.12.refs_11_) | copy-start | bytes 786436
  88.5 2.0 %copy-start.13 = (bf16[64,2048]{1,0:T(8,128)(2,1)}, bf16[64,2048]{1,0:T(8,128)(2,1)S(1)}, u32[]{:S(2)}) copy-start(bf16[64,2048]{1,0:T(8,128)(2,1)S(1)} %collective-permute-done.13.refs_12_) | copy-start | bytes 786436
  90.6 0.7 copy-start.14
  109.3 17.7 %collective-permute-start.17 = (bf16[512,512]{1,0:T(8,128)(2,1)}, bf16[512,512]{1,0:T(8,128)(2,1)S(1)}, u32[]{:S(2)}, u32[]{:S(2)}) collective-permute-start(bf16[512,512]{1,0:T(8,128)(2,1)} %shard_map.29), channel_id=1, source_target_pairs={{0,1},{1,0},{2,3},{3,2},{4,5},{5,4},{6,7},{7,6},{8,9},{9,8},{10,11... | collective-permute-start | bytes 1572872 | tf_op jit(solution)/shard_map/ppermute | solution.py:157
Sparse Core Ops, SparseCore 0:
  34.8 67.9 all-gather.1

commit v13 on v12

--- a/solution.py
+++ b/solution.py
@@ -159,7 +159,7 @@
     other = send(trajectories, swap_lag())
     early = send(trajectories, col_pairs(0))
     late = send(trajectories, col_pairs(1))
-    early, late, other = lax.optimization_barrier((early, late, other))
+    early, other = lax.optimization_barrier((early, other))
     rows = jnp.concatenate([trajectories, other], axis=1)
     rows = lax.all_gather(rows, ("z", "a"), axis=0, tiled=True)
 

time: 136 us -> 136 us (level)
  the two profiles are of different devices: /device:TPU:6 before, /device:TPU:192 now
where the time goes in v13:
time: 136 us
  starting transfers between devices  85.6 us (63%)
  waiting for transfers between devices  19.6 us (14%)
  between operations  13.8 us (10%)
  Pallas kernels  13.1 us (10%)
  other arithmetic  1.87 us (1%)
  local copies, waits for them, and re-layouts  1.61 us (1%)
    ppermute x18, starting transfers between devices, send(): return lax.ppermute(value, AX, to)  85.6 us
    ppermute x18, waiting for transfers between devices, send(): return lax.ppermute(value, AX, to)  19.6 us
    pallas_call x2, Pallas kernels, gram_tile(): pl.pallas_call(functools.partial(gram_kernel, keep, steps), out_shape=jax...  13.1 us
  transfers between devices with their start and end apart: 19, of which 6 were waited for; matrix products, arithmetic and copies ran while one was open for 0% of the time, Pallas kernels for 5%

profile of v13, /device:TPU:192, one launch (start us, length us, event | category | flops | bytes accessed | tf_op | source)
XLA Modules:
  0.0 135.6 jit_solution(15073080300147649461)
XLA Ops:
  6.5 0.0 all-gather.2.cloned.1.call-start
  6.5 2.8 %collective-permute-start = (bf16[64,2048]{1,0:T(8,128)(2,1)}, bf16[64,2048]{1,0:T(8,128)(2,1)S(1)}, u32[]{:S(2)}, u32[]{:S(2)}) collective-permute-start(bf16[64,2048]{1,0:T(8,128)(2,1)} %param.2), channel_id=1, source_target_pairs={{0,0},{1,32},{2,256},{3,288},{4,64},{5,96},{6,448},{7,480},{8,128}... | collective-permute-start | bytes 786440 | tf_op jit(solution)/shard_map/ppermute | solution.py:157
  9.3 4.9 %collective-permute-start.1 = (bf16[64,2048]{1,0:T(8,128)(2,1)}, bf16[64,2048]{1,0:T(8,128)(2,1)S(1)}, u32[]{:S(2)}, u32[]{:S(2)}) collective-permute-start(bf16[64,2048]{1,0:T(8,128)(2,1)} %param.2), channel_id=1, source_target_pairs={{0,1},{1,0},{2,3},{3,2},{4,5},{5,4},{6,7},{7,6},{8,9},{9,8},{10,11... | collective-permute-start | bytes 786440 | tf_op jit(solution)/shard_map/ppermute | solution.py:157
  14.2 7.5 %collective-permute-done.refs_0_ = bf16[64,2048]{1,0:T(8,128)(2,1)S(1)} collective-permute-done((bf16[64,2048]{1,0:T(8,128)(2,1)}, bf16[64,2048]{1,0:T(8,128)(2,1)S(1)}, u32[]{:S(2)}, u32[]{:S(2)}) %collective-permute-start) | collective-permute-done | bytes 262176 | tf_op jit(solution)/shard_map/ppermute | solution.py:157
  21.7 0.0 collective-permute-done.1
  21.7 1.9 %pad_maximum_fusion = bf16[64,4096]{1,0:T(8,128)(2,1)} fusion(bf16[64,2048]{1,0:T(8,128)(2,1)S(1)} %collective-permute-done.1, bf16[64,2048]{1,0:T(8,128)(2,1)} %param.2), kind=kLoop, calls=%fused_computation | loop fusion | flops 1048576 | bytes 1048576 | tf_op jit(solution)/shard_map/concatenate | solution.py:163
  23.6 0.0 all-gather.2.cloned.1.call-update
  23.6 12.0 %collective-permute-start.2 = (bf16[64,2048]{1,0:T(8,128)(2,1)}, bf16[64,2048]{1,0:T(8,128)(2,1)S(1)}, u32[]{:S(2)}, u32[]{:S(2)}) collective-permute-start(bf16[64,2048]{1,0:T(8,128)(2,1)} %param.2), channel_id=1, source_target_pairs={{0,32},{1,0},{2,288},{3,256},{4,96},{5,64},{6,480},{7,448},{8,160}... | collective-permute-start | bytes 786440 | tf_op jit(solution)/shard_map/ppermute | solution.py:157
  35.6 7.4 %collective-permute-start.3 = (bf16[64,2048]{1,0:T(8,128)(2,1)S(1)}, bf16[64,2048]{1,0:T(8,128)(2,1)S(1)}, u32[]{:S(2)}, u32[]{:S(2)}) collective-permute-start(bf16[64,2048]{1,0:T(8,128)(2,1)S(1)} %collective-permute-done.refs_0_), channel_id=1, source_target_pairs={{0,64},{1,65},{2,66},{3,67},{4,68},{5,69},{6,70},{7,71},{8,72},{9,... | collective-permute-start | bytes 786440 | tf_op jit(solution)/shard_map/ppermute | solution.py:157
  43.0 0.5 collective-permute-done.2.refs_1_
  43.5 12.9 %collective-permute-start.6 = (bf16[64,2048]{1,0:T(8,128)(2,1)S(1)}, bf16[64,2048]{1,0:T(8,128)(2,1)S(1)}, u32[]{:S(2)}, u32[]{:S(2)}) collective-permute-start(bf16[64,2048]{1,0:T(8,128)(2,1)S(1)} %collective-permute-done.2.refs_1_), channel_id=1, source_target_pairs={{0,448},{1,449},{2,450},{3,451},{4,452},{5,453},{6,454},{7,455},{8... | collective-permute-start | bytes 786440 | tf_op jit(solution)/shard_map/ppermute | solution.py:157
  56.4 8.9 %collective-permute-start.5 = (bf16[64,2048]{1,0:T(8,128)(2,1)S(1)}, bf16[64,2048]{1,0:T(8,128)(2,1)S(1)}, u32[]{:S(2)}, u32[]{:S(2)}) collective-permute-start(bf16[64,2048]{1,0:T(8,128)(2,1)S(1)} %collective-permute-done.refs_0_), channel_id=1, source_target_pairs={{0,448},{1,449},{2,450},{3,451},{4,452},{5,453},{6,454},{7,455},{8... | collective-permute-start | bytes 786440 | tf_op jit(solution)/shard_map/ppermute | solution.py:157
  65.4 1.9 %collective-permute-start.4 = (bf16[64,2048]{1,0:T(8,128)(2,1)S(1)}, bf16[64,2048]{1,0:T(8,128)(2,1)S(1)}, u32[]{:S(2)}, u32[]{:S(2)}) collective-permute-start(bf16[64,2048]{1,0:T(8,128)(2,1)S(1)} %collective-permute-done.2.refs_1_), channel_id=1, source_target_pairs={{0,64},{1,65},{2,66},{3,67},{4,68},{5,69},{6,70},{7,71},{8,72},{9,... | collective-permute-start | bytes 786440 | tf_op jit(solution)/shard_map/ppermute | solution.py:157
  67.3 0.0 collective-permute-done.3.refs_2_
  67.3 0.0 copy-start.2
  67.3 1.9 %collective-permute-start.7 = (bf16[64,2048]{1,0:T(8,128)(2,1)S(1)}, bf16[64,2048]{1,0:T(8,128)(2,1)S(1)}, u32[]{:S(2)}, u32[]{:S(2)}) collective-permute-start(bf16[64,2048]{1,0:T(8,128)(2,1)S(1)} %collective-permute-done.3.refs_2_), channel_id=1, source_target_pairs={{0,64},{1,65},{2,66},{3,67},{4,68},{5,69},{6,70},{7,71},{8,72},{9,... | collective-permute-start | bytes 786440 | tf_op jit(solution)/shard_map/ppermute | solution.py:157
  69.3 0.0 collective-permute-done.6.refs_5_
  69.3 0.0 copy-start.3
  69.3 5.1 %collective-permute-start.10 = (bf16[64,2048]{1,0:T(8,128)(2,1)S(1)}, bf16[64,2048]{1,0:T(8,128)(2,1)S(1)}, u32[]{:S(2)}, u32[]{:S(2)}) collective-permute-start(bf16[64,2048]{1,0:T(8,128)(2,1)S(1)} %collective-permute-done.6.refs_5_), channel_id=1, source_target_pairs={{0,448},{1,449},{2,450},{3,451},{4,452},{5,453},{6,454},{7,455},{8... | collective-permute-start | bytes 786440 | tf_op jit(solution)/shard_map/ppermute | solution.py:157
  74.4 0.0 collective-permute-done.5.refs_4_
  74.4 0.0 copy-start.4
  74.4 3.9 %collective-permute-start.9 = (bf16[64,2048]{1,0:T(8,128)(2,1)S(1)}, bf16[64,2048]{1,0:T(8,128)(2,1)S(1)}, u32[]{:S(2)}, u32[]{:S(2)}) collective-permute-start(bf16[64,2048]{1,0:T(8,128)(2,1)S(1)} %collective-permute-done.5.refs_4_), channel_id=1, source_target_pairs={{0,448},{1,449},{2,450},{3,451},{4,452},{5,453},{6,454},{7,455},{8... | collective-permute-start | bytes 786440 | tf_op jit(solution)/shard_map/ppermute | solution.py:157
  78.4 0.0 collective-permute-done.4.refs_3_
  78.4 0.0 copy-start.5
  78.4 1.9 %collective-permute-start.8 = (bf16[64,2048]{1,0:T(8,128)(2,1)S(1)}, bf16[64,2048]{1,0:T(8,128)(2,1)S(1)}, u32[]{:S(2)}, u32[]{:S(2)}) collective-permute-start(bf16[64,2048]{1,0:T(8,128)(2,1)S(1)} %collective-permute-done.4.refs_3_), channel_id=1, source_target_pairs={{0,64},{1,65},{2,66},{3,67},{4,68},{5,69},{6,70},{7,71},{8,72},{9,... | collective-permute-start | bytes 786440 | tf_op jit(solution)/shard_map/ppermute | solution.py:157
  80.3 1.4 %collective-permute-done.7.refs_6_ = bf16[64,2048]{1,0:T(8,128)(2,1)S(1)} collective-permute-done((bf16[64,2048]{1,0:T(8,128)(2,1)S(1)}, bf16[64,2048]{1,0:T(8,128)(2,1)S(1)}, u32[]{:S(2)}, u32[]{:S(2)}) %collective-permute-start.7) | collective-permute-done | bytes 262176 | tf_op jit(solution)/shard_map/ppermute | solution.py:157
  81.7 1.9 %collective-permute-start.11 = (bf16[64,2048]{1,0:T(8,128)(2,1)S(1)}, bf16[64,2048]{1,0:T(8,128)(2,1)S(1)}, u32[]{:S(2)}, u32[]{:S(2)}) collective-permute-start(bf16[64,2048]{1,0:T(8,128)(2,1)S(1)} %collective-permute-done.7.refs_6_), channel_id=1, source_target_pairs={{0,64},{1,65},{2,66},{3,67},{4,68},{5,69},{6,70},{7,71},{8,72},{9,... | collective-permute-start | bytes 786440 | tf_op jit(solution)/shard_map/ppermute | solution.py:157
  83.6 0.0 collective-permute-done.10.refs_9_
  83.6 0.0 copy-start.7
  83.6 5.1 %collective-permute-start.14 = (bf16[64,2048]{1,0:T(8,128)(2,1)S(1)}, bf16[64,2048]{1,0:T(8,128)(2,1)S(1)}, u32[]{:S(2)}, u32[]{:S(2)}) collective-permute-start(bf16[64,2048]{1,0:T(8,128)(2,1)S(1)} %collective-permute-done.10.refs_9_), channel_id=1, source_target_pairs={{0,448},{1,449},{2,450},{3,451},{4,452},{5,453},{6,454},{7,455},{8... | collective-permute-start | bytes 786440 | tf_op jit(solution)/shard_map/ppermute | solution.py:157
  88.8 0.0 collective-permute-done.9.refs_8_
  88.8 0.0 copy-start.8
  88.8 2.6 %collective-permute-start.13 = (bf16[64,2048]{1,0:T(8,128)(2,1)S(1)}, bf16[64,2048]{1,0:T(8,128)(2,1)S(1)}, u32[]{:S(2)}, u32[]{:S(2)}) collective-permute-start(bf16[64,2048]{1,0:T(8,128)(2,1)S(1)} %collective-permute-done.9.refs_8_), channel_id=1, source_target_pairs={{0,448},{1,449},{2,450},{3,451},{4,452},{5,453},{6,454},{7,455},{8... | collective-permute-start | bytes 786440 | tf_op jit(solution)/shard_map/ppermute | solution.py:157
  91.4 0.0 collective-permute-done.8.refs_7_
  91.4 0.0 copy-start.9
  91.4 3.3 %collective-permute-start.12 = (bf16[64,2048]{1,0:T(8,128)(2,1)S(1)}, bf16[64,2048]{1,0:T(8,128)(2,1)S(1)}, u32[]{:S(2)}, u32[]{:S(2)}) collective-permute-start(bf16[64,2048]{1,0:T(8,128)(2,1)S(1)} %collective-permute-done.8.refs_7_), channel_id=1, source_target_pairs={{0,64},{1,65},{2,66},{3,67},{4,68},{5,69},{6,70},{7,71},{8,72},{9,... | collective-permute-start | bytes 786440 | tf_op jit(solution)/shard_map/ppermute | solution.py:157
  94.7 0.0 collective-permute-done.11.refs_10_
  94.7 0.0 copy-start.10
  94.7 1.9 %collective-permute-start.15 = (bf16[64,2048]{1,0:T(8,128)(2,1)S(1)}, bf16[64,2048]{1,0:T(8,128)(2,1)S(1)}, u32[]{:S(2)}, u32[]{:S(2)}) collective-permute-start(bf16[64,2048]{1,0:T(8,128)(2,1)S(1)} %collective-permute-done.11.refs_10_), channel_id=1, source_target_pairs={{0,64},{1,65},{2,66},{3,67},{4,68},{5,69},{6,70},{7,71},{8,72},{9,... | collective-permute-start | bytes 786440 | tf_op jit(solution)/shard_map/ppermute | solution.py:157
  96.6 0.0 collective-permute-done.14.refs_13_
  96.6 5.1 %collective-permute-start.16 = (bf16[64,2048]{1,0:T(8,128)(2,1)S(1)}, bf16[64,2048]{1,0:T(8,128)(2,1)}, u32[]{:S(2)}, u32[]{:S(2)}) collective-permute-start(bf16[64,2048]{1,0:T(8,128)(2,1)S(1)} %collective-permute-done.14.refs_13_), channel_id=1, source_target_pairs={{0,448},{1,449},{2,450},{3,451},{4,452},{5,453},{6,454},{7,455},{8... | collective-permute-start | bytes 786440 | tf_op jit(solution)/shard_map/ppermute | solution.py:157
  101.8 0.0 collective-permute-done.13.refs_12_
  101.8 0.0 copy-start.12
  101.8 1.5 %collective-permute-done.12.refs_11_ = bf16[64,2048]{1,0:T(8,128)(2,1)S(1)} collective-permute-done((bf16[64,2048]{1,0:T(8,128)(2,1)S(1)}, bf16[64,2048]{1,0:T(8,128)(2,1)S(1)}, u32[]{:S(2)}, u32[]{:S(2)}) %collective-permute-start.12) | collective-permute-done | bytes 262176 | tf_op jit(solution)/shard_map/ppermute | solution.py:157
  103.3 2.8 %collective-permute-done.15.refs_14_ = bf16[64,2048]{1,0:T(8,128)(2,1)S(1)} collective-permute-done((bf16[64,2048]{1,0:T(8,128)(2,1)S(1)}, bf16[64,2048]{1,0:T(8,128)(2,1)S(1)}, u32[]{:S(2)}, u32[]{:S(2)}) %collective-permute-start.15) | collective-permute-done | bytes 262176 | tf_op jit(solution)/shard_map/ppermute | solution.py:157
  106.1 0.7 copy-done.14
  106.9 0.0 collective-permute-done.16.refs_15_
  106.9 0.0 copy-done.1
  106.9 0.0 copy-done.2
  106.9 0.0 copy-done.3
  106.9 0.0 copy-done.4
  106.9 0.0 copy-done.5
  106.9 0.0 copy-done.6
  106.9 0.0 copy-done.7
  106.9 0.0 copy-done.8
  106.9 0.0 copy-done.9
  107.0 0.0 copy-done.10
  107.0 0.0 copy-done.11
  107.0 0.0 copy-done.12
  107.0 6.5 %shard_map.29 = bf16[512,512]{1,0:T(8,128)(2,1)} custom-call(s32[16,16]{1,0:T(8,128)} %live_ref.3, bf16[1024,4096]{1,0:T(8,128)(2,1)} %all-gather.2.cloned.1.call-done.rows_hbm, bf16[64,2048]{1,0:T(8,128)(2,1)} %copy-done, bf16[64,2048]{1,0:T(8,128)(2,1)} %copy-done.1, bf16[64,2048]{1,0:T(8,128)(2,1)} %copy-done.2, bf16[64,2048]{1,0:T(8,128)(2,1)} %copy-done.5, ...), custom_call_target="tpu_custom_call" | custom-call | flops 2147483648 | bytes 9437184 | tf_op jit(solution)/shard_map/pallas_call | solution.py:130
  113.5 1.9 %collective-permute-start.17 = (bf16[512,512]{1,0:T(8,128)(2,1)}, bf16[512,512]{1,0:T(8,128)(2,1)S(1)}, u32[]{:S(2)}, u32[]{:S(2)}) collective-permute-start(bf16[512,512]{1,0:T(8,128)(2,1)} %shard_map.29), channel_id=1, source_target_pairs={{0,1},{1,0},{2,3},{3,2},{4,5},{5,4},{6,7},{7,6},{8,9},{9,8},{10,11... | collective-permute-start | bytes 1572872 | tf_op jit(solution)/shard_map/ppermute | solution.py:157
  115.4 6.6 %shard_map.28 = bf16[512,1024]{1,0:T(8,128)(2,1)} custom-call(s32[16,16]{1,0:T(8,128)} %live_ref.3, bf16[1024,4096]{1,0:T(8,128)(2,1)} %all-gather.2.cloned.1.call-done.rows_hbm, bf16[64,2048]{1,0:T(8,128)(2,1)} %copy-done, bf16[64,2048]{1,0:T(8,128)(2,1)} %copy-done.1, bf16[64,2048]{1,0:T(8,128)(2,1)} %copy-done.2, bf16[64,2048]{1,0:T(8,128)(2,1)} %copy-done.5, ...), custom_call_target="tpu_custom_call" | custom-call | flops 2147483648 | bytes 9437184 | tf_op jit(solution)/shard_map/pallas_call | solution.py:130
  122.0 5.9 %collective-permute-done.17 = bf16[512,512]{1,0:T(8,128)(2,1)S(1)} collective-permute-done((bf16[512,512]{1,0:T(8,128)(2,1)}, bf16[512,512]{1,0:T(8,128)(2,1)S(1)}, u32[]{:S(2)}, u32[]{:S(2)}) %collective-permute-start.17) | collective-permute-done | bytes 524320 | tf_op jit(solution)/shard_map/ppermute | solution.py:157
  127.9 0.8 constant_dynamic-update-slice_fusion
  (9 shorter events, 0.0 us)
Async XLA Ops:
  6.5 100.3 %all-gather.2.cloned.1.call-start = ((), (), s32[]{:S(2)}) async-start(), calls=%async_computation | async-start | bytes 8912896 | tf_op jit(solution)/shard_map/all_gather | solution.py:164
  6.5 15.1 %collective-permute-start = (bf16[64,2048]{1,0:T(8,128)(2,1)}, bf16[64,2048]{1,0:T(8,128)(2,1)S(1)}, u32[]{:S(2)}, u32[]{:S(2)}) collective-permute-start(bf16[64,2048]{1,0:T(8,128)(2,1)} %param.2), channel_id=1, source_target_pairs={{0,0},{1,32},{2,256},{3,288},{4,64},{5,96},{6,448},{7,480},{8,128}... | collective-permute-start | bytes 786440 | tf_op jit(solution)/shard_map/ppermute | solution.py:157
  9.3 12.4 %collective-permute-start.1 = (bf16[64,2048]{1,0:T(8,128)(2,1)}, bf16[64,2048]{1,0:T(8,128)(2,1)S(1)}, u32[]{:S(2)}, u32[]{:S(2)}) collective-permute-start(bf16[64,2048]{1,0:T(8,128)(2,1)} %param.2), channel_id=1, source_target_pairs={{0,1},{1,0},{2,3},{3,2},{4,5},{5,4},{6,7},{7,6},{8,9},{9,8},{10,11... | collective-permute-start | bytes 786440 | tf_op jit(solution)/shard_map/ppermute | solution.py:157
  21.7 85.2 %copy-start = (bf16[64,2048]{1,0:T(8,128)(2,1)}, bf16[64,2048]{1,0:T(8,128)(2,1)S(1)}, u32[]{:S(2)}) copy-start(bf16[64,2048]{1,0:T(8,128)(2,1)S(1)} %collective-permute-done.refs_0_) | copy-start | bytes 786436
  23.6 19.9 %collective-permute-start.2 = (bf16[64,2048]{1,0:T(8,128)(2,1)}, bf16[64,2048]{1,0:T(8,128)(2,1)S(1)}, u32[]{:S(2)}, u32[]{:S(2)}) collective-permute-start(bf16[64,2048]{1,0:T(8,128)(2,1)} %param.2), channel_id=1, source_target_pairs={{0,32},{1,0},{2,288},{3,256},{4,96},{5,64},{6,480},{7,448},{8,160}... | collective-permute-start | bytes 786440 | tf_op jit(solution)/shard_map/ppermute | solution.py:157
  35.6 31.7 %collective-permute-start.3 = (bf16[64,2048]{1,0:T(8,128)(2,1)S(1)}, bf16[64,2048]{1,0:T(8,128)(2,1)S(1)}, u32[]{:S(2)}, u32[]{:S(2)}) collective-permute-start(bf16[64,2048]{1,0:T(8,128)(2,1)S(1)} %collective-permute-done.refs_0_), channel_id=1, source_target_pairs={{0,64},{1,65},{2,66},{3,67},{4,68},{5,69},{6,70},{7,71},{8,72},{9,... | collective-permute-start | bytes 786440 | tf_op jit(solution)/shard_map/ppermute | solution.py:157
  43.5 63.4 %copy-start.1 = (bf16[64,2048]{1,0:T(8,128)(2,1)}, bf16[64,2048]{1,0:T(8,128)(2,1)S(1)}, u32[]{:S(2)}) copy-start(bf16[64,2048]{1,0:T(8,128)(2,1)S(1)} %collective-permute-done.2.refs_1_) | copy-start | bytes 786436
  43.5 25.8 %collective-permute-start.6 = (bf16[64,2048]{1,0:T(8,128)(2,1)S(1)}, bf16[64,2048]{1,0:T(8,128)(2,1)S(1)}, u32[]{:S(2)}, u32[]{:S(2)}) collective-permute-start(bf16[64,2048]{1,0:T(8,128)(2,1)S(1)} %collective-permute-done.2.refs_1_), channel_id=1, source_target_pairs={{0,448},{1,449},{2,450},{3,451},{4,452},{5,453},{6,454},{7,455},{8... | collective-permute-start | bytes 786440 | tf_op jit(solution)/shard_map/ppermute | solution.py:157
  56.4 18.0 %collective-permute-start.5 = (bf16[64,2048]{1,0:T(8,128)(2,1)S(1)}, bf16[64,2048]{1,0:T(8,128)(2,1)S(1)}, u32[]{:S(2)}, u32[]{:S(2)}) collective-permute-start(bf16[64,2048]{1,0:T(8,128)(2,1)S(1)} %collective-permute-done.refs_0_), channel_id=1, source_target_pairs={{0,448},{1,449},{2,450},{3,451},{4,452},{5,453},{6,454},{7,455},{8... | collective-permute-start | bytes 786440 | tf_op jit(solution)/shard_map/ppermute | solution.py:157
  65.4 13.0 %collective-permute-start.4 = (bf16[64,2048]{1,0:T(8,128)(2,1)S(1)}, bf16[64,2048]{1,0:T(8,128)(2,1)S(1)}, u32[]{:S(2)}, u32[]{:S(2)}) collective-permute-start(bf16[64,2048]{1,0:T(8,128)(2,1)S(1)} %collective-permute-done.2.refs_1_), channel_id=1, source_target_pairs={{0,64},{1,65},{2,66},{3,67},{4,68},{5,69},{6,70},{7,71},{8,72},{9,... | collective-permute-start | bytes 786440 | tf_op jit(solution)/shard_map/ppermute | solution.py:157
  67.3 39.5 %copy-start.2 = (bf16[64,2048]{1,0:T(8,128)(2,1)}, bf16[64,2048]{1,0:T(8,128)(2,1)S(1)}, u32[]{:S(2)}) copy-start(bf16[64,2048]{1,0:T(8,128)(2,1)S(1)} %collective-permute-done.3.refs_2_) | copy-start | bytes 786436
  67.3 14.3 %collective-permute-start.7 = (bf16[64,2048]{1,0:T(8,128)(2,1)S(1)}, bf16[64,2048]{1,0:T(8,128)(2,1)S(1)}, u32[]{:S(2)}, u32[]{:S(2)}) collective-permute-start(bf16[64,2048]{1,0:T(8,128)(2,1)S(1)} %collective-permute-done.3.refs_2_), channel_id=1, source_target_pairs={{0,64},{1,65},{2,66},{3,67},{4,68},{5,69},{6,70},{7,71},{8,72},{9,... | collective-permute-start | bytes 786440 | tf_op jit(solution)/shard_map/ppermute | solution.py:157
  69.3 37.6 %copy-start.3 = (bf16[64,2048]{1,0:T(8,128)(2,1)}, bf16[64,2048]{1,0:T(8,128)(2,1)S(1)}, u32[]{:S(2)}) copy-start(bf16[64,2048]{1,0:T(8,128)(2,1)S(1)} %collective-permute-done.6.refs_5_) | copy-start | bytes 786436
  69.3 14.3 %collective-permute-start.10 = (bf16[64,2048]{1,0:T(8,128)(2,1)S(1)}, bf16[64,2048]{1,0:T(8,128)(2,1)S(1)}, u32[]{:S(2)}, u32[]{:S(2)}) collective-permute-start(bf16[64,2048]{1,0:T(8,128)(2,1)S(1)} %collective-permute-done.6.refs_5_), channel_id=1, source_target_pairs={{0,448},{1,449},{2,450},{3,451},{4,452},{5,453},{6,454},{7,455},{8... | collective-permute-start | bytes 786440 | tf_op jit(solution)/shard_map/ppermute | solution.py:157
  74.4 32.5 %copy-start.4 = (bf16[64,2048]{1,0:T(8,128)(2,1)}, bf16[64,2048]{1,0:T(8,128)(2,1)S(1)}, u32[]{:S(2)}) copy-start(bf16[64,2048]{1,0:T(8,128)(2,1)S(1)} %collective-permute-done.5.refs_4_) | copy-start | bytes 786436
  74.4 14.3 %collective-permute-start.9 = (bf16[64,2048]{1,0:T(8,128)(2,1)S(1)}, bf16[64,2048]{1,0:T(8,128)(2,1)S(1)}, u32[]{:S(2)}, u32[]{:S(2)}) collective-permute-start(bf16[64,2048]{1,0:T(8,128)(2,1)S(1)} %collective-permute-done.5.refs_4_), channel_id=1, source_target_pairs={{0,448},{1,449},{2,450},{3,451},{4,452},{5,453},{6,454},{7,455},{8... | collective-permute-start | bytes 786440 | tf_op jit(solution)/shard_map/ppermute | solution.py:157
  78.4 28.5 %copy-start.5 = (bf16[64,2048]{1,0:T(8,128)(2,1)}, bf16[64,2048]{1,0:T(8,128)(2,1)S(1)}, u32[]{:S(2)}) copy-start(bf16[64,2048]{1,0:T(8,128)(2,1)S(1)} %collective-permute-done.4.refs_3_) | copy-start | bytes 786436
  78.4 13.0 %collective-permute-start.8 = (bf16[64,2048]{1,0:T(8,128)(2,1)S(1)}, bf16[64,2048]{1,0:T(8,128)(2,1)S(1)}, u32[]{:S(2)}, u32[]{:S(2)}) collective-permute-start(bf16[64,2048]{1,0:T(8,128)(2,1)S(1)} %collective-permute-done.4.refs_3_), channel_id=1, source_target_pairs={{0,64},{1,65},{2,66},{3,67},{4,68},{5,69},{6,70},{7,71},{8,72},{9,... | collective-permute-start | bytes 786440 | tf_op jit(solution)/shard_map/ppermute | solution.py:157
  81.7 25.2 %copy-start.6 = (bf16[64,2048]{1,0:T(8,128)(2,1)}, bf16[64,2048]{1,0:T(8,128)(2,1)S(1)}, u32[]{:S(2)}) copy-start(bf16[64,2048]{1,0:T(8,128)(2,1)S(1)} %collective-permute-done.7.refs_6_) | copy-start | bytes 786436
  81.7 13.0 %collective-permute-start.11 = (bf16[64,2048]{1,0:T(8,128)(2,1)S(1)}, bf16[64,2048]{1,0:T(8,128)(2,1)S(1)}, u32[]{:S(2)}, u32[]{:S(2)}) collective-permute-start(bf16[64,2048]{1,0:T(8,128)(2,1)S(1)} %collective-permute-done.7.refs_6_), channel_id=1, source_target_pairs={{0,64},{1,65},{2,66},{3,67},{4,68},{5,69},{6,70},{7,71},{8,72},{9,... | collective-permute-start | bytes 786440 | tf_op jit(solution)/shard_map/ppermute | solution.py:157
  83.6 23.3 %copy-start.7 = (bf16[64,2048]{1,0:T(8,128)(2,1)}, bf16[64,2048]{1,0:T(8,128)(2,1)S(1)}, u32[]{:S(2)}) copy-start(bf16[64,2048]{1,0:T(8,128)(2,1)S(1)} %collective-permute-done.10.refs_9_) | copy-start | bytes 786436
  83.6 13.0 %collective-permute-start.14 = (bf16[64,2048]{1,0:T(8,128)(2,1)S(1)}, bf16[64,2048]{1,0:T(8,128)(2,1)S(1)}, u32[]{:S(2)}, u32[]{:S(2)}) collective-permute-start(bf16[64,2048]{1,0:T(8,128)(2,1)S(1)} %collective-permute-done.10.refs_9_), channel_id=1, source_target_pairs={{0,448},{1,449},{2,450},{3,451},{4,452},{5,453},{6,454},{7,455},{8... | collective-permute-start | bytes 786440 | tf_op jit(solution)/shard_map/ppermute | solution.py:157
  88.8 18.2 %copy-start.8 = (bf16[64,2048]{1,0:T(8,128)(2,1)}, bf16[64,2048]{1,0:T(8,128)(2,1)S(1)}, u32[]{:S(2)}) copy-start(bf16[64,2048]{1,0:T(8,128)(2,1)S(1)} %collective-permute-done.9.refs_8_) | copy-start | bytes 786436
  88.8 13.0 %collective-permute-start.13 = (bf16[64,2048]{1,0:T(8,128)(2,1)S(1)}, bf16[64,2048]{1,0:T(8,128)(2,1)S(1)}, u32[]{:S(2)}, u32[]{:S(2)}) collective-permute-start(bf16[64,2048]{1,0:T(8,128)(2,1)S(1)} %collective-permute-done.9.refs_8_), channel_id=1, source_target_pairs={{0,448},{1,449},{2,450},{3,451},{4,452},{5,453},{6,454},{7,455},{8... | collective-permute-start | bytes 786440 | tf_op jit(solution)/shard_map/ppermute | solution.py:157
  91.4 15.5 %copy-start.9 = (bf16[64,2048]{1,0:T(8,128)(2,1)}, bf16[64,2048]{1,0:T(8,128)(2,1)S(1)}, u32[]{:S(2)}) copy-start(bf16[64,2048]{1,0:T(8,128)(2,1)S(1)} %collective-permute-done.8.refs_7_) | copy-start | bytes 786436
  91.4 11.9 %collective-permute-start.12 = (bf16[64,2048]{1,0:T(8,128)(2,1)S(1)}, bf16[64,2048]{1,0:T(8,128)(2,1)S(1)}, u32[]{:S(2)}, u32[]{:S(2)}) collective-permute-start(bf16[64,2048]{1,0:T(8,128)(2,1)S(1)} %collective-permute-done.8.refs_7_), channel_id=1, source_target_pairs={{0,64},{1,65},{2,66},{3,67},{4,68},{5,69},{6,70},{7,71},{8,72},{9,... | collective-permute-start | bytes 786440 | tf_op jit(solution)/shard_map/ppermute | solution.py:157
  94.7 12.3 %copy-start.10 = (bf16[64,2048]{1,0:T(8,128)(2,1)}, bf16[64,2048]{1,0:T(8,128)(2,1)S(1)}, u32[]{:S(2)}) copy-start(bf16[64,2048]{1,0:T(8,128)(2,1)S(1)} %collective-permute-done.11.refs_10_) | copy-start | bytes 786436
  94.7 11.4 %collective-permute-start.15 = (bf16[64,2048]{1,0:T(8,128)(2,1)S(1)}, bf16[64,2048]{1,0:T(8,128)(2,1)S(1)}, u32[]{:S(2)}, u32[]{:S(2)}) collective-permute-start(bf16[64,2048]{1,0:T(8,128)(2,1)S(1)} %collective-permute-done.11.refs_10_), channel_id=1, source_target_pairs={{0,64},{1,65},{2,66},{3,67},{4,68},{5,69},{6,70},{7,71},{8,72},{9,... | collective-permute-start | bytes 786440 | tf_op jit(solution)/shard_map/ppermute | solution.py:157
  96.6 10.3 %copy-start.11 = (bf16[64,2048]{1,0:T(8,128)(2,1)}, bf16[64,2048]{1,0:T(8,128)(2,1)S(1)}, u32[]{:S(2)}) copy-start(bf16[64,2048]{1,0:T(8,128)(2,1)S(1)} %collective-permute-done.14.refs_13_) | copy-start | bytes 786436
  96.6 10.2 %collective-permute-start.16 = (bf16[64,2048]{1,0:T(8,128)(2,1)S(1)}, bf16[64,2048]{1,0:T(8,128)(2,1)}, u32[]{:S(2)}, u32[]{:S(2)}) collective-permute-start(bf16[64,2048]{1,0:T(8,128)(2,1)S(1)} %collective-permute-done.14.refs_13_), channel_id=1, source_target_pairs={{0,448},{1,449},{2,450},{3,451},{4,452},{5,453},{6,454},{7,455},{8... | collective-permute-start | bytes 786440 | tf_op jit(solution)/shard_map/ppermute | solution.py:157
  101.8 5.2 %copy-start.12 = (bf16[64,2048]{1,0:T(8,128)(2,1)}, bf16[64,2048]{1,0:T(8,128)(2,1)S(1)}, u32[]{:S(2)}) copy-start(bf16[64,2048]{1,0:T(8,128)(2,1)S(1)} %collective-permute-done.13.refs_12_) | copy-start | bytes 786436
  103.3 2.8 %copy-start.13 = (bf16[64,2048]{1,0:T(8,128)(2,1)}, bf16[64,2048]{1,0:T(8,128)(2,1)S(1)}, u32[]{:S(2)}) copy-start(bf16[64,2048]{1,0:T(8,128)(2,1)S(1)} %collective-permute-done.12.refs_11_) | copy-start | bytes 786436
  106.1 0.7 copy-start.14
  113.5 14.5 %collective-permute-start.17 = (bf16[512,512]{1,0:T(8,128)(2,1)}, bf16[512,512]{1,0:T(8,128)(2,1)S(1)}, u32[]{:S(2)}, u32[]{:S(2)}) collective-permute-start(bf16[512,512]{1,0:T(8,128)(2,1)} %shard_map.29), channel_id=1, source_target_pairs={{0,1},{1,0},{2,3},{3,2},{4,5},{5,4},{6,7},{7,6},{8,9},{9,8},{10,11... | collective-permute-start | bytes 1572872 | tf_op jit(solution)/shard_map/ppermute | solution.py:157
Sparse Core Ops, SparseCore 0:
  23.7 67.5 all-gather.1
